TPU v7x, 32 devices: a whole 2x2x4 slice. The times are simulated.
32 devices in a mesh: seq: 16 (over z, x, core), head: 2 (over y).
Axes of the slice: x: 2, y: 2, z: 4, core: 2. Of those that a mesh axis runs over, the one named last changes fastest.
Arguments:
- queries: bfloat16 [2048, 2560], P('seq', 'head'), may hold values from -6 to 6
- keys: bfloat16 [2048, 2560], P('seq', 'head'), may hold values from -6 to 6
- values: bfloat16 [2048, 2560], P('seq', 'head'), may hold values from -6 to 6
- grad_out: bfloat16 [2048, 2560], P('seq', 'head'), may hold values from -6 to 6
- cache: bfloat16 [2048, 2560], P('seq', 'head'), may hold values from -6 to 6
- w_kv: bfloat16 [2, 2560, 2560], P(None, 'seq', 'head'), may hold values from -0.125 to 0.125
- doc_ids: int32 [2048], replicated, may hold values from 0 to 15, never falling along the last dimension, each value on 1 to 256 neighbouring positions
- routes: int32 [2048], replicated, may hold values from 0 to 15, as said below
Outputs:
- output: bfloat16 [2048, 2560], P('seq', 'head')
- grad_q: bfloat16 [2048, 2560], P('seq', 'head')
- grad_k: bfloat16 [2048, 2560], P('seq', 'head')
- grad_v: bfloat16 [2048, 2560], P('seq', 'head')
Inputs may be any that keep to these rules, and one draw needn't show every extreme that they name: `routes`: each device's aligned block of 128 rows names every destination at most 16 times; in every draw some destination is named exactly 16 times by every block.
All inputs are finite; a program needn't handle non-finite values.
Results may differ from a plain program's by a relative error of at most 0.03.
Values may be sent and summed in bfloat16 or wider, within the bound.
No kernel may reach another device: no remote copies, remote signals or barrier semaphores. Data moves between devices by JAX's collectives and lax.ppermute only.
A program may use at most 128 MiB of HBM per device.

v0:
```python
import jax
import jax.numpy as jnp
from jax import lax
from jax.experimental import pallas as pl
from jax.experimental.pallas import tpu as pltpu
from jax.sharding import Mesh, PartitionSpec as P

HD = 128
GROUPS = 4
SEQ = ("z", "p")
ROW_TILE = 16
RING = [0, 1, 3, 2]
VMEM = 24 * 1024 * 1024
SMALL_VMEM = 4 * 1024 * 1024
STATS = 16


def shifted(value, by):
    length = lax.axis_size("z") * lax.axis_size("p")
    pairs = [(i, i + by) for i in range(length) if 0 <= i + by < length]
    return lax.ppermute(value, SEQ, pairs)


def swapped(value, axis, mask):
    return lax.ppermute(value, axis, [(i, i ^ mask) for i in range(lax.axis_size(axis))])


def in_vmem(*arrays):
    return [pltpu.with_memory_space_constraint(array, pltpu.VMEM) for array in arrays]


def dot_t(a, b, dims):
    return lax.dot_general(a, b, (dims, ((), ())), preferred_element_type=jnp.float32)


def attend_kernel(
    q_ref, g_ref, k_ref, v_ref, kv1_ref, kv2_ref, mem_ref, bias_ref, out_ref, gq_ref, stats_ref
):
    rows, width = q_ref.shape
    scaling = HD ** (-0.5)
    bias = bias_ref[...]
    step = pl.program_id(0)
    heads = [slice(i * HD, (i + 1) * HD) for i in range(width // HD)]
    picked = [pl.ds(pl.multiple_of(step * width + i * HD, HD), HD) for i in range(len(heads))]
    ks, vs = (
        [
            jnp.concatenate(
                [
                    mem_ref[2 * step + which, :, cols],
                    kv2_ref[which, :, wide],
                    kv1_ref[which, :, wide],
                    own_ref[:, cols],
                ],
                0,
            )
            for cols, wide in zip(heads, picked)
        ]
        for which, own_ref in enumerate((k_ref, v_ref))
    )
    scores = [dot_t(q_ref[:, cols], kh, ((1,), (1,))) + bias for cols, kh in zip(heads, ks)]
    dprobs = [dot_t(g_ref[:, cols], vh, ((1,), (1,))) for cols, vh in zip(heads, vs)]
    tops, shares, probs = [], [], []
    for score in scores:
        top = jnp.max(score, axis=-1, keepdims=True)
        weights = jnp.exp((score - top) * scaling)
        share = 1.0 / jnp.sum(weights, axis=-1, keepdims=True)
        tops.append(top)
        shares.append(share)
        probs.append(weights * share)
    outs = [
        dot_t(prob.astype(jnp.bfloat16), vh, ((1,), (0,))).astype(jnp.bfloat16)
        for prob, vh in zip(probs, vs)
    ]
    deltas, dscores = [], []
    for cols, out_b, prob, dprob in zip(heads, outs, probs, dprobs):
        out_ref[:, cols] = out_b
        delta = jnp.sum(
            g_ref[:, cols].astype(jnp.float32) * out_b.astype(jnp.float32), axis=-1, keepdims=True
        )
        deltas.append(delta)
        dscores.append((prob * ((dprob - delta) * scaling)).astype(jnp.bfloat16))
    lane = lax.broadcasted_iota(jnp.int32, (rows, HD), 1)
    stats = jnp.zeros((rows, HD), jnp.float32)
    for i, column in enumerate(tops + shares + deltas):
        stats = jnp.where(lane == i, column, stats)
    stats_ref[0] = stats.T[:STATS]
    for cols, kh, dscore in zip(heads, ks, dscores):
        gq_ref[:, cols] = dot_t(dscore, kh, ((1,), (0,))).astype(jnp.bfloat16)


def attend(queries, grad_out, keys, values, kv1, kv2, memory, bias):
    rows, features = queries.shape
    steps = memory.shape[0] // 2
    slots, block = memory.shape[1:]
    heads = steps * block // HD
    flat = pl.BlockSpec((rows, block), lambda i: (0, i))
    whole = pl.BlockSpec(memory_space=pltpu.VMEM)
    keys_all = slots + 3 * rows
    return pl.pallas_call(
        attend_kernel,
        grid=(steps,),
        in_specs=[
            flat, flat, flat, flat, whole, whole, whole, whole,
        ],
        out_specs=[flat, flat, pl.BlockSpec((1, STATS, rows), lambda i: (i, 0, 0))],
        out_shape=[
            jax.ShapeDtypeStruct((rows, features), jnp.bfloat16),
            jax.ShapeDtypeStruct((rows, features), jnp.bfloat16),
            jax.ShapeDtypeStruct((steps, STATS, rows), jnp.float32),
        ],
        compiler_params=pltpu.CompilerParams(vmem_limit_bytes=VMEM),
        cost_estimate=pl.CostEstimate(
            flops=2 * 4 * rows * keys_all * HD * heads,
            bytes_accessed=6 * 1024 * 1024,
            transcendentals=rows * keys_all * heads,
        ),
        name="attend",
    )(queries, grad_out, keys, values, *in_vmem(kv1, kv2, memory, bias))


def key_grads_kernel(
    k_ref, v_ref, q_ref, g_ref, qg1_ref, qg2_ref, st0_ref, st1_ref, st2_ref, bias_ref,
    gk_ref, gv_ref,
):
    width = k_ref.shape[1]
    scaling = HD ** (-0.5)
    bias = bias_ref[...]
    heads = [slice(i * HD, (i + 1) * HD) for i in range(width // HD)]
    start = pl.program_id(0) * width
    picked = [pl.ds(pl.multiple_of(start + i * HD, HD), HD) for i in range(len(heads))]
    stats = jnp.concatenate([st0_ref[0], st1_ref[0], st2_ref[0]], 1)
    qs = [
        jnp.concatenate([q_ref[:, cols], qg1_ref[0, :, wide], qg2_ref[0, :, wide]], 0)
        for cols, wide in zip(heads, picked)
    ]
    gs = [
        jnp.concatenate([g_ref[:, cols], qg1_ref[1, :, wide], qg2_ref[1, :, wide]], 0)
        for cols, wide in zip(heads, picked)
    ]
    scores = [dot_t(k_ref[:, cols], qh, ((1,), (1,))) + bias for cols, qh in zip(heads, qs)]
    dprobs = [dot_t(v_ref[:, cols], gh, ((1,), (1,))) for cols, gh in zip(heads, gs)]
    probs, dscores = [], []
    for i, (score, dprob) in enumerate(zip(scores, dprobs)):
        top, share, delta = (stats[i + j * len(heads) : i + j * len(heads) + 1] for j in range(3))
        prob = jnp.exp((score - top) * scaling) * share
        probs.append(prob.astype(jnp.bfloat16))
        dscores.append((prob * ((dprob - delta) * scaling)).astype(jnp.bfloat16))
    for cols, qh, gh, prob, dscore in zip(heads, qs, gs, probs, dscores):
        gk_ref[:, cols] = dot_t(dscore, qh, ((1,), (0,))).astype(jnp.bfloat16)
        gv_ref[:, cols] = dot_t(prob, gh, ((1,), (0,))).astype(jnp.bfloat16)


def key_grads(keys, values, queries, grad_out, qg1, qg2, stats, bias):
    rows, features = keys.shape
    steps = stats[0].shape[0]
    block = features // steps
    flat = pl.BlockSpec((rows, block), lambda i: (0, i))
    whole = pl.BlockSpec(memory_space=pltpu.VMEM)
    stat = pl.BlockSpec((1, STATS, rows), lambda i: (i, 0, 0))
    heads = features // HD
    return pl.pallas_call(
        key_grads_kernel,
        grid=(steps,),
        in_specs=[
            flat, flat, flat, flat, whole, whole, stat, stat, stat, whole,
        ],
        out_specs=[flat, flat],
        out_shape=[jax.ShapeDtypeStruct((rows, features), jnp.bfloat16)] * 2,
        compiler_params=pltpu.CompilerParams(vmem_limit_bytes=VMEM),
        cost_estimate=pl.CostEstimate(
            flops=2 * 4 * rows * 3 * rows * HD * heads,
            bytes_accessed=4 * 1024 * 1024,
            transcendentals=rows * 3 * rows * heads,
        ),
        name="key_grads",
    )(keys, values, queries, grad_out, *in_vmem(qg1, qg2), *stats, *in_vmem(bias))


def project_kernel(place_ref, *refs):
    n_z, _, cache_rows = place_ref.shape
    out_ref, w_ref, a_ref = refs[-3:]
    rows, pieces = refs[: 2 * n_z], refs[2 * n_z : -3]
    n_p, (_, w_rows, block) = len(pieces), pieces[0].shape
    depth = rows[0].shape[1]
    devices, _, capacity, _ = out_ref.shape
    z, p, y = (lax.axis_index(name) for name in ("z", "p", "head"))
    place_in_ring = z ^ (z >> 1)
    for i, ref in enumerate(rows):
        source = (place_in_ring - i % n_z + n_z) & (n_z - 1)
        a_ref[y ^ (i // n_z), source ^ (source >> 1)] = ref[...]
    for m in range(n_p):
        for k in range(n_z):
            w_ref[z ^ k, p ^ m] = pieces[m][k]
    half = n_z // 2
    proj = sum(
        jnp.dot(
            a_ref[i].reshape(n_z * cache_rows, depth),
            w_ref[i * half : (i + 1) * half].reshape(depth, block),
            preferred_element_type=jnp.float32,
        )
        for i in range(2)
    ).astype(jnp.bfloat16)
    slot_ids = lax.broadcasted_iota(jnp.int32, (devices * capacity, cache_rows), 0)
    for z in range(n_z):
        chosen = jnp.where(slot_ids == place_ref[z], 1.0, 0.0).astype(jnp.bfloat16)
        slots = jnp.dot(
            chosen,
            proj[z * cache_rows : (z + 1) * cache_rows],
            preferred_element_type=jnp.float32,
        ).astype(jnp.bfloat16)
        out_ref[:, z] = slots.reshape(devices, capacity, block)


def project(place, rows, pieces, devices, capacity):
    n_z, _, cache_rows = place.shape
    depth = rows[0].shape[1]
    n_p = len(pieces)
    _, w_rows, block = pieces[0].shape
    whole = pl.BlockSpec(memory_space=pltpu.VMEM)
    return pl.pallas_call(
        project_kernel,
        in_specs=[whole] * (1 + len(rows) + n_p),
        out_specs=whole,
        out_shape=pltpu.VMEM((devices, n_z, capacity, block), jnp.bfloat16),
        scratch_shapes=[
            pltpu.VMEM((n_z, n_p, w_rows, block), jnp.bfloat16),
            pltpu.VMEM((2, n_z, cache_rows, depth), jnp.bfloat16),
        ],
        compiler_params=pltpu.CompilerParams(vmem_limit_bytes=VMEM),
        cost_estimate=pl.CostEstimate(
            flops=4 * n_z * cache_rows * depth * block,
            bytes_accessed=8 * 1024 * 1024,
            transcendentals=0,
        ),
        name="project",
    )(*in_vmem(place, *rows, *pieces))


def prepare_kernel(routes_ref, ids_ref, place_ref, bias_ref, back_ref):
    n_z, _, rows = place_ref.shape
    devices = routes_ref.shape[0]
    n_p = devices // n_z
    capacity = 2 * rows // devices
    slots = bias_ref.shape[1] - 3 * rows
    p = lax.axis_index("p")
    me = lax.axis_index("z") * n_p + p
    row = lax.broadcasted_iota(jnp.int32, (rows, rows), 0)
    lane = lax.broadcasted_iota(jnp.int32, (rows, rows), 1)

    def both_ways(line):
        wide = jnp.broadcast_to(line.astype(jnp.float32), (rows, rows))
        return wide, wide.T

    for z in range(n_z):
        across, down = both_ways(routes_ref[pl.ds(z * n_p + p, 1), :])
        ranks = jnp.sum(
            jnp.where((across == down) & (row < lane), 1.0, 0.0), axis=0, keepdims=True
        )
        place_ref[z] = (across[:1] * capacity + ranks).astype(jnp.int32)

    def ids_of(segment):
        return ids_ref[pl.ds(jnp.clip(segment, 0, devices - 1), 1), :].astype(jnp.float32)

    _, own = both_ways(ids_ref[pl.ds(me, 1), :])
    for i in range(3):
        earlier, later = me - 2 + i, me + i
        same = (own == ids_of(earlier)) & (earlier >= 0)
        same_back = (own == ids_of(later)) & (later < devices)
        if i == 2:
            same = same & (lane <= row)
        if i == 0:
            same_back = same_back & (lane >= row)
        bias_ref[:, slots + i * rows : slots + (i + 1) * rows] = jnp.where(same, 0.0, -1e30)
        back_ref[:, i * rows : (i + 1) * rows] = jnp.where(same_back, 0.0, -1e30)

    mine = jnp.where(routes_ref[...] == me, 1.0, 0.0).astype(jnp.bfloat16)
    counts = dot_t(jnp.ones((8, rows), jnp.bfloat16), mine, ((1,), (1,))).astype(jnp.bfloat16)
    source = lax.broadcasted_iota(jnp.int32, (devices, slots), 0)
    slot = lax.broadcasted_iota(jnp.int32, (devices, slots), 1) // capacity
    expand = jnp.where(source == (slot % n_z) * n_p + slot // n_z, 1.0, 0.0).astype(jnp.bfloat16)
    filled = jnp.dot(counts, expand, preferred_element_type=jnp.float32)[:1]
    rank = lax.broadcasted_iota(jnp.int32, (1, slots), 1) % capacity
    live = jnp.where(rank.astype(jnp.float32) < filled, 0.0, -1e30)
    bias_ref[:, :slots] = jnp.broadcast_to(live, (rows, slots))


def prepare(routes, doc_ids, n_z, devices, rows):
    slots = 2 * rows
    return pl.pallas_call(
        prepare_kernel,
        out_shape=[
            jax.ShapeDtypeStruct((n_z, 1, rows), jnp.int32),
            jax.ShapeDtypeStruct((rows, slots + 3 * rows), jnp.float32),
            jax.ShapeDtypeStruct((rows, 3 * rows), jnp.float32),
        ],
        compiler_params=pltpu.CompilerParams(vmem_limit_bytes=SMALL_VMEM),
        name="prepare",
    )(routes.reshape(devices, rows), doc_ids.reshape(devices, rows))


def column_block(w_kv, target):
    _, w_rows, features = w_kv.shape
    half = features // (GROUPS // 2)
    start = (target & 1, 0, (target >> 1) * half)
    return lax.dynamic_slice(w_kv, start, (1, w_rows, half))[0]


def ring_step(value):
    return lax.ppermute(value, "z", [(a, b) for a, b in zip(RING, RING[1:] + RING[:1])])


def memory_slots(cache, w_kv, place, capacity, stream, back):
    n_z, n_p = lax.axis_size("z"), lax.axis_size("p")
    devices = n_z * n_p
    cache_rows, depth = cache.shape
    _, w_rows, features = w_kv.shape
    z = lax.axis_index("z")
    if n_p == 4 and capacity % ROW_TILE == 0 and w_rows % ROW_TILE == 0:
        blocks = [column_block(w_kv, z ^ mask) for mask in range(n_z)]
        own = jnp.stack(
            [blocks[0]] + [swapped(blocks[mask], "z", mask) for mask in range(1, n_z)], 0
        )
        row1, other0 = ring_step(cache), swapped(cache, "head", 1)
        own, row1, other0, stream = lax.optimization_barrier((own, row1, other0, stream))
        across = swapped(own, "p", 2)
        beside = swapped(own, "p", 1)
        row2, other1 = ring_step(row1), swapped(row1, "head", 1)
        row2, other1, beside, stream, back = lax.optimization_barrier(
            (row2, other1, beside, stream, back)
        )
        row3, other2 = ring_step(row2), swapped(row2, "head", 1)
        near, back1 = shifted(stream, 1), shifted(back, -1)
        across, row3, other2, near, back1 = lax.optimization_barrier(
            (across, row3, other2, near, back1)
        )
        pieces = [own, beside, across, swapped(across, "p", 1)]
        rows = [cache, row1, row2, row3, other0, other1, other2, swapped(row3, "head", 1)]
        slots = project(place, rows, pieces, devices, capacity)
        return slots, near, back1
    near = shifted(stream, 1)
    back1 = shifted(back, -1)
    targets = [column_block(w_kv, jnp.int32(i)) for i in range(n_z)]
    w_z = lax.all_to_all(jnp.stack(targets, 0), "z", split_axis=0, concat_axis=0, tiled=True)
    w_all = lax.all_gather(w_z, "p", axis=1, tiled=True).reshape(devices * w_rows, -1)
    rows = lax.all_gather(cache, ("head", "z"), axis=0, tiled=False)
    rows = rows.reshape(-1, n_z * cache_rows, depth)
    proj = sum(
        jnp.dot(
            rows[i], w_all[i * depth : (i + 1) * depth], preferred_element_type=jnp.float32
        )
        for i in range(rows.shape[0])
    ).astype(jnp.bfloat16)
    slot_ids = jnp.arange(devices * capacity, dtype=jnp.int32)
    chosen = (slot_ids[None, :, None] == place).astype(jnp.bfloat16)
    slots = jnp.einsum(
        "zsi,zic->zsc",
        chosen,
        proj.reshape(n_z, cache_rows, -1),
        preferred_element_type=jnp.float32,
    ).astype(jnp.bfloat16)
    return slots.reshape(n_z, devices, capacity, -1).transpose(1, 0, 2, 3), near, back1


def body(queries, keys, values, grad_out, cache, w_kv, doc_ids, routes):
    n_z, n_p = lax.axis_size("z"), lax.axis_size("p")
    devices = n_z * n_p
    seg_rows = queries.shape[0]
    cache_rows = cache.shape[0]
    capacity = 2 * cache_rows // devices
    slot_count = capacity * devices

    place, bias, back_bias = prepare(routes, doc_ids, n_z, devices, seg_rows)
    slots, kv1, qg1 = memory_slots(
        cache,
        w_kv,
        place,
        capacity,
        jnp.stack([keys, values], 0),
        jnp.stack([queries, grad_out], 0),
    )
    kv2, qg2 = shifted(kv1, 1), shifted(qg1, -1)
    memory = lax.all_to_all(slots, SEQ, split_axis=0, concat_axis=0, tiled=True)
    memory = memory.reshape(n_z, slot_count, slots.shape[-1])

    qg2, bias = lax.optimization_barrier((qg2, bias))

    output, grad_q, stats = attend(queries, grad_out, keys, values, kv1, kv2, memory, bias)
    all_stats = [stats, shifted(stats, -1), shifted(stats, -2)]
    grad_k, grad_v = key_grads(
        keys, values, queries, grad_out, qg1, qg2, all_stats, back_bias
    )
    return (output, grad_q, grad_k, grad_v)


def solution(mesh):
    n_seq, n_head = mesh.devices.shape
    grid = Mesh(mesh.devices.reshape(GROUPS, n_seq // GROUPS, n_head), ("z", "p", "head"))
    rows = P(SEQ, "head")
    return jax.shard_map(
        body,
        mesh=grid,
        in_specs=(rows, rows, rows, rows, rows, P(None, SEQ, "head"), P(), P()),
        out_specs=(rows, rows, rows, rows),
        check_vma=False,
    )
```

profile of v0, /device:TPU:16, one launch (start us, length us, event | category | flops | bytes accessed | tf_op | source)
XLA Modules:
  0.0 143.8 jit_solution(17159207916536948837)
XLA Ops:
  0.6 0.0 copy-start.2
  0.6 0.0 copy-start.3
  0.7 0.1 collective-permute-start.3
  0.7 1.8 %collective-permute-start.4 = (bf16[128,1280]{1,0:T(8,128)(2,1)}, bf16[128,1280]{1,0:T(8,128)(2,1)S(1)}, u32[]{:S(2)}, u32[]{:S(2)}) collective-permute-start(bf16[128,1280]{1,0:T(8,128)(2,1)} %refs_0_.1), channel_id=1, source_target_pairs={{0,1},{1,0},{2,3},{3,2},{4,5},{5,4},{6,7},{7,6},{8,9},{9,8},{10,11... | collective-permute-start | bytes 983048 | tf_op jit(solution)/shard_map/ppermute | solution.py:25
  2.6 1.3 constant_dynamic-slice_fusion
  3.9 1.8 %collective-permute-start = (bf16[160,640]{1,0:T(8,128)(2,1)S(1)}, bf16[160,640]{1,0:T(8,128)(2,1)S(1)}, u32[]{:S(2)}, u32[]{:S(2)}) collective-permute-start(bf16[160,640]{1,0:T(8,128)(2,1)S(1)} %get-tuple-element.53), channel_id=1, source_target_pairs={{0,8},{8,0},{16,24},{24,16},{1,9},{9,1},{17,25},{25,17},{2,10},{10... | collective-permute-start | bytes 614408 | tf_op jit(solution)/shard_map/ppermute | solution.py:25
  5.6 2.5 %collective-permute-start.1 = (bf16[160,640]{1,0:T(8,128)(2,1)S(1)}, bf16[160,640]{1,0:T(8,128)(2,1)S(1)}, u32[]{:S(2)}, u32[]{:S(2)}) collective-permute-start(bf16[160,640]{1,0:T(8,128)(2,1)S(1)} %get-tuple-element.55), channel_id=1, source_target_pairs={{0,16},{8,24},{16,0},{24,8},{1,17},{9,25},{17,1},{25,9},{2,18},{10... | collective-permute-start | bytes 614408 | tf_op jit(solution)/shard_map/ppermute | solution.py:25
  8.1 0.0 collective-permute-start.2
  8.1 0.0 copy-done.2
  8.1 0.0 copy-done.3
  8.1 0.0 copy-start
  8.1 0.0 copy-start.1
  8.1 0.1 pad_maximum_fusion.1
  8.2 10.7 %collective-permute-done = bf16[160,640]{1,0:T(8,128)(2,1)S(1)} collective-permute-done((bf16[160,640]{1,0:T(8,128)(2,1)S(1)}, bf16[160,640]{1,0:T(8,128)(2,1)S(1)}, u32[]{:S(2)}, u32[]{:S(2)}) %collective-permute-start) | collective-permute-done | bytes 204832 | tf_op jit(solution)/shard_map/ppermute | solution.py:25
  19.0 1.3 collective-permute-done.1
  20.3 8.7 %collective-permute-done.2 = bf16[160,640]{1,0:T(8,128)(2,1)S(1)} collective-permute-done((bf16[160,640]{1,0:T(8,128)(2,1)S(1)}, bf16[160,640]{1,0:T(8,128)(2,1)S(1)}, u32[]{:S(2)}, u32[]{:S(2)}) %collective-permute-start.2) | collective-permute-done | bytes 204832 | tf_op jit(solution)/shard_map/ppermute | solution.py:25
  29.0 0.1 pad_maximum_fusion.refs_8_
  29.1 0.0 collective-permute-done.3.refs_1_
  29.1 0.0 collective-permute-done.4.refs_4_
  29.1 0.1 collective-permute-start.8
  29.2 0.1 collective-permute-start.6
  29.3 1.6 %collective-permute-start.7 = (bf16[128,1280]{1,0:T(8,128)(2,1)S(1)}, bf16[128,1280]{1,0:T(8,128)(2,1)S(1)}, u32[]{:S(2)}, u32[]{:S(2)}) collective-permute-start(bf16[128,1280]{1,0:T(8,128)(2,1)S(1)} %collective-permute-done.3.refs_1_), channel_id=1, source_target_pairs={{0,1},{1,0},{2,3},{3,2},{4,5},{5,4},{6,7},{7,6},{8,9},{9,8},{10,11... | collective-permute-start | bytes 983048 | tf_op jit(solution)/shard_map/ppermute | solution.py:25
  30.9 1.5 %collective-permute-start.5 = (bf16[4,160,640]{2,1,0:T(8,128)(2,1)S(1)}, bf16[4,160,640]{2,1,0:T(8,128)(2,1)S(1)}, u32[]{:S(2)}, u32[]{:S(2)}) collective-permute-start(bf16[4,160,640]{2,1,0:T(8,128)(2,1)S(1)} %pad_maximum_fusion.refs_8_), channel_id=1, source_target_pairs={{0,4},{2,6},{4,0},{6,2},{1,5},{3,7},{5,1},{7,3},{8,12},{10,14},{12... | collective-permute-start | bytes 2457608 | tf_op jit(solution)/shard_map/ppermute | solution.py:25
  32.4 0.0 copy-done
  32.4 0.1 pad_maximum_fusion.2
  32.4 6.9 %collective-permute-done.6.refs_2_ = bf16[128,1280]{1,0:T(8,128)(2,1)S(1)} collective-permute-done((bf16[128,1280]{1,0:T(8,128)(2,1)S(1)}, bf16[128,1280]{1,0:T(8,128)(2,1)S(1)}, u32[]{:S(2)}, u32[]{:S(2)}) %collective-permute-start.6) | collective-permute-done | bytes 327712 | tf_op jit(solution)/shard_map/ppermute | solution.py:309
  39.3 0.0 collective-permute-done.7.refs_5_
  39.3 0.0 collective-permute-done.8.refs_9_
  39.3 1.9 %collective-permute-start.11 = (bf16[2,128,1280]{2,1,0:T(8,128)(2,1)S(1)}, bf16[2,128,1280]{2,1,0:T(8,128)(2,1)S(1)}, u32[]{:S(2)}, u32[]{:S(2)}) collective-permute-start(bf16[2,128,1280]{2,1,0:T(8,128)(2,1)S(1)} %pad_maximum_fusion.1), channel_id=1, source_target_pairs={{0,2},{2,4},{4,6},{6,8},{8,10},{10,12},{12,14},{14,16},{16,18},{18... | collective-permute-start | bytes 1966088 | tf_op jit(solution)/shard_map/ppermute | solution.py:21
  41.2 4.5 %collective-permute-start.12 = (bf16[2,128,1280]{2,1,0:T(8,128)(2,1)S(1)}, bf16[2,128,1280]{2,1,0:T(8,128)(2,1)S(1)}, u32[]{:S(2)}, u32[]{:S(2)}) collective-permute-start(bf16[2,128,1280]{2,1,0:T(8,128)(2,1)S(1)} %pad_maximum_fusion.2), channel_id=1, source_target_pairs={{2,0},{4,2},{6,4},{8,6},{10,8},{12,10},{14,12},{16,14},{18,16},{20... | collective-permute-start | bytes 1966088 | tf_op jit(solution)/shard_map/ppermute | solution.py:21
  45.8 1.6 %collective-permute-start.10 = (bf16[128,1280]{1,0:T(8,128)(2,1)S(1)}, bf16[128,1280]{1,0:T(8,128)(2,1)S(1)}, u32[]{:S(2)}, u32[]{:S(2)}) collective-permute-start(bf16[128,1280]{1,0:T(8,128)(2,1)S(1)} %collective-permute-done.6.refs_2_), channel_id=1, source_target_pairs={{0,1},{1,0},{2,3},{3,2},{4,5},{5,4},{6,7},{7,6},{8,9},{9,8},{10,11... | collective-permute-start | bytes 983048 | tf_op jit(solution)/shard_map/ppermute | solution.py:25
  47.4 0.0 collective-permute-start.9
  47.4 10.7 %collective-permute-done.5.refs_10_ = bf16[4,160,640]{2,1,0:T(8,128)(2,1)S(1)} collective-permute-done((bf16[4,160,640]{2,1,0:T(8,128)(2,1)S(1)}, bf16[4,160,640]{2,1,0:T(8,128)(2,1)S(1)}, u32[]{:S(2)}, u32[]{:S(2)}) %collective-permute-start.5) | collective-permute-done | bytes 819232 | tf_op jit(solution)/shard_map/ppermute | solution.py:25
  58.1 0.0 collective-permute-done.10.refs_6_
  58.1 4.6 %collective-permute-done.9.refs_3_ = bf16[128,1280]{1,0:T(8,128)(2,1)S(1)} collective-permute-done((bf16[128,1280]{1,0:T(8,128)(2,1)S(1)}, bf16[128,1280]{1,0:T(8,128)(2,1)S(1)}, u32[]{:S(2)}, u32[]{:S(2)}) %collective-permute-start.9) | collective-permute-done | bytes 327712 | tf_op jit(solution)/shard_map/ppermute | solution.py:309
  62.7 0.0 collective-permute-done.11.kv1_ref
  62.7 0.0 collective-permute-done.12.qg1_ref
  62.7 0.8 copy-done.6
  63.6 1.6 %collective-permute-start.15 = (bf16[4,160,640]{2,1,0:T(8,128)(2,1)S(1)}, bf16[4,160,640]{2,1,0:T(8,128)(2,1)S(1)}, u32[]{:S(2)}, u32[]{:S(2)}) collective-permute-start(bf16[4,160,640]{2,1,0:T(8,128)(2,1)S(1)} %collective-permute-done.5.refs_10_), channel_id=1, source_target_pairs={{0,2},{2,0},{4,6},{6,4},{1,3},{3,1},{5,7},{7,5},{8,10},{10,8},{12,... | collective-permute-start | bytes 2457608 | tf_op jit(solution)/shard_map/ppermute | solution.py:25
  65.1 0.5 collective-permute-start.14
  65.6 0.0 copy-done.14
  65.6 0.3 prepare.1
  65.9 0.0 copy-start.10
  65.9 0.7 copy-done.10
  66.6 8.1 %collective-permute-done.14.refs_7_ = bf16[128,1280]{1,0:T(8,128)(2,1)S(1)} collective-permute-done((bf16[128,1280]{1,0:T(8,128)(2,1)S(1)}, bf16[128,1280]{1,0:T(8,128)(2,1)S(1)}, u32[]{:S(2)}, u32[]{:S(2)}) %collective-permute-start.14) | collective-permute-done | bytes 327712 | tf_op jit(solution)/shard_map/ppermute | solution.py:25
  74.7 0.0 collective-permute-done.15.refs_11_
  74.7 4.6 %project.1 = bf16[16,4,16,640]{3,2,1,0:T(8,128)(2,1)} custom-call(s32[4,1,128]{2,1,0:T(1,128)S(1)} %get-tuple-element.35.place_ref, bf16[128,1280]{1,0:T(8,128)(2,1)S(1)} %copy-done.12, bf16[128,1280]{1,0:T(8,128)(2,1)S(1)} %collective-permute-done.3.refs_1_, bf16[128,1280]{1,0:T(8,128)(2,1)S(1)} %collective-permute-done.6.refs_2_, ...), custom_call_target="tpu_custom_call" | custom-call | flops 1677721600 | bytes 8388608 | tf_op jit(solution)/shard_map/project/pallas_call | solution.py:220
  79.3 6.5 %all-to-all-start = ((bf16[16,4,16,640]{3,2,1,0:T(8,128)(2,1)}), bf16[16,4,16,640]{3,2,1,0:T(8,128)(2,1)S(1)}, u32[]{:S(2)}, u32[]{:S(2)}) async-start(bf16[16,4,16,640]{3,2,1,0:T(8,128)(2,1)} %project.1), calls=%async_computation | async-start | bytes 2621440 | tf_op jit(solution)/shard_map/all_to_all | solution.py:382
  85.9 3.1 %collective-permute-start.16 = (bf16[2,128,1280]{2,1,0:T(8,128)(2,1)S(1)}, bf16[2,128,1280]{2,1,0:T(8,128)(2,1)S(1)}, u32[]{:S(2)}, u32[]{:S(2)}) collective-permute-start(bf16[2,128,1280]{2,1,0:T(8,128)(2,1)S(1)} %collective-permute-done.12.qg1_ref), channel_id=1, source_target_pairs={{2,0},{4,2},{6,4},{8,6},{10,8},{12,10},{14,12},{16,14},{18,16},{20... | collective-permute-start | bytes 1966088 | tf_op jit(solution)/shard_map/ppermute | solution.py:21
  89.0 1.9 %collective-permute-start.13 = (bf16[2,128,1280]{2,1,0:T(8,128)(2,1)}, bf16[2,128,1280]{2,1,0:T(8,128)(2,1)S(1)}, u32[]{:S(2)}, u32[]{:S(2)}) collective-permute-start(bf16[2,128,1280]{2,1,0:T(8,128)(2,1)} %copy-done.6), channel_id=1, source_target_pairs={{0,2},{2,4},{4,6},{6,8},{8,10},{10,12},{12,14},{14,16},{16,18},{18... | collective-permute-start | bytes 1966088 | tf_op jit(solution)/shard_map/ppermute | solution.py:21
  90.9 30.9 %collective-permute-done.16.qg2_ref = bf16[2,128,1280]{2,1,0:T(8,128)(2,1)S(1)} collective-permute-done((bf16[2,128,1280]{2,1,0:T(8,128)(2,1)S(1)}, bf16[2,128,1280]{2,1,0:T(8,128)(2,1)S(1)}, u32[]{:S(2)}, u32[]{:S(2)}) %collective-permute-start.16) | collective-permute-done | bytes 655392 | tf_op jit(solution)/shard_map/ppermute | solution.py:21
  121.9 0.8 copy-done.4
  122.7 1.1 collective-permute-done.13.kv2_ref
  123.8 0.8 copy-done.8
  124.6 0.0 all-to-all-done
  124.6 1.1 copy-done.7
  125.7 1.1 copy-done.9
  126.8 1.0 copy-done.11
  127.8 4.1 %attend.1 = (bf16[128,1280]{1,0:T(8,128)(2,1)}, bf16[128,1280]{1,0:T(8,128)(2,1)}, f32[2,16,128]{2,1,0:T(8,128)S(1)}) custom-call(bf16[128,1280]{1,0:T(8,128)(2,1)S(1)} %copy-done, bf16[128,1280]{1,0:T(8,128)(2,1)S(1)} %copy-done.1, bf16[128,1280]{1,0:T(8,128)(2,1)S(1)} %copy-done.2, bf16[128,1280]{1,0:T(8,128)(2,1)S(1)} %copy-done.3, ...), custom_call_target="tpu_custom_call" | custom-call | flops 838860800 | bytes 6291456 | tf_op jit(solution)/shard_map/attend/pallas_call | solution.py:99
  131.8 3.6 %collective-permute-start.17 = (f32[2,16,128]{2,1,0:T(8,128)S(1)}, f32[2,16,128]{2,1,0:T(8,128)S(1)}, u32[]{:S(2)}, u32[]{:S(2)}) collective-permute-start(f32[2,16,128]{2,1,0:T(8,128)S(1)} %get-tuple-element.48.st0_ref), channel_id=1, source_target_pairs={{2,0},{4,2},{6,4},{8,6},{10,8},{12,10},{14,12},{16,14},{18,16},{20... | collective-permute-start | bytes 49160 | tf_op jit(solution)/shard_map/ppermute | solution.py:21
  135.5 1.9 %collective-permute-start.18 = (f32[2,16,128]{2,1,0:T(8,128)S(1)}, f32[2,16,128]{2,1,0:T(8,128)S(1)}, u32[]{:S(2)}, u32[]{:S(2)}) collective-permute-start(f32[2,16,128]{2,1,0:T(8,128)S(1)} %get-tuple-element.48.st0_ref), channel_id=1, source_target_pairs={{4,0},{6,2},{8,4},{10,6},{12,8},{14,10},{16,12},{18,14},{20,16},{2... | collective-permute-start | bytes 49160 | tf_op jit(solution)/shard_map/ppermute | solution.py:21
  137.4 0.0 collective-permute-done.17.st1_ref
  137.4 3.7 %collective-permute-done.18.st2_ref = f32[2,16,128]{2,1,0:T(8,128)S(1)} collective-permute-done((f32[2,16,128]{2,1,0:T(8,128)S(1)}, f32[2,16,128]{2,1,0:T(8,128)S(1)}, u32[]{:S(2)}, u32[]{:S(2)}) %collective-permute-start.18) | collective-permute-done | bytes 16416 | tf_op jit(solution)/shard_map/ppermute | solution.py:21
  141.1 2.7 %key_grads.1 = (bf16[128,1280]{1,0:T(8,128)(2,1)}, bf16[128,1280]{1,0:T(8,128)(2,1)}) custom-call(bf16[128,1280]{1,0:T(8,128)(2,1)S(1)} %copy-done.2, bf16[128,1280]{1,0:T(8,128)(2,1)S(1)} %copy-done.3, bf16[128,1280]{1,0:T(8,128)(2,1)S(1)} %copy-done, bf16[128,1280]{1,0:T(8,128)(2,1)S(1)} %copy-done.1, ...), custom_call_target="tpu_custom_call" | custom-call | flops 503316480 | bytes 4194304 | tf_op jit(solution)/shard_map/key_grads/pallas_call | solution.py:161
  (14 shorter events, 0.0 us)
Async XLA Ops:
  0.6 7.5 %copy-start.2 = (bf16[128,1280]{1,0:T(8,128)(2,1)S(1)}, bf16[128,1280]{1,0:T(8,128)(2,1)}, u32[]{:S(2)}) copy-start(bf16[128,1280]{1,0:T(8,128)(2,1)} %k_ref.3) | copy-start | bytes 983044
  0.6 7.5 %copy-start.3 = (bf16[128,1280]{1,0:T(8,128)(2,1)S(1)}, bf16[128,1280]{1,0:T(8,128)(2,1)}, u32[]{:S(2)}) copy-start(bf16[128,1280]{1,0:T(8,128)(2,1)} %v_ref.3) | copy-start | bytes 983044
  0.7 28.5 %collective-permute-start.3 = (bf16[128,1280]{1,0:T(8,128)(2,1)}, bf16[128,1280]{1,0:T(8,128)(2,1)S(1)}, u32[]{:S(2)}, u32[]{:S(2)}) collective-permute-start(bf16[128,1280]{1,0:T(8,128)(2,1)} %refs_0_.1), channel_id=1, source_target_pairs={{0,8},{8,24},{24,16},{16,0},{1,9},{9,25},{25,17},{17,1},{2,10},{10... | collective-permute-start | bytes 983048 | tf_op jit(solution)/shard_map/ppermute | solution.py:309
  0.7 28.4 %collective-permute-start.4 = (bf16[128,1280]{1,0:T(8,128)(2,1)}, bf16[128,1280]{1,0:T(8,128)(2,1)S(1)}, u32[]{:S(2)}, u32[]{:S(2)}) collective-permute-start(bf16[128,1280]{1,0:T(8,128)(2,1)} %refs_0_.1), channel_id=1, source_target_pairs={{0,1},{1,0},{2,3},{3,2},{4,5},{5,4},{6,7},{7,6},{8,9},{9,8},{10,11... | collective-permute-start | bytes 983048 | tf_op jit(solution)/shard_map/ppermute | solution.py:25
  3.9 15.1 %collective-permute-start = (bf16[160,640]{1,0:T(8,128)(2,1)S(1)}, bf16[160,640]{1,0:T(8,128)(2,1)S(1)}, u32[]{:S(2)}, u32[]{:S(2)}) collective-permute-start(bf16[160,640]{1,0:T(8,128)(2,1)S(1)} %get-tuple-element.53), channel_id=1, source_target_pairs={{0,8},{8,0},{16,24},{24,16},{1,9},{9,1},{17,25},{25,17},{2,10},{10... | collective-permute-start | bytes 614408 | tf_op jit(solution)/shard_map/ppermute | solution.py:25
  5.6 14.6 %collective-permute-start.1 = (bf16[160,640]{1,0:T(8,128)(2,1)S(1)}, bf16[160,640]{1,0:T(8,128)(2,1)S(1)}, u32[]{:S(2)}, u32[]{:S(2)}) collective-permute-start(bf16[160,640]{1,0:T(8,128)(2,1)S(1)} %get-tuple-element.55), channel_id=1, source_target_pairs={{0,16},{8,24},{16,0},{24,8},{1,17},{9,25},{17,1},{25,9},{2,18},{10... | collective-permute-start | bytes 614408 | tf_op jit(solution)/shard_map/ppermute | solution.py:25
  8.1 20.9 %collective-permute-start.2 = (bf16[160,640]{1,0:T(8,128)(2,1)S(1)}, bf16[160,640]{1,0:T(8,128)(2,1)S(1)}, u32[]{:S(2)}, u32[]{:S(2)}) collective-permute-start(bf16[160,640]{1,0:T(8,128)(2,1)S(1)} %get-tuple-element.54), channel_id=1, source_target_pairs={{0,24},{8,16},{16,8},{24,0},{1,25},{9,17},{17,9},{25,1},{2,26},{10... | collective-permute-start | bytes 614408 | tf_op jit(solution)/shard_map/ppermute | solution.py:25
  8.1 24.3 %copy-start = (bf16[128,1280]{1,0:T(8,128)(2,1)S(1)}, bf16[128,1280]{1,0:T(8,128)(2,1)}, u32[]{:S(2)}) copy-start(bf16[128,1280]{1,0:T(8,128)(2,1)} %q_ref.3) | copy-start | bytes 983044
  8.1 24.2 %copy-start.1 = (bf16[128,1280]{1,0:T(8,128)(2,1)S(1)}, bf16[128,1280]{1,0:T(8,128)(2,1)}, u32[]{:S(2)}) copy-start(bf16[128,1280]{1,0:T(8,128)(2,1)} %g_ref.3) | copy-start | bytes 983044
  29.0 36.6 %copy-start.13 = (s32[2048]{0:T(1024)S(1)}, s32[2048]{0:T(1024)}, u32[]{:S(2)}) copy-start(s32[2048]{0:T(1024)} %param.15) | copy-start | bytes 24580
  29.0 36.6 %copy-start.14 = (s32[2048]{0:T(1024)S(1)}, s32[2048]{0:T(1024)}, u32[]{:S(2)}) copy-start(s32[2048]{0:T(1024)} %param.14) | copy-start | bytes 24580
  29.0 45.8 %copy-start.12 = (bf16[128,1280]{1,0:T(8,128)(2,1)S(1)}, bf16[128,1280]{1,0:T(8,128)(2,1)}, u32[]{:S(2)}) copy-start(bf16[128,1280]{1,0:T(8,128)(2,1)} %refs_0_.1) | copy-start | bytes 983044
  29.1 10.2 %collective-permute-start.8 = (bf16[4,160,640]{2,1,0:T(8,128)(2,1)S(1)}, bf16[4,160,640]{2,1,0:T(8,128)(2,1)S(1)}, u32[]{:S(2)}, u32[]{:S(2)}) collective-permute-start(bf16[4,160,640]{2,1,0:T(8,128)(2,1)S(1)} %pad_maximum_fusion.refs_8_), channel_id=1, source_target_pairs={{0,2},{2,0},{4,6},{6,4},{1,3},{3,1},{5,7},{7,5},{8,10},{10,8},{12,... | collective-permute-start | bytes 2457608 | tf_op jit(solution)/shard_map/ppermute | solution.py:25
  29.2 10.1 %collective-permute-start.6 = (bf16[128,1280]{1,0:T(8,128)(2,1)S(1)}, bf16[128,1280]{1,0:T(8,128)(2,1)S(1)}, u32[]{:S(2)}, u32[]{:S(2)}) collective-permute-start(bf16[128,1280]{1,0:T(8,128)(2,1)S(1)} %collective-permute-done.3.refs_1_), channel_id=1, source_target_pairs={{0,8},{8,24},{24,16},{16,0},{1,9},{9,25},{25,17},{17,1},{2,10},{10... | collective-permute-start | bytes 983048 | tf_op jit(solution)/shard_map/ppermute | solution.py:309
  29.3 10.0 %collective-permute-start.7 = (bf16[128,1280]{1,0:T(8,128)(2,1)S(1)}, bf16[128,1280]{1,0:T(8,128)(2,1)S(1)}, u32[]{:S(2)}, u32[]{:S(2)}) collective-permute-start(bf16[128,1280]{1,0:T(8,128)(2,1)S(1)} %collective-permute-done.3.refs_1_), channel_id=1, source_target_pairs={{0,1},{1,0},{2,3},{3,2},{4,5},{5,4},{6,7},{7,6},{8,9},{9,8},{10,11... | collective-permute-start | bytes 983048 | tf_op jit(solution)/shard_map/ppermute | solution.py:25
  30.9 27.2 %collective-permute-start.5 = (bf16[4,160,640]{2,1,0:T(8,128)(2,1)S(1)}, bf16[4,160,640]{2,1,0:T(8,128)(2,1)S(1)}, u32[]{:S(2)}, u32[]{:S(2)}) collective-permute-start(bf16[4,160,640]{2,1,0:T(8,128)(2,1)S(1)} %pad_maximum_fusion.refs_8_), channel_id=1, source_target_pairs={{0,4},{2,6},{4,0},{6,2},{1,5},{3,7},{5,1},{7,3},{8,12},{10,14},{12... | collective-permute-start | bytes 2457608 | tf_op jit(solution)/shard_map/ppermute | solution.py:25
  39.3 23.4 %collective-permute-start.11 = (bf16[2,128,1280]{2,1,0:T(8,128)(2,1)S(1)}, bf16[2,128,1280]{2,1,0:T(8,128)(2,1)S(1)}, u32[]{:S(2)}, u32[]{:S(2)}) collective-permute-start(bf16[2,128,1280]{2,1,0:T(8,128)(2,1)S(1)} %pad_maximum_fusion.1), channel_id=1, source_target_pairs={{0,2},{2,4},{4,6},{6,8},{8,10},{10,12},{12,14},{14,16},{16,18},{18... | collective-permute-start | bytes 1966088 | tf_op jit(solution)/shard_map/ppermute | solution.py:21
  41.2 21.5 %collective-permute-start.12 = (bf16[2,128,1280]{2,1,0:T(8,128)(2,1)S(1)}, bf16[2,128,1280]{2,1,0:T(8,128)(2,1)S(1)}, u32[]{:S(2)}, u32[]{:S(2)}) collective-permute-start(bf16[2,128,1280]{2,1,0:T(8,128)(2,1)S(1)} %pad_maximum_fusion.2), channel_id=1, source_target_pairs={{2,0},{4,2},{6,4},{8,6},{10,8},{12,10},{14,12},{16,14},{18,16},{20... | collective-permute-start | bytes 1966088 | tf_op jit(solution)/shard_map/ppermute | solution.py:21
  45.8 12.3 %collective-permute-start.10 = (bf16[128,1280]{1,0:T(8,128)(2,1)S(1)}, bf16[128,1280]{1,0:T(8,128)(2,1)S(1)}, u32[]{:S(2)}, u32[]{:S(2)}) collective-permute-start(bf16[128,1280]{1,0:T(8,128)(2,1)S(1)} %collective-permute-done.6.refs_2_), channel_id=1, source_target_pairs={{0,1},{1,0},{2,3},{3,2},{4,5},{5,4},{6,7},{7,6},{8,9},{9,8},{10,11... | collective-permute-start | bytes 983048 | tf_op jit(solution)/shard_map/ppermute | solution.py:25
  47.4 15.3 %collective-permute-start.9 = (bf16[128,1280]{1,0:T(8,128)(2,1)S(1)}, bf16[128,1280]{1,0:T(8,128)(2,1)S(1)}, u32[]{:S(2)}, u32[]{:S(2)}) collective-permute-start(bf16[128,1280]{1,0:T(8,128)(2,1)S(1)} %collective-permute-done.6.refs_2_), channel_id=1, source_target_pairs={{0,8},{8,24},{24,16},{16,0},{1,9},{9,25},{25,17},{17,1},{2,10},{10... | collective-permute-start | bytes 983048 | tf_op jit(solution)/shard_map/ppermute | solution.py:309
  62.7 0.8 copy-start.6
  63.6 11.2 %collective-permute-start.15 = (bf16[4,160,640]{2,1,0:T(8,128)(2,1)S(1)}, bf16[4,160,640]{2,1,0:T(8,128)(2,1)S(1)}, u32[]{:S(2)}, u32[]{:S(2)}) collective-permute-start(bf16[4,160,640]{2,1,0:T(8,128)(2,1)S(1)} %collective-permute-done.5.refs_10_), channel_id=1, source_target_pairs={{0,2},{2,0},{4,6},{6,4},{1,3},{3,1},{5,7},{7,5},{8,10},{10,8},{12,... | collective-permute-start | bytes 2457608 | tf_op jit(solution)/shard_map/ppermute | solution.py:25
  65.1 9.6 %collective-permute-start.14 = (bf16[128,1280]{1,0:T(8,128)(2,1)S(1)}, bf16[128,1280]{1,0:T(8,128)(2,1)S(1)}, u32[]{:S(2)}, u32[]{:S(2)}) collective-permute-start(bf16[128,1280]{1,0:T(8,128)(2,1)S(1)} %collective-permute-done.9.refs_3_), channel_id=1, source_target_pairs={{0,1},{1,0},{2,3},{3,2},{4,5},{5,4},{6,7},{7,6},{8,9},{9,8},{10,11... | collective-permute-start | bytes 983048 | tf_op jit(solution)/shard_map/ppermute | solution.py:25
  65.9 0.7 copy-start.10
  79.3 45.3 %all-to-all-start = ((bf16[16,4,16,640]{3,2,1,0:T(8,128)(2,1)}), bf16[16,4,16,640]{3,2,1,0:T(8,128)(2,1)S(1)}, u32[]{:S(2)}, u32[]{:S(2)}) async-start(bf16[16,4,16,640]{3,2,1,0:T(8,128)(2,1)} %project.1), calls=%async_computation | async-start | bytes 2621440 | tf_op jit(solution)/shard_map/all_to_all | solution.py:382
  85.9 36.0 %collective-permute-start.16 = (bf16[2,128,1280]{2,1,0:T(8,128)(2,1)S(1)}, bf16[2,128,1280]{2,1,0:T(8,128)(2,1)S(1)}, u32[]{:S(2)}, u32[]{:S(2)}) collective-permute-start(bf16[2,128,1280]{2,1,0:T(8,128)(2,1)S(1)} %collective-permute-done.12.qg1_ref), channel_id=1, source_target_pairs={{2,0},{4,2},{6,4},{8,6},{10,8},{12,10},{14,12},{16,14},{18,16},{20... | collective-permute-start | bytes 1966088 | tf_op jit(solution)/shard_map/ppermute | solution.py:21
  89.0 34.8 %collective-permute-start.13 = (bf16[2,128,1280]{2,1,0:T(8,128)(2,1)}, bf16[2,128,1280]{2,1,0:T(8,128)(2,1)S(1)}, u32[]{:S(2)}, u32[]{:S(2)}) collective-permute-start(bf16[2,128,1280]{2,1,0:T(8,128)(2,1)} %copy-done.6), channel_id=1, source_target_pairs={{0,2},{2,4},{4,6},{6,8},{8,10},{10,12},{12,14},{14,16},{16,18},{18... | collective-permute-start | bytes 1966088 | tf_op jit(solution)/shard_map/ppermute | solution.py:21
  121.9 0.8 copy-start.4
  123.8 0.8 copy-start.8
  124.6 1.1 copy-start.7
  125.7 1.1 copy-start.9
  126.8 1.0 copy-start.11
  127.8 13.3 %copy-start.5 = (bf16[2,128,1280]{2,1,0:T(8,128)(2,1)S(1)}, bf16[2,128,1280]{2,1,0:T(8,128)(2,1)}, u32[]{:S(2)}) copy-start(bf16[2,128,1280]{2,1,0:T(8,128)(2,1)} %copy-done.4) | copy-start | bytes 1966084
  131.8 5.6 %collective-permute-start.17 = (f32[2,16,128]{2,1,0:T(8,128)S(1)}, f32[2,16,128]{2,1,0:T(8,128)S(1)}, u32[]{:S(2)}, u32[]{:S(2)}) collective-permute-start(f32[2,16,128]{2,1,0:T(8,128)S(1)} %get-tuple-element.48.st0_ref), channel_id=1, source_target_pairs={{2,0},{4,2},{6,4},{8,6},{10,8},{12,10},{14,12},{16,14},{18,16},{20... | collective-permute-start | bytes 49160 | tf_op jit(solution)/shard_map/ppermute | solution.py:21
  135.5 5.6 %collective-permute-start.18 = (f32[2,16,128]{2,1,0:T(8,128)S(1)}, f32[2,16,128]{2,1,0:T(8,128)S(1)}, u32[]{:S(2)}, u32[]{:S(2)}) collective-permute-start(f32[2,16,128]{2,1,0:T(8,128)S(1)} %get-tuple-element.48.st0_ref), channel_id=1, source_target_pairs={{4,0},{6,2},{8,4},{10,6},{12,8},{14,10},{16,12},{18,14},{20,16},{2... | collective-permute-start | bytes 49160 | tf_op jit(solution)/shard_map/ppermute | solution.py:21
where the time goes:
time: 144 us
  waiting for transfers between devices  86.8 us (60%)
  starting transfers between devices  36.6 us (25%)
  Pallas kernels  11.6 us (8%)
  local copies, waits for them, and re-layouts  7.73 us (5%)
    ppermute x10, waiting for transfers between devices, swapped(): lax.ppermute(value, axis, [(i, i ^ mask) for i in range(lax.axis_size(axi...  39.6 us
    ppermute x6, waiting for transfers between devices, shifted(): return lax.ppermute(value, SEQ, pairs)  35.7 us
    ppermute x6, starting transfers between devices, shifted(): return lax.ppermute(value, SEQ, pairs)  17 us
    ppermute x10, starting transfers between devices, swapped(): lax.ppermute(value, axis, [(i, i ^ mask) for i in range(lax.axis_size(axi...  12.9 us
    ppermute x3, waiting for transfers between devices, ring_step(): lax.ppermute(value, 'z', [(a, b) for a, b in zip(RING, RING[1:] + RING[:1...  11.5 us
    all_to_all x1, starting transfers between devices, body(): memory = lax.all_to_all(slots, SEQ, split_axis=0, concat_axis=0, tiled=True)  6.53 us
    unnamed x30, local copies, waits for them, and re-layouts  6.43 us
    pallas_call x1, Pallas kernels, project(): pl.pallas_call(project_kernel, in_specs=[whole] * (1 + len(rows) + n_p),...  4.6 us
  transfers between devices with their start and end apart: 20, of which 10 were waited for; matrix products, arithmetic and copies ran while one was open for 1% of the time, Pallas kernels for 0%

commit v1 on v0

--- a/solution.py
+++ b/solution.py
@@ -29,6 +29,10 @@
     return [pltpu.with_memory_space_constraint(array, pltpu.VMEM) for array in arrays]
 
 
+def in_hbm(*arrays):
+    return [pltpu.with_memory_space_constraint(array, pltpu.HBM) for array in arrays]
+
+
 def dot_t(a, b, dims):
     return lax.dot_general(a, b, (dims, ((), ())), preferred_element_type=jnp.float32)
 
@@ -38,22 +42,21 @@
 ):
     rows, width = q_ref.shape
     scaling = HD ** (-0.5)
-    bias = bias_ref[...]
+    bias = bias_ref[...].astype(jnp.float32)
     step = pl.program_id(0)
     heads = [slice(i * HD, (i + 1) * HD) for i in range(width // HD)]
-    picked = [pl.ds(pl.multiple_of(step * width + i * HD, HD), HD) for i in range(len(heads))]
     ks, vs = (
         [
             jnp.concatenate(
                 [
                     mem_ref[2 * step + which, :, cols],
-                    kv2_ref[which, :, wide],
-                    kv1_ref[which, :, wide],
+                    kv2_ref[which, :, cols],
+                    kv1_ref[which, :, cols],
                     own_ref[:, cols],
                 ],
                 0,
             )
-            for cols, wide in zip(heads, picked)
+            for cols in heads
         ]
         for which, own_ref in enumerate((k_ref, v_ref))
     )
@@ -94,13 +97,15 @@
     slots, block = memory.shape[1:]
     heads = steps * block // HD
     flat = pl.BlockSpec((rows, block), lambda i: (0, i))
+    pair = pl.BlockSpec((2, rows, block), lambda i: (0, 0, i))
     whole = pl.BlockSpec(memory_space=pltpu.VMEM)
     keys_all = slots + 3 * rows
     return pl.pallas_call(
         attend_kernel,
         grid=(steps,),
         in_specs=[
-            flat, flat, flat, flat, whole, whole, whole, whole,
+            flat, flat, flat, flat, pair, pair, whole,
+            pl.BlockSpec((rows, keys_all), lambda i: (0, 0)),
         ],
         out_specs=[flat, flat, pl.BlockSpec((1, STATS, rows), lambda i: (i, 0, 0))],
         out_shape=[
@@ -115,7 +120,7 @@
             transcendentals=rows * keys_all * heads,
         ),
         name="attend",
-    )(queries, grad_out, keys, values, *in_vmem(kv1, kv2, memory, bias))
+    )(queries, grad_out, keys, values, *in_hbm(kv1, kv2), *in_vmem(memory), *in_hbm(bias))
 
 
 def key_grads_kernel(
@@ -270,7 +275,9 @@
             same = same & (lane <= row)
         if i == 0:
             same_back = same_back & (lane >= row)
-        bias_ref[:, slots + i * rows : slots + (i + 1) * rows] = jnp.where(same, 0.0, -1e30)
+        bias_ref[:, slots + i * rows : slots + (i + 1) * rows] = jnp.where(same, 0.0, -1e30).astype(
+            jnp.bfloat16
+        )
         back_ref[:, i * rows : (i + 1) * rows] = jnp.where(same_back, 0.0, -1e30)
 
     mine = jnp.where(routes_ref[...] == me, 1.0, 0.0).astype(jnp.bfloat16)
@@ -281,7 +288,7 @@
     filled = jnp.dot(counts, expand, preferred_element_type=jnp.float32)[:1]
     rank = lax.broadcasted_iota(jnp.int32, (1, slots), 1) % capacity
     live = jnp.where(rank.astype(jnp.float32) < filled, 0.0, -1e30)
-    bias_ref[:, :slots] = jnp.broadcast_to(live, (rows, slots))
+    bias_ref[:, :slots] = jnp.broadcast_to(live, (rows, slots)).astype(jnp.bfloat16)
 
 
 def prepare(routes, doc_ids, n_z, devices, rows):
@@ -290,7 +297,7 @@
         prepare_kernel,
         out_shape=[
             jax.ShapeDtypeStruct((n_z, 1, rows), jnp.int32),
-            jax.ShapeDtypeStruct((rows, slots + 3 * rows), jnp.float32),
+            jax.ShapeDtypeStruct((rows, slots + 3 * rows), jnp.bfloat16),
             jax.ShapeDtypeStruct((rows, 3 * rows), jnp.float32),
         ],
         compiler_params=pltpu.CompilerParams(vmem_limit_bytes=SMALL_VMEM),
@@ -321,24 +328,25 @@
             [blocks[0]] + [swapped(blocks[mask], "z", mask) for mask in range(1, n_z)], 0
         )
         row1, other0 = ring_step(cache), swapped(cache, "head", 1)
-        own, row1, other0, stream = lax.optimization_barrier((own, row1, other0, stream))
+        near, back1 = shifted(stream, 1), shifted(back, -1)
+        own, row1, other0, near, back1 = lax.optimization_barrier(
+            (own, row1, other0, near, back1)
+        )
         across = swapped(own, "p", 2)
         beside = swapped(own, "p", 1)
         row2, other1 = ring_step(row1), swapped(row1, "head", 1)
-        row2, other1, beside, stream, back = lax.optimization_barrier(
-            (row2, other1, beside, stream, back)
-        )
+        row2, other1, beside = lax.optimization_barrier((row2, other1, beside))
         row3, other2 = ring_step(row2), swapped(row2, "head", 1)
-        near, back1 = shifted(stream, 1), shifted(back, -1)
         across, row3, other2, near, back1 = lax.optimization_barrier(
             (across, row3, other2, near, back1)
         )
         pieces = [own, beside, across, swapped(across, "p", 1)]
+        far, back2 = shifted(near, 1), shifted(back1, -1)
         rows = [cache, row1, row2, row3, other0, other1, other2, swapped(row3, "head", 1)]
         slots = project(place, rows, pieces, devices, capacity)
-        return slots, near, back1
-    near = shifted(stream, 1)
-    back1 = shifted(back, -1)
+        return lax.optimization_barrier((slots, near, far, back1, back2))
+    near, back1 = shifted(stream, 1), shifted(back, -1)
+    far, back2 = shifted(near, 1), shifted(back1, -1)
     targets = [column_block(w_kv, jnp.int32(i)) for i in range(n_z)]
     w_z = lax.all_to_all(jnp.stack(targets, 0), "z", split_axis=0, concat_axis=0, tiled=True)
     w_all = lax.all_gather(w_z, "p", axis=1, tiled=True).reshape(devices * w_rows, -1)
@@ -358,7 +366,8 @@
         proj.reshape(n_z, cache_rows, -1),
         preferred_element_type=jnp.float32,
     ).astype(jnp.bfloat16)
-    return slots.reshape(n_z, devices, capacity, -1).transpose(1, 0, 2, 3), near, back1
+    slots = slots.reshape(n_z, devices, capacity, -1).transpose(1, 0, 2, 3)
+    return slots, near, far, back1, back2
 
 
 def body(queries, keys, values, grad_out, cache, w_kv, doc_ids, routes):
@@ -370,7 +379,7 @@
     slot_count = capacity * devices
 
     place, bias, back_bias = prepare(routes, doc_ids, n_z, devices, seg_rows)
-    slots, kv1, qg1 = memory_slots(
+    slots, kv1, kv2, qg1, qg2 = memory_slots(
         cache,
         w_kv,
         place,
@@ -378,11 +387,8 @@
         jnp.stack([keys, values], 0),
         jnp.stack([queries, grad_out], 0),
     )
-    kv2, qg2 = shifted(kv1, 1), shifted(qg1, -1)
     memory = lax.all_to_all(slots, SEQ, split_axis=0, concat_axis=0, tiled=True)
     memory = memory.reshape(n_z, slot_count, slots.shape[-1])
-
-    qg2, bias = lax.optimization_barrier((qg2, bias))
 
     output, grad_q, stats = attend(queries, grad_out, keys, values, kv1, kv2, memory, bias)
     all_stats = [stats, shifted(stats, -1), shifted(stats, -2)]

time: 144 us -> 140 us (0.972); the launches traced: 144 us -> 138 us
  blocking collectives: 0 us -> 35.9 us
  waiting for transfers between devices: 86.8 us -> 53.4 us
  local copies, waits for them, and re-layouts: 7.73 us -> 0.14 us
  starting transfers between devices: 36.6 us -> 33.4 us
  other arithmetic: 0.25 us -> 3.14 us
    all_to_all x0 -> x1, blocking collectives: none -> 35.9 us  [body(): memory = lax.all_to_all(slots, SEQ, split_axis=0, concat_axis=0, tiled=True)]
    ppermute x6, waiting for transfers between devices: 35.7 us -> 2.42 us  [shifted(): return lax.ppermute(value, SEQ, pairs)]
    all_to_all x1 -> x0, starting transfers between devices: 6.53 us -> none  [body(): memory = lax.all_to_all(slots, SEQ, split_axis=0, concat_axis=0, tiled=True)]
    unnamed x30 -> x22, local copies, waits for them, and re-layouts: 6.43 us -> 0.06 us
    ppermute x3, starting transfers between devices: 0.12 us -> 4.63 us  [ring_step(): lax.ppermute(value, 'z', [(a, b) for a, b in zip(RING, RING[1:] + RING[:1...]
    ppermute x10, starting transfers between devices: 12.9 us -> 9.84 us  [swapped(): lax.ppermute(value, axis, [(i, i ^ mask) for i in range(lax.axis_size(axi...]
    another operation x1, other arithmetic: 0.06 us -> 2.08 us  [body(): jnp.stack([keys, values], 0)]
    ppermute x6, starting transfers between devices: 17 us -> 18.9 us  [shifted(): return lax.ppermute(value, SEQ, pairs)]
  transfers between devices with their start and end apart: 20 -> 19, of which waited for: 10 -> 12; matrix products, arithmetic and copies ran while one was open for 1% -> 1% of each run, Pallas kernels for 0% -> 3%
where the time goes in v1:
time: 140 us; the launch traced here: 138 us
  waiting for transfers between devices  53.4 us (38%)
  blocking collectives  35.9 us (26%)
  starting transfers between devices  33.4 us (24%)
  Pallas kernels  11.5 us (8%)
  other arithmetic  3.14 us (2%)
    ppermute x10, waiting for transfers between devices, swapped(): lax.ppermute(value, axis, [(i, i ^ mask) for i in range(lax.axis_size(axi...  40.2 us
    all_to_all x1, blocking collectives, body(): memory = lax.all_to_all(slots, SEQ, split_axis=0, concat_axis=0, tiled=True)  35.9 us
    ppermute x6, starting transfers between devices, shifted(): return lax.ppermute(value, SEQ, pairs)  18.9 us
    ppermute x3, waiting for transfers between devices, ring_step(): lax.ppermute(value, 'z', [(a, b) for a, b in zip(RING, RING[1:] + RING[:1...  10.8 us
    ppermute x10, starting transfers between devices, swapped(): lax.ppermute(value, axis, [(i, i ^ mask) for i in range(lax.axis_size(axi...  9.84 us
    pallas_call x1, Pallas kernels, attend(): pl.pallas_call(attend_kernel, grid=(steps,), in_specs=[flat, flat, flat,...  5.01 us
    ppermute x3, starting transfers between devices, ring_step(): lax.ppermute(value, 'z', [(a, b) for a, b in zip(RING, RING[1:] + RING[:1...  4.63 us
    pallas_call x1, Pallas kernels, project(): pl.pallas_call(project_kernel, in_specs=[whole] * (1 + len(rows) + n_p),...  3.51 us
  transfers between devices with their start and end apart: 19, of which 12 were waited for; matrix products, arithmetic and copies ran while one was open for 1% of the time, Pallas kernels for 3%

profile of v1, /device:TPU:16, one launch (start us, length us, event | category | flops | bytes accessed | tf_op | source)
XLA Modules:
  0.0 138.3 jit_solution(17701985518369939505)
XLA Ops:
  0.6 0.0 copy-start
  0.6 0.0 copy-start.1
  0.7 0.0 copy-start.8
  0.7 2.1 %pad_maximum_fusion.1 = bf16[2,128,1280]{2,1,0:T(8,128)(2,1)} fusion(bf16[1,128,1280]{2,1,0:T(8,128)(2,1)} %bitcast.20, bf16[1,128,1280]{2,1,0:T(8,128)(2,1)} %bitcast.19), kind=kLoop, calls=%fused_computation.1 | loop fusion | flops 327680 | bytes 1310720 | tf_op jit(solution)/shard_map/stack | solution.py:387
  2.7 1.9 %collective-permute-start.5 = (bf16[2,128,1280]{2,1,0:T(8,128)(2,1)}, bf16[2,128,1280]{2,1,0:T(8,128)(2,1)S(1)}, u32[]{:S(2)}, u32[]{:S(2)}) collective-permute-start(bf16[2,128,1280]{2,1,0:T(8,128)(2,1)} %pad_maximum_fusion.1), channel_id=1, source_target_pairs={{0,2},{2,4},{4,6},{6,8},{8,10},{10,12},{12,14},{14,16},{16,18},{18... | collective-permute-start | bytes 1966088 | tf_op jit(solution)/shard_map/ppermute | solution.py:21
  4.7 0.0 copy-done
  4.7 0.0 copy-done.1
  4.7 0.0 copy-start.4
  4.7 0.9 pad_maximum_fusion.2
  5.6 4.5 %collective-permute-start.6 = (bf16[2,128,1280]{2,1,0:T(8,128)(2,1)}, bf16[2,128,1280]{2,1,0:T(8,128)(2,1)S(1)}, u32[]{:S(2)}, u32[]{:S(2)}) collective-permute-start(bf16[2,128,1280]{2,1,0:T(8,128)(2,1)} %pad_maximum_fusion.2), channel_id=1, source_target_pairs={{2,0},{4,2},{6,4},{8,6},{10,8},{12,10},{14,12},{16,14},{18,16},{20... | collective-permute-start | bytes 1966088 | tf_op jit(solution)/shard_map/ppermute | solution.py:21
  10.2 0.0 copy-done.8
  10.2 0.0 copy-start.6
  10.2 0.0 copy-start.7
  10.2 0.1 constant_dynamic-slice_fusion
  10.3 1.6 %collective-permute-start = (bf16[160,640]{1,0:T(8,128)(2,1)S(1)}, bf16[160,640]{1,0:T(8,128)(2,1)S(1)}, u32[]{:S(2)}, u32[]{:S(2)}) collective-permute-start(bf16[160,640]{1,0:T(8,128)(2,1)S(1)} %get-tuple-element.57), channel_id=1, source_target_pairs={{0,8},{8,0},{16,24},{24,16},{1,9},{9,1},{17,25},{25,17},{2,10},{10... | collective-permute-start | bytes 614408 | tf_op jit(solution)/shard_map/ppermute | solution.py:25
  12.0 0.3 collective-permute-start.1
  12.3 1.6 %collective-permute-start.2 = (bf16[160,640]{1,0:T(8,128)(2,1)S(1)}, bf16[160,640]{1,0:T(8,128)(2,1)S(1)}, u32[]{:S(2)}, u32[]{:S(2)}) collective-permute-start(bf16[160,640]{1,0:T(8,128)(2,1)S(1)} %get-tuple-element.58), channel_id=1, source_target_pairs={{0,24},{8,16},{16,8},{24,0},{1,25},{9,17},{17,9},{25,1},{2,26},{10... | collective-permute-start | bytes 614408 | tf_op jit(solution)/shard_map/ppermute | solution.py:25
  13.9 17.4 %collective-permute-done = bf16[160,640]{1,0:T(8,128)(2,1)S(1)} collective-permute-done((bf16[160,640]{1,0:T(8,128)(2,1)S(1)}, bf16[160,640]{1,0:T(8,128)(2,1)S(1)}, u32[]{:S(2)}, u32[]{:S(2)}) %collective-permute-start) | collective-permute-done | bytes 204832 | tf_op jit(solution)/shard_map/ppermute | solution.py:25
  31.3 0.0 copy-done.4
  31.3 0.0 collective-permute-start.3
  31.3 5.7 %collective-permute-done.1 = bf16[160,640]{1,0:T(8,128)(2,1)S(1)} collective-permute-done((bf16[160,640]{1,0:T(8,128)(2,1)S(1)}, bf16[160,640]{1,0:T(8,128)(2,1)S(1)}, u32[]{:S(2)}, u32[]{:S(2)}) %collective-permute-start.1) | collective-permute-done | bytes 204832 | tf_op jit(solution)/shard_map/ppermute | solution.py:25
  37.0 1.5 %collective-permute-start.4 = (bf16[128,1280]{1,0:T(8,128)(2,1)S(1)}, bf16[128,1280]{1,0:T(8,128)(2,1)S(1)}, u32[]{:S(2)}, u32[]{:S(2)}) collective-permute-start(bf16[128,1280]{1,0:T(8,128)(2,1)S(1)} %copy-done.4), channel_id=1, source_target_pairs={{0,1},{1,0},{2,3},{3,2},{4,5},{5,4},{6,7},{7,6},{8,9},{9,8},{10,11... | collective-permute-start | bytes 983048 | tf_op jit(solution)/shard_map/ppermute | solution.py:25
  38.5 0.7 collective-permute-done.2
  39.2 0.1 pad_maximum_fusion.refs_8_
  39.3 3.4 %collective-permute-done.3.refs_1_ = bf16[128,1280]{1,0:T(8,128)(2,1)S(1)} collective-permute-done((bf16[128,1280]{1,0:T(8,128)(2,1)S(1)}, bf16[128,1280]{1,0:T(8,128)(2,1)S(1)}, u32[]{:S(2)}, u32[]{:S(2)}) %collective-permute-start.3) | collective-permute-done | bytes 327712 | tf_op jit(solution)/shard_map/ppermute | solution.py:316
  42.7 1.4 collective-permute-done.4.refs_4_
  44.1 0.0 collective-permute-done.5.kv1_ref
  44.1 0.0 collective-permute-done.6.qg1_ref
  44.1 0.1 collective-permute-start.9
  44.2 0.1 collective-permute-start.10
  44.2 3.4 %collective-permute-start.7 = (bf16[128,1280]{1,0:T(8,128)(2,1)S(1)}, bf16[128,1280]{1,0:T(8,128)(2,1)S(1)}, u32[]{:S(2)}, u32[]{:S(2)}) collective-permute-start(bf16[128,1280]{1,0:T(8,128)(2,1)S(1)} %collective-permute-done.3.refs_1_), channel_id=1, source_target_pairs={{0,8},{8,24},{24,16},{16,0},{1,9},{9,25},{25,17},{17,1},{2,10},{10... | collective-permute-start | bytes 983048 | tf_op jit(solution)/shard_map/ppermute | solution.py:316
  47.7 1.5 %collective-permute-start.8 = (bf16[128,1280]{1,0:T(8,128)(2,1)S(1)}, bf16[128,1280]{1,0:T(8,128)(2,1)S(1)}, u32[]{:S(2)}, u32[]{:S(2)}) collective-permute-start(bf16[128,1280]{1,0:T(8,128)(2,1)S(1)} %collective-permute-done.3.refs_1_), channel_id=1, source_target_pairs={{0,1},{1,0},{2,3},{3,2},{4,5},{5,4},{6,7},{7,6},{8,9},{9,8},{10,11... | collective-permute-start | bytes 983048 | tf_op jit(solution)/shard_map/ppermute | solution.py:25
  49.2 6.0 %collective-permute-done.7.refs_2_ = bf16[128,1280]{1,0:T(8,128)(2,1)S(1)} collective-permute-done((bf16[128,1280]{1,0:T(8,128)(2,1)S(1)}, bf16[128,1280]{1,0:T(8,128)(2,1)S(1)}, u32[]{:S(2)}, u32[]{:S(2)}) %collective-permute-start.7) | collective-permute-done | bytes 327712 | tf_op jit(solution)/shard_map/ppermute | solution.py:316
  55.2 2.2 %collective-permute-done.8.refs_5_ = bf16[128,1280]{1,0:T(8,128)(2,1)S(1)} collective-permute-done((bf16[128,1280]{1,0:T(8,128)(2,1)S(1)}, bf16[128,1280]{1,0:T(8,128)(2,1)S(1)}, u32[]{:S(2)}, u32[]{:S(2)}) %collective-permute-start.8) | collective-permute-done | bytes 327712 | tf_op jit(solution)/shard_map/ppermute | solution.py:25
  57.4 0.0 collective-permute-done.9.refs_9_
  57.4 1.2 collective-permute-start.11
  58.6 1.5 %collective-permute-start.12 = (bf16[128,1280]{1,0:T(8,128)(2,1)S(1)}, bf16[128,1280]{1,0:T(8,128)(2,1)S(1)}, u32[]{:S(2)}, u32[]{:S(2)}) collective-permute-start(bf16[128,1280]{1,0:T(8,128)(2,1)S(1)} %collective-permute-done.7.refs_2_), channel_id=1, source_target_pairs={{0,1},{1,0},{2,3},{3,2},{4,5},{5,4},{6,7},{7,6},{8,9},{9,8},{10,11... | collective-permute-start | bytes 983048 | tf_op jit(solution)/shard_map/ppermute | solution.py:25
  60.1 4.7 %collective-permute-done.10.refs_10_ = bf16[4,160,640]{2,1,0:T(8,128)(2,1)S(1)} collective-permute-done((bf16[4,160,640]{2,1,0:T(8,128)(2,1)S(1)}, bf16[4,160,640]{2,1,0:T(8,128)(2,1)S(1)}, u32[]{:S(2)}, u32[]{:S(2)}) %collective-permute-start.10) | collective-permute-done | bytes 819232 | tf_op jit(solution)/shard_map/ppermute | solution.py:25
  64.8 1.4 %collective-permute-done.11.refs_3_ = bf16[128,1280]{1,0:T(8,128)(2,1)S(1)} collective-permute-done((bf16[128,1280]{1,0:T(8,128)(2,1)S(1)}, bf16[128,1280]{1,0:T(8,128)(2,1)S(1)}, u32[]{:S(2)}, u32[]{:S(2)}) %collective-permute-start.11) | collective-permute-done | bytes 327712 | tf_op jit(solution)/shard_map/ppermute | solution.py:316
  66.2 1.2 collective-permute-done.12.refs_6_
  67.4 0.0 collective-permute-start.14
  67.5 2.4 %collective-permute-start.15 = (bf16[2,128,1280]{2,1,0:T(8,128)(2,1)S(1)}, bf16[2,128,1280]{2,1,0:T(8,128)(2,1)S(1)}, u32[]{:S(2)}, u32[]{:S(2)}) collective-permute-start(bf16[2,128,1280]{2,1,0:T(8,128)(2,1)S(1)} %collective-permute-done.5.kv1_ref), channel_id=1, source_target_pairs={{0,2},{2,4},{4,6},{6,8},{8,10},{10,12},{12,14},{14,16},{16,18},{18... | collective-permute-start | bytes 1966088 | tf_op jit(solution)/shard_map/ppermute | solution.py:21
  69.9 4.0 %collective-permute-start.16 = (bf16[2,128,1280]{2,1,0:T(8,128)(2,1)S(1)}, bf16[2,128,1280]{2,1,0:T(8,128)(2,1)S(1)}, u32[]{:S(2)}, u32[]{:S(2)}) collective-permute-start(bf16[2,128,1280]{2,1,0:T(8,128)(2,1)S(1)} %collective-permute-done.6.qg1_ref), channel_id=1, source_target_pairs={{2,0},{4,2},{6,4},{8,6},{10,8},{12,10},{14,12},{16,14},{18,16},{20... | collective-permute-start | bytes 1966088 | tf_op jit(solution)/shard_map/ppermute | solution.py:21
  73.9 1.6 %collective-permute-start.13 = (bf16[128,1280]{1,0:T(8,128)(2,1)S(1)}, bf16[128,1280]{1,0:T(8,128)(2,1)S(1)}, u32[]{:S(2)}, u32[]{:S(2)}) collective-permute-start(bf16[128,1280]{1,0:T(8,128)(2,1)S(1)} %collective-permute-done.11.refs_3_), channel_id=1, source_target_pairs={{0,1},{1,0},{2,3},{3,2},{4,5},{5,4},{6,7},{7,6},{8,9},{9,8},{10,11... | collective-permute-start | bytes 983048 | tf_op jit(solution)/shard_map/ppermute | solution.py:25
  75.5 0.0 copy-done.6
  75.5 0.0 copy-done.7
  75.5 0.2 prepare.1
  75.8 6.9 %collective-permute-done.13.refs_7_ = bf16[128,1280]{1,0:T(8,128)(2,1)S(1)} collective-permute-done((bf16[128,1280]{1,0:T(8,128)(2,1)S(1)}, bf16[128,1280]{1,0:T(8,128)(2,1)S(1)}, u32[]{:S(2)}, u32[]{:S(2)}) %collective-permute-start.13) | collective-permute-done | bytes 327712 | tf_op jit(solution)/shard_map/ppermute | solution.py:25
  82.6 0.0 collective-permute-done.14.refs_11_
  82.6 3.5 %project.1 = bf16[16,4,16,640]{3,2,1,0:T(8,128)(2,1)S(1)} custom-call(s32[4,1,128]{2,1,0:T(1,128)S(1)} %get-tuple-element.30.place_ref, bf16[128,1280]{1,0:T(8,128)(2,1)S(1)} %copy-done.4, bf16[128,1280]{1,0:T(8,128)(2,1)S(1)} %collective-permute-done.3.refs_1_, bf16[128,1280]{1,0:T(8,128)(2,1)S(1)} %collective-permute-done.7.refs_2_, ...), custom_call_target="tpu_custom_call" | custom-call | flops 1677721600 | bytes 8388608 | tf_op jit(solution)/shard_map/project/pallas_call | solution.py:225
  86.1 0.0 copy-done.9
  86.2 0.0 copy-done.5
  86.2 0.0 copy-start.2
  86.2 0.0 copy-start.3
  86.2 0.0 collective-permute-done.15.kv2_ref
  86.2 0.0 collective-permute-done.16.qg2_ref
  86.2 35.9 %all_to_all.5 = bf16[16,4,16,640]{3,2,1,0:T(8,128)(2,1)S(1)} all-to-all(bf16[16,4,16,640]{3,2,1,0:T(8,128)(2,1)S(1)} %project.1), channel_id=1, replica_groups=mesh['z'=4,'p'=4,'head'=2] {'z','p'}, dimensions={0} | all-to-all | bytes 2621440 | tf_op jit(solution)/shard_map/all_to_all | solution.py:390
  122.1 0.0 copy-done.3
  122.1 5.0 %attend.1 = (bf16[128,1280]{1,0:T(8,128)(2,1)}, bf16[128,1280]{1,0:T(8,128)(2,1)}, f32[2,16,128]{2,1,0:T(8,128)S(1)}) custom-call(bf16[128,1280]{1,0:T(8,128)(2,1)S(1)} %copy-done, bf16[128,1280]{1,0:T(8,128)(2,1)S(1)} %copy-done.1, bf16[128,1280]{1,0:T(8,128)(2,1)S(1)} %copy-done.2, bf16[128,1280]{1,0:T(8,128)(2,1)S(1)} %copy-done.3, ...), custom_call_target="tpu_custom_call" | custom-call | flops 838860800 | bytes 6291456 | tf_op jit(solution)/shard_map/attend/pallas_call | solution.py:103
  127.1 2.8 %collective-permute-start.17 = (f32[2,16,128]{2,1,0:T(8,128)S(1)}, f32[2,16,128]{2,1,0:T(8,128)S(1)}, u32[]{:S(2)}, u32[]{:S(2)}) collective-permute-start(f32[2,16,128]{2,1,0:T(8,128)S(1)} %get-tuple-element.52.st0_ref), channel_id=1, source_target_pairs={{2,0},{4,2},{6,4},{8,6},{10,8},{12,10},{14,12},{16,14},{18,16},{20... | collective-permute-start | bytes 49160 | tf_op jit(solution)/shard_map/ppermute | solution.py:21
  129.9 3.2 %collective-permute-start.18 = (f32[2,16,128]{2,1,0:T(8,128)S(1)}, f32[2,16,128]{2,1,0:T(8,128)S(1)}, u32[]{:S(2)}, u32[]{:S(2)}) collective-permute-start(f32[2,16,128]{2,1,0:T(8,128)S(1)} %get-tuple-element.52.st0_ref), channel_id=1, source_target_pairs={{4,0},{6,2},{8,4},{10,6},{12,8},{14,10},{16,12},{18,14},{20,16},{2... | collective-permute-start | bytes 49160 | tf_op jit(solution)/shard_map/ppermute | solution.py:21
  133.2 0.0 collective-permute-done.17.st1_ref
  133.2 2.4 %collective-permute-done.18.st2_ref = f32[2,16,128]{2,1,0:T(8,128)S(1)} collective-permute-done((f32[2,16,128]{2,1,0:T(8,128)S(1)}, f32[2,16,128]{2,1,0:T(8,128)S(1)}, u32[]{:S(2)}, u32[]{:S(2)}) %collective-permute-start.18) | collective-permute-done | bytes 16416 | tf_op jit(solution)/shard_map/ppermute | solution.py:21
  135.6 2.7 %key_grads.1 = (bf16[128,1280]{1,0:T(8,128)(2,1)}, bf16[128,1280]{1,0:T(8,128)(2,1)}) custom-call(bf16[128,1280]{1,0:T(8,128)(2,1)S(1)} %copy-done.2, bf16[128,1280]{1,0:T(8,128)(2,1)S(1)} %copy-done.3, bf16[128,1280]{1,0:T(8,128)(2,1)S(1)} %copy-done, bf16[128,1280]{1,0:T(8,128)(2,1)S(1)} %copy-done.1, ...), custom_call_target="tpu_custom_call" | custom-call | flops 503316480 | bytes 4194304 | tf_op jit(solution)/shard_map/key_grads/pallas_call | solution.py:166
  (5 shorter events, 0.0 us)
Async XLA Ops:
  0.6 4.0 %copy-start = (bf16[128,1280]{1,0:T(8,128)(2,1)S(1)}, bf16[128,1280]{1,0:T(8,128)(2,1)}, u32[]{:S(2)}) copy-start(bf16[128,1280]{1,0:T(8,128)(2,1)} %q_ref.3) | copy-start | bytes 983044
  0.6 4.0 %copy-start.1 = (bf16[128,1280]{1,0:T(8,128)(2,1)S(1)}, bf16[128,1280]{1,0:T(8,128)(2,1)}, u32[]{:S(2)}) copy-start(bf16[128,1280]{1,0:T(8,128)(2,1)} %g_ref.3) | copy-start | bytes 983044
  0.7 9.5 %copy-start.8 = (bf16[2,160,1280]{2,1,0:T(8,128)(2,1)S(1)}, bf16[2,160,1280]{2,1,0:T(8,128)(2,1)}, u32[]{:S(2)}) copy-start(bf16[2,160,1280]{2,1,0:T(8,128)(2,1)} %param.13) | copy-start | bytes 2457604
  2.7 41.3 %collective-permute-start.5 = (bf16[2,128,1280]{2,1,0:T(8,128)(2,1)}, bf16[2,128,1280]{2,1,0:T(8,128)(2,1)S(1)}, u32[]{:S(2)}, u32[]{:S(2)}) collective-permute-start(bf16[2,128,1280]{2,1,0:T(8,128)(2,1)} %pad_maximum_fusion.1), channel_id=1, source_target_pairs={{0,2},{2,4},{4,6},{6,8},{8,10},{10,12},{12,14},{14,16},{16,18},{18... | collective-permute-start | bytes 1966088 | tf_op jit(solution)/shard_map/ppermute | solution.py:21
  4.7 26.6 %copy-start.4 = (bf16[128,1280]{1,0:T(8,128)(2,1)S(1)}, bf16[128,1280]{1,0:T(8,128)(2,1)}, u32[]{:S(2)}) copy-start(bf16[128,1280]{1,0:T(8,128)(2,1)} %refs_0_.1) | copy-start | bytes 983044
  5.6 38.5 %collective-permute-start.6 = (bf16[2,128,1280]{2,1,0:T(8,128)(2,1)}, bf16[2,128,1280]{2,1,0:T(8,128)(2,1)S(1)}, u32[]{:S(2)}, u32[]{:S(2)}) collective-permute-start(bf16[2,128,1280]{2,1,0:T(8,128)(2,1)} %pad_maximum_fusion.2), channel_id=1, source_target_pairs={{2,0},{4,2},{6,4},{8,6},{10,8},{12,10},{14,12},{16,14},{18,16},{20... | collective-permute-start | bytes 1966088 | tf_op jit(solution)/shard_map/ppermute | solution.py:21
  10.2 65.3 %copy-start.6 = (s32[2048]{0:T(1024)S(1)}, s32[2048]{0:T(1024)}, u32[]{:S(2)}) copy-start(s32[2048]{0:T(1024)} %param.15) | copy-start | bytes 24580
  10.2 65.3 %copy-start.7 = (s32[2048]{0:T(1024)S(1)}, s32[2048]{0:T(1024)}, u32[]{:S(2)}) copy-start(s32[2048]{0:T(1024)} %param.14) | copy-start | bytes 24580
  10.3 20.9 %collective-permute-start = (bf16[160,640]{1,0:T(8,128)(2,1)S(1)}, bf16[160,640]{1,0:T(8,128)(2,1)S(1)}, u32[]{:S(2)}, u32[]{:S(2)}) collective-permute-start(bf16[160,640]{1,0:T(8,128)(2,1)S(1)} %get-tuple-element.57), channel_id=1, source_target_pairs={{0,8},{8,0},{16,24},{24,16},{1,9},{9,1},{17,25},{25,17},{2,10},{10... | collective-permute-start | bytes 614408 | tf_op jit(solution)/shard_map/ppermute | solution.py:25
  12.0 25.0 %collective-permute-start.1 = (bf16[160,640]{1,0:T(8,128)(2,1)S(1)}, bf16[160,640]{1,0:T(8,128)(2,1)S(1)}, u32[]{:S(2)}, u32[]{:S(2)}) collective-permute-start(bf16[160,640]{1,0:T(8,128)(2,1)S(1)} %get-tuple-element.59), channel_id=1, source_target_pairs={{0,16},{8,24},{16,0},{24,8},{1,17},{9,25},{17,1},{25,9},{2,18},{10... | collective-permute-start | bytes 614408 | tf_op jit(solution)/shard_map/ppermute | solution.py:25
  12.3 26.9 %collective-permute-start.2 = (bf16[160,640]{1,0:T(8,128)(2,1)S(1)}, bf16[160,640]{1,0:T(8,128)(2,1)S(1)}, u32[]{:S(2)}, u32[]{:S(2)}) collective-permute-start(bf16[160,640]{1,0:T(8,128)(2,1)S(1)} %get-tuple-element.58), channel_id=1, source_target_pairs={{0,24},{8,16},{16,8},{24,0},{1,25},{9,17},{17,9},{25,1},{2,26},{10... | collective-permute-start | bytes 614408 | tf_op jit(solution)/shard_map/ppermute | solution.py:25
  31.3 11.4 %collective-permute-start.3 = (bf16[128,1280]{1,0:T(8,128)(2,1)S(1)}, bf16[128,1280]{1,0:T(8,128)(2,1)S(1)}, u32[]{:S(2)}, u32[]{:S(2)}) collective-permute-start(bf16[128,1280]{1,0:T(8,128)(2,1)S(1)} %copy-done.4), channel_id=1, source_target_pairs={{0,8},{8,24},{24,16},{16,0},{1,9},{9,25},{25,17},{17,1},{2,10},{10... | collective-permute-start | bytes 983048 | tf_op jit(solution)/shard_map/ppermute | solution.py:316
  37.0 7.1 %collective-permute-start.4 = (bf16[128,1280]{1,0:T(8,128)(2,1)S(1)}, bf16[128,1280]{1,0:T(8,128)(2,1)S(1)}, u32[]{:S(2)}, u32[]{:S(2)}) collective-permute-start(bf16[128,1280]{1,0:T(8,128)(2,1)S(1)} %copy-done.4), channel_id=1, source_target_pairs={{0,1},{1,0},{2,3},{3,2},{4,5},{5,4},{6,7},{7,6},{8,9},{9,8},{10,11... | collective-permute-start | bytes 983048 | tf_op jit(solution)/shard_map/ppermute | solution.py:25
  44.1 42.1 %copy-start.9 = (bf16[2,128,1280]{2,1,0:T(8,128)(2,1)}, bf16[2,128,1280]{2,1,0:T(8,128)(2,1)S(1)}, u32[]{:S(2)}) copy-start(bf16[2,128,1280]{2,1,0:T(8,128)(2,1)S(1)} %collective-permute-done.5.kv1_ref) | copy-start | bytes 1966084
  44.1 13.3 %collective-permute-start.9 = (bf16[4,160,640]{2,1,0:T(8,128)(2,1)S(1)}, bf16[4,160,640]{2,1,0:T(8,128)(2,1)S(1)}, u32[]{:S(2)}, u32[]{:S(2)}) collective-permute-start(bf16[4,160,640]{2,1,0:T(8,128)(2,1)S(1)} %pad_maximum_fusion.refs_8_), channel_id=1, source_target_pairs={{0,2},{2,0},{4,6},{6,4},{1,3},{3,1},{5,7},{7,5},{8,10},{10,8},{12,... | collective-permute-start | bytes 2457608 | tf_op jit(solution)/shard_map/ppermute | solution.py:25
  44.2 20.7 %collective-permute-start.10 = (bf16[4,160,640]{2,1,0:T(8,128)(2,1)S(1)}, bf16[4,160,640]{2,1,0:T(8,128)(2,1)S(1)}, u32[]{:S(2)}, u32[]{:S(2)}) collective-permute-start(bf16[4,160,640]{2,1,0:T(8,128)(2,1)S(1)} %pad_maximum_fusion.refs_8_), channel_id=1, source_target_pairs={{0,4},{2,6},{4,0},{6,2},{1,5},{3,7},{5,1},{7,3},{8,12},{10,14},{12... | collective-permute-start | bytes 2457608 | tf_op jit(solution)/shard_map/ppermute | solution.py:25
  44.2 10.9 %collective-permute-start.7 = (bf16[128,1280]{1,0:T(8,128)(2,1)S(1)}, bf16[128,1280]{1,0:T(8,128)(2,1)S(1)}, u32[]{:S(2)}, u32[]{:S(2)}) collective-permute-start(bf16[128,1280]{1,0:T(8,128)(2,1)S(1)} %collective-permute-done.3.refs_1_), channel_id=1, source_target_pairs={{0,8},{8,24},{24,16},{16,0},{1,9},{9,25},{25,17},{17,1},{2,10},{10... | collective-permute-start | bytes 983048 | tf_op jit(solution)/shard_map/ppermute | solution.py:316
  47.7 9.7 %collective-permute-start.8 = (bf16[128,1280]{1,0:T(8,128)(2,1)S(1)}, bf16[128,1280]{1,0:T(8,128)(2,1)S(1)}, u32[]{:S(2)}, u32[]{:S(2)}) collective-permute-start(bf16[128,1280]{1,0:T(8,128)(2,1)S(1)} %collective-permute-done.3.refs_1_), channel_id=1, source_target_pairs={{0,1},{1,0},{2,3},{3,2},{4,5},{5,4},{6,7},{7,6},{8,9},{9,8},{10,11... | collective-permute-start | bytes 983048 | tf_op jit(solution)/shard_map/ppermute | solution.py:25
  57.4 8.8 %collective-permute-start.11 = (bf16[128,1280]{1,0:T(8,128)(2,1)S(1)}, bf16[128,1280]{1,0:T(8,128)(2,1)S(1)}, u32[]{:S(2)}, u32[]{:S(2)}) collective-permute-start(bf16[128,1280]{1,0:T(8,128)(2,1)S(1)} %collective-permute-done.7.refs_2_), channel_id=1, source_target_pairs={{0,8},{8,24},{24,16},{16,0},{1,9},{9,25},{25,17},{17,1},{2,10},{10... | collective-permute-start | bytes 983048 | tf_op jit(solution)/shard_map/ppermute | solution.py:316
  58.6 8.9 %collective-permute-start.12 = (bf16[128,1280]{1,0:T(8,128)(2,1)S(1)}, bf16[128,1280]{1,0:T(8,128)(2,1)S(1)}, u32[]{:S(2)}, u32[]{:S(2)}) collective-permute-start(bf16[128,1280]{1,0:T(8,128)(2,1)S(1)} %collective-permute-done.7.refs_2_), channel_id=1, source_target_pairs={{0,1},{1,0},{2,3},{3,2},{4,5},{5,4},{6,7},{7,6},{8,9},{9,8},{10,11... | collective-permute-start | bytes 983048 | tf_op jit(solution)/shard_map/ppermute | solution.py:25
  67.4 15.2 %collective-permute-start.14 = (bf16[4,160,640]{2,1,0:T(8,128)(2,1)S(1)}, bf16[4,160,640]{2,1,0:T(8,128)(2,1)S(1)}, u32[]{:S(2)}, u32[]{:S(2)}) collective-permute-start(bf16[4,160,640]{2,1,0:T(8,128)(2,1)S(1)} %collective-permute-done.10.refs_10_), channel_id=1, source_target_pairs={{0,2},{2,0},{4,6},{6,4},{1,3},{3,1},{5,7},{7,5},{8,10},{10,8},{12,... | collective-permute-start | bytes 2457608 | tf_op jit(solution)/shard_map/ppermute | solution.py:25
  67.5 18.7 %collective-permute-start.15 = (bf16[2,128,1280]{2,1,0:T(8,128)(2,1)S(1)}, bf16[2,128,1280]{2,1,0:T(8,128)(2,1)S(1)}, u32[]{:S(2)}, u32[]{:S(2)}) collective-permute-start(bf16[2,128,1280]{2,1,0:T(8,128)(2,1)S(1)} %collective-permute-done.5.kv1_ref), channel_id=1, source_target_pairs={{0,2},{2,4},{4,6},{6,8},{8,10},{10,12},{12,14},{14,16},{16,18},{18... | collective-permute-start | bytes 1966088 | tf_op jit(solution)/shard_map/ppermute | solution.py:21
  69.9 16.4 %collective-permute-start.16 = (bf16[2,128,1280]{2,1,0:T(8,128)(2,1)S(1)}, bf16[2,128,1280]{2,1,0:T(8,128)(2,1)S(1)}, u32[]{:S(2)}, u32[]{:S(2)}) collective-permute-start(bf16[2,128,1280]{2,1,0:T(8,128)(2,1)S(1)} %collective-permute-done.6.qg1_ref), channel_id=1, source_target_pairs={{2,0},{4,2},{6,4},{8,6},{10,8},{12,10},{14,12},{16,14},{18,16},{20... | collective-permute-start | bytes 1966088 | tf_op jit(solution)/shard_map/ppermute | solution.py:21
  73.9 8.7 %collective-permute-start.13 = (bf16[128,1280]{1,0:T(8,128)(2,1)S(1)}, bf16[128,1280]{1,0:T(8,128)(2,1)S(1)}, u32[]{:S(2)}, u32[]{:S(2)}) collective-permute-start(bf16[128,1280]{1,0:T(8,128)(2,1)S(1)} %collective-permute-done.11.refs_3_), channel_id=1, source_target_pairs={{0,1},{1,0},{2,3},{3,2},{4,5},{5,4},{6,7},{7,6},{8,9},{9,8},{10,11... | collective-permute-start | bytes 983048 | tf_op jit(solution)/shard_map/ppermute | solution.py:25
  75.8 10.4 %copy-start.5 = (bf16[128,640]{1,0:T(8,128)(2,1)}, bf16[128,640]{1,0:T(8,128)(2,1)S(1)}, u32[]{:S(2)}) copy-start(bf16[128,640]{1,0:T(8,128)(2,1)S(1)} %get-tuple-element.47.bias_ref) | copy-start | bytes 491524
  86.2 35.9 %copy-start.2 = (bf16[128,1280]{1,0:T(8,128)(2,1)S(1)}, bf16[128,1280]{1,0:T(8,128)(2,1)}, u32[]{:S(2)}) copy-start(bf16[128,1280]{1,0:T(8,128)(2,1)} %k_ref.3) | copy-start | bytes 983044
  86.2 35.9 %copy-start.3 = (bf16[128,1280]{1,0:T(8,128)(2,1)S(1)}, bf16[128,1280]{1,0:T(8,128)(2,1)}, u32[]{:S(2)}) copy-start(bf16[128,1280]{1,0:T(8,128)(2,1)} %v_ref.3) | copy-start | bytes 983044
  86.2 35.9 %copy-start.10 = (bf16[2,128,1280]{2,1,0:T(8,128)(2,1)}, bf16[2,128,1280]{2,1,0:T(8,128)(2,1)S(1)}, u32[]{:S(2)}) copy-start(bf16[2,128,1280]{2,1,0:T(8,128)(2,1)S(1)} %collective-permute-done.15.kv2_ref) | copy-start | bytes 1966084
  127.1 6.0 %collective-permute-start.17 = (f32[2,16,128]{2,1,0:T(8,128)S(1)}, f32[2,16,128]{2,1,0:T(8,128)S(1)}, u32[]{:S(2)}, u32[]{:S(2)}) collective-permute-start(f32[2,16,128]{2,1,0:T(8,128)S(1)} %get-tuple-element.52.st0_ref), channel_id=1, source_target_pairs={{2,0},{4,2},{6,4},{8,6},{10,8},{12,10},{14,12},{16,14},{18,16},{20... | collective-permute-start | bytes 49160 | tf_op jit(solution)/shard_map/ppermute | solution.py:21
  129.9 5.6 %collective-permute-start.18 = (f32[2,16,128]{2,1,0:T(8,128)S(1)}, f32[2,16,128]{2,1,0:T(8,128)S(1)}, u32[]{:S(2)}, u32[]{:S(2)}) collective-permute-start(f32[2,16,128]{2,1,0:T(8,128)S(1)} %get-tuple-element.52.st0_ref), channel_id=1, source_target_pairs={{4,0},{6,2},{8,4},{10,6},{12,8},{14,10},{16,12},{18,14},{20,16},{2... | collective-permute-start | bytes 49160 | tf_op jit(solution)/shard_map/ppermute | solution.py:21

commit v2 on v1

--- a/solution.py
+++ b/solution.py
@@ -328,25 +328,21 @@
             [blocks[0]] + [swapped(blocks[mask], "z", mask) for mask in range(1, n_z)], 0
         )
         row1, other0 = ring_step(cache), swapped(cache, "head", 1)
-        near, back1 = shifted(stream, 1), shifted(back, -1)
-        own, row1, other0, near, back1 = lax.optimization_barrier(
-            (own, row1, other0, near, back1)
-        )
+        own, row1, other0 = lax.optimization_barrier((own, row1, other0))
         across = swapped(own, "p", 2)
         beside = swapped(own, "p", 1)
         row2, other1 = ring_step(row1), swapped(row1, "head", 1)
         row2, other1, beside = lax.optimization_barrier((row2, other1, beside))
         row3, other2 = ring_step(row2), swapped(row2, "head", 1)
-        across, row3, other2, near, back1 = lax.optimization_barrier(
-            (across, row3, other2, near, back1)
-        )
+        across, row3, other2, stream = lax.optimization_barrier((across, row3, other2, stream))
         pieces = [own, beside, across, swapped(across, "p", 1)]
-        far, back2 = shifted(near, 1), shifted(back1, -1)
+        near = shifted(stream, 1)
         rows = [cache, row1, row2, row3, other0, other1, other2, swapped(row3, "head", 1)]
         slots = project(place, rows, pieces, devices, capacity)
-        return lax.optimization_barrier((slots, near, far, back1, back2))
+        slots, near, back = lax.optimization_barrier((slots, near, back))
+        return slots, near, shifted(near, 1), shifted(back, -1)
     near, back1 = shifted(stream, 1), shifted(back, -1)
-    far, back2 = shifted(near, 1), shifted(back1, -1)
+    far = shifted(near, 1)
     targets = [column_block(w_kv, jnp.int32(i)) for i in range(n_z)]
     w_z = lax.all_to_all(jnp.stack(targets, 0), "z", split_axis=0, concat_axis=0, tiled=True)
     w_all = lax.all_gather(w_z, "p", axis=1, tiled=True).reshape(devices * w_rows, -1)
@@ -367,7 +363,7 @@
         preferred_element_type=jnp.float32,
     ).astype(jnp.bfloat16)
     slots = slots.reshape(n_z, devices, capacity, -1).transpose(1, 0, 2, 3)
-    return slots, near, far, back1, back2
+    return slots, near, far, back1
 
 
 def body(queries, keys, values, grad_out, cache, w_kv, doc_ids, routes):
@@ -379,7 +375,7 @@
     slot_count = capacity * devices
 
     place, bias, back_bias = prepare(routes, doc_ids, n_z, devices, seg_rows)
-    slots, kv1, kv2, qg1, qg2 = memory_slots(
+    slots, kv1, kv2, qg1 = memory_slots(
         cache,
         w_kv,
         place,
@@ -390,6 +386,8 @@
     memory = lax.all_to_all(slots, SEQ, split_axis=0, concat_axis=0, tiled=True)
     memory = memory.reshape(n_z, slot_count, slots.shape[-1])
 
+    memory, qg1 = lax.optimization_barrier((memory, qg1))
+    qg2 = shifted(qg1, -1)
     output, grad_q, stats = attend(queries, grad_out, keys, values, kv1, kv2, memory, bias)
     all_stats = [stats, shifted(stats, -1), shifted(stats, -2)]
     grad_k, grad_v = key_grads(

time: 140 us -> 133 us (0.950)
  blocking collectives: 35.9 us -> 0 us
  waiting for transfers between devices: 53.4 us -> 77.9 us
  starting transfers between devices: 33.4 us -> 38 us
  local copies, waits for them, and re-layouts: 0.14 us -> 2.25 us
  other arithmetic: 3.14 us -> 1.08 us
    all_to_all x1 -> x0, blocking collectives: 35.9 us -> none  [body(): memory = lax.all_to_all(slots, SEQ, split_axis=0, concat_axis=0, tiled=True)]
    ppermute x6, waiting for transfers between devices: 2.42 us -> 34.8 us  [shifted(): return lax.ppermute(value, SEQ, pairs)]
    ppermute x10, waiting for transfers between devices: 40.2 us -> 31.8 us  [swapped(): lax.ppermute(value, axis, [(i, i ^ mask) for i in range(lax.axis_size(axi...]
    all_to_all x0 -> x1, starting transfers between devices: none -> 6.16 us  [body(): memory = lax.all_to_all(slots, SEQ, split_axis=0, concat_axis=0, tiled=True)]
    ppermute x6, starting transfers between devices: 18.9 us -> 15.9 us  [shifted(): return lax.ppermute(value, SEQ, pairs)]
    another operation x1, other arithmetic: 2.08 us -> 0.06 us  [body(): jnp.stack([keys, values], 0)]
  transfers between devices with their start and end apart: 19 -> 20, of which waited for: 12 -> 12; matrix products, arithmetic and copies ran while one was open for 1% -> 1% of each run, Pallas kernels for 3% -> 7%
where the time goes in v2:
time: 133 us
  waiting for transfers between devices  77.9 us (59%)
  starting transfers between devices  38 us (29%)
  Pallas kernels  12.5 us (9%)
  local copies, waits for them, and re-layouts  2.25 us (2%)
    ppermute x6, waiting for transfers between devices, shifted(): return lax.ppermute(value, SEQ, pairs)  34.8 us
    ppermute x10, waiting for transfers between devices, swapped(): lax.ppermute(value, axis, [(i, i ^ mask) for i in range(lax.axis_size(axi...  31.8 us
    ppermute x6, starting transfers between devices, shifted(): return lax.ppermute(value, SEQ, pairs)  15.9 us
    ppermute x3, waiting for transfers between devices, ring_step(): lax.ppermute(value, 'z', [(a, b) for a, b in zip(RING, RING[1:] + RING[:1...  11.4 us
    ppermute x10, starting transfers between devices, swapped(): lax.ppermute(value, axis, [(i, i ^ mask) for i in range(lax.axis_size(axi...  10.4 us
    all_to_all x1, starting transfers between devices, body(): memory = lax.all_to_all(slots, SEQ, split_axis=0, concat_axis=0, tiled=True)  6.16 us
    ppermute x3, starting transfers between devices, ring_step(): lax.ppermute(value, 'z', [(a, b) for a, b in zip(RING, RING[1:] + RING[:1...  5.58 us
    pallas_call x1, Pallas kernels, attend(): pl.pallas_call(attend_kernel, grid=(steps,), in_specs=[flat, flat, flat,...  5.01 us
  transfers between devices with their start and end apart: 20, of which 12 were waited for; matrix products, arithmetic and copies ran while one was open for 1% of the time, Pallas kernels for 7%

profile of v2, /device:TPU:16, one launch (start us, length us, event | category | flops | bytes accessed | tf_op | source)
XLA Modules:
  0.0 132.5 jit_solution(4098855987528781193)
XLA Ops:
  0.6 0.0 copy-start.4
  0.7 0.0 copy-start.2
  0.7 0.0 copy-start.3
  0.7 1.4 %constant_dynamic-slice_fusion = (bf16[1,160,640]{2,1,0:T(8,128)(2,1)S(1)}, bf16[160,640]{1,0:T(8,128)(2,1)S(1)}, bf16[160,640]{1,0:T(8,128)(2,1)S(1)}, bf16[160,640]{1,0:T(8,128)(2,1)S(1)}) fusion(bf16[2,160,1280]{2,1,0:T(8,128)(2,1)} %param.13, s32[]{:T(128)S(6)} %select_n.24, s32[]{:T(128)S(6)} %select_n.25, s32[]{:T(128)S(6)} %select_n.26, ...), kind=kLoop, calls=%fused_computation.6 | loop fusion | bytes 1638432 | tf_op jit(solution)/shard_map/dynamic_slice | solution.py:312
  2.1 1.6 %collective-permute-start = (bf16[160,640]{1,0:T(8,128)(2,1)S(1)}, bf16[160,640]{1,0:T(8,128)(2,1)S(1)}, u32[]{:S(2)}, u32[]{:S(2)}) collective-permute-start(bf16[160,640]{1,0:T(8,128)(2,1)S(1)} %get-tuple-element.51), channel_id=1, source_target_pairs={{0,8},{8,0},{16,24},{24,16},{1,9},{9,1},{17,25},{25,17},{2,10},{10... | collective-permute-start | bytes 614408 | tf_op jit(solution)/shard_map/ppermute | solution.py:25
  3.7 0.3 collective-permute-start.1
  4.1 1.6 %collective-permute-start.2 = (bf16[160,640]{1,0:T(8,128)(2,1)S(1)}, bf16[160,640]{1,0:T(8,128)(2,1)S(1)}, u32[]{:S(2)}, u32[]{:S(2)}) collective-permute-start(bf16[160,640]{1,0:T(8,128)(2,1)S(1)} %get-tuple-element.52), channel_id=1, source_target_pairs={{0,24},{8,16},{16,8},{24,0},{1,25},{9,17},{17,9},{25,1},{2,26},{10... | collective-permute-start | bytes 614408 | tf_op jit(solution)/shard_map/ppermute | solution.py:25
  5.6 0.0 copy-done.4
  5.6 1.0 collective-permute-start.3
  6.6 1.7 %collective-permute-start.4 = (bf16[128,1280]{1,0:T(8,128)(2,1)S(1)}, bf16[128,1280]{1,0:T(8,128)(2,1)S(1)}, u32[]{:S(2)}, u32[]{:S(2)}) collective-permute-start(bf16[128,1280]{1,0:T(8,128)(2,1)S(1)} %copy-done.4), channel_id=1, source_target_pairs={{0,1},{1,0},{2,3},{3,2},{4,5},{5,4},{6,7},{7,6},{8,9},{9,8},{10,11... | collective-permute-start | bytes 983048 | tf_op jit(solution)/shard_map/ppermute | solution.py:25
  8.4 2.7 %collective-permute-done = bf16[160,640]{1,0:T(8,128)(2,1)S(1)} collective-permute-done((bf16[160,640]{1,0:T(8,128)(2,1)S(1)}, bf16[160,640]{1,0:T(8,128)(2,1)S(1)}, u32[]{:S(2)}, u32[]{:S(2)}) %collective-permute-start) | collective-permute-done | bytes 204832 | tf_op jit(solution)/shard_map/ppermute | solution.py:25
  11.1 7.1 %collective-permute-done.1 = bf16[160,640]{1,0:T(8,128)(2,1)S(1)} collective-permute-done((bf16[160,640]{1,0:T(8,128)(2,1)S(1)}, bf16[160,640]{1,0:T(8,128)(2,1)S(1)}, u32[]{:S(2)}, u32[]{:S(2)}) %collective-permute-start.1) | collective-permute-done | bytes 204832 | tf_op jit(solution)/shard_map/ppermute | solution.py:25
  18.2 6.6 %collective-permute-done.2 = bf16[160,640]{1,0:T(8,128)(2,1)S(1)} collective-permute-done((bf16[160,640]{1,0:T(8,128)(2,1)S(1)}, bf16[160,640]{1,0:T(8,128)(2,1)S(1)}, u32[]{:S(2)}, u32[]{:S(2)}) %collective-permute-start.2) | collective-permute-done | bytes 204832 | tf_op jit(solution)/shard_map/ppermute | solution.py:25
  24.8 0.0 copy-start.6
  24.8 0.0 copy-start.7
  24.8 0.0 copy-start
  24.8 0.0 copy-start.1
  24.8 0.1 pad_maximum_fusion.refs_8_
  24.9 3.4 %collective-permute-done.3.refs_1_ = bf16[128,1280]{1,0:T(8,128)(2,1)S(1)} collective-permute-done((bf16[128,1280]{1,0:T(8,128)(2,1)S(1)}, bf16[128,1280]{1,0:T(8,128)(2,1)S(1)}, u32[]{:S(2)}, u32[]{:S(2)}) %collective-permute-start.3) | collective-permute-done | bytes 327712 | tf_op jit(solution)/shard_map/ppermute | solution.py:316
  28.3 0.0 collective-permute-done.4.refs_4_
  28.3 0.0 collective-permute-start.7
  28.4 1.5 %collective-permute-start.8 = (bf16[4,160,640]{2,1,0:T(8,128)(2,1)S(1)}, bf16[4,160,640]{2,1,0:T(8,128)(2,1)S(1)}, u32[]{:S(2)}, u32[]{:S(2)}) collective-permute-start(bf16[4,160,640]{2,1,0:T(8,128)(2,1)S(1)} %pad_maximum_fusion.refs_8_), channel_id=1, source_target_pairs={{0,4},{2,6},{4,0},{6,2},{1,5},{3,7},{5,1},{7,3},{8,12},{10,14},{12... | collective-permute-start | bytes 2457608 | tf_op jit(solution)/shard_map/ppermute | solution.py:25
  29.8 3.4 %collective-permute-start.5 = (bf16[128,1280]{1,0:T(8,128)(2,1)S(1)}, bf16[128,1280]{1,0:T(8,128)(2,1)S(1)}, u32[]{:S(2)}, u32[]{:S(2)}) collective-permute-start(bf16[128,1280]{1,0:T(8,128)(2,1)S(1)} %collective-permute-done.3.refs_1_), channel_id=1, source_target_pairs={{0,8},{8,24},{24,16},{16,0},{1,9},{9,25},{25,17},{17,1},{2,10},{10... | collective-permute-start | bytes 983048 | tf_op jit(solution)/shard_map/ppermute | solution.py:316
  33.2 1.5 %collective-permute-start.6 = (bf16[128,1280]{1,0:T(8,128)(2,1)S(1)}, bf16[128,1280]{1,0:T(8,128)(2,1)S(1)}, u32[]{:S(2)}, u32[]{:S(2)}) collective-permute-start(bf16[128,1280]{1,0:T(8,128)(2,1)S(1)} %collective-permute-done.3.refs_1_), channel_id=1, source_target_pairs={{0,1},{1,0},{2,3},{3,2},{4,5},{5,4},{6,7},{7,6},{8,9},{9,8},{10,11... | collective-permute-start | bytes 983048 | tf_op jit(solution)/shard_map/ppermute | solution.py:25
  34.7 6.7 %collective-permute-done.5.refs_2_ = bf16[128,1280]{1,0:T(8,128)(2,1)S(1)} collective-permute-done((bf16[128,1280]{1,0:T(8,128)(2,1)S(1)}, bf16[128,1280]{1,0:T(8,128)(2,1)S(1)}, u32[]{:S(2)}, u32[]{:S(2)}) %collective-permute-start.5) | collective-permute-done | bytes 327712 | tf_op jit(solution)/shard_map/ppermute | solution.py:316
  41.4 1.4 %collective-permute-done.6.refs_5_ = bf16[128,1280]{1,0:T(8,128)(2,1)S(1)} collective-permute-done((bf16[128,1280]{1,0:T(8,128)(2,1)S(1)}, bf16[128,1280]{1,0:T(8,128)(2,1)S(1)}, u32[]{:S(2)}, u32[]{:S(2)}) %collective-permute-start.6) | collective-permute-done | bytes 327712 | tf_op jit(solution)/shard_map/ppermute | solution.py:25
  42.8 0.0 collective-permute-done.7.refs_9_
  42.8 1.5 %collective-permute-start.10 = (bf16[128,1280]{1,0:T(8,128)(2,1)S(1)}, bf16[128,1280]{1,0:T(8,128)(2,1)S(1)}, u32[]{:S(2)}, u32[]{:S(2)}) collective-permute-start(bf16[128,1280]{1,0:T(8,128)(2,1)S(1)} %collective-permute-done.5.refs_2_), channel_id=1, source_target_pairs={{0,1},{1,0},{2,3},{3,2},{4,5},{5,4},{6,7},{7,6},{8,9},{9,8},{10,11... | collective-permute-start | bytes 983048 | tf_op jit(solution)/shard_map/ppermute | solution.py:25
  44.3 1.2 collective-permute-start.9
  45.5 0.0 copy-done.2
  45.5 0.0 copy-done.3
  45.5 0.1 pad_maximum_fusion.1
  45.6 3.4 %collective-permute-done.8.refs_10_ = bf16[4,160,640]{2,1,0:T(8,128)(2,1)S(1)} collective-permute-done((bf16[4,160,640]{2,1,0:T(8,128)(2,1)S(1)}, bf16[4,160,640]{2,1,0:T(8,128)(2,1)S(1)}, u32[]{:S(2)}, u32[]{:S(2)}) %collective-permute-start.8) | collective-permute-done | bytes 819232 | tf_op jit(solution)/shard_map/ppermute | solution.py:25
  49.0 2.5 %collective-permute-done.10.refs_6_ = bf16[128,1280]{1,0:T(8,128)(2,1)S(1)} collective-permute-done((bf16[128,1280]{1,0:T(8,128)(2,1)S(1)}, bf16[128,1280]{1,0:T(8,128)(2,1)S(1)}, u32[]{:S(2)}, u32[]{:S(2)}) %collective-permute-start.10) | collective-permute-done | bytes 327712 | tf_op jit(solution)/shard_map/ppermute | solution.py:25
  51.5 1.2 collective-permute-done.9.refs_3_
  52.7 0.0 collective-permute-start.12
  52.7 2.4 %collective-permute-start.13 = (bf16[2,128,1280]{2,1,0:T(8,128)(2,1)S(1)}, bf16[2,128,1280]{2,1,0:T(8,128)(2,1)S(1)}, u32[]{:S(2)}, u32[]{:S(2)}) collective-permute-start(bf16[2,128,1280]{2,1,0:T(8,128)(2,1)S(1)} %pad_maximum_fusion.1), channel_id=1, source_target_pairs={{0,2},{2,4},{4,6},{6,8},{8,10},{10,12},{12,14},{14,16},{16,18},{18... | collective-permute-start | bytes 1966088 | tf_op jit(solution)/shard_map/ppermute | solution.py:21
  55.2 0.6 collective-permute-start.11
  55.7 0.0 copy-done.6
  55.7 0.0 copy-done.7
  55.7 0.2 prepare.1
  56.0 0.0 copy-done
  56.0 0.0 copy-done.1
  56.0 0.9 pad_maximum_fusion.2
  56.9 8.1 %collective-permute-done.11.refs_7_ = bf16[128,1280]{1,0:T(8,128)(2,1)S(1)} collective-permute-done((bf16[128,1280]{1,0:T(8,128)(2,1)S(1)}, bf16[128,1280]{1,0:T(8,128)(2,1)S(1)}, u32[]{:S(2)}, u32[]{:S(2)}) %collective-permute-start.11) | collective-permute-done | bytes 327712 | tf_op jit(solution)/shard_map/ppermute | solution.py:25
  65.0 0.0 collective-permute-done.12.refs_11_
  65.0 4.6 %project.1 = bf16[16,4,16,640]{3,2,1,0:T(8,128)(2,1)} custom-call(s32[4,1,128]{2,1,0:T(1,128)S(1)} %get-tuple-element.27.place_ref, bf16[128,1280]{1,0:T(8,128)(2,1)S(1)} %copy-done.4, bf16[128,1280]{1,0:T(8,128)(2,1)S(1)} %collective-permute-done.3.refs_1_, bf16[128,1280]{1,0:T(8,128)(2,1)S(1)} %collective-permute-done.5.refs_2_, ...), custom_call_target="tpu_custom_call" | custom-call | flops 1677721600 | bytes 8388608 | tf_op jit(solution)/shard_map/project/pallas_call | solution.py:225
  69.6 0.0 copy-done.5
  69.6 0.0 collective-permute-done.13.kv1_ref
  69.6 0.8 copy-done.8
  70.4 6.2 %all-to-all-start = ((bf16[16,4,16,640]{3,2,1,0:T(8,128)(2,1)}), bf16[16,4,16,640]{3,2,1,0:T(8,128)(2,1)S(1)}, u32[]{:S(2)}, u32[]{:S(2)}) async-start(bf16[16,4,16,640]{3,2,1,0:T(8,128)(2,1)} %project.1), calls=%async_computation | async-start | bytes 2621440 | tf_op jit(solution)/shard_map/all_to_all | solution.py:386
  76.6 3.1 %collective-permute-start.15 = (bf16[2,128,1280]{2,1,0:T(8,128)(2,1)}, bf16[2,128,1280]{2,1,0:T(8,128)(2,1)S(1)}, u32[]{:S(2)}, u32[]{:S(2)}) collective-permute-start(bf16[2,128,1280]{2,1,0:T(8,128)(2,1)} %pad_maximum_fusion.2), channel_id=1, source_target_pairs={{2,0},{4,2},{6,4},{8,6},{10,8},{12,10},{14,12},{16,14},{18,16},{20... | collective-permute-start | bytes 1966088 | tf_op jit(solution)/shard_map/ppermute | solution.py:21
  79.7 1.9 %collective-permute-start.14 = (bf16[2,128,1280]{2,1,0:T(8,128)(2,1)}, bf16[2,128,1280]{2,1,0:T(8,128)(2,1)}, u32[]{:S(2)}, u32[]{:S(2)}) collective-permute-start(bf16[2,128,1280]{2,1,0:T(8,128)(2,1)} %copy-done.8), channel_id=1, source_target_pairs={{0,2},{2,4},{4,6},{6,8},{8,10},{10,12},{12,14},{14,16},{16,18},{18... | collective-permute-start | bytes 1966088 | tf_op jit(solution)/shard_map/ppermute | solution.py:21
  81.6 31.0 %collective-permute-done.15.qg1_ref = bf16[2,128,1280]{2,1,0:T(8,128)(2,1)S(1)} collective-permute-done((bf16[2,128,1280]{2,1,0:T(8,128)(2,1)}, bf16[2,128,1280]{2,1,0:T(8,128)(2,1)S(1)}, u32[]{:S(2)}, u32[]{:S(2)}) %collective-permute-start.15) | collective-permute-done | bytes 655392 | tf_op jit(solution)/shard_map/ppermute | solution.py:21
  112.7 0.0 all-to-all-done
  112.7 4.6 %collective-permute-start.16 = (bf16[2,128,1280]{2,1,0:T(8,128)(2,1)S(1)}, bf16[2,128,1280]{2,1,0:T(8,128)(2,1)S(1)}, u32[]{:S(2)}, u32[]{:S(2)}) collective-permute-start(bf16[2,128,1280]{2,1,0:T(8,128)(2,1)S(1)} %collective-permute-done.15.qg1_ref), channel_id=1, source_target_pairs={{2,0},{4,2},{6,4},{8,6},{10,8},{12,10},{14,12},{16,14},{18,16},{20... | collective-permute-start | bytes 1966088 | tf_op jit(solution)/shard_map/ppermute | solution.py:21
  117.3 0.0 collective-permute-done.14.kv2_ref
  117.3 5.0 %attend.1 = (bf16[128,1280]{1,0:T(8,128)(2,1)}, bf16[128,1280]{1,0:T(8,128)(2,1)}, f32[2,16,128]{2,1,0:T(8,128)S(1)}) custom-call(bf16[128,1280]{1,0:T(8,128)(2,1)S(1)} %copy-done, bf16[128,1280]{1,0:T(8,128)(2,1)S(1)} %copy-done.1, bf16[128,1280]{1,0:T(8,128)(2,1)S(1)} %copy-done.2, bf16[128,1280]{1,0:T(8,128)(2,1)S(1)} %copy-done.3, ...), custom_call_target="tpu_custom_call" | custom-call | flops 838860800 | bytes 6291456 | tf_op jit(solution)/shard_map/attend/pallas_call | solution.py:103
  122.3 1.9 %collective-permute-start.17 = (f32[2,16,128]{2,1,0:T(8,128)S(1)}, f32[2,16,128]{2,1,0:T(8,128)S(1)}, u32[]{:S(2)}, u32[]{:S(2)}) collective-permute-start(f32[2,16,128]{2,1,0:T(8,128)S(1)} %get-tuple-element.46.st0_ref), channel_id=1, source_target_pairs={{2,0},{4,2},{6,4},{8,6},{10,8},{12,10},{14,12},{16,14},{18,16},{20... | collective-permute-start | bytes 49160 | tf_op jit(solution)/shard_map/ppermute | solution.py:21
  124.2 1.9 %collective-permute-start.18 = (f32[2,16,128]{2,1,0:T(8,128)S(1)}, f32[2,16,128]{2,1,0:T(8,128)S(1)}, u32[]{:S(2)}, u32[]{:S(2)}) collective-permute-start(f32[2,16,128]{2,1,0:T(8,128)S(1)} %get-tuple-element.46.st0_ref), channel_id=1, source_target_pairs={{4,0},{6,2},{8,4},{10,6},{12,8},{14,10},{16,12},{18,14},{20,16},{2... | collective-permute-start | bytes 49160 | tf_op jit(solution)/shard_map/ppermute | solution.py:21
  126.2 0.0 collective-permute-done.17.st1_ref
  126.2 3.7 %collective-permute-done.18.st2_ref = f32[2,16,128]{2,1,0:T(8,128)S(1)} collective-permute-done((f32[2,16,128]{2,1,0:T(8,128)S(1)}, f32[2,16,128]{2,1,0:T(8,128)S(1)}, u32[]{:S(2)}, u32[]{:S(2)}) %collective-permute-start.18) | collective-permute-done | bytes 16416 | tf_op jit(solution)/shard_map/ppermute | solution.py:21
  129.9 0.0 collective-permute-done.16.qg2_ref
  129.9 2.7 %key_grads.1 = (bf16[128,1280]{1,0:T(8,128)(2,1)}, bf16[128,1280]{1,0:T(8,128)(2,1)}) custom-call(bf16[128,1280]{1,0:T(8,128)(2,1)S(1)} %copy-done.2, bf16[128,1280]{1,0:T(8,128)(2,1)S(1)} %copy-done.3, bf16[128,1280]{1,0:T(8,128)(2,1)S(1)} %copy-done, bf16[128,1280]{1,0:T(8,128)(2,1)S(1)} %copy-done.1, ...), custom_call_target="tpu_custom_call" | custom-call | flops 503316480 | bytes 4194304 | tf_op jit(solution)/shard_map/key_grads/pallas_call | solution.py:166
  (2 shorter events, 0.0 us)
Async XLA Ops:
  0.6 5.0 %copy-start.4 = (bf16[128,1280]{1,0:T(8,128)(2,1)S(1)}, bf16[128,1280]{1,0:T(8,128)(2,1)}, u32[]{:S(2)}) copy-start(bf16[128,1280]{1,0:T(8,128)(2,1)} %refs_0_.1) | copy-start | bytes 983044
  0.7 44.8 %copy-start.2 = (bf16[128,1280]{1,0:T(8,128)(2,1)S(1)}, bf16[128,1280]{1,0:T(8,128)(2,1)}, u32[]{:S(2)}) copy-start(bf16[128,1280]{1,0:T(8,128)(2,1)} %k_ref.3) | copy-start | bytes 983044
  0.7 44.8 %copy-start.3 = (bf16[128,1280]{1,0:T(8,128)(2,1)S(1)}, bf16[128,1280]{1,0:T(8,128)(2,1)}, u32[]{:S(2)}) copy-start(bf16[128,1280]{1,0:T(8,128)(2,1)} %v_ref.3) | copy-start | bytes 983044
  2.1 9.0 %collective-permute-start = (bf16[160,640]{1,0:T(8,128)(2,1)S(1)}, bf16[160,640]{1,0:T(8,128)(2,1)S(1)}, u32[]{:S(2)}, u32[]{:S(2)}) collective-permute-start(bf16[160,640]{1,0:T(8,128)(2,1)S(1)} %get-tuple-element.51), channel_id=1, source_target_pairs={{0,8},{8,0},{16,24},{24,16},{1,9},{9,1},{17,25},{25,17},{2,10},{10... | collective-permute-start | bytes 614408 | tf_op jit(solution)/shard_map/ppermute | solution.py:25
  3.7 14.5 %collective-permute-start.1 = (bf16[160,640]{1,0:T(8,128)(2,1)S(1)}, bf16[160,640]{1,0:T(8,128)(2,1)S(1)}, u32[]{:S(2)}, u32[]{:S(2)}) collective-permute-start(bf16[160,640]{1,0:T(8,128)(2,1)S(1)} %get-tuple-element.53), channel_id=1, source_target_pairs={{0,16},{8,24},{16,0},{24,8},{1,17},{9,25},{17,1},{25,9},{2,18},{10... | collective-permute-start | bytes 614408 | tf_op jit(solution)/shard_map/ppermute | solution.py:25
  4.1 20.7 %collective-permute-start.2 = (bf16[160,640]{1,0:T(8,128)(2,1)S(1)}, bf16[160,640]{1,0:T(8,128)(2,1)S(1)}, u32[]{:S(2)}, u32[]{:S(2)}) collective-permute-start(bf16[160,640]{1,0:T(8,128)(2,1)S(1)} %get-tuple-element.52), channel_id=1, source_target_pairs={{0,24},{8,16},{16,8},{24,0},{1,25},{9,17},{17,9},{25,1},{2,26},{10... | collective-permute-start | bytes 614408 | tf_op jit(solution)/shard_map/ppermute | solution.py:25
  5.6 22.7 %collective-permute-start.3 = (bf16[128,1280]{1,0:T(8,128)(2,1)S(1)}, bf16[128,1280]{1,0:T(8,128)(2,1)S(1)}, u32[]{:S(2)}, u32[]{:S(2)}) collective-permute-start(bf16[128,1280]{1,0:T(8,128)(2,1)S(1)} %copy-done.4), channel_id=1, source_target_pairs={{0,8},{8,24},{24,16},{16,0},{1,9},{9,25},{25,17},{17,1},{2,10},{10... | collective-permute-start | bytes 983048 | tf_op jit(solution)/shard_map/ppermute | solution.py:316
  6.6 21.7 %collective-permute-start.4 = (bf16[128,1280]{1,0:T(8,128)(2,1)S(1)}, bf16[128,1280]{1,0:T(8,128)(2,1)S(1)}, u32[]{:S(2)}, u32[]{:S(2)}) collective-permute-start(bf16[128,1280]{1,0:T(8,128)(2,1)S(1)} %copy-done.4), channel_id=1, source_target_pairs={{0,1},{1,0},{2,3},{3,2},{4,5},{5,4},{6,7},{7,6},{8,9},{9,8},{10,11... | collective-permute-start | bytes 983048 | tf_op jit(solution)/shard_map/ppermute | solution.py:25
  24.8 31.0 %copy-start.6 = (s32[2048]{0:T(1024)S(1)}, s32[2048]{0:T(1024)}, u32[]{:S(2)}) copy-start(s32[2048]{0:T(1024)} %param.15) | copy-start | bytes 24580
  24.8 31.0 %copy-start.7 = (s32[2048]{0:T(1024)S(1)}, s32[2048]{0:T(1024)}, u32[]{:S(2)}) copy-start(s32[2048]{0:T(1024)} %param.14) | copy-start | bytes 24580
  24.8 31.2 %copy-start = (bf16[128,1280]{1,0:T(8,128)(2,1)S(1)}, bf16[128,1280]{1,0:T(8,128)(2,1)}, u32[]{:S(2)}) copy-start(bf16[128,1280]{1,0:T(8,128)(2,1)} %q_ref.3) | copy-start | bytes 983044
  24.8 31.2 %copy-start.1 = (bf16[128,1280]{1,0:T(8,128)(2,1)S(1)}, bf16[128,1280]{1,0:T(8,128)(2,1)}, u32[]{:S(2)}) copy-start(bf16[128,1280]{1,0:T(8,128)(2,1)} %g_ref.3) | copy-start | bytes 983044
  28.3 14.4 %collective-permute-start.7 = (bf16[4,160,640]{2,1,0:T(8,128)(2,1)S(1)}, bf16[4,160,640]{2,1,0:T(8,128)(2,1)S(1)}, u32[]{:S(2)}, u32[]{:S(2)}) collective-permute-start(bf16[4,160,640]{2,1,0:T(8,128)(2,1)S(1)} %pad_maximum_fusion.refs_8_), channel_id=1, source_target_pairs={{0,2},{2,0},{4,6},{6,4},{1,3},{3,1},{5,7},{7,5},{8,10},{10,8},{12,... | collective-permute-start | bytes 2457608 | tf_op jit(solution)/shard_map/ppermute | solution.py:25
  28.4 20.7 %collective-permute-start.8 = (bf16[4,160,640]{2,1,0:T(8,128)(2,1)S(1)}, bf16[4,160,640]{2,1,0:T(8,128)(2,1)S(1)}, u32[]{:S(2)}, u32[]{:S(2)}) collective-permute-start(bf16[4,160,640]{2,1,0:T(8,128)(2,1)S(1)} %pad_maximum_fusion.refs_8_), channel_id=1, source_target_pairs={{0,4},{2,6},{4,0},{6,2},{1,5},{3,7},{5,1},{7,3},{8,12},{10,14},{12... | collective-permute-start | bytes 2457608 | tf_op jit(solution)/shard_map/ppermute | solution.py:25
  29.8 11.6 %collective-permute-start.5 = (bf16[128,1280]{1,0:T(8,128)(2,1)S(1)}, bf16[128,1280]{1,0:T(8,128)(2,1)S(1)}, u32[]{:S(2)}, u32[]{:S(2)}) collective-permute-start(bf16[128,1280]{1,0:T(8,128)(2,1)S(1)} %collective-permute-done.3.refs_1_), channel_id=1, source_target_pairs={{0,8},{8,24},{24,16},{16,0},{1,9},{9,25},{25,17},{17,1},{2,10},{10... | collective-permute-start | bytes 983048 | tf_op jit(solution)/shard_map/ppermute | solution.py:316
  33.2 9.6 %collective-permute-start.6 = (bf16[128,1280]{1,0:T(8,128)(2,1)S(1)}, bf16[128,1280]{1,0:T(8,128)(2,1)S(1)}, u32[]{:S(2)}, u32[]{:S(2)}) collective-permute-start(bf16[128,1280]{1,0:T(8,128)(2,1)S(1)} %collective-permute-done.3.refs_1_), channel_id=1, source_target_pairs={{0,1},{1,0},{2,3},{3,2},{4,5},{5,4},{6,7},{7,6},{8,9},{9,8},{10,11... | collective-permute-start | bytes 983048 | tf_op jit(solution)/shard_map/ppermute | solution.py:25
  42.8 8.7 %collective-permute-start.10 = (bf16[128,1280]{1,0:T(8,128)(2,1)S(1)}, bf16[128,1280]{1,0:T(8,128)(2,1)S(1)}, u32[]{:S(2)}, u32[]{:S(2)}) collective-permute-start(bf16[128,1280]{1,0:T(8,128)(2,1)S(1)} %collective-permute-done.5.refs_2_), channel_id=1, source_target_pairs={{0,1},{1,0},{2,3},{3,2},{4,5},{5,4},{6,7},{7,6},{8,9},{9,8},{10,11... | collective-permute-start | bytes 983048 | tf_op jit(solution)/shard_map/ppermute | solution.py:25
  44.3 8.4 %collective-permute-start.9 = (bf16[128,1280]{1,0:T(8,128)(2,1)S(1)}, bf16[128,1280]{1,0:T(8,128)(2,1)S(1)}, u32[]{:S(2)}, u32[]{:S(2)}) collective-permute-start(bf16[128,1280]{1,0:T(8,128)(2,1)S(1)} %collective-permute-done.5.refs_2_), channel_id=1, source_target_pairs={{0,8},{8,24},{24,16},{16,0},{1,9},{9,25},{25,17},{17,1},{2,10},{10... | collective-permute-start | bytes 983048 | tf_op jit(solution)/shard_map/ppermute | solution.py:316
  52.7 12.2 %collective-permute-start.12 = (bf16[4,160,640]{2,1,0:T(8,128)(2,1)S(1)}, bf16[4,160,640]{2,1,0:T(8,128)(2,1)S(1)}, u32[]{:S(2)}, u32[]{:S(2)}) collective-permute-start(bf16[4,160,640]{2,1,0:T(8,128)(2,1)S(1)} %collective-permute-done.8.refs_10_), channel_id=1, source_target_pairs={{0,2},{2,0},{4,6},{6,4},{1,3},{3,1},{5,7},{7,5},{8,10},{10,8},{12,... | collective-permute-start | bytes 2457608 | tf_op jit(solution)/shard_map/ppermute | solution.py:25
  52.7 16.8 %collective-permute-start.13 = (bf16[2,128,1280]{2,1,0:T(8,128)(2,1)S(1)}, bf16[2,128,1280]{2,1,0:T(8,128)(2,1)S(1)}, u32[]{:S(2)}, u32[]{:S(2)}) collective-permute-start(bf16[2,128,1280]{2,1,0:T(8,128)(2,1)S(1)} %pad_maximum_fusion.1), channel_id=1, source_target_pairs={{0,2},{2,4},{4,6},{6,8},{8,10},{10,12},{12,14},{14,16},{16,18},{18... | collective-permute-start | bytes 1966088 | tf_op jit(solution)/shard_map/ppermute | solution.py:21
  55.2 9.8 %collective-permute-start.11 = (bf16[128,1280]{1,0:T(8,128)(2,1)S(1)}, bf16[128,1280]{1,0:T(8,128)(2,1)S(1)}, u32[]{:S(2)}, u32[]{:S(2)}) collective-permute-start(bf16[128,1280]{1,0:T(8,128)(2,1)S(1)} %collective-permute-done.9.refs_3_), channel_id=1, source_target_pairs={{0,1},{1,0},{2,3},{3,2},{4,5},{5,4},{6,7},{7,6},{8,9},{9,8},{10,11... | collective-permute-start | bytes 983048 | tf_op jit(solution)/shard_map/ppermute | solution.py:25
  56.0 13.6 %copy-start.5 = (bf16[128,640]{1,0:T(8,128)(2,1)}, bf16[128,640]{1,0:T(8,128)(2,1)S(1)}, u32[]{:S(2)}) copy-start(bf16[128,640]{1,0:T(8,128)(2,1)S(1)} %get-tuple-element.42.bias_ref) | copy-start | bytes 491524
  69.6 0.8 copy-start.8
  70.4 42.3 %all-to-all-start = ((bf16[16,4,16,640]{3,2,1,0:T(8,128)(2,1)}), bf16[16,4,16,640]{3,2,1,0:T(8,128)(2,1)S(1)}, u32[]{:S(2)}, u32[]{:S(2)}) async-start(bf16[16,4,16,640]{3,2,1,0:T(8,128)(2,1)} %project.1), calls=%async_computation | async-start | bytes 2621440 | tf_op jit(solution)/shard_map/all_to_all | solution.py:386
  76.6 36.1 %collective-permute-start.15 = (bf16[2,128,1280]{2,1,0:T(8,128)(2,1)}, bf16[2,128,1280]{2,1,0:T(8,128)(2,1)S(1)}, u32[]{:S(2)}, u32[]{:S(2)}) collective-permute-start(bf16[2,128,1280]{2,1,0:T(8,128)(2,1)} %pad_maximum_fusion.2), channel_id=1, source_target_pairs={{2,0},{4,2},{6,4},{8,6},{10,8},{12,10},{14,12},{16,14},{18,16},{20... | collective-permute-start | bytes 1966088 | tf_op jit(solution)/shard_map/ppermute | solution.py:21
  79.7 37.6 %collective-permute-start.14 = (bf16[2,128,1280]{2,1,0:T(8,128)(2,1)}, bf16[2,128,1280]{2,1,0:T(8,128)(2,1)}, u32[]{:S(2)}, u32[]{:S(2)}) collective-permute-start(bf16[2,128,1280]{2,1,0:T(8,128)(2,1)} %copy-done.8), channel_id=1, source_target_pairs={{0,2},{2,4},{4,6},{6,8},{8,10},{10,12},{12,14},{14,16},{16,18},{18... | collective-permute-start | bytes 1966088 | tf_op jit(solution)/shard_map/ppermute | solution.py:21
  112.7 17.2 %collective-permute-start.16 = (bf16[2,128,1280]{2,1,0:T(8,128)(2,1)S(1)}, bf16[2,128,1280]{2,1,0:T(8,128)(2,1)S(1)}, u32[]{:S(2)}, u32[]{:S(2)}) collective-permute-start(bf16[2,128,1280]{2,1,0:T(8,128)(2,1)S(1)} %collective-permute-done.15.qg1_ref), channel_id=1, source_target_pairs={{2,0},{4,2},{6,4},{8,6},{10,8},{12,10},{14,12},{16,14},{18,16},{20... | collective-permute-start | bytes 1966088 | tf_op jit(solution)/shard_map/ppermute | solution.py:21
  122.3 3.9 %collective-permute-start.17 = (f32[2,16,128]{2,1,0:T(8,128)S(1)}, f32[2,16,128]{2,1,0:T(8,128)S(1)}, u32[]{:S(2)}, u32[]{:S(2)}) collective-permute-start(f32[2,16,128]{2,1,0:T(8,128)S(1)} %get-tuple-element.46.st0_ref), channel_id=1, source_target_pairs={{2,0},{4,2},{6,4},{8,6},{10,8},{12,10},{14,12},{16,14},{18,16},{20... | collective-permute-start | bytes 49160 | tf_op jit(solution)/shard_map/ppermute | solution.py:21
  124.2 5.6 %collective-permute-start.18 = (f32[2,16,128]{2,1,0:T(8,128)S(1)}, f32[2,16,128]{2,1,0:T(8,128)S(1)}, u32[]{:S(2)}, u32[]{:S(2)}) collective-permute-start(f32[2,16,128]{2,1,0:T(8,128)S(1)} %get-tuple-element.46.st0_ref), channel_id=1, source_target_pairs={{4,0},{6,2},{8,4},{10,6},{12,8},{14,10},{16,12},{18,14},{20,16},{2... | collective-permute-start | bytes 49160 | tf_op jit(solution)/shard_map/ppermute | solution.py:21

commit v3 on v2

--- a/solution.py
+++ b/solution.py
@@ -312,8 +312,9 @@
     return lax.dynamic_slice(w_kv, start, (1, w_rows, half))[0]
 
 
-def ring_step(value):
-    return lax.ppermute(value, "z", [(a, b) for a, b in zip(RING, RING[1:] + RING[:1])])
+def ring_step(value, back=False):
+    pairs = list(zip(RING, RING[1:] + RING[:1]))
+    return lax.ppermute(value, "z", [(b, a) for a, b in pairs] if back else pairs)
 
 
 def memory_slots(cache, w_kv, place, capacity, stream, back):
@@ -328,19 +329,23 @@
             [blocks[0]] + [swapped(blocks[mask], "z", mask) for mask in range(1, n_z)], 0
         )
         row1, other0 = ring_step(cache), swapped(cache, "head", 1)
-        own, row1, other0 = lax.optimization_barrier((own, row1, other0))
+        own, row1, other0, cache = lax.optimization_barrier((own, row1, other0, cache))
         across = swapped(own, "p", 2)
         beside = swapped(own, "p", 1)
-        row2, other1 = ring_step(row1), swapped(row1, "head", 1)
-        row2, other1, beside = lax.optimization_barrier((row2, other1, beside))
-        row3, other2 = ring_step(row2), swapped(row2, "head", 1)
-        across, row3, other2, stream = lax.optimization_barrier((across, row3, other2, stream))
+        row2, row3, other1 = ring_step(row1), ring_step(cache, back=True), swapped(row1, "head", 1)
+        beside, stream, back = lax.optimization_barrier((beside, stream, back))
+        near, back1 = shifted(stream, 1), shifted(back, -1)
+        row2, row3, other1 = lax.optimization_barrier((row2, row3, other1))
+        other2, other3 = swapped(row2, "head", 1), swapped(row3, "head", 1)
+        across, other2, other3, near, back1 = lax.optimization_barrier(
+            (across, other2, other3, near, back1)
+        )
         pieces = [own, beside, across, swapped(across, "p", 1)]
-        near = shifted(stream, 1)
-        rows = [cache, row1, row2, row3, other0, other1, other2, swapped(row3, "head", 1)]
+        far = shifted(near, 1)
+        rows = [cache, row1, row2, row3, other0, other1, other2, other3]
         slots = project(place, rows, pieces, devices, capacity)
-        slots, near, back = lax.optimization_barrier((slots, near, back))
-        return slots, near, shifted(near, 1), shifted(back, -1)
+        slots, far = lax.optimization_barrier((slots, far))
+        return slots, near, far, back1
     near, back1 = shifted(stream, 1), shifted(back, -1)
     far = shifted(near, 1)
     targets = [column_block(w_kv, jnp.int32(i)) for i in range(n_z)]
@@ -386,7 +391,6 @@
     memory = lax.all_to_all(slots, SEQ, split_axis=0, concat_axis=0, tiled=True)
     memory = memory.reshape(n_z, slot_count, slots.shape[-1])
 
-    memory, qg1 = lax.optimization_barrier((memory, qg1))
     qg2 = shifted(qg1, -1)
     output, grad_q, stats = attend(queries, grad_out, keys, values, kv1, kv2, memory, bias)
     all_stats = [stats, shifted(stats, -1), shifted(stats, -2)]

time: 133 us -> 135 us (1.015)
  starting transfers between devices: 38 us -> 45.9 us
  waiting for transfers between devices: 77.9 us -> 72.1 us
    all_to_all x1, waiting for transfers between devices: 0.01 us -> 27.7 us  [body(): memory = lax.all_to_all(slots, SEQ, split_axis=0, concat_axis=0, tiled=True)]
    ppermute x6, waiting for transfers between devices: 34.8 us -> 9.68 us  [shifted(): return lax.ppermute(value, SEQ, pairs)]
    ppermute x6, starting transfers between devices: 15.9 us -> 21.5 us  [shifted(): return lax.ppermute(value, SEQ, pairs)]
    ppermute x3, waiting for transfers between devices: 11.4 us -> 6.79 us  [ring_step(): lax.ppermute(value, 'z', [(b, a) for a, b in pairs] if back else pairs)]
    ppermute x10, waiting for transfers between devices: 31.8 us -> 28 us  [swapped(): lax.ppermute(value, axis, [(i, i ^ mask) for i in range(lax.axis_size(axi...]
    ppermute x10, starting transfers between devices: 10.4 us -> 12.6 us  [swapped(): lax.ppermute(value, axis, [(i, i ^ mask) for i in range(lax.axis_size(axi...]
  transfers between devices with their start and end apart: 20 -> 20, of which waited for: 12 -> 10; matrix products, arithmetic and copies ran while one was open for 1% -> 0% of each run, Pallas kernels for 7% -> 7%
where the time goes in v3:
time: 135 us
  waiting for transfers between devices  72.1 us (53%)
  starting transfers between devices  45.9 us (34%)
  Pallas kernels  13.6 us (10%)
  local copies, waits for them, and re-layouts  2.31 us (2%)
    ppermute x10, waiting for transfers between devices, swapped(): lax.ppermute(value, axis, [(i, i ^ mask) for i in range(lax.axis_size(axi...  28 us
    all_to_all x1, waiting for transfers between devices, body(): memory = lax.all_to_all(slots, SEQ, split_axis=0, concat_axis=0, tiled=True)  27.7 us
    ppermute x6, starting transfers between devices, shifted(): return lax.ppermute(value, SEQ, pairs)  21.5 us
    ppermute x10, starting transfers between devices, swapped(): lax.ppermute(value, axis, [(i, i ^ mask) for i in range(lax.axis_size(axi...  12.6 us
    ppermute x6, waiting for transfers between devices, shifted(): return lax.ppermute(value, SEQ, pairs)  9.68 us
    all_to_all x1, starting transfers between devices, body(): memory = lax.all_to_all(slots, SEQ, split_axis=0, concat_axis=0, tiled=True)  7.14 us
    ppermute x3, waiting for transfers between devices, ring_step(): lax.ppermute(value, 'z', [(b, a) for a, b in pairs] if back else pairs)  6.79 us
    pallas_call x1, Pallas kernels, attend(): pl.pallas_call(attend_kernel, grid=(steps,), in_specs=[flat, flat, flat,...  4.98 us
  transfers between devices with their start and end apart: 20, of which 10 were waited for; matrix products, arithmetic and copies ran while one was open for 0% of the time, Pallas kernels for 7%

profile of v3, /device:TPU:16, one launch (start us, length us, event | category | flops | bytes accessed | tf_op | source)
XLA Modules:
  0.0 135.0 jit_solution(10224393208017050365)
XLA Ops:
  0.6 0.0 copy-start.4
  0.7 0.0 copy-start
  0.7 0.0 copy-start.1
  0.7 0.0 copy-start.2
  0.7 0.0 copy-start.3
  0.7 1.4 %constant_dynamic-slice_fusion = (bf16[1,160,640]{2,1,0:T(8,128)(2,1)S(1)}, bf16[160,640]{1,0:T(8,128)(2,1)S(1)}, bf16[160,640]{1,0:T(8,128)(2,1)S(1)}, bf16[160,640]{1,0:T(8,128)(2,1)S(1)}) fusion(bf16[2,160,1280]{2,1,0:T(8,128)(2,1)} %param.13, s32[]{:T(128)S(6)} %select_n.24, s32[]{:T(128)S(6)} %select_n.25, s32[]{:T(128)S(6)} %select_n.26, ...), kind=kLoop, calls=%fused_computation.6 | loop fusion | bytes 1638432 | tf_op jit(solution)/shard_map/dynamic_slice | solution.py:312
  2.1 1.6 %collective-permute-start = (bf16[160,640]{1,0:T(8,128)(2,1)S(1)}, bf16[160,640]{1,0:T(8,128)(2,1)S(1)}, u32[]{:S(2)}, u32[]{:S(2)}) collective-permute-start(bf16[160,640]{1,0:T(8,128)(2,1)S(1)} %get-tuple-element.55), channel_id=1, source_target_pairs={{0,8},{8,0},{16,24},{24,16},{1,9},{9,1},{17,25},{25,17},{2,10},{10... | collective-permute-start | bytes 614408 | tf_op jit(solution)/shard_map/ppermute | solution.py:25
  3.8 0.3 collective-permute-start.1
  4.1 1.6 %collective-permute-start.2 = (bf16[160,640]{1,0:T(8,128)(2,1)S(1)}, bf16[160,640]{1,0:T(8,128)(2,1)S(1)}, u32[]{:S(2)}, u32[]{:S(2)}) collective-permute-start(bf16[160,640]{1,0:T(8,128)(2,1)S(1)} %get-tuple-element.56), channel_id=1, source_target_pairs={{0,24},{8,16},{16,8},{24,0},{1,25},{9,17},{17,9},{25,1},{2,26},{10... | collective-permute-start | bytes 614408 | tf_op jit(solution)/shard_map/ppermute | solution.py:25
  5.7 0.0 copy-done.4
  5.7 1.0 collective-permute-start.3
  6.7 1.7 %collective-permute-start.4 = (bf16[128,1280]{1,0:T(8,128)(2,1)S(1)}, bf16[128,1280]{1,0:T(8,128)(2,1)S(1)}, u32[]{:S(2)}, u32[]{:S(2)}) collective-permute-start(bf16[128,1280]{1,0:T(8,128)(2,1)S(1)} %copy-done.4), channel_id=1, source_target_pairs={{0,1},{1,0},{2,3},{3,2},{4,5},{5,4},{6,7},{7,6},{8,9},{9,8},{10,11... | collective-permute-start | bytes 983048 | tf_op jit(solution)/shard_map/ppermute | solution.py:25
  8.4 2.7 %collective-permute-done = bf16[160,640]{1,0:T(8,128)(2,1)S(1)} collective-permute-done((bf16[160,640]{1,0:T(8,128)(2,1)S(1)}, bf16[160,640]{1,0:T(8,128)(2,1)S(1)}, u32[]{:S(2)}, u32[]{:S(2)}) %collective-permute-start) | collective-permute-done | bytes 204832 | tf_op jit(solution)/shard_map/ppermute | solution.py:25
  11.2 7.1 %collective-permute-done.1 = bf16[160,640]{1,0:T(8,128)(2,1)S(1)} collective-permute-done((bf16[160,640]{1,0:T(8,128)(2,1)S(1)}, bf16[160,640]{1,0:T(8,128)(2,1)S(1)}, u32[]{:S(2)}, u32[]{:S(2)}) %collective-permute-start.1) | collective-permute-done | bytes 204832 | tf_op jit(solution)/shard_map/ppermute | solution.py:25
  18.3 6.6 %collective-permute-done.2 = bf16[160,640]{1,0:T(8,128)(2,1)S(1)} collective-permute-done((bf16[160,640]{1,0:T(8,128)(2,1)S(1)}, bf16[160,640]{1,0:T(8,128)(2,1)S(1)}, u32[]{:S(2)}, u32[]{:S(2)}) %collective-permute-start.2) | collective-permute-done | bytes 204832 | tf_op jit(solution)/shard_map/ppermute | solution.py:25
  24.8 0.1 pad_maximum_fusion.refs_8_
  25.0 3.4 %collective-permute-done.3.refs_1_ = bf16[128,1280]{1,0:T(8,128)(2,1)S(1)} collective-permute-done((bf16[128,1280]{1,0:T(8,128)(2,1)S(1)}, bf16[128,1280]{1,0:T(8,128)(2,1)S(1)}, u32[]{:S(2)}, u32[]{:S(2)}) %collective-permute-start.3) | collective-permute-done | bytes 327712 | tf_op jit(solution)/shard_map/ppermute | solution.py:317
  28.4 0.0 collective-permute-done.4.refs_4_
  28.4 0.0 collective-permute-start.11
  28.4 3.4 %collective-permute-start.6 = (bf16[128,1280]{1,0:T(8,128)(2,1)S(1)}, bf16[128,1280]{1,0:T(8,128)(2,1)S(1)}, u32[]{:S(2)}, u32[]{:S(2)}) collective-permute-start(bf16[128,1280]{1,0:T(8,128)(2,1)S(1)} %collective-permute-done.3.refs_1_), channel_id=1, source_target_pairs={{0,8},{8,24},{24,16},{16,0},{1,9},{9,25},{25,17},{17,1},{2,10},{10... | collective-permute-start | bytes 983048 | tf_op jit(solution)/shard_map/ppermute | solution.py:317
  31.8 1.5 %collective-permute-start.5 = (bf16[4,160,640]{2,1,0:T(8,128)(2,1)S(1)}, bf16[4,160,640]{2,1,0:T(8,128)(2,1)S(1)}, u32[]{:S(2)}, u32[]{:S(2)}) collective-permute-start(bf16[4,160,640]{2,1,0:T(8,128)(2,1)S(1)} %pad_maximum_fusion.refs_8_), channel_id=1, source_target_pairs={{0,4},{2,6},{4,0},{6,2},{1,5},{3,7},{5,1},{7,3},{8,12},{10,14},{12... | collective-permute-start | bytes 2457608 | tf_op jit(solution)/shard_map/ppermute | solution.py:25
  33.3 0.0 copy-done
  33.3 0.0 copy-done.1
  33.3 0.0 copy-done.2
  33.3 0.0 copy-done.3
  33.3 0.0 copy-start.6
  33.3 0.0 copy-start.7
  33.3 0.1 pad_maximum_fusion.1
  33.4 0.2 collective-permute-start.7
  33.7 1.5 %collective-permute-start.8 = (bf16[128,1280]{1,0:T(8,128)(2,1)S(1)}, bf16[128,1280]{1,0:T(8,128)(2,1)S(1)}, u32[]{:S(2)}, u32[]{:S(2)}) collective-permute-start(bf16[128,1280]{1,0:T(8,128)(2,1)S(1)} %collective-permute-done.3.refs_1_), channel_id=1, source_target_pairs={{0,1},{1,0},{2,3},{3,2},{4,5},{5,4},{6,7},{7,6},{8,9},{9,8},{10,11... | collective-permute-start | bytes 983048 | tf_op jit(solution)/shard_map/ppermute | solution.py:25
  35.2 0.0 collective-permute-done.11.refs_9_
  35.2 1.9 %collective-permute-start.12 = (bf16[2,128,1280]{2,1,0:T(8,128)(2,1)S(1)}, bf16[2,128,1280]{2,1,0:T(8,128)(2,1)S(1)}, u32[]{:S(2)}, u32[]{:S(2)}) collective-permute-start(bf16[2,128,1280]{2,1,0:T(8,128)(2,1)S(1)} %get-tuple-element.34), channel_id=1, source_target_pairs={{0,2},{2,4},{4,6},{6,8},{8,10},{10,12},{12,14},{14,16},{16,18},{18... | collective-permute-start | bytes 1966088 | tf_op jit(solution)/shard_map/ppermute | solution.py:21
  37.1 3.3 %collective-permute-done.6.refs_2_ = bf16[128,1280]{1,0:T(8,128)(2,1)S(1)} collective-permute-done((bf16[128,1280]{1,0:T(8,128)(2,1)S(1)}, bf16[128,1280]{1,0:T(8,128)(2,1)S(1)}, u32[]{:S(2)}, u32[]{:S(2)}) %collective-permute-start.6) | collective-permute-done | bytes 327712 | tf_op jit(solution)/shard_map/ppermute | solution.py:317
  40.5 9.6 %collective-permute-start.13 = (bf16[2,128,1280]{2,1,0:T(8,128)(2,1)S(1)}, bf16[2,128,1280]{2,1,0:T(8,128)(2,1)S(1)}, u32[]{:S(2)}, u32[]{:S(2)}) collective-permute-start(bf16[2,128,1280]{2,1,0:T(8,128)(2,1)S(1)} %get-tuple-element.35), channel_id=1, source_target_pairs={{2,0},{4,2},{6,4},{8,6},{10,8},{12,10},{14,12},{16,14},{18,16},{20... | collective-permute-start | bytes 1966088 | tf_op jit(solution)/shard_map/ppermute | solution.py:21
  50.1 0.0 collective-permute-done.7.refs_3_
  50.1 0.0 collective-permute-done.8.refs_5_
  50.1 1.6 %collective-permute-start.10 = (bf16[128,1280]{1,0:T(8,128)(2,1)S(1)}, bf16[128,1280]{1,0:T(8,128)(2,1)S(1)}, u32[]{:S(2)}, u32[]{:S(2)}) collective-permute-start(bf16[128,1280]{1,0:T(8,128)(2,1)S(1)} %collective-permute-done.7.refs_3_), channel_id=1, source_target_pairs={{0,1},{1,0},{2,3},{3,2},{4,5},{5,4},{6,7},{7,6},{8,9},{9,8},{10,11... | collective-permute-start | bytes 983048 | tf_op jit(solution)/shard_map/ppermute | solution.py:25
  51.7 0.5 collective-permute-start.9
  52.2 8.1 %collective-permute-done.10.refs_7_ = bf16[128,1280]{1,0:T(8,128)(2,1)S(1)} collective-permute-done((bf16[128,1280]{1,0:T(8,128)(2,1)S(1)}, bf16[128,1280]{1,0:T(8,128)(2,1)S(1)}, u32[]{:S(2)}, u32[]{:S(2)}) %collective-permute-start.10) | collective-permute-done | bytes 327712 | tf_op jit(solution)/shard_map/ppermute | solution.py:25
  60.3 3.5 %collective-permute-done.9.refs_6_ = bf16[128,1280]{1,0:T(8,128)(2,1)S(1)} collective-permute-done((bf16[128,1280]{1,0:T(8,128)(2,1)S(1)}, bf16[128,1280]{1,0:T(8,128)(2,1)S(1)}, u32[]{:S(2)}, u32[]{:S(2)}) %collective-permute-start.9) | collective-permute-done | bytes 327712 | tf_op jit(solution)/shard_map/ppermute | solution.py:25
  63.8 0.0 collective-permute-done.5.refs_10_
  63.8 0.0 collective-permute-done.12.kv1_ref
  63.8 0.0 collective-permute-done.13.qg1_ref
  63.8 2.2 %collective-permute-start.14 = (bf16[4,160,640]{2,1,0:T(8,128)(2,1)S(1)}, bf16[4,160,640]{2,1,0:T(8,128)(2,1)S(1)}, u32[]{:S(2)}, u32[]{:S(2)}) collective-permute-start(bf16[4,160,640]{2,1,0:T(8,128)(2,1)S(1)} %collective-permute-done.5.refs_10_), channel_id=1, source_target_pairs={{0,2},{2,0},{4,6},{6,4},{1,3},{3,1},{5,7},{7,5},{8,10},{10,8},{12,... | collective-permute-start | bytes 2457608 | tf_op jit(solution)/shard_map/ppermute | solution.py:25
  66.0 1.9 %collective-permute-start.15 = (bf16[2,128,1280]{2,1,0:T(8,128)(2,1)S(1)}, bf16[2,128,1280]{2,1,0:T(8,128)(2,1)S(1)}, u32[]{:S(2)}, u32[]{:S(2)}) collective-permute-start(bf16[2,128,1280]{2,1,0:T(8,128)(2,1)S(1)} %collective-permute-done.12.kv1_ref), channel_id=1, source_target_pairs={{0,2},{2,4},{4,6},{6,8},{8,10},{10,12},{12,14},{14,16},{16,18},{18... | collective-permute-start | bytes 1966088 | tf_op jit(solution)/shard_map/ppermute | solution.py:21
  67.9 0.0 copy-done.6
  68.0 0.0 copy-done.7
  68.0 0.3 prepare.1
  68.2 0.0 collective-permute-done.14.refs_11_
  68.2 4.6 %project.1 = bf16[16,4,16,640]{3,2,1,0:T(8,128)(2,1)} custom-call(s32[4,1,128]{2,1,0:T(1,128)S(1)} %get-tuple-element.37.place_ref, bf16[128,1280]{1,0:T(8,128)(2,1)S(1)} %copy-done.4, bf16[128,1280]{1,0:T(8,128)(2,1)S(1)} %collective-permute-done.3.refs_1_, bf16[128,1280]{1,0:T(8,128)(2,1)S(1)} %collective-permute-done.6.refs_2_, ...), custom_call_target="tpu_custom_call" | custom-call | flops 1677721600 | bytes 8388608 | tf_op jit(solution)/shard_map/project/pallas_call | solution.py:225
  72.8 0.0 copy-done.8
  72.8 0.0 copy-done.5
  72.8 6.2 %collective-permute-done.15.kv2_ref = bf16[2,128,1280]{2,1,0:T(8,128)(2,1)S(1)} collective-permute-done((bf16[2,128,1280]{2,1,0:T(8,128)(2,1)S(1)}, bf16[2,128,1280]{2,1,0:T(8,128)(2,1)S(1)}, u32[]{:S(2)}, u32[]{:S(2)}) %collective-permute-start.15) | collective-permute-done | bytes 655392 | tf_op jit(solution)/shard_map/ppermute | solution.py:21
  79.0 0.8 copy-done.9
  79.8 7.1 %all-to-all-start = ((bf16[16,4,16,640]{3,2,1,0:T(8,128)(2,1)}), bf16[16,4,16,640]{3,2,1,0:T(8,128)(2,1)S(1)}, u32[]{:S(2)}, u32[]{:S(2)}) async-start(bf16[16,4,16,640]{3,2,1,0:T(8,128)(2,1)} %project.1), calls=%async_computation | async-start | bytes 2621440 | tf_op jit(solution)/shard_map/all_to_all | solution.py:391
  87.0 3.1 %collective-permute-start.16 = (bf16[2,128,1280]{2,1,0:T(8,128)(2,1)S(1)}, bf16[2,128,1280]{2,1,0:T(8,128)(2,1)}, u32[]{:S(2)}, u32[]{:S(2)}) collective-permute-start(bf16[2,128,1280]{2,1,0:T(8,128)(2,1)S(1)} %collective-permute-done.13.qg1_ref), channel_id=1, source_target_pairs={{2,0},{4,2},{6,4},{8,6},{10,8},{12,10},{14,12},{16,14},{18,16},{20... | collective-permute-start | bytes 1966088 | tf_op jit(solution)/shard_map/ppermute | solution.py:21
  90.1 27.7 %all-to-all-done = bf16[16,4,16,640]{3,2,1,0:T(8,128)(2,1)S(1)} async-done(((bf16[16,4,16,640]{3,2,1,0:T(8,128)(2,1)}), bf16[16,4,16,640]{3,2,1,0:T(8,128)(2,1)S(1)}, u32[]{:S(2)}, u32[]{:S(2)}) %all-to-all-start) | async-done | bytes 1310752 | tf_op jit(solution)/shard_map/all_to_all | solution.py:391
  117.8 5.0 %attend.1 = (bf16[128,1280]{1,0:T(8,128)(2,1)}, bf16[128,1280]{1,0:T(8,128)(2,1)}, f32[2,16,128]{2,1,0:T(8,128)S(1)}) custom-call(bf16[128,1280]{1,0:T(8,128)(2,1)S(1)} %copy-done, bf16[128,1280]{1,0:T(8,128)(2,1)S(1)} %copy-done.1, bf16[128,1280]{1,0:T(8,128)(2,1)S(1)} %copy-done.2, bf16[128,1280]{1,0:T(8,128)(2,1)S(1)} %copy-done.3, ...), custom_call_target="tpu_custom_call" | custom-call | flops 838860800 | bytes 6291456 | tf_op jit(solution)/shard_map/attend/pallas_call | solution.py:103
  122.8 2.9 %collective-permute-start.17 = (f32[2,16,128]{2,1,0:T(8,128)S(1)}, f32[2,16,128]{2,1,0:T(8,128)S(1)}, u32[]{:S(2)}, u32[]{:S(2)}) collective-permute-start(f32[2,16,128]{2,1,0:T(8,128)S(1)} %get-tuple-element.50.st0_ref), channel_id=1, source_target_pairs={{2,0},{4,2},{6,4},{8,6},{10,8},{12,10},{14,12},{16,14},{18,16},{20... | collective-permute-start | bytes 49160 | tf_op jit(solution)/shard_map/ppermute | solution.py:21
  125.7 2.1 %collective-permute-start.18 = (f32[2,16,128]{2,1,0:T(8,128)S(1)}, f32[2,16,128]{2,1,0:T(8,128)S(1)}, u32[]{:S(2)}, u32[]{:S(2)}) collective-permute-start(f32[2,16,128]{2,1,0:T(8,128)S(1)} %get-tuple-element.50.st0_ref), channel_id=1, source_target_pairs={{4,0},{6,2},{8,4},{10,6},{12,8},{14,10},{16,12},{18,14},{20,16},{2... | collective-permute-start | bytes 49160 | tf_op jit(solution)/shard_map/ppermute | solution.py:21
  127.8 0.0 collective-permute-done.16.qg2_ref
  127.8 0.0 collective-permute-done.17.st1_ref
  127.8 3.5 %collective-permute-done.18.st2_ref = f32[2,16,128]{2,1,0:T(8,128)S(1)} collective-permute-done((f32[2,16,128]{2,1,0:T(8,128)S(1)}, f32[2,16,128]{2,1,0:T(8,128)S(1)}, u32[]{:S(2)}, u32[]{:S(2)}) %collective-permute-start.18) | collective-permute-done | bytes 16416 | tf_op jit(solution)/shard_map/ppermute | solution.py:21
  131.3 3.7 %key_grads.1 = (bf16[128,1280]{1,0:T(8,128)(2,1)}, bf16[128,1280]{1,0:T(8,128)(2,1)}) custom-call(bf16[128,1280]{1,0:T(8,128)(2,1)S(1)} %copy-done.2, bf16[128,1280]{1,0:T(8,128)(2,1)S(1)} %copy-done.3, bf16[128,1280]{1,0:T(8,128)(2,1)S(1)} %copy-done, bf16[128,1280]{1,0:T(8,128)(2,1)S(1)} %copy-done.1, ...), custom_call_target="tpu_custom_call" | custom-call | flops 503316480 | bytes 4194304 | tf_op jit(solution)/shard_map/key_grads/pallas_call | solution.py:166
  (3 shorter events, 0.0 us)
Async XLA Ops:
  0.6 5.1 %copy-start.4 = (bf16[128,1280]{1,0:T(8,128)(2,1)S(1)}, bf16[128,1280]{1,0:T(8,128)(2,1)}, u32[]{:S(2)}) copy-start(bf16[128,1280]{1,0:T(8,128)(2,1)} %refs_0_) | copy-start | bytes 983044
  0.7 32.6 %copy-start = (bf16[128,1280]{1,0:T(8,128)(2,1)S(1)}, bf16[128,1280]{1,0:T(8,128)(2,1)}, u32[]{:S(2)}) copy-start(bf16[128,1280]{1,0:T(8,128)(2,1)} %q_ref.3) | copy-start | bytes 983044
  0.7 32.6 %copy-start.1 = (bf16[128,1280]{1,0:T(8,128)(2,1)S(1)}, bf16[128,1280]{1,0:T(8,128)(2,1)}, u32[]{:S(2)}) copy-start(bf16[128,1280]{1,0:T(8,128)(2,1)} %g_ref.3) | copy-start | bytes 983044
  0.7 32.6 %copy-start.2 = (bf16[128,1280]{1,0:T(8,128)(2,1)S(1)}, bf16[128,1280]{1,0:T(8,128)(2,1)}, u32[]{:S(2)}) copy-start(bf16[128,1280]{1,0:T(8,128)(2,1)} %k_ref.3) | copy-start | bytes 983044
  0.7 32.6 %copy-start.3 = (bf16[128,1280]{1,0:T(8,128)(2,1)S(1)}, bf16[128,1280]{1,0:T(8,128)(2,1)}, u32[]{:S(2)}) copy-start(bf16[128,1280]{1,0:T(8,128)(2,1)} %v_ref.3) | copy-start | bytes 983044
  2.1 9.0 %collective-permute-start = (bf16[160,640]{1,0:T(8,128)(2,1)S(1)}, bf16[160,640]{1,0:T(8,128)(2,1)S(1)}, u32[]{:S(2)}, u32[]{:S(2)}) collective-permute-start(bf16[160,640]{1,0:T(8,128)(2,1)S(1)} %get-tuple-element.55), channel_id=1, source_target_pairs={{0,8},{8,0},{16,24},{24,16},{1,9},{9,1},{17,25},{25,17},{2,10},{10... | collective-permute-start | bytes 614408 | tf_op jit(solution)/shard_map/ppermute | solution.py:25
  3.8 14.5 %collective-permute-start.1 = (bf16[160,640]{1,0:T(8,128)(2,1)S(1)}, bf16[160,640]{1,0:T(8,128)(2,1)S(1)}, u32[]{:S(2)}, u32[]{:S(2)}) collective-permute-start(bf16[160,640]{1,0:T(8,128)(2,1)S(1)} %get-tuple-element.57), channel_id=1, source_target_pairs={{0,16},{8,24},{16,0},{24,8},{1,17},{9,25},{17,1},{25,9},{2,18},{10... | collective-permute-start | bytes 614408 | tf_op jit(solution)/shard_map/ppermute | solution.py:25
  4.1 20.7 %collective-permute-start.2 = (bf16[160,640]{1,0:T(8,128)(2,1)S(1)}, bf16[160,640]{1,0:T(8,128)(2,1)S(1)}, u32[]{:S(2)}, u32[]{:S(2)}) collective-permute-start(bf16[160,640]{1,0:T(8,128)(2,1)S(1)} %get-tuple-element.56), channel_id=1, source_target_pairs={{0,24},{8,16},{16,8},{24,0},{1,25},{9,17},{17,9},{25,1},{2,26},{10... | collective-permute-start | bytes 614408 | tf_op jit(solution)/shard_map/ppermute | solution.py:25
  5.7 22.7 %collective-permute-start.3 = (bf16[128,1280]{1,0:T(8,128)(2,1)S(1)}, bf16[128,1280]{1,0:T(8,128)(2,1)S(1)}, u32[]{:S(2)}, u32[]{:S(2)}) collective-permute-start(bf16[128,1280]{1,0:T(8,128)(2,1)S(1)} %copy-done.4), channel_id=1, source_target_pairs={{0,8},{8,24},{24,16},{16,0},{1,9},{9,25},{25,17},{17,1},{2,10},{10... | collective-permute-start | bytes 983048 | tf_op jit(solution)/shard_map/ppermute | solution.py:317
  6.7 21.7 %collective-permute-start.4 = (bf16[128,1280]{1,0:T(8,128)(2,1)S(1)}, bf16[128,1280]{1,0:T(8,128)(2,1)S(1)}, u32[]{:S(2)}, u32[]{:S(2)}) collective-permute-start(bf16[128,1280]{1,0:T(8,128)(2,1)S(1)} %copy-done.4), channel_id=1, source_target_pairs={{0,1},{1,0},{2,3},{3,2},{4,5},{5,4},{6,7},{7,6},{8,9},{9,8},{10,11... | collective-permute-start | bytes 983048 | tf_op jit(solution)/shard_map/ppermute | solution.py:25
  28.4 6.8 %collective-permute-start.11 = (bf16[4,160,640]{2,1,0:T(8,128)(2,1)S(1)}, bf16[4,160,640]{2,1,0:T(8,128)(2,1)S(1)}, u32[]{:S(2)}, u32[]{:S(2)}) collective-permute-start(bf16[4,160,640]{2,1,0:T(8,128)(2,1)S(1)} %pad_maximum_fusion.refs_8_), channel_id=1, source_target_pairs={{0,2},{2,0},{4,6},{6,4},{1,3},{3,1},{5,7},{7,5},{8,10},{10,8},{12,... | collective-permute-start | bytes 2457608 | tf_op jit(solution)/shard_map/ppermute | solution.py:25
  28.4 12.1 %collective-permute-start.6 = (bf16[128,1280]{1,0:T(8,128)(2,1)S(1)}, bf16[128,1280]{1,0:T(8,128)(2,1)S(1)}, u32[]{:S(2)}, u32[]{:S(2)}) collective-permute-start(bf16[128,1280]{1,0:T(8,128)(2,1)S(1)} %collective-permute-done.3.refs_1_), channel_id=1, source_target_pairs={{0,8},{8,24},{24,16},{16,0},{1,9},{9,25},{25,17},{17,1},{2,10},{10... | collective-permute-start | bytes 983048 | tf_op jit(solution)/shard_map/ppermute | solution.py:317
  31.8 32.0 %collective-permute-start.5 = (bf16[4,160,640]{2,1,0:T(8,128)(2,1)S(1)}, bf16[4,160,640]{2,1,0:T(8,128)(2,1)S(1)}, u32[]{:S(2)}, u32[]{:S(2)}) collective-permute-start(bf16[4,160,640]{2,1,0:T(8,128)(2,1)S(1)} %pad_maximum_fusion.refs_8_), channel_id=1, source_target_pairs={{0,4},{2,6},{4,0},{6,2},{1,5},{3,7},{5,1},{7,3},{8,12},{10,14},{12... | collective-permute-start | bytes 2457608 | tf_op jit(solution)/shard_map/ppermute | solution.py:25
  33.3 34.7 %copy-start.6 = (s32[2048]{0:T(1024)S(1)}, s32[2048]{0:T(1024)}, u32[]{:S(2)}) copy-start(s32[2048]{0:T(1024)} %param.15) | copy-start | bytes 24580
  33.3 34.7 %copy-start.7 = (s32[2048]{0:T(1024)S(1)}, s32[2048]{0:T(1024)}, u32[]{:S(2)}) copy-start(s32[2048]{0:T(1024)} %param.14) | copy-start | bytes 24580
  33.4 16.7 %collective-permute-start.7 = (bf16[128,1280]{1,0:T(8,128)(2,1)S(1)}, bf16[128,1280]{1,0:T(8,128)(2,1)S(1)}, u32[]{:S(2)}, u32[]{:S(2)}) collective-permute-start(bf16[128,1280]{1,0:T(8,128)(2,1)S(1)} %copy-done.4), channel_id=1, source_target_pairs={{8,0},{24,8},{16,24},{0,16},{9,1},{25,9},{17,25},{1,17},{10,2},{26... | collective-permute-start | bytes 983048 | tf_op jit(solution)/shard_map/ppermute | solution.py:317
  33.7 16.4 %collective-permute-start.8 = (bf16[128,1280]{1,0:T(8,128)(2,1)S(1)}, bf16[128,1280]{1,0:T(8,128)(2,1)S(1)}, u32[]{:S(2)}, u32[]{:S(2)}) collective-permute-start(bf16[128,1280]{1,0:T(8,128)(2,1)S(1)} %collective-permute-done.3.refs_1_), channel_id=1, source_target_pairs={{0,1},{1,0},{2,3},{3,2},{4,5},{5,4},{6,7},{7,6},{8,9},{9,8},{10,11... | collective-permute-start | bytes 983048 | tf_op jit(solution)/shard_map/ppermute | solution.py:25
  35.2 28.6 %collective-permute-start.12 = (bf16[2,128,1280]{2,1,0:T(8,128)(2,1)S(1)}, bf16[2,128,1280]{2,1,0:T(8,128)(2,1)S(1)}, u32[]{:S(2)}, u32[]{:S(2)}) collective-permute-start(bf16[2,128,1280]{2,1,0:T(8,128)(2,1)S(1)} %get-tuple-element.34), channel_id=1, source_target_pairs={{0,2},{2,4},{4,6},{6,8},{8,10},{10,12},{12,14},{14,16},{16,18},{18... | collective-permute-start | bytes 1966088 | tf_op jit(solution)/shard_map/ppermute | solution.py:21
  40.5 23.4 %collective-permute-start.13 = (bf16[2,128,1280]{2,1,0:T(8,128)(2,1)S(1)}, bf16[2,128,1280]{2,1,0:T(8,128)(2,1)S(1)}, u32[]{:S(2)}, u32[]{:S(2)}) collective-permute-start(bf16[2,128,1280]{2,1,0:T(8,128)(2,1)S(1)} %get-tuple-element.35), channel_id=1, source_target_pairs={{2,0},{4,2},{6,4},{8,6},{10,8},{12,10},{14,12},{16,14},{18,16},{20... | collective-permute-start | bytes 1966088 | tf_op jit(solution)/shard_map/ppermute | solution.py:21
  50.1 10.2 %collective-permute-start.10 = (bf16[128,1280]{1,0:T(8,128)(2,1)S(1)}, bf16[128,1280]{1,0:T(8,128)(2,1)S(1)}, u32[]{:S(2)}, u32[]{:S(2)}) collective-permute-start(bf16[128,1280]{1,0:T(8,128)(2,1)S(1)} %collective-permute-done.7.refs_3_), channel_id=1, source_target_pairs={{0,1},{1,0},{2,3},{3,2},{4,5},{5,4},{6,7},{7,6},{8,9},{9,8},{10,11... | collective-permute-start | bytes 983048 | tf_op jit(solution)/shard_map/ppermute | solution.py:25
  51.7 12.1 %collective-permute-start.9 = (bf16[128,1280]{1,0:T(8,128)(2,1)S(1)}, bf16[128,1280]{1,0:T(8,128)(2,1)S(1)}, u32[]{:S(2)}, u32[]{:S(2)}) collective-permute-start(bf16[128,1280]{1,0:T(8,128)(2,1)S(1)} %collective-permute-done.6.refs_2_), channel_id=1, source_target_pairs={{0,1},{1,0},{2,3},{3,2},{4,5},{5,4},{6,7},{7,6},{8,9},{9,8},{10,11... | collective-permute-start | bytes 983048 | tf_op jit(solution)/shard_map/ppermute | solution.py:25
  63.8 9.0 %copy-start.8 = (bf16[2,128,1280]{2,1,0:T(8,128)(2,1)}, bf16[2,128,1280]{2,1,0:T(8,128)(2,1)S(1)}, u32[]{:S(2)}) copy-start(bf16[2,128,1280]{2,1,0:T(8,128)(2,1)S(1)} %collective-permute-done.12.kv1_ref) | copy-start | bytes 1966084
  63.8 4.4 %collective-permute-start.14 = (bf16[4,160,640]{2,1,0:T(8,128)(2,1)S(1)}, bf16[4,160,640]{2,1,0:T(8,128)(2,1)S(1)}, u32[]{:S(2)}, u32[]{:S(2)}) collective-permute-start(bf16[4,160,640]{2,1,0:T(8,128)(2,1)S(1)} %collective-permute-done.5.refs_10_), channel_id=1, source_target_pairs={{0,2},{2,0},{4,6},{6,4},{1,3},{3,1},{5,7},{7,5},{8,10},{10,8},{12,... | collective-permute-start | bytes 2457608 | tf_op jit(solution)/shard_map/ppermute | solution.py:25
  66.0 13.0 %collective-permute-start.15 = (bf16[2,128,1280]{2,1,0:T(8,128)(2,1)S(1)}, bf16[2,128,1280]{2,1,0:T(8,128)(2,1)S(1)}, u32[]{:S(2)}, u32[]{:S(2)}) collective-permute-start(bf16[2,128,1280]{2,1,0:T(8,128)(2,1)S(1)} %collective-permute-done.12.kv1_ref), channel_id=1, source_target_pairs={{0,2},{2,4},{4,6},{6,8},{8,10},{10,12},{12,14},{14,16},{16,18},{18... | collective-permute-start | bytes 1966088 | tf_op jit(solution)/shard_map/ppermute | solution.py:21
  68.2 4.6 %copy-start.5 = (bf16[128,640]{1,0:T(8,128)(2,1)}, bf16[128,640]{1,0:T(8,128)(2,1)S(1)}, u32[]{:S(2)}) copy-start(bf16[128,640]{1,0:T(8,128)(2,1)S(1)} %get-tuple-element.46.bias_ref) | copy-start | bytes 491524
  79.0 0.9 copy-start.9
  79.8 37.9 %all-to-all-start = ((bf16[16,4,16,640]{3,2,1,0:T(8,128)(2,1)}), bf16[16,4,16,640]{3,2,1,0:T(8,128)(2,1)S(1)}, u32[]{:S(2)}, u32[]{:S(2)}) async-start(bf16[16,4,16,640]{3,2,1,0:T(8,128)(2,1)} %project.1), calls=%async_computation | async-start | bytes 2621440 | tf_op jit(solution)/shard_map/all_to_all | solution.py:391
  87.0 40.8 %collective-permute-start.16 = (bf16[2,128,1280]{2,1,0:T(8,128)(2,1)S(1)}, bf16[2,128,1280]{2,1,0:T(8,128)(2,1)}, u32[]{:S(2)}, u32[]{:S(2)}) collective-permute-start(bf16[2,128,1280]{2,1,0:T(8,128)(2,1)S(1)} %collective-permute-done.13.qg1_ref), channel_id=1, source_target_pairs={{2,0},{4,2},{6,4},{8,6},{10,8},{12,10},{14,12},{16,14},{18,16},{20... | collective-permute-start | bytes 1966088 | tf_op jit(solution)/shard_map/ppermute | solution.py:21
  122.8 5.0 %collective-permute-start.17 = (f32[2,16,128]{2,1,0:T(8,128)S(1)}, f32[2,16,128]{2,1,0:T(8,128)S(1)}, u32[]{:S(2)}, u32[]{:S(2)}) collective-permute-start(f32[2,16,128]{2,1,0:T(8,128)S(1)} %get-tuple-element.50.st0_ref), channel_id=1, source_target_pairs={{2,0},{4,2},{6,4},{8,6},{10,8},{12,10},{14,12},{16,14},{18,16},{20... | collective-permute-start | bytes 49160 | tf_op jit(solution)/shard_map/ppermute | solution.py:21
  125.7 5.6 %collective-permute-start.18 = (f32[2,16,128]{2,1,0:T(8,128)S(1)}, f32[2,16,128]{2,1,0:T(8,128)S(1)}, u32[]{:S(2)}, u32[]{:S(2)}) collective-permute-start(f32[2,16,128]{2,1,0:T(8,128)S(1)} %get-tuple-element.50.st0_ref), channel_id=1, source_target_pairs={{4,0},{6,2},{8,4},{10,6},{12,8},{14,10},{16,12},{18,14},{20,16},{2... | collective-permute-start | bytes 49160 | tf_op jit(solution)/shard_map/ppermute | solution.py:21

commit v4 on v3

--- a/solution.py
+++ b/solution.py
@@ -328,21 +328,23 @@
         own = jnp.stack(
             [blocks[0]] + [swapped(blocks[mask], "z", mask) for mask in range(1, n_z)], 0
         )
-        row1, other0 = ring_step(cache), swapped(cache, "head", 1)
-        own, row1, other0, cache = lax.optimization_barrier((own, row1, other0, cache))
-        across = swapped(own, "p", 2)
-        beside = swapped(own, "p", 1)
-        row2, row3, other1 = ring_step(row1), ring_step(cache, back=True), swapped(row1, "head", 1)
+        other0 = swapped(cache, "head", 1)
+        own, other0, cache = lax.optimization_barrier((own, other0, cache))
+        across, beside = swapped(own, "p", 2), swapped(own, "p", 1)
+        row1, row3 = ring_step(cache), ring_step(cache, back=True)
         beside, stream, back = lax.optimization_barrier((beside, stream, back))
         near, back1 = shifted(stream, 1), shifted(back, -1)
-        row2, row3, other1 = lax.optimization_barrier((row2, row3, other1))
-        other2, other3 = swapped(row2, "head", 1), swapped(row3, "head", 1)
-        across, other2, other3, near, back1 = lax.optimization_barrier(
-            (across, other2, other3, near, back1)
+        row1, row3 = lax.optimization_barrier((row1, row3))
+        row2 = ring_step(row1)
+        others13 = swapped(jnp.stack([row1, row3], 0), "head", 1)
+        row2 = lax.optimization_barrier(row2)
+        other2 = swapped(row2, "head", 1)
+        across, others13, other2, near, back1 = lax.optimization_barrier(
+            (across, others13, other2, near, back1)
         )
         pieces = [own, beside, across, swapped(across, "p", 1)]
         far = shifted(near, 1)
-        rows = [cache, row1, row2, row3, other0, other1, other2, other3]
+        rows = [cache, row1, row2, row3, other0, others13[0], other2, others13[1]]
         slots = project(place, rows, pieces, devices, capacity)
         slots, far = lax.optimization_barrier((slots, far))
         return slots, near, far, back1

time: 135 us -> 132 us (0.978)
  starting transfers between devices: 45.9 us -> 34.3 us
  waiting for transfers between devices: 72.1 us -> 79.5 us
    ppermute x3, waiting for transfers between devices: 6.79 us -> 13.2 us  [ring_step(): lax.ppermute(value, 'z', [(b, a) for a, b in pairs] if back else pairs)]
    ppermute x6, starting transfers between devices: 21.5 us -> 16.9 us  [shifted(): return lax.ppermute(value, SEQ, pairs)]
    all_to_all x1, starting transfers between devices: 7.14 us -> 4.24 us  [body(): memory = lax.all_to_all(slots, SEQ, split_axis=0, concat_axis=0, tiled=True)]
    ppermute x10 -> x9, starting transfers between devices: 12.6 us -> 9.73 us  [swapped(): lax.ppermute(value, axis, [(i, i ^ mask) for i in range(lax.axis_size(axi...]
    ppermute x10 -> x9, waiting for transfers between devices: 28 us -> 30.2 us  [swapped(): lax.ppermute(value, axis, [(i, i ^ mask) for i in range(lax.axis_size(axi...]
  transfers between devices with their start and end apart: 20 -> 19, of which waited for: 10 -> 10; matrix products, arithmetic and copies ran while one was open for 0% -> 0% of each run, Pallas kernels for 7% -> 7%
where the time goes in v4:
time: 132 us
  waiting for transfers between devices  79.5 us (60%)
  starting transfers between devices  34.3 us (26%)
  Pallas kernels  13.6 us (10%)
  local copies, waits for them, and re-layouts  3.02 us (2%)
    ppermute x9, waiting for transfers between devices, swapped(): lax.ppermute(value, axis, [(i, i ^ mask) for i in range(lax.axis_size(axi...  30.2 us
    all_to_all x1, waiting for transfers between devices, body(): memory = lax.all_to_all(slots, SEQ, split_axis=0, concat_axis=0, tiled=True)  27.7 us
    ppermute x6, starting transfers between devices, shifted(): return lax.ppermute(value, SEQ, pairs)  16.9 us
    ppermute x3, waiting for transfers between devices, ring_step(): lax.ppermute(value, 'z', [(b, a) for a, b in pairs] if back else pairs)  13.2 us
    ppermute x9, starting transfers between devices, swapped(): lax.ppermute(value, axis, [(i, i ^ mask) for i in range(lax.axis_size(axi...  9.73 us
    ppermute x6, waiting for transfers between devices, shifted(): return lax.ppermute(value, SEQ, pairs)  8.34 us
    pallas_call x1, Pallas kernels, attend(): pl.pallas_call(attend_kernel, grid=(steps,), in_specs=[flat, flat, flat,...  4.99 us
    pallas_call x1, Pallas kernels, project(): pl.pallas_call(project_kernel, in_specs=[whole] * (1 + len(rows) + n_p),...  4.6 us
  transfers between devices with their start and end apart: 19, of which 10 were waited for; matrix products, arithmetic and copies ran while one was open for 0% of the time, Pallas kernels for 7%

profile of v4, /device:TPU:16, one launch (start us, length us, event | category | flops | bytes accessed | tf_op | source)
XLA Modules:
  0.0 131.5 jit_solution(18310505451597248939)
XLA Ops:
  0.6 0.0 copy-start.4
  0.7 0.0 copy-start
  0.7 0.0 copy-start.1
  0.7 0.0 copy-start.2
  0.7 0.0 copy-start.3
  0.7 1.4 %constant_dynamic-slice_fusion = (bf16[1,160,640]{2,1,0:T(8,128)(2,1)S(1)}, bf16[160,640]{1,0:T(8,128)(2,1)S(1)}, bf16[160,640]{1,0:T(8,128)(2,1)S(1)}, bf16[160,640]{1,0:T(8,128)(2,1)S(1)}) fusion(bf16[2,160,1280]{2,1,0:T(8,128)(2,1)} %param.13, s32[]{:T(128)S(6)} %select_n.24, s32[]{:T(128)S(6)} %select_n.25, s32[]{:T(128)S(6)} %select_n.26, ...), kind=kLoop, calls=%fused_computation.9 | loop fusion | bytes 1638432 | tf_op jit(solution)/shard_map/dynamic_slice | solution.py:312
  2.1 1.6 %collective-permute-start = (bf16[160,640]{1,0:T(8,128)(2,1)S(1)}, bf16[160,640]{1,0:T(8,128)(2,1)S(1)}, u32[]{:S(2)}, u32[]{:S(2)}) collective-permute-start(bf16[160,640]{1,0:T(8,128)(2,1)S(1)} %get-tuple-element.51), channel_id=1, source_target_pairs={{0,8},{8,0},{16,24},{24,16},{1,9},{9,1},{17,25},{25,17},{2,10},{10... | collective-permute-start | bytes 614408 | tf_op jit(solution)/shard_map/ppermute | solution.py:25
  3.8 0.3 collective-permute-start.1
  4.1 1.6 %collective-permute-start.2 = (bf16[160,640]{1,0:T(8,128)(2,1)S(1)}, bf16[160,640]{1,0:T(8,128)(2,1)S(1)}, u32[]{:S(2)}, u32[]{:S(2)}) collective-permute-start(bf16[160,640]{1,0:T(8,128)(2,1)S(1)} %get-tuple-element.52), channel_id=1, source_target_pairs={{0,24},{8,16},{16,8},{24,0},{1,25},{9,17},{17,9},{25,1},{2,26},{10... | collective-permute-start | bytes 614408 | tf_op jit(solution)/shard_map/ppermute | solution.py:25
  5.7 0.0 copy-done.4
  5.7 1.5 %collective-permute-start.3 = (bf16[128,1280]{1,0:T(8,128)(2,1)S(1)}, bf16[128,1280]{1,0:T(8,128)(2,1)S(1)}, u32[]{:S(2)}, u32[]{:S(2)}) collective-permute-start(bf16[128,1280]{1,0:T(8,128)(2,1)S(1)} %copy-done.4), channel_id=1, source_target_pairs={{0,1},{1,0},{2,3},{3,2},{4,5},{5,4},{6,7},{7,6},{8,9},{9,8},{10,11... | collective-permute-start | bytes 983048 | tf_op jit(solution)/shard_map/ppermute | solution.py:25
  7.2 4.0 %collective-permute-done = bf16[160,640]{1,0:T(8,128)(2,1)S(1)} collective-permute-done((bf16[160,640]{1,0:T(8,128)(2,1)S(1)}, bf16[160,640]{1,0:T(8,128)(2,1)S(1)}, u32[]{:S(2)}, u32[]{:S(2)}) %collective-permute-start) | collective-permute-done | bytes 204832 | tf_op jit(solution)/shard_map/ppermute | solution.py:25
  11.2 7.2 %collective-permute-done.1 = bf16[160,640]{1,0:T(8,128)(2,1)S(1)} collective-permute-done((bf16[160,640]{1,0:T(8,128)(2,1)S(1)}, bf16[160,640]{1,0:T(8,128)(2,1)S(1)}, u32[]{:S(2)}, u32[]{:S(2)}) %collective-permute-start.1) | collective-permute-done | bytes 204832 | tf_op jit(solution)/shard_map/ppermute | solution.py:25
  18.4 5.0 %collective-permute-done.2 = bf16[160,640]{1,0:T(8,128)(2,1)S(1)} collective-permute-done((bf16[160,640]{1,0:T(8,128)(2,1)S(1)}, bf16[160,640]{1,0:T(8,128)(2,1)S(1)}, u32[]{:S(2)}, u32[]{:S(2)}) %collective-permute-start.2) | collective-permute-done | bytes 204832 | tf_op jit(solution)/shard_map/ppermute | solution.py:25
  23.4 0.1 pad_maximum_fusion.refs_8_
  23.5 0.0 collective-permute-done.3.refs_4_
  23.5 0.1 collective-permute-start.10
  23.6 0.1 collective-permute-start.5
  23.7 2.0 %collective-permute-start.6 = (bf16[128,1280]{1,0:T(8,128)(2,1)S(1)}, bf16[128,1280]{1,0:T(8,128)(2,1)S(1)}, u32[]{:S(2)}, u32[]{:S(2)}) collective-permute-start(bf16[128,1280]{1,0:T(8,128)(2,1)S(1)} %copy-done.4), channel_id=1, source_target_pairs={{8,0},{24,8},{16,24},{0,16},{9,1},{25,9},{17,25},{1,17},{10,2},{26... | collective-permute-start | bytes 983048 | tf_op jit(solution)/shard_map/ppermute | solution.py:317
  25.7 0.0 copy-done
  25.7 0.0 copy-done.1
  25.7 0.0 copy-done.2
  25.7 0.0 copy-done.3
  25.7 0.1 pad_maximum_fusion.2
  25.8 0.0 copy-start.6
  25.9 0.0 copy-start.7
  25.9 1.6 %collective-permute-start.4 = (bf16[4,160,640]{2,1,0:T(8,128)(2,1)S(1)}, bf16[4,160,640]{2,1,0:T(8,128)(2,1)S(1)}, u32[]{:S(2)}, u32[]{:S(2)}) collective-permute-start(bf16[4,160,640]{2,1,0:T(8,128)(2,1)S(1)} %pad_maximum_fusion.refs_8_), channel_id=1, source_target_pairs={{0,4},{2,6},{4,0},{6,2},{1,5},{3,7},{5,1},{7,3},{8,12},{10,14},{12... | collective-permute-start | bytes 2457608 | tf_op jit(solution)/shard_map/ppermute | solution.py:25
  27.4 6.8 %collective-permute-done.5.refs_1_ = bf16[128,1280]{1,0:T(8,128)(2,1)S(1)} collective-permute-done((bf16[128,1280]{1,0:T(8,128)(2,1)S(1)}, bf16[128,1280]{1,0:T(8,128)(2,1)S(1)}, u32[]{:S(2)}, u32[]{:S(2)}) %collective-permute-start.5) | collective-permute-done | bytes 327712 | tf_op jit(solution)/shard_map/ppermute | solution.py:317
  34.2 6.5 %collective-permute-done.6.refs_3_ = bf16[128,1280]{1,0:T(8,128)(2,1)S(1)} collective-permute-done((bf16[128,1280]{1,0:T(8,128)(2,1)S(1)}, bf16[128,1280]{1,0:T(8,128)(2,1)S(1)}, u32[]{:S(2)}, u32[]{:S(2)}) %collective-permute-start.6) | collective-permute-done | bytes 327712 | tf_op jit(solution)/shard_map/ppermute | solution.py:317
  40.6 1.3 collective-permute-start.8
  41.9 0.1 pad_maximum_fusion.1
  42.0 1.6 %collective-permute-start.7 = (bf16[2,128,1280]{2,1,0:T(8,128)(2,1)S(1)}, bf16[2,128,1280]{2,1,0:T(8,128)(2,1)S(1)}, u32[]{:S(2)}, u32[]{:S(2)}) collective-permute-start(bf16[2,128,1280]{2,1,0:T(8,128)(2,1)S(1)} %pad_maximum_fusion.1), channel_id=1, source_target_pairs={{0,1},{1,0},{2,3},{3,2},{4,5},{5,4},{6,7},{7,6},{8,9},{9,8},{10,11... | collective-permute-start | bytes 1966088 | tf_op jit(solution)/shard_map/ppermute | solution.py:25
  43.6 0.0 collective-permute-done.10.refs_9_
  43.6 1.9 %collective-permute-start.11 = (bf16[2,128,1280]{2,1,0:T(8,128)(2,1)S(1)}, bf16[2,128,1280]{2,1,0:T(8,128)(2,1)S(1)}, u32[]{:S(2)}, u32[]{:S(2)}) collective-permute-start(bf16[2,128,1280]{2,1,0:T(8,128)(2,1)S(1)} %get-tuple-element.31), channel_id=1, source_target_pairs={{0,2},{2,4},{4,6},{6,8},{8,10},{10,12},{12,14},{14,16},{16,18},{18... | collective-permute-start | bytes 1966088 | tf_op jit(solution)/shard_map/ppermute | solution.py:21
  45.5 4.5 %collective-permute-start.12 = (bf16[2,128,1280]{2,1,0:T(8,128)(2,1)S(1)}, bf16[2,128,1280]{2,1,0:T(8,128)(2,1)S(1)}, u32[]{:S(2)}, u32[]{:S(2)}) collective-permute-start(bf16[2,128,1280]{2,1,0:T(8,128)(2,1)S(1)} %get-tuple-element.32), channel_id=1, source_target_pairs={{2,0},{4,2},{6,4},{8,6},{10,8},{12,10},{14,12},{16,14},{18,16},{20... | collective-permute-start | bytes 1966088 | tf_op jit(solution)/shard_map/ppermute | solution.py:21
  50.1 0.0 collective-permute-done.8.refs_2_
  50.1 1.4 %collective-permute-start.9 = (bf16[128,1280]{1,0:T(8,128)(2,1)S(1)}, bf16[128,1280]{1,0:T(8,128)(2,1)S(1)}, u32[]{:S(2)}, u32[]{:S(2)}) collective-permute-start(bf16[128,1280]{1,0:T(8,128)(2,1)S(1)} %collective-permute-done.8.refs_2_), channel_id=1, source_target_pairs={{0,1},{1,0},{2,3},{3,2},{4,5},{5,4},{6,7},{7,6},{8,9},{9,8},{10,11... | collective-permute-start | bytes 983048 | tf_op jit(solution)/shard_map/ppermute | solution.py:25
  51.4 0.0 collective-permute-done.4.refs_10_
  51.4 8.3 %collective-permute-done.7 = bf16[2,128,1280]{2,1,0:T(8,128)(2,1)S(1)} collective-permute-done((bf16[2,128,1280]{2,1,0:T(8,128)(2,1)S(1)}, bf16[2,128,1280]{2,1,0:T(8,128)(2,1)S(1)}, u32[]{:S(2)}, u32[]{:S(2)}) %collective-permute-start.7) | collective-permute-done | bytes 655392 | tf_op jit(solution)/shard_map/ppermute | solution.py:25
  59.7 5.8 %collective-permute-done.9.refs_6_ = bf16[128,1280]{1,0:T(8,128)(2,1)S(1)} collective-permute-done((bf16[128,1280]{1,0:T(8,128)(2,1)S(1)}, bf16[128,1280]{1,0:T(8,128)(2,1)S(1)}, u32[]{:S(2)}, u32[]{:S(2)}) %collective-permute-start.9) | collective-permute-done | bytes 327712 | tf_op jit(solution)/shard_map/ppermute | solution.py:25
  65.5 0.0 collective-permute-done.11.kv1_ref
  65.5 0.0 copy-start.8
  65.5 0.0 collective-permute-done.12.qg1_ref
  65.5 0.1 collective-permute-start.13
  65.6 2.4 %collective-permute-start.14 = (bf16[2,128,1280]{2,1,0:T(8,128)(2,1)S(1)}, bf16[2,128,1280]{2,1,0:T(8,128)(2,1)S(1)}, u32[]{:S(2)}, u32[]{:S(2)}) collective-permute-start(bf16[2,128,1280]{2,1,0:T(8,128)(2,1)S(1)} %collective-permute-done.11.kv1_ref), channel_id=1, source_target_pairs={{0,2},{2,4},{4,6},{6,8},{8,10},{10,12},{12,14},{14,16},{16,18},{18... | collective-permute-start | bytes 1966088 | tf_op jit(solution)/shard_map/ppermute | solution.py:21
  68.0 0.0 copy-done.6
  68.0 0.0 copy-done.7
  68.0 0.3 prepare.1
  68.3 0.7 copy-done.5
  69.0 0.0 collective-permute-done.13.refs_11_
  69.0 4.6 %project.1 = bf16[16,4,16,640]{3,2,1,0:T(8,128)(2,1)} custom-call(s32[4,1,128]{2,1,0:T(1,128)S(1)} %get-tuple-element.34.place_ref, bf16[128,1280]{1,0:T(8,128)(2,1)S(1)} %copy-done.4, bf16[128,1280]{1,0:T(8,128)(2,1)S(1)} %collective-permute-done.5.refs_1_, bf16[128,1280]{1,0:T(8,128)(2,1)S(1)} %collective-permute-done.8.refs_2_, ...), custom_call_target="tpu_custom_call" | custom-call | flops 1677721600 | bytes 8388608 | tf_op jit(solution)/shard_map/project/pallas_call | solution.py:225
  73.6 0.0 copy-done.8
  73.6 4.8 %collective-permute-done.14.kv2_ref = bf16[2,128,1280]{2,1,0:T(8,128)(2,1)S(1)} collective-permute-done((bf16[2,128,1280]{2,1,0:T(8,128)(2,1)S(1)}, bf16[2,128,1280]{2,1,0:T(8,128)(2,1)S(1)}, u32[]{:S(2)}, u32[]{:S(2)}) %collective-permute-start.14) | collective-permute-done | bytes 655392 | tf_op jit(solution)/shard_map/ppermute | solution.py:21
  78.4 0.8 copy-done.9
  79.2 4.2 %all-to-all-start = ((bf16[16,4,16,640]{3,2,1,0:T(8,128)(2,1)}), bf16[16,4,16,640]{3,2,1,0:T(8,128)(2,1)S(1)}, u32[]{:S(2)}, u32[]{:S(2)}) async-start(bf16[16,4,16,640]{3,2,1,0:T(8,128)(2,1)} %project.1), calls=%async_computation | async-start | bytes 2621440 | tf_op jit(solution)/shard_map/all_to_all | solution.py:393
  83.5 3.1 %collective-permute-start.15 = (bf16[2,128,1280]{2,1,0:T(8,128)(2,1)S(1)}, bf16[2,128,1280]{2,1,0:T(8,128)(2,1)}, u32[]{:S(2)}, u32[]{:S(2)}) collective-permute-start(bf16[2,128,1280]{2,1,0:T(8,128)(2,1)S(1)} %collective-permute-done.12.qg1_ref), channel_id=1, source_target_pairs={{2,0},{4,2},{6,4},{8,6},{10,8},{12,10},{14,12},{16,14},{18,16},{20... | collective-permute-start | bytes 1966088 | tf_op jit(solution)/shard_map/ppermute | solution.py:21
  86.6 27.7 %all-to-all-done = bf16[16,4,16,640]{3,2,1,0:T(8,128)(2,1)S(1)} async-done(((bf16[16,4,16,640]{3,2,1,0:T(8,128)(2,1)}), bf16[16,4,16,640]{3,2,1,0:T(8,128)(2,1)S(1)}, u32[]{:S(2)}, u32[]{:S(2)}) %all-to-all-start) | async-done | bytes 1310752 | tf_op jit(solution)/shard_map/all_to_all | solution.py:393
  114.3 5.0 %attend.1 = (bf16[128,1280]{1,0:T(8,128)(2,1)}, bf16[128,1280]{1,0:T(8,128)(2,1)}, f32[2,16,128]{2,1,0:T(8,128)S(1)}) custom-call(bf16[128,1280]{1,0:T(8,128)(2,1)S(1)} %copy-done, bf16[128,1280]{1,0:T(8,128)(2,1)S(1)} %copy-done.1, bf16[128,1280]{1,0:T(8,128)(2,1)S(1)} %copy-done.2, bf16[128,1280]{1,0:T(8,128)(2,1)S(1)} %copy-done.3, ...), custom_call_target="tpu_custom_call" | custom-call | flops 838860800 | bytes 6291456 | tf_op jit(solution)/shard_map/attend/pallas_call | solution.py:103
  119.3 2.9 %collective-permute-start.16 = (f32[2,16,128]{2,1,0:T(8,128)S(1)}, f32[2,16,128]{2,1,0:T(8,128)S(1)}, u32[]{:S(2)}, u32[]{:S(2)}) collective-permute-start(f32[2,16,128]{2,1,0:T(8,128)S(1)} %get-tuple-element.46.st0_ref), channel_id=1, source_target_pairs={{2,0},{4,2},{6,4},{8,6},{10,8},{12,10},{14,12},{16,14},{18,16},{20... | collective-permute-start | bytes 49160 | tf_op jit(solution)/shard_map/ppermute | solution.py:21
  122.1 2.1 %collective-permute-start.17 = (f32[2,16,128]{2,1,0:T(8,128)S(1)}, f32[2,16,128]{2,1,0:T(8,128)S(1)}, u32[]{:S(2)}, u32[]{:S(2)}) collective-permute-start(f32[2,16,128]{2,1,0:T(8,128)S(1)} %get-tuple-element.46.st0_ref), channel_id=1, source_target_pairs={{4,0},{6,2},{8,4},{10,6},{12,8},{14,10},{16,12},{18,14},{20,16},{2... | collective-permute-start | bytes 49160 | tf_op jit(solution)/shard_map/ppermute | solution.py:21
  124.2 0.0 collective-permute-done.15.qg2_ref
  124.2 0.0 collective-permute-done.16.st1_ref
  124.3 3.5 %collective-permute-done.17.st2_ref = f32[2,16,128]{2,1,0:T(8,128)S(1)} collective-permute-done((f32[2,16,128]{2,1,0:T(8,128)S(1)}, f32[2,16,128]{2,1,0:T(8,128)S(1)}, u32[]{:S(2)}, u32[]{:S(2)}) %collective-permute-start.17) | collective-permute-done | bytes 16416 | tf_op jit(solution)/shard_map/ppermute | solution.py:21
  127.8 3.7 %key_grads.1 = (bf16[128,1280]{1,0:T(8,128)(2,1)}, bf16[128,1280]{1,0:T(8,128)(2,1)}) custom-call(bf16[128,1280]{1,0:T(8,128)(2,1)S(1)} %copy-done.2, bf16[128,1280]{1,0:T(8,128)(2,1)S(1)} %copy-done.3, bf16[128,1280]{1,0:T(8,128)(2,1)S(1)} %copy-done, bf16[128,1280]{1,0:T(8,128)(2,1)S(1)} %copy-done.1, ...), custom_call_target="tpu_custom_call" | custom-call | flops 503316480 | bytes 4194304 | tf_op jit(solution)/shard_map/key_grads/pallas_call | solution.py:166
  (3 shorter events, 0.0 us)
Async XLA Ops:
  0.6 5.1 %copy-start.4 = (bf16[128,1280]{1,0:T(8,128)(2,1)S(1)}, bf16[128,1280]{1,0:T(8,128)(2,1)}, u32[]{:S(2)}) copy-start(bf16[128,1280]{1,0:T(8,128)(2,1)} %refs_0_) | copy-start | bytes 983044
  0.7 25.0 %copy-start = (bf16[128,1280]{1,0:T(8,128)(2,1)S(1)}, bf16[128,1280]{1,0:T(8,128)(2,1)}, u32[]{:S(2)}) copy-start(bf16[128,1280]{1,0:T(8,128)(2,1)} %q_ref.3) | copy-start | bytes 983044
  0.7 25.0 %copy-start.1 = (bf16[128,1280]{1,0:T(8,128)(2,1)S(1)}, bf16[128,1280]{1,0:T(8,128)(2,1)}, u32[]{:S(2)}) copy-start(bf16[128,1280]{1,0:T(8,128)(2,1)} %g_ref.3) | copy-start | bytes 983044
  0.7 25.0 %copy-start.2 = (bf16[128,1280]{1,0:T(8,128)(2,1)S(1)}, bf16[128,1280]{1,0:T(8,128)(2,1)}, u32[]{:S(2)}) copy-start(bf16[128,1280]{1,0:T(8,128)(2,1)} %k_ref.3) | copy-start | bytes 983044
  0.7 25.0 %copy-start.3 = (bf16[128,1280]{1,0:T(8,128)(2,1)S(1)}, bf16[128,1280]{1,0:T(8,128)(2,1)}, u32[]{:S(2)}) copy-start(bf16[128,1280]{1,0:T(8,128)(2,1)} %v_ref.3) | copy-start | bytes 983044
  2.1 9.0 %collective-permute-start = (bf16[160,640]{1,0:T(8,128)(2,1)S(1)}, bf16[160,640]{1,0:T(8,128)(2,1)S(1)}, u32[]{:S(2)}, u32[]{:S(2)}) collective-permute-start(bf16[160,640]{1,0:T(8,128)(2,1)S(1)} %get-tuple-element.51), channel_id=1, source_target_pairs={{0,8},{8,0},{16,24},{24,16},{1,9},{9,1},{17,25},{25,17},{2,10},{10... | collective-permute-start | bytes 614408 | tf_op jit(solution)/shard_map/ppermute | solution.py:25
  3.8 14.6 %collective-permute-start.1 = (bf16[160,640]{1,0:T(8,128)(2,1)S(1)}, bf16[160,640]{1,0:T(8,128)(2,1)S(1)}, u32[]{:S(2)}, u32[]{:S(2)}) collective-permute-start(bf16[160,640]{1,0:T(8,128)(2,1)S(1)} %get-tuple-element.53), channel_id=1, source_target_pairs={{0,16},{8,24},{16,0},{24,8},{1,17},{9,25},{17,1},{25,9},{2,18},{10... | collective-permute-start | bytes 614408 | tf_op jit(solution)/shard_map/ppermute | solution.py:25
  4.1 19.3 %collective-permute-start.2 = (bf16[160,640]{1,0:T(8,128)(2,1)S(1)}, bf16[160,640]{1,0:T(8,128)(2,1)S(1)}, u32[]{:S(2)}, u32[]{:S(2)}) collective-permute-start(bf16[160,640]{1,0:T(8,128)(2,1)S(1)} %get-tuple-element.52), channel_id=1, source_target_pairs={{0,24},{8,16},{16,8},{24,0},{1,25},{9,17},{17,9},{25,1},{2,26},{10... | collective-permute-start | bytes 614408 | tf_op jit(solution)/shard_map/ppermute | solution.py:25
  5.7 17.8 %collective-permute-start.3 = (bf16[128,1280]{1,0:T(8,128)(2,1)S(1)}, bf16[128,1280]{1,0:T(8,128)(2,1)S(1)}, u32[]{:S(2)}, u32[]{:S(2)}) collective-permute-start(bf16[128,1280]{1,0:T(8,128)(2,1)S(1)} %copy-done.4), channel_id=1, source_target_pairs={{0,1},{1,0},{2,3},{3,2},{4,5},{5,4},{6,7},{7,6},{8,9},{9,8},{10,11... | collective-permute-start | bytes 983048 | tf_op jit(solution)/shard_map/ppermute | solution.py:25
  23.5 20.0 %collective-permute-start.10 = (bf16[4,160,640]{2,1,0:T(8,128)(2,1)S(1)}, bf16[4,160,640]{2,1,0:T(8,128)(2,1)S(1)}, u32[]{:S(2)}, u32[]{:S(2)}) collective-permute-start(bf16[4,160,640]{2,1,0:T(8,128)(2,1)S(1)} %pad_maximum_fusion.refs_8_), channel_id=1, source_target_pairs={{0,2},{2,0},{4,6},{6,4},{1,3},{3,1},{5,7},{7,5},{8,10},{10,8},{12,... | collective-permute-start | bytes 2457608 | tf_op jit(solution)/shard_map/ppermute | solution.py:25
  23.6 10.6 %collective-permute-start.5 = (bf16[128,1280]{1,0:T(8,128)(2,1)S(1)}, bf16[128,1280]{1,0:T(8,128)(2,1)S(1)}, u32[]{:S(2)}, u32[]{:S(2)}) collective-permute-start(bf16[128,1280]{1,0:T(8,128)(2,1)S(1)} %copy-done.4), channel_id=1, source_target_pairs={{0,8},{8,24},{24,16},{16,0},{1,9},{9,25},{25,17},{17,1},{2,10},{10... | collective-permute-start | bytes 983048 | tf_op jit(solution)/shard_map/ppermute | solution.py:317
  23.7 17.0 %collective-permute-start.6 = (bf16[128,1280]{1,0:T(8,128)(2,1)S(1)}, bf16[128,1280]{1,0:T(8,128)(2,1)S(1)}, u32[]{:S(2)}, u32[]{:S(2)}) collective-permute-start(bf16[128,1280]{1,0:T(8,128)(2,1)S(1)} %copy-done.4), channel_id=1, source_target_pairs={{8,0},{24,8},{16,24},{0,16},{9,1},{25,9},{17,25},{1,17},{10,2},{26... | collective-permute-start | bytes 983048 | tf_op jit(solution)/shard_map/ppermute | solution.py:317
  25.8 42.1 %copy-start.6 = (s32[2048]{0:T(1024)S(1)}, s32[2048]{0:T(1024)}, u32[]{:S(2)}) copy-start(s32[2048]{0:T(1024)} %param.15) | copy-start | bytes 24580
  25.9 42.1 %copy-start.7 = (s32[2048]{0:T(1024)S(1)}, s32[2048]{0:T(1024)}, u32[]{:S(2)}) copy-start(s32[2048]{0:T(1024)} %param.14) | copy-start | bytes 24580
  25.9 25.6 %collective-permute-start.4 = (bf16[4,160,640]{2,1,0:T(8,128)(2,1)S(1)}, bf16[4,160,640]{2,1,0:T(8,128)(2,1)S(1)}, u32[]{:S(2)}, u32[]{:S(2)}) collective-permute-start(bf16[4,160,640]{2,1,0:T(8,128)(2,1)S(1)} %pad_maximum_fusion.refs_8_), channel_id=1, source_target_pairs={{0,4},{2,6},{4,0},{6,2},{1,5},{3,7},{5,1},{7,3},{8,12},{10,14},{12... | collective-permute-start | bytes 2457608 | tf_op jit(solution)/shard_map/ppermute | solution.py:25
  40.6 9.4 %collective-permute-start.8 = (bf16[128,1280]{1,0:T(8,128)(2,1)S(1)}, bf16[128,1280]{1,0:T(8,128)(2,1)S(1)}, u32[]{:S(2)}, u32[]{:S(2)}) collective-permute-start(bf16[128,1280]{1,0:T(8,128)(2,1)S(1)} %collective-permute-done.5.refs_1_), channel_id=1, source_target_pairs={{0,8},{8,24},{24,16},{16,0},{1,9},{9,25},{25,17},{17,1},{2,10},{10... | collective-permute-start | bytes 983048 | tf_op jit(solution)/shard_map/ppermute | solution.py:317
  42.0 17.7 %collective-permute-start.7 = (bf16[2,128,1280]{2,1,0:T(8,128)(2,1)S(1)}, bf16[2,128,1280]{2,1,0:T(8,128)(2,1)S(1)}, u32[]{:S(2)}, u32[]{:S(2)}) collective-permute-start(bf16[2,128,1280]{2,1,0:T(8,128)(2,1)S(1)} %pad_maximum_fusion.1), channel_id=1, source_target_pairs={{0,1},{1,0},{2,3},{3,2},{4,5},{5,4},{6,7},{7,6},{8,9},{9,8},{10,11... | collective-permute-start | bytes 1966088 | tf_op jit(solution)/shard_map/ppermute | solution.py:25
  43.6 21.9 %collective-permute-start.11 = (bf16[2,128,1280]{2,1,0:T(8,128)(2,1)S(1)}, bf16[2,128,1280]{2,1,0:T(8,128)(2,1)S(1)}, u32[]{:S(2)}, u32[]{:S(2)}) collective-permute-start(bf16[2,128,1280]{2,1,0:T(8,128)(2,1)S(1)} %get-tuple-element.31), channel_id=1, source_target_pairs={{0,2},{2,4},{4,6},{6,8},{8,10},{10,12},{12,14},{14,16},{16,18},{18... | collective-permute-start | bytes 1966088 | tf_op jit(solution)/shard_map/ppermute | solution.py:21
  45.5 20.0 %collective-permute-start.12 = (bf16[2,128,1280]{2,1,0:T(8,128)(2,1)S(1)}, bf16[2,128,1280]{2,1,0:T(8,128)(2,1)S(1)}, u32[]{:S(2)}, u32[]{:S(2)}) collective-permute-start(bf16[2,128,1280]{2,1,0:T(8,128)(2,1)S(1)} %get-tuple-element.32), channel_id=1, source_target_pairs={{2,0},{4,2},{6,4},{8,6},{10,8},{12,10},{14,12},{16,14},{18,16},{20... | collective-permute-start | bytes 1966088 | tf_op jit(solution)/shard_map/ppermute | solution.py:21
  50.1 15.4 %collective-permute-start.9 = (bf16[128,1280]{1,0:T(8,128)(2,1)S(1)}, bf16[128,1280]{1,0:T(8,128)(2,1)S(1)}, u32[]{:S(2)}, u32[]{:S(2)}) collective-permute-start(bf16[128,1280]{1,0:T(8,128)(2,1)S(1)} %collective-permute-done.8.refs_2_), channel_id=1, source_target_pairs={{0,1},{1,0},{2,3},{3,2},{4,5},{5,4},{6,7},{7,6},{8,9},{9,8},{10,11... | collective-permute-start | bytes 983048 | tf_op jit(solution)/shard_map/ppermute | solution.py:25
  65.5 8.1 %copy-start.8 = (bf16[2,128,1280]{2,1,0:T(8,128)(2,1)}, bf16[2,128,1280]{2,1,0:T(8,128)(2,1)S(1)}, u32[]{:S(2)}) copy-start(bf16[2,128,1280]{2,1,0:T(8,128)(2,1)S(1)} %collective-permute-done.11.kv1_ref) | copy-start | bytes 1966084
  65.5 3.5 %collective-permute-start.13 = (bf16[4,160,640]{2,1,0:T(8,128)(2,1)S(1)}, bf16[4,160,640]{2,1,0:T(8,128)(2,1)S(1)}, u32[]{:S(2)}, u32[]{:S(2)}) collective-permute-start(bf16[4,160,640]{2,1,0:T(8,128)(2,1)S(1)} %collective-permute-done.4.refs_10_), channel_id=1, source_target_pairs={{0,2},{2,0},{4,6},{6,4},{1,3},{3,1},{5,7},{7,5},{8,10},{10,8},{12,... | collective-permute-start | bytes 2457608 | tf_op jit(solution)/shard_map/ppermute | solution.py:25
  65.6 12.8 %collective-permute-start.14 = (bf16[2,128,1280]{2,1,0:T(8,128)(2,1)S(1)}, bf16[2,128,1280]{2,1,0:T(8,128)(2,1)S(1)}, u32[]{:S(2)}, u32[]{:S(2)}) collective-permute-start(bf16[2,128,1280]{2,1,0:T(8,128)(2,1)S(1)} %collective-permute-done.11.kv1_ref), channel_id=1, source_target_pairs={{0,2},{2,4},{4,6},{6,8},{8,10},{10,12},{12,14},{14,16},{16,18},{18... | collective-permute-start | bytes 1966088 | tf_op jit(solution)/shard_map/ppermute | solution.py:21
  68.2 0.7 copy-start.5
  78.4 0.9 copy-start.9
  79.2 35.0 %all-to-all-start = ((bf16[16,4,16,640]{3,2,1,0:T(8,128)(2,1)}), bf16[16,4,16,640]{3,2,1,0:T(8,128)(2,1)S(1)}, u32[]{:S(2)}, u32[]{:S(2)}) async-start(bf16[16,4,16,640]{3,2,1,0:T(8,128)(2,1)} %project.1), calls=%async_computation | async-start | bytes 2621440 | tf_op jit(solution)/shard_map/all_to_all | solution.py:393
  83.5 40.8 %collective-permute-start.15 = (bf16[2,128,1280]{2,1,0:T(8,128)(2,1)S(1)}, bf16[2,128,1280]{2,1,0:T(8,128)(2,1)}, u32[]{:S(2)}, u32[]{:S(2)}) collective-permute-start(bf16[2,128,1280]{2,1,0:T(8,128)(2,1)S(1)} %collective-permute-done.12.qg1_ref), channel_id=1, source_target_pairs={{2,0},{4,2},{6,4},{8,6},{10,8},{12,10},{14,12},{16,14},{18,16},{20... | collective-permute-start | bytes 1966088 | tf_op jit(solution)/shard_map/ppermute | solution.py:21
  119.3 5.0 %collective-permute-start.16 = (f32[2,16,128]{2,1,0:T(8,128)S(1)}, f32[2,16,128]{2,1,0:T(8,128)S(1)}, u32[]{:S(2)}, u32[]{:S(2)}) collective-permute-start(f32[2,16,128]{2,1,0:T(8,128)S(1)} %get-tuple-element.46.st0_ref), channel_id=1, source_target_pairs={{2,0},{4,2},{6,4},{8,6},{10,8},{12,10},{14,12},{16,14},{18,16},{20... | collective-permute-start | bytes 49160 | tf_op jit(solution)/shard_map/ppermute | solution.py:21
  122.1 5.6 %collective-permute-start.17 = (f32[2,16,128]{2,1,0:T(8,128)S(1)}, f32[2,16,128]{2,1,0:T(8,128)S(1)}, u32[]{:S(2)}, u32[]{:S(2)}) collective-permute-start(f32[2,16,128]{2,1,0:T(8,128)S(1)} %get-tuple-element.46.st0_ref), channel_id=1, source_target_pairs={{4,0},{6,2},{8,4},{10,6},{12,8},{14,10},{16,12},{18,14},{20,16},{2... | collective-permute-start | bytes 49160 | tf_op jit(solution)/shard_map/ppermute | solution.py:21

commit v5 on v3

--- a/solution.py
+++ b/solution.py
@@ -325,27 +325,24 @@
     z = lax.axis_index("z")
     if n_p == 4 and capacity % ROW_TILE == 0 and w_rows % ROW_TILE == 0:
         blocks = [column_block(w_kv, z ^ mask) for mask in range(n_z)]
-        own = jnp.stack(
-            [blocks[0]] + [swapped(blocks[mask], "z", mask) for mask in range(1, n_z)], 0
-        )
+        arrived = [blocks[0]] + [swapped(blocks[mask], "z", mask) for mask in range(1, n_z)]
         row1, other0 = ring_step(cache), swapped(cache, "head", 1)
-        own, row1, other0, cache = lax.optimization_barrier((own, row1, other0, cache))
-        across = swapped(own, "p", 2)
-        beside = swapped(own, "p", 1)
-        row2, row3, other1 = ring_step(row1), ring_step(cache, back=True), swapped(row1, "head", 1)
-        beside, stream, back = lax.optimization_barrier((beside, stream, back))
+        row1, arrived[1], arrived[2] = lax.optimization_barrier((row1, arrived[1], arrived[2]))
+        row2, other1 = ring_step(row1), swapped(row1, "head", 1)
+        own, row2, other0, other1 = lax.optimization_barrier(
+            (jnp.stack(arrived, 0), row2, other0, other1)
+        )
+        across, beside = swapped(own, "p", 2), swapped(own, "p", 1)
+        row3, other2 = ring_step(row2), swapped(row2, "head", 1)
+        row3, other2, beside = lax.optimization_barrier((row3, other2, beside))
+        other3 = swapped(row3, "head", 1)
+        across, other3, stream, back = lax.optimization_barrier((across, other3, stream, back))
+        pieces = [own, beside, across, swapped(across, "p", 1)]
         near, back1 = shifted(stream, 1), shifted(back, -1)
-        row2, row3, other1 = lax.optimization_barrier((row2, row3, other1))
-        other2, other3 = swapped(row2, "head", 1), swapped(row3, "head", 1)
-        across, other2, other3, near, back1 = lax.optimization_barrier(
-            (across, other2, other3, near, back1)
-        )
-        pieces = [own, beside, across, swapped(across, "p", 1)]
-        far = shifted(near, 1)
         rows = [cache, row1, row2, row3, other0, other1, other2, other3]
         slots = project(place, rows, pieces, devices, capacity)
-        slots, far = lax.optimization_barrier((slots, far))
-        return slots, near, far, back1
+        slots, near, back1 = lax.optimization_barrier((slots, near, back1))
+        return slots, near, shifted(near, 1), back1
     near, back1 = shifted(stream, 1), shifted(back, -1)
     far = shifted(near, 1)
     targets = [column_block(w_kv, jnp.int32(i)) for i in range(n_z)]

time: 135 us -> 137 us (1.015); the launches traced: 135 us -> 135 us
  waiting for transfers between devices: 72.1 us -> 75.5 us
  starting transfers between devices: 45.9 us -> 43.3 us
    all_to_all x1, waiting for transfers between devices: 27.7 us -> 0.01 us  [body(): memory = lax.all_to_all(slots, SEQ, split_axis=0, concat_axis=0, tiled=True)]
    ppermute x6, waiting for transfers between devices: 9.68 us -> 36.6 us  [shifted(): return lax.ppermute(value, SEQ, pairs)]
    ppermute x6, starting transfers between devices: 21.5 us -> 16.7 us  [shifted(): return lax.ppermute(value, SEQ, pairs)]
    ppermute x10, waiting for transfers between devices: 28 us -> 32.2 us  [swapped(): lax.ppermute(value, axis, [(i, i ^ mask) for i in range(lax.axis_size(axi...]
    all_to_all x1, starting transfers between devices: 7.14 us -> 10.6 us  [body(): memory = lax.all_to_all(slots, SEQ, split_axis=0, concat_axis=0, tiled=True)]
    ppermute x10, starting transfers between devices: 12.6 us -> 10.1 us  [swapped(): lax.ppermute(value, axis, [(i, i ^ mask) for i in range(lax.axis_size(axi...]
  transfers between devices with their start and end apart: 20 -> 20, of which waited for: 10 -> 12; matrix products, arithmetic and copies ran while one was open for 0% -> 1% of each run, Pallas kernels for 7% -> 7%
where the time goes in v5:
time: 137 us; the launch traced here: 135 us
  waiting for transfers between devices  75.5 us (55%)
  starting transfers between devices  43.3 us (32%)
  Pallas kernels  13.6 us (10%)
  local copies, waits for them, and re-layouts  1.44 us (1%)
    ppermute x6, waiting for transfers between devices, shifted(): return lax.ppermute(value, SEQ, pairs)  36.6 us
    ppermute x10, waiting for transfers between devices, swapped(): lax.ppermute(value, axis, [(i, i ^ mask) for i in range(lax.axis_size(axi...  32.2 us
    ppermute x6, starting transfers between devices, shifted(): return lax.ppermute(value, SEQ, pairs)  16.7 us
    all_to_all x1, starting transfers between devices, body(): memory = lax.all_to_all(slots, SEQ, split_axis=0, concat_axis=0, tiled=True)  10.6 us
    ppermute x10, starting transfers between devices, swapped(): lax.ppermute(value, axis, [(i, i ^ mask) for i in range(lax.axis_size(axi...  10.1 us
    ppermute x3, waiting for transfers between devices, ring_step(): lax.ppermute(value, 'z', [(b, a) for a, b in pairs] if back else pairs)  6.69 us
    ppermute x3, starting transfers between devices, ring_step(): lax.ppermute(value, 'z', [(b, a) for a, b in pairs] if back else pairs)  5.83 us
    pallas_call x1, Pallas kernels, attend(): pl.pallas_call(attend_kernel, grid=(steps,), in_specs=[flat, flat, flat,...  5 us
  transfers between devices with their start and end apart: 20, of which 12 were waited for; matrix products, arithmetic and copies ran while one was open for 1% of the time, Pallas kernels for 7%

profile of v5, /device:TPU:16, one launch (start us, length us, event | category | flops | bytes accessed | tf_op | source)
XLA Modules:
  0.0 134.9 jit_solution(15964973373247693797)
XLA Ops:
  0.6 0.0 copy-start.4
  0.6 0.1 collective-permute-start
  0.7 0.0 copy-start
  0.7 0.0 copy-start.1
  0.8 0.0 copy-start.2
  0.8 0.0 copy-start.3
  0.8 1.4 %constant_dynamic-slice_fusion = (bf16[1,160,640]{2,1,0:T(8,128)(2,1)S(1)}, bf16[160,640]{1,0:T(8,128)(2,1)S(1)}, bf16[160,640]{1,0:T(8,128)(2,1)S(1)}, bf16[160,640]{1,0:T(8,128)(2,1)S(1)}) fusion(bf16[2,160,1280]{2,1,0:T(8,128)(2,1)} %param.13, s32[]{:T(128)S(6)} %select_n.28, s32[]{:T(128)S(6)} %select_n.29, s32[]{:T(128)S(6)} %select_n.26, ...), kind=kLoop, calls=%fused_computation.6 | loop fusion | bytes 1638432 | tf_op jit(solution)/shard_map/dynamic_slice | solution.py:312
  2.2 1.9 %collective-permute-start.2 = (bf16[160,640]{1,0:T(8,128)(2,1)S(1)}, bf16[160,640]{1,0:T(8,128)(2,1)S(1)}, u32[]{:S(2)}, u32[]{:S(2)}) collective-permute-start(bf16[160,640]{1,0:T(8,128)(2,1)S(1)} %get-tuple-element.55), channel_id=1, source_target_pairs={{0,16},{8,24},{16,0},{24,8},{1,17},{9,25},{17,1},{25,9},{2,18},{10... | collective-permute-start | bytes 614408 | tf_op jit(solution)/shard_map/ppermute | solution.py:25
  4.1 2.6 %collective-permute-start.1 = (bf16[160,640]{1,0:T(8,128)(2,1)S(1)}, bf16[160,640]{1,0:T(8,128)(2,1)S(1)}, u32[]{:S(2)}, u32[]{:S(2)}) collective-permute-start(bf16[160,640]{1,0:T(8,128)(2,1)S(1)} %get-tuple-element.56), channel_id=1, source_target_pairs={{0,8},{8,0},{16,24},{24,16},{1,9},{9,1},{17,25},{25,17},{2,10},{10... | collective-permute-start | bytes 614408 | tf_op jit(solution)/shard_map/ppermute | solution.py:25
  6.7 0.0 collective-permute-start.3
  6.7 0.0 copy-done.4
  6.7 1.5 %collective-permute-start.5 = (bf16[128,1280]{1,0:T(8,128)(2,1)S(1)}, bf16[128,1280]{1,0:T(8,128)(2,1)S(1)}, u32[]{:S(2)}, u32[]{:S(2)}) collective-permute-start(bf16[128,1280]{1,0:T(8,128)(2,1)S(1)} %copy-done.4), channel_id=1, source_target_pairs={{0,1},{1,0},{2,3},{3,2},{4,5},{5,4},{6,7},{7,6},{8,9},{9,8},{10,11... | collective-permute-start | bytes 983048 | tf_op jit(solution)/shard_map/ppermute | solution.py:25
  8.2 9.9 %collective-permute-done.2 = bf16[160,640]{1,0:T(8,128)(2,1)S(1)} collective-permute-done((bf16[160,640]{1,0:T(8,128)(2,1)S(1)}, bf16[160,640]{1,0:T(8,128)(2,1)S(1)}, u32[]{:S(2)}, u32[]{:S(2)}) %collective-permute-start.2) | collective-permute-done | bytes 204832 | tf_op jit(solution)/shard_map/ppermute | solution.py:25
  18.1 2.2 %collective-permute-done.1 = bf16[160,640]{1,0:T(8,128)(2,1)S(1)} collective-permute-done((bf16[160,640]{1,0:T(8,128)(2,1)S(1)}, bf16[160,640]{1,0:T(8,128)(2,1)S(1)}, u32[]{:S(2)}, u32[]{:S(2)}) %collective-permute-start.1) | collective-permute-done | bytes 204832 | tf_op jit(solution)/shard_map/ppermute | solution.py:25
  20.3 0.0 collective-permute-done.refs_1_
  20.3 1.5 %collective-permute-start.6 = (bf16[128,1280]{1,0:T(8,128)(2,1)S(1)}, bf16[128,1280]{1,0:T(8,128)(2,1)S(1)}, u32[]{:S(2)}, u32[]{:S(2)}) collective-permute-start(bf16[128,1280]{1,0:T(8,128)(2,1)S(1)} %collective-permute-done.refs_1_), channel_id=1, source_target_pairs={{0,1},{1,0},{2,3},{3,2},{4,5},{5,4},{6,7},{7,6},{8,9},{9,8},{10,11... | collective-permute-start | bytes 983048 | tf_op jit(solution)/shard_map/ppermute | solution.py:25
  21.9 2.4 %collective-permute-start.4 = (bf16[128,1280]{1,0:T(8,128)(2,1)S(1)}, bf16[128,1280]{1,0:T(8,128)(2,1)S(1)}, u32[]{:S(2)}, u32[]{:S(2)}) collective-permute-start(bf16[128,1280]{1,0:T(8,128)(2,1)S(1)} %collective-permute-done.refs_1_), channel_id=1, source_target_pairs={{0,8},{8,24},{24,16},{16,0},{1,9},{9,25},{25,17},{17,1},{2,10},{10... | collective-permute-start | bytes 983048 | tf_op jit(solution)/shard_map/ppermute | solution.py:317
  24.2 5.9 %collective-permute-done.3 = bf16[160,640]{1,0:T(8,128)(2,1)S(1)} collective-permute-done((bf16[160,640]{1,0:T(8,128)(2,1)S(1)}, bf16[160,640]{1,0:T(8,128)(2,1)S(1)}, u32[]{:S(2)}, u32[]{:S(2)}) %collective-permute-start.3) | collective-permute-done | bytes 204832 | tf_op jit(solution)/shard_map/ppermute | solution.py:25
  30.1 0.1 pad_maximum_fusion.refs_8_
  30.2 0.0 collective-permute-done.5.refs_4_
  30.3 0.0 collective-permute-done.6.refs_5_
  30.3 3.5 %collective-permute-done.4.refs_2_ = bf16[128,1280]{1,0:T(8,128)(2,1)S(1)} collective-permute-done((bf16[128,1280]{1,0:T(8,128)(2,1)S(1)}, bf16[128,1280]{1,0:T(8,128)(2,1)S(1)}, u32[]{:S(2)}, u32[]{:S(2)}) %collective-permute-start.4) | collective-permute-done | bytes 327712 | tf_op jit(solution)/shard_map/ppermute | solution.py:317
  33.8 0.0 collective-permute-start.9
  33.8 1.5 %collective-permute-start.10 = (bf16[4,160,640]{2,1,0:T(8,128)(2,1)S(1)}, bf16[4,160,640]{2,1,0:T(8,128)(2,1)S(1)}, u32[]{:S(2)}, u32[]{:S(2)}) collective-permute-start(bf16[4,160,640]{2,1,0:T(8,128)(2,1)S(1)} %pad_maximum_fusion.refs_8_), channel_id=1, source_target_pairs={{0,4},{2,6},{4,0},{6,2},{1,5},{3,7},{5,1},{7,3},{8,12},{10,14},{12... | collective-permute-start | bytes 2457608 | tf_op jit(solution)/shard_map/ppermute | solution.py:25
  35.3 0.6 collective-permute-start.8
  35.8 3.4 %collective-permute-start.7 = (bf16[128,1280]{1,0:T(8,128)(2,1)S(1)}, bf16[128,1280]{1,0:T(8,128)(2,1)S(1)}, u32[]{:S(2)}, u32[]{:S(2)}) collective-permute-start(bf16[128,1280]{1,0:T(8,128)(2,1)S(1)} %collective-permute-done.4.refs_2_), channel_id=1, source_target_pairs={{0,8},{8,24},{24,16},{16,0},{1,9},{9,25},{25,17},{17,1},{2,10},{10... | collective-permute-start | bytes 983048 | tf_op jit(solution)/shard_map/ppermute | solution.py:317
  39.2 5.9 %collective-permute-done.8.refs_6_ = bf16[128,1280]{1,0:T(8,128)(2,1)S(1)} collective-permute-done((bf16[128,1280]{1,0:T(8,128)(2,1)S(1)}, bf16[128,1280]{1,0:T(8,128)(2,1)S(1)}, u32[]{:S(2)}, u32[]{:S(2)}) %collective-permute-start.8) | collective-permute-done | bytes 327712 | tf_op jit(solution)/shard_map/ppermute | solution.py:25
  45.1 3.2 %collective-permute-done.7.refs_3_ = bf16[128,1280]{1,0:T(8,128)(2,1)S(1)} collective-permute-done((bf16[128,1280]{1,0:T(8,128)(2,1)S(1)}, bf16[128,1280]{1,0:T(8,128)(2,1)S(1)}, u32[]{:S(2)}, u32[]{:S(2)}) %collective-permute-start.7) | collective-permute-done | bytes 327712 | tf_op jit(solution)/shard_map/ppermute | solution.py:317
  48.3 0.0 collective-permute-done.9.refs_9_
  48.3 0.5 collective-permute-start.11
  48.8 0.0 copy-done
  48.8 0.0 copy-done.1
  48.8 0.0 copy-done.2
  48.8 0.0 copy-done.3
  48.8 0.0 copy-start.6
  48.8 0.0 copy-start.7
  48.8 0.1 pad_maximum_fusion.1
  49.0 5.5 %collective-permute-done.10.refs_10_ = bf16[4,160,640]{2,1,0:T(8,128)(2,1)S(1)} collective-permute-done((bf16[4,160,640]{2,1,0:T(8,128)(2,1)S(1)}, bf16[4,160,640]{2,1,0:T(8,128)(2,1)S(1)}, u32[]{:S(2)}, u32[]{:S(2)}) %collective-permute-start.10) | collective-permute-done | bytes 819232 | tf_op jit(solution)/shard_map/ppermute | solution.py:25
  54.4 2.9 %collective-permute-done.11.refs_7_ = bf16[128,1280]{1,0:T(8,128)(2,1)S(1)} collective-permute-done((bf16[128,1280]{1,0:T(8,128)(2,1)S(1)}, bf16[128,1280]{1,0:T(8,128)(2,1)S(1)}, u32[]{:S(2)}, u32[]{:S(2)}) %collective-permute-start.11) | collective-permute-done | bytes 327712 | tf_op jit(solution)/shard_map/ppermute | solution.py:25
  57.3 0.0 collective-permute-start.12
  57.3 2.4 %collective-permute-start.13 = (bf16[2,128,1280]{2,1,0:T(8,128)(2,1)S(1)}, bf16[2,128,1280]{2,1,0:T(8,128)(2,1)}, u32[]{:S(2)}, u32[]{:S(2)}) collective-permute-start(bf16[2,128,1280]{2,1,0:T(8,128)(2,1)S(1)} %get-tuple-element.42), channel_id=1, source_target_pairs={{0,2},{2,4},{4,6},{6,8},{8,10},{10,12},{12,14},{14,16},{16,18},{18... | collective-permute-start | bytes 1966088 | tf_op jit(solution)/shard_map/ppermute | solution.py:21
  59.7 4.0 %collective-permute-start.14 = (bf16[2,128,1280]{2,1,0:T(8,128)(2,1)S(1)}, bf16[2,128,1280]{2,1,0:T(8,128)(2,1)S(1)}, u32[]{:S(2)}, u32[]{:S(2)}) collective-permute-start(bf16[2,128,1280]{2,1,0:T(8,128)(2,1)S(1)} %get-tuple-element.43), channel_id=1, source_target_pairs={{2,0},{4,2},{6,4},{8,6},{10,8},{12,10},{14,12},{16,14},{18,16},{20... | collective-permute-start | bytes 1966088 | tf_op jit(solution)/shard_map/ppermute | solution.py:21
  63.8 0.0 copy-done.6
  63.8 0.0 copy-done.7
  63.8 0.3 prepare.1
  64.1 0.0 copy-start.5
  64.1 0.0 collective-permute-done.12.refs_11_
  64.1 4.6 %project.1 = bf16[16,4,16,640]{3,2,1,0:T(8,128)(2,1)} custom-call(s32[4,1,128]{2,1,0:T(1,128)S(1)} %get-tuple-element.29.place_ref, bf16[128,1280]{1,0:T(8,128)(2,1)S(1)} %copy-done.4, bf16[128,1280]{1,0:T(8,128)(2,1)S(1)} %collective-permute-done.refs_1_, bf16[128,1280]{1,0:T(8,128)(2,1)S(1)} %collective-permute-done.4.refs_2_, ...), custom_call_target="tpu_custom_call" | custom-call | flops 1677721600 | bytes 8388608 | tf_op jit(solution)/shard_map/project/pallas_call | solution.py:225
  68.7 0.0 copy-done.5
  68.7 1.7 %collective-permute-done.13.kv1_ref = bf16[2,128,1280]{2,1,0:T(8,128)(2,1)} collective-permute-done((bf16[2,128,1280]{2,1,0:T(8,128)(2,1)S(1)}, bf16[2,128,1280]{2,1,0:T(8,128)(2,1)}, u32[]{:S(2)}, u32[]{:S(2)}) %collective-permute-start.13) | collective-permute-done | bytes 655392 | tf_op jit(solution)/shard_map/ppermute | solution.py:21
  70.3 1.6 %collective-permute-done.14.qg1_ref = bf16[2,128,1280]{2,1,0:T(8,128)(2,1)S(1)} collective-permute-done((bf16[2,128,1280]{2,1,0:T(8,128)(2,1)S(1)}, bf16[2,128,1280]{2,1,0:T(8,128)(2,1)S(1)}, u32[]{:S(2)}, u32[]{:S(2)}) %collective-permute-start.14) | collective-permute-done | bytes 655392 | tf_op jit(solution)/shard_map/ppermute | solution.py:21
  71.9 10.6 %all-to-all-start = ((bf16[16,4,16,640]{3,2,1,0:T(8,128)(2,1)}), bf16[16,4,16,640]{3,2,1,0:T(8,128)(2,1)S(1)}, u32[]{:S(2)}, u32[]{:S(2)}) async-start(bf16[16,4,16,640]{3,2,1,0:T(8,128)(2,1)} %project.1), calls=%async_computation | async-start | bytes 2621440 | tf_op jit(solution)/shard_map/all_to_all | solution.py:388
  82.5 2.0 %collective-permute-start.15 = (bf16[2,128,1280]{2,1,0:T(8,128)(2,1)}, bf16[2,128,1280]{2,1,0:T(8,128)(2,1)}, u32[]{:S(2)}, u32[]{:S(2)}) collective-permute-start(bf16[2,128,1280]{2,1,0:T(8,128)(2,1)} %collective-permute-done.13.kv1_ref), channel_id=1, source_target_pairs={{0,2},{2,4},{4,6},{6,8},{8,10},{10,12},{12,14},{14,16},{16,18},{18... | collective-permute-start | bytes 1966088 | tf_op jit(solution)/shard_map/ppermute | solution.py:21
  84.6 4.4 %collective-permute-start.16 = (bf16[2,128,1280]{2,1,0:T(8,128)(2,1)S(1)}, bf16[2,128,1280]{2,1,0:T(8,128)(2,1)}, u32[]{:S(2)}, u32[]{:S(2)}) collective-permute-start(bf16[2,128,1280]{2,1,0:T(8,128)(2,1)S(1)} %collective-permute-done.14.qg1_ref), channel_id=1, source_target_pairs={{2,0},{4,2},{6,4},{8,6},{10,8},{12,10},{14,12},{16,14},{18,16},{20... | collective-permute-start | bytes 1966088 | tf_op jit(solution)/shard_map/ppermute | solution.py:21
  89.0 31.5 %collective-permute-done.15.kv2_ref = bf16[2,128,1280]{2,1,0:T(8,128)(2,1)} collective-permute-done((bf16[2,128,1280]{2,1,0:T(8,128)(2,1)}, bf16[2,128,1280]{2,1,0:T(8,128)(2,1)}, u32[]{:S(2)}, u32[]{:S(2)}) %collective-permute-start.15) | collective-permute-done | bytes 655392 | tf_op jit(solution)/shard_map/ppermute | solution.py:21
  120.5 0.0 all-to-all-done
  120.5 5.0 %attend.1 = (bf16[128,1280]{1,0:T(8,128)(2,1)}, bf16[128,1280]{1,0:T(8,128)(2,1)}, f32[2,16,128]{2,1,0:T(8,128)S(1)}) custom-call(bf16[128,1280]{1,0:T(8,128)(2,1)S(1)} %copy-done, bf16[128,1280]{1,0:T(8,128)(2,1)S(1)} %copy-done.1, bf16[128,1280]{1,0:T(8,128)(2,1)S(1)} %copy-done.2, bf16[128,1280]{1,0:T(8,128)(2,1)S(1)} %copy-done.3, ...), custom_call_target="tpu_custom_call" | custom-call | flops 838860800 | bytes 6291456 | tf_op jit(solution)/shard_map/attend/pallas_call | solution.py:103
  125.6 1.9 %collective-permute-start.18 = (f32[2,16,128]{2,1,0:T(8,128)S(1)}, f32[2,16,128]{2,1,0:T(8,128)S(1)}, u32[]{:S(2)}, u32[]{:S(2)}) collective-permute-start(f32[2,16,128]{2,1,0:T(8,128)S(1)} %get-tuple-element.50.st0_ref), channel_id=1, source_target_pairs={{4,0},{6,2},{8,4},{10,6},{12,8},{14,10},{16,12},{18,14},{20,16},{2... | collective-permute-start | bytes 49160 | tf_op jit(solution)/shard_map/ppermute | solution.py:21
  127.5 1.9 %collective-permute-start.17 = (f32[2,16,128]{2,1,0:T(8,128)S(1)}, f32[2,16,128]{2,1,0:T(8,128)S(1)}, u32[]{:S(2)}, u32[]{:S(2)}) collective-permute-start(f32[2,16,128]{2,1,0:T(8,128)S(1)} %get-tuple-element.50.st0_ref), channel_id=1, source_target_pairs={{2,0},{4,2},{6,4},{8,6},{10,8},{12,10},{14,12},{16,14},{18,16},{20... | collective-permute-start | bytes 49160 | tf_op jit(solution)/shard_map/ppermute | solution.py:21
  129.4 0.0 collective-permute-done.16.qg2_ref
  129.4 1.8 %collective-permute-done.18.st2_ref = f32[2,16,128]{2,1,0:T(8,128)S(1)} collective-permute-done((f32[2,16,128]{2,1,0:T(8,128)S(1)}, f32[2,16,128]{2,1,0:T(8,128)S(1)}, u32[]{:S(2)}, u32[]{:S(2)}) %collective-permute-start.18) | collective-permute-done | bytes 16416 | tf_op jit(solution)/shard_map/ppermute | solution.py:21
  131.2 0.0 collective-permute-done.17.st1_ref
  131.2 3.7 %key_grads.1 = (bf16[128,1280]{1,0:T(8,128)(2,1)}, bf16[128,1280]{1,0:T(8,128)(2,1)}) custom-call(bf16[128,1280]{1,0:T(8,128)(2,1)S(1)} %copy-done.2, bf16[128,1280]{1,0:T(8,128)(2,1)S(1)} %copy-done.3, bf16[128,1280]{1,0:T(8,128)(2,1)S(1)} %copy-done, bf16[128,1280]{1,0:T(8,128)(2,1)S(1)} %copy-done.1, ...), custom_call_target="tpu_custom_call" | custom-call | flops 503316480 | bytes 4194304 | tf_op jit(solution)/shard_map/key_grads/pallas_call | solution.py:166
Async XLA Ops:
  0.6 6.1 %copy-start.4 = (bf16[128,1280]{1,0:T(8,128)(2,1)S(1)}, bf16[128,1280]{1,0:T(8,128)(2,1)}, u32[]{:S(2)}) copy-start(bf16[128,1280]{1,0:T(8,128)(2,1)} %refs_0_.1) | copy-start | bytes 983044
  0.6 19.7 %collective-permute-start = (bf16[128,1280]{1,0:T(8,128)(2,1)}, bf16[128,1280]{1,0:T(8,128)(2,1)S(1)}, u32[]{:S(2)}, u32[]{:S(2)}) collective-permute-start(bf16[128,1280]{1,0:T(8,128)(2,1)} %refs_0_.1), channel_id=1, source_target_pairs={{0,8},{8,24},{24,16},{16,0},{1,9},{9,25},{25,17},{17,1},{2,10},{10... | collective-permute-start | bytes 983048 | tf_op jit(solution)/shard_map/ppermute | solution.py:317
  0.7 48.1 %copy-start = (bf16[128,1280]{1,0:T(8,128)(2,1)S(1)}, bf16[128,1280]{1,0:T(8,128)(2,1)}, u32[]{:S(2)}) copy-start(bf16[128,1280]{1,0:T(8,128)(2,1)} %q_ref.3) | copy-start | bytes 983044
  0.7 48.1 %copy-start.1 = (bf16[128,1280]{1,0:T(8,128)(2,1)S(1)}, bf16[128,1280]{1,0:T(8,128)(2,1)}, u32[]{:S(2)}) copy-start(bf16[128,1280]{1,0:T(8,128)(2,1)} %g_ref.3) | copy-start | bytes 983044
  0.8 48.1 %copy-start.2 = (bf16[128,1280]{1,0:T(8,128)(2,1)S(1)}, bf16[128,1280]{1,0:T(8,128)(2,1)}, u32[]{:S(2)}) copy-start(bf16[128,1280]{1,0:T(8,128)(2,1)} %k_ref.3) | copy-start | bytes 983044
  0.8 48.0 %copy-start.3 = (bf16[128,1280]{1,0:T(8,128)(2,1)S(1)}, bf16[128,1280]{1,0:T(8,128)(2,1)}, u32[]{:S(2)}) copy-start(bf16[128,1280]{1,0:T(8,128)(2,1)} %v_ref.3) | copy-start | bytes 983044
  2.2 15.9 %collective-permute-start.2 = (bf16[160,640]{1,0:T(8,128)(2,1)S(1)}, bf16[160,640]{1,0:T(8,128)(2,1)S(1)}, u32[]{:S(2)}, u32[]{:S(2)}) collective-permute-start(bf16[160,640]{1,0:T(8,128)(2,1)S(1)} %get-tuple-element.55), channel_id=1, source_target_pairs={{0,16},{8,24},{16,0},{24,8},{1,17},{9,25},{17,1},{25,9},{2,18},{10... | collective-permute-start | bytes 614408 | tf_op jit(solution)/shard_map/ppermute | solution.py:25
  4.1 16.2 %collective-permute-start.1 = (bf16[160,640]{1,0:T(8,128)(2,1)S(1)}, bf16[160,640]{1,0:T(8,128)(2,1)S(1)}, u32[]{:S(2)}, u32[]{:S(2)}) collective-permute-start(bf16[160,640]{1,0:T(8,128)(2,1)S(1)} %get-tuple-element.56), channel_id=1, source_target_pairs={{0,8},{8,0},{16,24},{24,16},{1,9},{9,1},{17,25},{25,17},{2,10},{10... | collective-permute-start | bytes 614408 | tf_op jit(solution)/shard_map/ppermute | solution.py:25
  6.7 23.4 %collective-permute-start.3 = (bf16[160,640]{1,0:T(8,128)(2,1)S(1)}, bf16[160,640]{1,0:T(8,128)(2,1)S(1)}, u32[]{:S(2)}, u32[]{:S(2)}) collective-permute-start(bf16[160,640]{1,0:T(8,128)(2,1)S(1)} %get-tuple-element.57), channel_id=1, source_target_pairs={{0,24},{8,16},{16,8},{24,0},{1,25},{9,17},{17,9},{25,1},{2,26},{10... | collective-permute-start | bytes 614408 | tf_op jit(solution)/shard_map/ppermute | solution.py:25
  6.7 23.6 %collective-permute-start.5 = (bf16[128,1280]{1,0:T(8,128)(2,1)S(1)}, bf16[128,1280]{1,0:T(8,128)(2,1)S(1)}, u32[]{:S(2)}, u32[]{:S(2)}) collective-permute-start(bf16[128,1280]{1,0:T(8,128)(2,1)S(1)} %copy-done.4), channel_id=1, source_target_pairs={{0,1},{1,0},{2,3},{3,2},{4,5},{5,4},{6,7},{7,6},{8,9},{9,8},{10,11... | collective-permute-start | bytes 983048 | tf_op jit(solution)/shard_map/ppermute | solution.py:25
  20.3 9.9 %collective-permute-start.6 = (bf16[128,1280]{1,0:T(8,128)(2,1)S(1)}, bf16[128,1280]{1,0:T(8,128)(2,1)S(1)}, u32[]{:S(2)}, u32[]{:S(2)}) collective-permute-start(bf16[128,1280]{1,0:T(8,128)(2,1)S(1)} %collective-permute-done.refs_1_), channel_id=1, source_target_pairs={{0,1},{1,0},{2,3},{3,2},{4,5},{5,4},{6,7},{7,6},{8,9},{9,8},{10,11... | collective-permute-start | bytes 983048 | tf_op jit(solution)/shard_map/ppermute | solution.py:25
  21.9 11.9 %collective-permute-start.4 = (bf16[128,1280]{1,0:T(8,128)(2,1)S(1)}, bf16[128,1280]{1,0:T(8,128)(2,1)S(1)}, u32[]{:S(2)}, u32[]{:S(2)}) collective-permute-start(bf16[128,1280]{1,0:T(8,128)(2,1)S(1)} %collective-permute-done.refs_1_), channel_id=1, source_target_pairs={{0,8},{8,24},{24,16},{16,0},{1,9},{9,25},{25,17},{17,1},{2,10},{10... | collective-permute-start | bytes 983048 | tf_op jit(solution)/shard_map/ppermute | solution.py:317
  33.8 14.5 %collective-permute-start.9 = (bf16[4,160,640]{2,1,0:T(8,128)(2,1)S(1)}, bf16[4,160,640]{2,1,0:T(8,128)(2,1)S(1)}, u32[]{:S(2)}, u32[]{:S(2)}) collective-permute-start(bf16[4,160,640]{2,1,0:T(8,128)(2,1)S(1)} %pad_maximum_fusion.refs_8_), channel_id=1, source_target_pairs={{0,2},{2,0},{4,6},{6,4},{1,3},{3,1},{5,7},{7,5},{8,10},{10,8},{12,... | collective-permute-start | bytes 2457608 | tf_op jit(solution)/shard_map/ppermute | solution.py:25
  33.8 20.7 %collective-permute-start.10 = (bf16[4,160,640]{2,1,0:T(8,128)(2,1)S(1)}, bf16[4,160,640]{2,1,0:T(8,128)(2,1)S(1)}, u32[]{:S(2)}, u32[]{:S(2)}) collective-permute-start(bf16[4,160,640]{2,1,0:T(8,128)(2,1)S(1)} %pad_maximum_fusion.refs_8_), channel_id=1, source_target_pairs={{0,4},{2,6},{4,0},{6,2},{1,5},{3,7},{5,1},{7,3},{8,12},{10,14},{12... | collective-permute-start | bytes 2457608 | tf_op jit(solution)/shard_map/ppermute | solution.py:25
  35.3 9.8 %collective-permute-start.8 = (bf16[128,1280]{1,0:T(8,128)(2,1)S(1)}, bf16[128,1280]{1,0:T(8,128)(2,1)S(1)}, u32[]{:S(2)}, u32[]{:S(2)}) collective-permute-start(bf16[128,1280]{1,0:T(8,128)(2,1)S(1)} %collective-permute-done.4.refs_2_), channel_id=1, source_target_pairs={{0,1},{1,0},{2,3},{3,2},{4,5},{5,4},{6,7},{7,6},{8,9},{9,8},{10,11... | collective-permute-start | bytes 983048 | tf_op jit(solution)/shard_map/ppermute | solution.py:25
  35.8 12.4 %collective-permute-start.7 = (bf16[128,1280]{1,0:T(8,128)(2,1)S(1)}, bf16[128,1280]{1,0:T(8,128)(2,1)S(1)}, u32[]{:S(2)}, u32[]{:S(2)}) collective-permute-start(bf16[128,1280]{1,0:T(8,128)(2,1)S(1)} %collective-permute-done.4.refs_2_), channel_id=1, source_target_pairs={{0,8},{8,24},{24,16},{16,0},{1,9},{9,25},{25,17},{17,1},{2,10},{10... | collective-permute-start | bytes 983048 | tf_op jit(solution)/shard_map/ppermute | solution.py:317
  48.3 9.0 %collective-permute-start.11 = (bf16[128,1280]{1,0:T(8,128)(2,1)S(1)}, bf16[128,1280]{1,0:T(8,128)(2,1)S(1)}, u32[]{:S(2)}, u32[]{:S(2)}) collective-permute-start(bf16[128,1280]{1,0:T(8,128)(2,1)S(1)} %collective-permute-done.7.refs_3_), channel_id=1, source_target_pairs={{0,1},{1,0},{2,3},{3,2},{4,5},{5,4},{6,7},{7,6},{8,9},{9,8},{10,11... | collective-permute-start | bytes 983048 | tf_op jit(solution)/shard_map/ppermute | solution.py:25
  48.8 15.0 %copy-start.6 = (s32[2048]{0:T(1024)S(1)}, s32[2048]{0:T(1024)}, u32[]{:S(2)}) copy-start(s32[2048]{0:T(1024)} %param.15) | copy-start | bytes 24580
  48.8 15.0 %copy-start.7 = (s32[2048]{0:T(1024)S(1)}, s32[2048]{0:T(1024)}, u32[]{:S(2)}) copy-start(s32[2048]{0:T(1024)} %param.14) | copy-start | bytes 24580
  57.3 6.7 %collective-permute-start.12 = (bf16[4,160,640]{2,1,0:T(8,128)(2,1)S(1)}, bf16[4,160,640]{2,1,0:T(8,128)(2,1)S(1)}, u32[]{:S(2)}, u32[]{:S(2)}) collective-permute-start(bf16[4,160,640]{2,1,0:T(8,128)(2,1)S(1)} %collective-permute-done.10.refs_10_), channel_id=1, source_target_pairs={{0,2},{2,0},{4,6},{6,4},{1,3},{3,1},{5,7},{7,5},{8,10},{10,8},{12,... | collective-permute-start | bytes 2457608 | tf_op jit(solution)/shard_map/ppermute | solution.py:25
  57.3 13.0 %collective-permute-start.13 = (bf16[2,128,1280]{2,1,0:T(8,128)(2,1)S(1)}, bf16[2,128,1280]{2,1,0:T(8,128)(2,1)}, u32[]{:S(2)}, u32[]{:S(2)}) collective-permute-start(bf16[2,128,1280]{2,1,0:T(8,128)(2,1)S(1)} %get-tuple-element.42), channel_id=1, source_target_pairs={{0,2},{2,4},{4,6},{6,8},{8,10},{10,12},{12,14},{14,16},{16,18},{18... | collective-permute-start | bytes 1966088 | tf_op jit(solution)/shard_map/ppermute | solution.py:21
  59.7 12.2 %collective-permute-start.14 = (bf16[2,128,1280]{2,1,0:T(8,128)(2,1)S(1)}, bf16[2,128,1280]{2,1,0:T(8,128)(2,1)S(1)}, u32[]{:S(2)}, u32[]{:S(2)}) collective-permute-start(bf16[2,128,1280]{2,1,0:T(8,128)(2,1)S(1)} %get-tuple-element.43), channel_id=1, source_target_pairs={{2,0},{4,2},{6,4},{8,6},{10,8},{12,10},{14,12},{16,14},{18,16},{20... | collective-permute-start | bytes 1966088 | tf_op jit(solution)/shard_map/ppermute | solution.py:21
  64.1 4.6 %copy-start.5 = (bf16[128,640]{1,0:T(8,128)(2,1)}, bf16[128,640]{1,0:T(8,128)(2,1)S(1)}, u32[]{:S(2)}) copy-start(bf16[128,640]{1,0:T(8,128)(2,1)S(1)} %get-tuple-element.46.bias_ref) | copy-start | bytes 491524
  71.9 48.6 %all-to-all-start = ((bf16[16,4,16,640]{3,2,1,0:T(8,128)(2,1)}), bf16[16,4,16,640]{3,2,1,0:T(8,128)(2,1)S(1)}, u32[]{:S(2)}, u32[]{:S(2)}) async-start(bf16[16,4,16,640]{3,2,1,0:T(8,128)(2,1)} %project.1), calls=%async_computation | async-start | bytes 2621440 | tf_op jit(solution)/shard_map/all_to_all | solution.py:388
  82.5 38.0 %collective-permute-start.15 = (bf16[2,128,1280]{2,1,0:T(8,128)(2,1)}, bf16[2,128,1280]{2,1,0:T(8,128)(2,1)}, u32[]{:S(2)}, u32[]{:S(2)}) collective-permute-start(bf16[2,128,1280]{2,1,0:T(8,128)(2,1)} %collective-permute-done.13.kv1_ref), channel_id=1, source_target_pairs={{0,2},{2,4},{4,6},{6,8},{8,10},{10,12},{12,14},{14,16},{16,18},{18... | collective-permute-start | bytes 1966088 | tf_op jit(solution)/shard_map/ppermute | solution.py:21
  84.6 44.8 %collective-permute-start.16 = (bf16[2,128,1280]{2,1,0:T(8,128)(2,1)S(1)}, bf16[2,128,1280]{2,1,0:T(8,128)(2,1)}, u32[]{:S(2)}, u32[]{:S(2)}) collective-permute-start(bf16[2,128,1280]{2,1,0:T(8,128)(2,1)S(1)} %collective-permute-done.14.qg1_ref), channel_id=1, source_target_pairs={{2,0},{4,2},{6,4},{8,6},{10,8},{12,10},{14,12},{16,14},{18,16},{20... | collective-permute-start | bytes 1966088 | tf_op jit(solution)/shard_map/ppermute | solution.py:21
  125.6 5.6 %collective-permute-start.18 = (f32[2,16,128]{2,1,0:T(8,128)S(1)}, f32[2,16,128]{2,1,0:T(8,128)S(1)}, u32[]{:S(2)}, u32[]{:S(2)}) collective-permute-start(f32[2,16,128]{2,1,0:T(8,128)S(1)} %get-tuple-element.50.st0_ref), channel_id=1, source_target_pairs={{4,0},{6,2},{8,4},{10,6},{12,8},{14,10},{16,12},{18,14},{20,16},{2... | collective-permute-start | bytes 49160 | tf_op jit(solution)/shard_map/ppermute | solution.py:21
  127.5 3.7 %collective-permute-start.17 = (f32[2,16,128]{2,1,0:T(8,128)S(1)}, f32[2,16,128]{2,1,0:T(8,128)S(1)}, u32[]{:S(2)}, u32[]{:S(2)}) collective-permute-start(f32[2,16,128]{2,1,0:T(8,128)S(1)} %get-tuple-element.50.st0_ref), channel_id=1, source_target_pairs={{2,0},{4,2},{6,4},{8,6},{10,8},{12,10},{14,12},{16,14},{18,16},{20... | collective-permute-start | bytes 49160 | tf_op jit(solution)/shard_map/ppermute | solution.py:21

commit v6 on v5

--- a/solution.py
+++ b/solution.py
@@ -329,20 +329,19 @@
         row1, other0 = ring_step(cache), swapped(cache, "head", 1)
         row1, arrived[1], arrived[2] = lax.optimization_barrier((row1, arrived[1], arrived[2]))
         row2, other1 = ring_step(row1), swapped(row1, "head", 1)
-        own, row2, other0, other1 = lax.optimization_barrier(
-            (jnp.stack(arrived, 0), row2, other0, other1)
-        )
+        own, other0, other1 = lax.optimization_barrier((jnp.stack(arrived, 0), other0, other1))
         across, beside = swapped(own, "p", 2), swapped(own, "p", 1)
-        row3, other2 = ring_step(row2), swapped(row2, "head", 1)
-        row3, other2, beside = lax.optimization_barrier((row3, other2, beside))
+        row2, beside, stream = lax.optimization_barrier((row2, beside, stream))
+        row3, other2, near = ring_step(row2), swapped(row2, "head", 1), shifted(stream, 1)
+        row3, other2 = lax.optimization_barrier((row3, other2))
         other3 = swapped(row3, "head", 1)
-        across, other3, stream, back = lax.optimization_barrier((across, other3, stream, back))
+        across, other3, near = lax.optimization_barrier((across, other3, near))
         pieces = [own, beside, across, swapped(across, "p", 1)]
-        near, back1 = shifted(stream, 1), shifted(back, -1)
+        far = shifted(near, 1)
         rows = [cache, row1, row2, row3, other0, other1, other2, other3]
         slots = project(place, rows, pieces, devices, capacity)
-        slots, near, back1 = lax.optimization_barrier((slots, near, back1))
-        return slots, near, shifted(near, 1), back1
+        slots, far, back = lax.optimization_barrier((slots, far, back))
+        return slots, near, far, shifted(back, -1)
     near, back1 = shifted(stream, 1), shifted(back, -1)
     far = shifted(near, 1)
     targets = [column_block(w_kv, jnp.int32(i)) for i in range(n_z)]
@@ -388,8 +387,9 @@
     memory = lax.all_to_all(slots, SEQ, split_axis=0, concat_axis=0, tiled=True)
     memory = memory.reshape(n_z, slot_count, slots.shape[-1])
 
+    output, grad_q, stats = attend(queries, grad_out, keys, values, kv1, kv2, memory, bias)
+    qg1, stats = lax.optimization_barrier((qg1, stats))
     qg2 = shifted(qg1, -1)
-    output, grad_q, stats = attend(queries, grad_out, keys, values, kv1, kv2, memory, bias)
     all_stats = [stats, shifted(stats, -1), shifted(stats, -2)]
     grad_k, grad_v = key_grads(
         keys, values, queries, grad_out, qg1, qg2, all_stats, back_bias

time: 137 us -> 136 us (level)
  starting transfers between devices: 43.3 us -> 34.2 us
  waiting for transfers between devices: 75.5 us -> 82.5 us
    all_to_all x1, waiting for transfers between devices: 0.01 us -> 27.7 us  [body(): memory = lax.all_to_all(slots, SEQ, split_axis=0, concat_axis=0, tiled=True)]
    ppermute x6, waiting for transfers between devices: 36.6 us -> 10.4 us  [shifted(): return lax.ppermute(value, SEQ, pairs)]
    ppermute x3, waiting for transfers between devices: 6.69 us -> 17.9 us  [ring_step(): lax.ppermute(value, 'z', [(b, a) for a, b in pairs] if back else pairs)]
    ppermute x10, waiting for transfers between devices: 32.2 us -> 26.5 us  [swapped(): lax.ppermute(value, axis, [(i, i ^ mask) for i in range(lax.axis_size(axi...]
    all_to_all x1, starting transfers between devices: 10.6 us -> 5.36 us  [body(): memory = lax.all_to_all(slots, SEQ, split_axis=0, concat_axis=0, tiled=True)]
    ppermute x3, starting transfers between devices: 5.83 us -> 0.82 us  [ring_step(): lax.ppermute(value, 'z', [(b, a) for a, b in pairs] if back else pairs)]
    ppermute x10, starting transfers between devices: 10.1 us -> 12.2 us  [swapped(): lax.ppermute(value, axis, [(i, i ^ mask) for i in range(lax.axis_size(axi...]
  transfers between devices with their start and end apart: 20 -> 20, of which waited for: 12 -> 12; matrix products, arithmetic and copies ran while one was open for 1% -> 2% of each run, Pallas kernels for 7% -> 7%
where the time goes in v6:
time: 136 us; the launch traced here: 133 us
  waiting for transfers between devices  82.5 us (61%)
  starting transfers between devices  34.2 us (25%)
  Pallas kernels  12.5 us (9%)
  local copies, waits for them, and re-layouts  2.25 us (2%)
    all_to_all x1, waiting for transfers between devices, body(): memory = lax.all_to_all(slots, SEQ, split_axis=0, concat_axis=0, tiled=True)  27.7 us
    ppermute x10, waiting for transfers between devices, swapped(): lax.ppermute(value, axis, [(i, i ^ mask) for i in range(lax.axis_size(axi...  26.5 us
    ppermute x3, waiting for transfers between devices, ring_step(): lax.ppermute(value, 'z', [(b, a) for a, b in pairs] if back else pairs)  17.9 us
    ppermute x6, starting transfers between devices, shifted(): return lax.ppermute(value, SEQ, pairs)  15.9 us
    ppermute x10, starting transfers between devices, swapped(): lax.ppermute(value, axis, [(i, i ^ mask) for i in range(lax.axis_size(axi...  12.2 us
    ppermute x6, waiting for transfers between devices, shifted(): return lax.ppermute(value, SEQ, pairs)  10.4 us
    all_to_all x1, starting transfers between devices, body(): memory = lax.all_to_all(slots, SEQ, split_axis=0, concat_axis=0, tiled=True)  5.36 us
    pallas_call x1, Pallas kernels, attend(): pl.pallas_call(attend_kernel, grid=(steps,), in_specs=[flat, flat, flat,...  4.99 us
  transfers between devices with their start and end apart: 20, of which 12 were waited for; matrix products, arithmetic and copies ran while one was open for 2% of the time, Pallas kernels for 7%

profile of v6, /device:TPU:16, one launch (start us, length us, event | category | flops | bytes accessed | tf_op | source)
XLA Modules:
  0.0 133.4 jit_solution(13472495085269419020)
XLA Ops:
  0.6 0.0 copy-start.4
  0.6 0.1 collective-permute-start
  0.7 0.0 copy-start.2
  0.7 0.0 copy-start.3
  0.8 1.4 %constant_dynamic-slice_fusion = (bf16[1,160,640]{2,1,0:T(8,128)(2,1)S(1)}, bf16[160,640]{1,0:T(8,128)(2,1)S(1)}, bf16[160,640]{1,0:T(8,128)(2,1)S(1)}, bf16[160,640]{1,0:T(8,128)(2,1)S(1)}) fusion(bf16[2,160,1280]{2,1,0:T(8,128)(2,1)} %param.13, s32[]{:T(128)S(6)} %select_n.24, s32[]{:T(128)S(6)} %select_n.25, s32[]{:T(128)S(6)} %select_n.26, ...), kind=kLoop, calls=%fused_computation.6 | loop fusion | bytes 1638432 | tf_op jit(solution)/shard_map/dynamic_slice | solution.py:312
  2.1 2.0 %collective-permute-start.1 = (bf16[160,640]{1,0:T(8,128)(2,1)S(1)}, bf16[160,640]{1,0:T(8,128)(2,1)S(1)}, u32[]{:S(2)}, u32[]{:S(2)}) collective-permute-start(bf16[160,640]{1,0:T(8,128)(2,1)S(1)} %get-tuple-element.59), channel_id=1, source_target_pairs={{0,8},{8,0},{16,24},{24,16},{1,9},{9,1},{17,25},{25,17},{2,10},{10... | collective-permute-start | bytes 614408 | tf_op jit(solution)/shard_map/ppermute | solution.py:25
  4.2 2.5 %collective-permute-start.2 = (bf16[160,640]{1,0:T(8,128)(2,1)S(1)}, bf16[160,640]{1,0:T(8,128)(2,1)S(1)}, u32[]{:S(2)}, u32[]{:S(2)}) collective-permute-start(bf16[160,640]{1,0:T(8,128)(2,1)S(1)} %get-tuple-element.61), channel_id=1, source_target_pairs={{0,16},{8,24},{16,0},{24,8},{1,17},{9,25},{17,1},{25,9},{2,18},{10... | collective-permute-start | bytes 614408 | tf_op jit(solution)/shard_map/ppermute | solution.py:25
  6.6 0.0 collective-permute-start.3
  6.6 0.0 copy-done.4
  6.6 1.5 %collective-permute-start.4 = (bf16[128,1280]{1,0:T(8,128)(2,1)S(1)}, bf16[128,1280]{1,0:T(8,128)(2,1)S(1)}, u32[]{:S(2)}, u32[]{:S(2)}) collective-permute-start(bf16[128,1280]{1,0:T(8,128)(2,1)S(1)} %copy-done.4), channel_id=1, source_target_pairs={{0,1},{1,0},{2,3},{3,2},{4,5},{5,4},{6,7},{7,6},{8,9},{9,8},{10,11... | collective-permute-start | bytes 983048 | tf_op jit(solution)/shard_map/ppermute | solution.py:25
  8.2 10.8 %collective-permute-done.1 = bf16[160,640]{1,0:T(8,128)(2,1)S(1)} collective-permute-done((bf16[160,640]{1,0:T(8,128)(2,1)S(1)}, bf16[160,640]{1,0:T(8,128)(2,1)S(1)}, u32[]{:S(2)}, u32[]{:S(2)}) %collective-permute-start.1) | collective-permute-done | bytes 204832 | tf_op jit(solution)/shard_map/ppermute | solution.py:25
  18.9 1.3 collective-permute-done.2
  20.3 0.0 collective-permute-done.refs_1_
  20.3 1.5 %collective-permute-start.5 = (bf16[128,1280]{1,0:T(8,128)(2,1)S(1)}, bf16[128,1280]{1,0:T(8,128)(2,1)S(1)}, u32[]{:S(2)}, u32[]{:S(2)}) collective-permute-start(bf16[128,1280]{1,0:T(8,128)(2,1)S(1)} %collective-permute-done.refs_1_), channel_id=1, source_target_pairs={{0,1},{1,0},{2,3},{3,2},{4,5},{5,4},{6,7},{7,6},{8,9},{9,8},{10,11... | collective-permute-start | bytes 983048 | tf_op jit(solution)/shard_map/ppermute | solution.py:25
  21.8 7.2 %collective-permute-done.3 = bf16[160,640]{1,0:T(8,128)(2,1)S(1)} collective-permute-done((bf16[160,640]{1,0:T(8,128)(2,1)S(1)}, bf16[160,640]{1,0:T(8,128)(2,1)S(1)}, u32[]{:S(2)}, u32[]{:S(2)}) %collective-permute-start.3) | collective-permute-done | bytes 204832 | tf_op jit(solution)/shard_map/ppermute | solution.py:25
  29.0 0.0 copy-start.6
  29.0 0.0 copy-start.7
  29.0 0.0 copy-start
  29.0 0.1 pad_maximum_fusion.refs_8_
  29.1 0.0 collective-permute-done.4.refs_4_
  29.1 0.0 collective-permute-done.5.refs_5_
  29.1 0.1 collective-permute-start.8
  29.2 0.8 collective-permute-start.7
  30.0 1.5 %collective-permute-start.6 = (bf16[4,160,640]{2,1,0:T(8,128)(2,1)S(1)}, bf16[4,160,640]{2,1,0:T(8,128)(2,1)S(1)}, u32[]{:S(2)}, u32[]{:S(2)}) collective-permute-start(bf16[4,160,640]{2,1,0:T(8,128)(2,1)S(1)} %pad_maximum_fusion.refs_8_), channel_id=1, source_target_pairs={{0,4},{2,6},{4,0},{6,2},{1,5},{3,7},{5,1},{7,3},{8,12},{10,14},{12... | collective-permute-start | bytes 2457608 | tf_op jit(solution)/shard_map/ppermute | solution.py:25
  31.5 0.0 copy-done.2
  31.5 0.0 copy-done.3
  31.5 0.1 pad_maximum_fusion.1
  31.6 11.1 %collective-permute-done.7.refs_2_ = bf16[128,1280]{1,0:T(8,128)(2,1)S(1)} collective-permute-done((bf16[128,1280]{1,0:T(8,128)(2,1)S(1)}, bf16[128,1280]{1,0:T(8,128)(2,1)S(1)}, u32[]{:S(2)}, u32[]{:S(2)}) %collective-permute-start.7) | collective-permute-done | bytes 327712 | tf_op jit(solution)/shard_map/ppermute | solution.py:317
  42.7 0.0 collective-permute-done.8.refs_9_
  42.7 0.0 collective-permute-start.9
  42.7 1.5 %collective-permute-start.10 = (bf16[128,1280]{1,0:T(8,128)(2,1)S(1)}, bf16[128,1280]{1,0:T(8,128)(2,1)S(1)}, u32[]{:S(2)}, u32[]{:S(2)}) collective-permute-start(bf16[128,1280]{1,0:T(8,128)(2,1)S(1)} %collective-permute-done.7.refs_2_), channel_id=1, source_target_pairs={{0,1},{1,0},{2,3},{3,2},{4,5},{5,4},{6,7},{7,6},{8,9},{9,8},{10,11... | collective-permute-start | bytes 983048 | tf_op jit(solution)/shard_map/ppermute | solution.py:25
  44.2 1.9 %collective-permute-start.12 = (bf16[2,128,1280]{2,1,0:T(8,128)(2,1)S(1)}, bf16[2,128,1280]{2,1,0:T(8,128)(2,1)S(1)}, u32[]{:S(2)}, u32[]{:S(2)}) collective-permute-start(bf16[2,128,1280]{2,1,0:T(8,128)(2,1)S(1)} %pad_maximum_fusion.1), channel_id=1, source_target_pairs={{0,2},{2,4},{4,6},{6,8},{8,10},{10,12},{12,14},{14,16},{16,18},{18... | collective-permute-start | bytes 1966088 | tf_op jit(solution)/shard_map/ppermute | solution.py:21
  46.1 6.8 %collective-permute-done.9.refs_3_ = bf16[128,1280]{1,0:T(8,128)(2,1)S(1)} collective-permute-done((bf16[128,1280]{1,0:T(8,128)(2,1)S(1)}, bf16[128,1280]{1,0:T(8,128)(2,1)S(1)}, u32[]{:S(2)}, u32[]{:S(2)}) %collective-permute-start.9) | collective-permute-done | bytes 327712 | tf_op jit(solution)/shard_map/ppermute | solution.py:317
  52.9 0.0 collective-permute-done.10.refs_6_
  52.9 1.5 %collective-permute-start.11 = (bf16[128,1280]{1,0:T(8,128)(2,1)S(1)}, bf16[128,1280]{1,0:T(8,128)(2,1)S(1)}, u32[]{:S(2)}, u32[]{:S(2)}) collective-permute-start(bf16[128,1280]{1,0:T(8,128)(2,1)S(1)} %collective-permute-done.9.refs_3_), channel_id=1, source_target_pairs={{0,1},{1,0},{2,3},{3,2},{4,5},{5,4},{6,7},{7,6},{8,9},{9,8},{10,11... | collective-permute-start | bytes 983048 | tf_op jit(solution)/shard_map/ppermute | solution.py:25
  54.4 0.0 collective-permute-done.6.refs_10_
  54.4 7.2 %collective-permute-done.11.refs_7_ = bf16[128,1280]{1,0:T(8,128)(2,1)S(1)} collective-permute-done((bf16[128,1280]{1,0:T(8,128)(2,1)S(1)}, bf16[128,1280]{1,0:T(8,128)(2,1)S(1)}, u32[]{:S(2)}, u32[]{:S(2)}) %collective-permute-start.11) | collective-permute-done | bytes 327712 | tf_op jit(solution)/shard_map/ppermute | solution.py:25
  61.7 0.4 collective-permute-done.12.kv1_ref
  62.1 0.0 collective-permute-start.13
  62.1 2.4 %collective-permute-start.14 = (bf16[2,128,1280]{2,1,0:T(8,128)(2,1)S(1)}, bf16[2,128,1280]{2,1,0:T(8,128)(2,1)S(1)}, u32[]{:S(2)}, u32[]{:S(2)}) collective-permute-start(bf16[2,128,1280]{2,1,0:T(8,128)(2,1)S(1)} %collective-permute-done.12.kv1_ref), channel_id=1, source_target_pairs={{0,2},{2,4},{4,6},{6,8},{8,10},{10,12},{12,14},{14,16},{16,18},{18... | collective-permute-start | bytes 1966088 | tf_op jit(solution)/shard_map/ppermute | solution.py:21
  64.5 0.0 copy-done.6
  64.5 0.0 copy-done.7
  64.5 0.3 prepare.1
  64.8 0.0 copy-done
  64.8 0.0 copy-done.1
  64.8 0.9 pad_maximum_fusion.2
  65.7 0.0 collective-permute-done.13.refs_11_
  65.7 4.6 %project.1 = bf16[16,4,16,640]{3,2,1,0:T(8,128)(2,1)} custom-call(s32[4,1,128]{2,1,0:T(1,128)S(1)} %get-tuple-element.39.place_ref, bf16[128,1280]{1,0:T(8,128)(2,1)S(1)} %copy-done.4, bf16[128,1280]{1,0:T(8,128)(2,1)S(1)} %collective-permute-done.refs_1_, bf16[128,1280]{1,0:T(8,128)(2,1)S(1)} %collective-permute-done.7.refs_2_, ...), custom_call_target="tpu_custom_call" | custom-call | flops 1677721600 | bytes 8388608 | tf_op jit(solution)/shard_map/project/pallas_call | solution.py:225
  70.3 0.0 copy-done.8
  70.3 0.0 copy-done.5
  70.3 4.9 %collective-permute-done.14.kv2_ref = bf16[2,128,1280]{2,1,0:T(8,128)(2,1)S(1)} collective-permute-done((bf16[2,128,1280]{2,1,0:T(8,128)(2,1)S(1)}, bf16[2,128,1280]{2,1,0:T(8,128)(2,1)S(1)}, u32[]{:S(2)}, u32[]{:S(2)}) %collective-permute-start.14) | collective-permute-done | bytes 655392 | tf_op jit(solution)/shard_map/ppermute | solution.py:21
  75.2 0.8 copy-done.9
  76.0 5.4 %all-to-all-start = ((bf16[16,4,16,640]{3,2,1,0:T(8,128)(2,1)}), bf16[16,4,16,640]{3,2,1,0:T(8,128)(2,1)S(1)}, u32[]{:S(2)}, u32[]{:S(2)}) async-start(bf16[16,4,16,640]{3,2,1,0:T(8,128)(2,1)} %project.1), calls=%async_computation | async-start | bytes 2621440 | tf_op jit(solution)/shard_map/all_to_all | solution.py:387
  81.4 3.1 %collective-permute-start.15 = (bf16[2,128,1280]{2,1,0:T(8,128)(2,1)}, bf16[2,128,1280]{2,1,0:T(8,128)(2,1)S(1)}, u32[]{:S(2)}, u32[]{:S(2)}) collective-permute-start(bf16[2,128,1280]{2,1,0:T(8,128)(2,1)} %pad_maximum_fusion.2), channel_id=1, source_target_pairs={{2,0},{4,2},{6,4},{8,6},{10,8},{12,10},{14,12},{16,14},{18,16},{20... | collective-permute-start | bytes 1966088 | tf_op jit(solution)/shard_map/ppermute | solution.py:21
  84.5 27.7 %all-to-all-done = bf16[16,4,16,640]{3,2,1,0:T(8,128)(2,1)S(1)} async-done(((bf16[16,4,16,640]{3,2,1,0:T(8,128)(2,1)}), bf16[16,4,16,640]{3,2,1,0:T(8,128)(2,1)S(1)}, u32[]{:S(2)}, u32[]{:S(2)}) %all-to-all-start) | async-done | bytes 1310752 | tf_op jit(solution)/shard_map/all_to_all | solution.py:387
  112.2 5.0 %attend.1 = (bf16[128,1280]{1,0:T(8,128)(2,1)}, bf16[128,1280]{1,0:T(8,128)(2,1)}, f32[2,16,128]{2,1,0:T(8,128)S(1)}) custom-call(bf16[128,1280]{1,0:T(8,128)(2,1)S(1)} %copy-done, bf16[128,1280]{1,0:T(8,128)(2,1)S(1)} %copy-done.1, bf16[128,1280]{1,0:T(8,128)(2,1)S(1)} %copy-done.2, bf16[128,1280]{1,0:T(8,128)(2,1)S(1)} %copy-done.3, ...), custom_call_target="tpu_custom_call" | custom-call | flops 838860800 | bytes 6291456 | tf_op jit(solution)/shard_map/attend/pallas_call | solution.py:103
  117.2 0.3 collective-permute-done.15.qg1_ref
  117.5 4.6 %collective-permute-start.16 = (bf16[2,128,1280]{2,1,0:T(8,128)(2,1)S(1)}, bf16[2,128,1280]{2,1,0:T(8,128)(2,1)S(1)}, u32[]{:S(2)}, u32[]{:S(2)}) collective-permute-start(bf16[2,128,1280]{2,1,0:T(8,128)(2,1)S(1)} %collective-permute-done.15.qg1_ref), channel_id=1, source_target_pairs={{2,0},{4,2},{6,4},{8,6},{10,8},{12,10},{14,12},{16,14},{18,16},{20... | collective-permute-start | bytes 1966088 | tf_op jit(solution)/shard_map/ppermute | solution.py:21
  122.1 1.9 %collective-permute-start.17 = (f32[2,16,128]{2,1,0:T(8,128)S(1)}, f32[2,16,128]{2,1,0:T(8,128)S(1)}, u32[]{:S(2)}, u32[]{:S(2)}) collective-permute-start(f32[2,16,128]{2,1,0:T(8,128)S(1)} %get-tuple-element.54.st0_ref), channel_id=1, source_target_pairs={{2,0},{4,2},{6,4},{8,6},{10,8},{12,10},{14,12},{16,14},{18,16},{20... | collective-permute-start | bytes 49160 | tf_op jit(solution)/shard_map/ppermute | solution.py:21
  124.0 1.9 %collective-permute-start.18 = (f32[2,16,128]{2,1,0:T(8,128)S(1)}, f32[2,16,128]{2,1,0:T(8,128)S(1)}, u32[]{:S(2)}, u32[]{:S(2)}) collective-permute-start(f32[2,16,128]{2,1,0:T(8,128)S(1)} %get-tuple-element.54.st0_ref), channel_id=1, source_target_pairs={{4,0},{6,2},{8,4},{10,6},{12,8},{14,10},{16,12},{18,14},{20,16},{2... | collective-permute-start | bytes 49160 | tf_op jit(solution)/shard_map/ppermute | solution.py:21
  125.9 4.6 %collective-permute-done.17.st1_ref = f32[2,16,128]{2,1,0:T(8,128)S(1)} collective-permute-done((f32[2,16,128]{2,1,0:T(8,128)S(1)}, f32[2,16,128]{2,1,0:T(8,128)S(1)}, u32[]{:S(2)}, u32[]{:S(2)}) %collective-permute-start.17) | collective-permute-done | bytes 16416 | tf_op jit(solution)/shard_map/ppermute | solution.py:21
  130.5 0.2 collective-permute-done.18.st2_ref
  130.7 0.0 collective-permute-done.16.qg2_ref
  130.7 2.7 %key_grads.1 = (bf16[128,1280]{1,0:T(8,128)(2,1)}, bf16[128,1280]{1,0:T(8,128)(2,1)}) custom-call(bf16[128,1280]{1,0:T(8,128)(2,1)S(1)} %copy-done.2, bf16[128,1280]{1,0:T(8,128)(2,1)S(1)} %copy-done.3, bf16[128,1280]{1,0:T(8,128)(2,1)S(1)} %copy-done, bf16[128,1280]{1,0:T(8,128)(2,1)S(1)} %copy-done.1, ...), custom_call_target="tpu_custom_call" | custom-call | flops 503316480 | bytes 4194304 | tf_op jit(solution)/shard_map/key_grads/pallas_call | solution.py:166
  (4 shorter events, 0.0 us)
Async XLA Ops:
  0.6 6.0 %copy-start.4 = (bf16[128,1280]{1,0:T(8,128)(2,1)S(1)}, bf16[128,1280]{1,0:T(8,128)(2,1)}, u32[]{:S(2)}) copy-start(bf16[128,1280]{1,0:T(8,128)(2,1)} %refs_0_.1) | copy-start | bytes 983044
  0.6 19.6 %collective-permute-start = (bf16[128,1280]{1,0:T(8,128)(2,1)}, bf16[128,1280]{1,0:T(8,128)(2,1)S(1)}, u32[]{:S(2)}, u32[]{:S(2)}) collective-permute-start(bf16[128,1280]{1,0:T(8,128)(2,1)} %refs_0_.1), channel_id=1, source_target_pairs={{0,8},{8,24},{24,16},{16,0},{1,9},{9,25},{25,17},{17,1},{2,10},{10... | collective-permute-start | bytes 983048 | tf_op jit(solution)/shard_map/ppermute | solution.py:317
  0.7 30.8 %copy-start.2 = (bf16[128,1280]{1,0:T(8,128)(2,1)S(1)}, bf16[128,1280]{1,0:T(8,128)(2,1)}, u32[]{:S(2)}) copy-start(bf16[128,1280]{1,0:T(8,128)(2,1)} %k_ref.3) | copy-start | bytes 983044
  0.7 30.8 %copy-start.3 = (bf16[128,1280]{1,0:T(8,128)(2,1)S(1)}, bf16[128,1280]{1,0:T(8,128)(2,1)}, u32[]{:S(2)}) copy-start(bf16[128,1280]{1,0:T(8,128)(2,1)} %v_ref.3) | copy-start | bytes 983044
  2.1 16.8 %collective-permute-start.1 = (bf16[160,640]{1,0:T(8,128)(2,1)S(1)}, bf16[160,640]{1,0:T(8,128)(2,1)S(1)}, u32[]{:S(2)}, u32[]{:S(2)}) collective-permute-start(bf16[160,640]{1,0:T(8,128)(2,1)S(1)} %get-tuple-element.59), channel_id=1, source_target_pairs={{0,8},{8,0},{16,24},{24,16},{1,9},{9,1},{17,25},{25,17},{2,10},{10... | collective-permute-start | bytes 614408 | tf_op jit(solution)/shard_map/ppermute | solution.py:25
  4.2 16.1 %collective-permute-start.2 = (bf16[160,640]{1,0:T(8,128)(2,1)S(1)}, bf16[160,640]{1,0:T(8,128)(2,1)S(1)}, u32[]{:S(2)}, u32[]{:S(2)}) collective-permute-start(bf16[160,640]{1,0:T(8,128)(2,1)S(1)} %get-tuple-element.61), channel_id=1, source_target_pairs={{0,16},{8,24},{16,0},{24,8},{1,17},{9,25},{17,1},{25,9},{2,18},{10... | collective-permute-start | bytes 614408 | tf_op jit(solution)/shard_map/ppermute | solution.py:25
  6.6 22.3 %collective-permute-start.3 = (bf16[160,640]{1,0:T(8,128)(2,1)S(1)}, bf16[160,640]{1,0:T(8,128)(2,1)S(1)}, u32[]{:S(2)}, u32[]{:S(2)}) collective-permute-start(bf16[160,640]{1,0:T(8,128)(2,1)S(1)} %get-tuple-element.60), channel_id=1, source_target_pairs={{0,24},{8,16},{16,8},{24,0},{1,25},{9,17},{17,9},{25,1},{2,26},{10... | collective-permute-start | bytes 614408 | tf_op jit(solution)/shard_map/ppermute | solution.py:25
  6.6 22.5 %collective-permute-start.4 = (bf16[128,1280]{1,0:T(8,128)(2,1)S(1)}, bf16[128,1280]{1,0:T(8,128)(2,1)S(1)}, u32[]{:S(2)}, u32[]{:S(2)}) collective-permute-start(bf16[128,1280]{1,0:T(8,128)(2,1)S(1)} %copy-done.4), channel_id=1, source_target_pairs={{0,1},{1,0},{2,3},{3,2},{4,5},{5,4},{6,7},{7,6},{8,9},{9,8},{10,11... | collective-permute-start | bytes 983048 | tf_op jit(solution)/shard_map/ppermute | solution.py:25
  20.3 8.9 %collective-permute-start.5 = (bf16[128,1280]{1,0:T(8,128)(2,1)S(1)}, bf16[128,1280]{1,0:T(8,128)(2,1)S(1)}, u32[]{:S(2)}, u32[]{:S(2)}) collective-permute-start(bf16[128,1280]{1,0:T(8,128)(2,1)S(1)} %collective-permute-done.refs_1_), channel_id=1, source_target_pairs={{0,1},{1,0},{2,3},{3,2},{4,5},{5,4},{6,7},{7,6},{8,9},{9,8},{10,11... | collective-permute-start | bytes 983048 | tf_op jit(solution)/shard_map/ppermute | solution.py:25
  29.0 35.5 %copy-start.6 = (s32[2048]{0:T(1024)S(1)}, s32[2048]{0:T(1024)}, u32[]{:S(2)}) copy-start(s32[2048]{0:T(1024)} %param.15) | copy-start | bytes 24580
  29.0 35.5 %copy-start.7 = (s32[2048]{0:T(1024)S(1)}, s32[2048]{0:T(1024)}, u32[]{:S(2)}) copy-start(s32[2048]{0:T(1024)} %param.14) | copy-start | bytes 24580
  29.0 35.8 %copy-start = (bf16[128,1280]{1,0:T(8,128)(2,1)S(1)}, bf16[128,1280]{1,0:T(8,128)(2,1)}, u32[]{:S(2)}) copy-start(bf16[128,1280]{1,0:T(8,128)(2,1)} %q_ref.3) | copy-start | bytes 983044
  29.0 35.8 %copy-start.1 = (bf16[128,1280]{1,0:T(8,128)(2,1)S(1)}, bf16[128,1280]{1,0:T(8,128)(2,1)}, u32[]{:S(2)}) copy-start(bf16[128,1280]{1,0:T(8,128)(2,1)} %g_ref.3) | copy-start | bytes 983044
  29.1 13.5 %collective-permute-start.8 = (bf16[4,160,640]{2,1,0:T(8,128)(2,1)S(1)}, bf16[4,160,640]{2,1,0:T(8,128)(2,1)S(1)}, u32[]{:S(2)}, u32[]{:S(2)}) collective-permute-start(bf16[4,160,640]{2,1,0:T(8,128)(2,1)S(1)} %pad_maximum_fusion.refs_8_), channel_id=1, source_target_pairs={{0,2},{2,0},{4,6},{6,4},{1,3},{3,1},{5,7},{7,5},{8,10},{10,8},{12,... | collective-permute-start | bytes 2457608 | tf_op jit(solution)/shard_map/ppermute | solution.py:25
  29.2 13.4 %collective-permute-start.7 = (bf16[128,1280]{1,0:T(8,128)(2,1)S(1)}, bf16[128,1280]{1,0:T(8,128)(2,1)S(1)}, u32[]{:S(2)}, u32[]{:S(2)}) collective-permute-start(bf16[128,1280]{1,0:T(8,128)(2,1)S(1)} %collective-permute-done.refs_1_), channel_id=1, source_target_pairs={{0,8},{8,24},{24,16},{16,0},{1,9},{9,25},{25,17},{17,1},{2,10},{10... | collective-permute-start | bytes 983048 | tf_op jit(solution)/shard_map/ppermute | solution.py:317
  30.0 24.5 %collective-permute-start.6 = (bf16[4,160,640]{2,1,0:T(8,128)(2,1)S(1)}, bf16[4,160,640]{2,1,0:T(8,128)(2,1)S(1)}, u32[]{:S(2)}, u32[]{:S(2)}) collective-permute-start(bf16[4,160,640]{2,1,0:T(8,128)(2,1)S(1)} %pad_maximum_fusion.refs_8_), channel_id=1, source_target_pairs={{0,4},{2,6},{4,0},{6,2},{1,5},{3,7},{5,1},{7,3},{8,12},{10,14},{12... | collective-permute-start | bytes 2457608 | tf_op jit(solution)/shard_map/ppermute | solution.py:25
  42.7 10.2 %collective-permute-start.9 = (bf16[128,1280]{1,0:T(8,128)(2,1)S(1)}, bf16[128,1280]{1,0:T(8,128)(2,1)S(1)}, u32[]{:S(2)}, u32[]{:S(2)}) collective-permute-start(bf16[128,1280]{1,0:T(8,128)(2,1)S(1)} %collective-permute-done.7.refs_2_), channel_id=1, source_target_pairs={{0,8},{8,24},{24,16},{16,0},{1,9},{9,25},{25,17},{17,1},{2,10},{10... | collective-permute-start | bytes 983048 | tf_op jit(solution)/shard_map/ppermute | solution.py:317
  42.7 10.2 %collective-permute-start.10 = (bf16[128,1280]{1,0:T(8,128)(2,1)S(1)}, bf16[128,1280]{1,0:T(8,128)(2,1)S(1)}, u32[]{:S(2)}, u32[]{:S(2)}) collective-permute-start(bf16[128,1280]{1,0:T(8,128)(2,1)S(1)} %collective-permute-done.7.refs_2_), channel_id=1, source_target_pairs={{0,1},{1,0},{2,3},{3,2},{4,5},{5,4},{6,7},{7,6},{8,9},{9,8},{10,11... | collective-permute-start | bytes 983048 | tf_op jit(solution)/shard_map/ppermute | solution.py:25
  44.2 17.9 %collective-permute-start.12 = (bf16[2,128,1280]{2,1,0:T(8,128)(2,1)S(1)}, bf16[2,128,1280]{2,1,0:T(8,128)(2,1)S(1)}, u32[]{:S(2)}, u32[]{:S(2)}) collective-permute-start(bf16[2,128,1280]{2,1,0:T(8,128)(2,1)S(1)} %pad_maximum_fusion.1), channel_id=1, source_target_pairs={{0,2},{2,4},{4,6},{6,8},{8,10},{10,12},{12,14},{14,16},{16,18},{18... | collective-permute-start | bytes 1966088 | tf_op jit(solution)/shard_map/ppermute | solution.py:21
  52.9 8.8 %collective-permute-start.11 = (bf16[128,1280]{1,0:T(8,128)(2,1)S(1)}, bf16[128,1280]{1,0:T(8,128)(2,1)S(1)}, u32[]{:S(2)}, u32[]{:S(2)}) collective-permute-start(bf16[128,1280]{1,0:T(8,128)(2,1)S(1)} %collective-permute-done.9.refs_3_), channel_id=1, source_target_pairs={{0,1},{1,0},{2,3},{3,2},{4,5},{5,4},{6,7},{7,6},{8,9},{9,8},{10,11... | collective-permute-start | bytes 983048 | tf_op jit(solution)/shard_map/ppermute | solution.py:25
  62.1 8.2 %copy-start.8 = (bf16[2,128,1280]{2,1,0:T(8,128)(2,1)}, bf16[2,128,1280]{2,1,0:T(8,128)(2,1)S(1)}, u32[]{:S(2)}) copy-start(bf16[2,128,1280]{2,1,0:T(8,128)(2,1)S(1)} %collective-permute-done.12.kv1_ref) | copy-start | bytes 1966084
  62.1 3.6 %collective-permute-start.13 = (bf16[4,160,640]{2,1,0:T(8,128)(2,1)S(1)}, bf16[4,160,640]{2,1,0:T(8,128)(2,1)S(1)}, u32[]{:S(2)}, u32[]{:S(2)}) collective-permute-start(bf16[4,160,640]{2,1,0:T(8,128)(2,1)S(1)} %collective-permute-done.6.refs_10_), channel_id=1, source_target_pairs={{0,2},{2,0},{4,6},{6,4},{1,3},{3,1},{5,7},{7,5},{8,10},{10,8},{12,... | collective-permute-start | bytes 2457608 | tf_op jit(solution)/shard_map/ppermute | solution.py:25
  62.1 13.1 %collective-permute-start.14 = (bf16[2,128,1280]{2,1,0:T(8,128)(2,1)S(1)}, bf16[2,128,1280]{2,1,0:T(8,128)(2,1)S(1)}, u32[]{:S(2)}, u32[]{:S(2)}) collective-permute-start(bf16[2,128,1280]{2,1,0:T(8,128)(2,1)S(1)} %collective-permute-done.12.kv1_ref), channel_id=1, source_target_pairs={{0,2},{2,4},{4,6},{6,8},{8,10},{10,12},{12,14},{14,16},{16,18},{18... | collective-permute-start | bytes 1966088 | tf_op jit(solution)/shard_map/ppermute | solution.py:21
  64.8 5.5 %copy-start.5 = (bf16[128,640]{1,0:T(8,128)(2,1)}, bf16[128,640]{1,0:T(8,128)(2,1)S(1)}, u32[]{:S(2)}) copy-start(bf16[128,640]{1,0:T(8,128)(2,1)S(1)} %get-tuple-element.48.bias_ref) | copy-start | bytes 491524
  75.2 0.8 copy-start.9
  76.0 36.2 %all-to-all-start = ((bf16[16,4,16,640]{3,2,1,0:T(8,128)(2,1)}), bf16[16,4,16,640]{3,2,1,0:T(8,128)(2,1)S(1)}, u32[]{:S(2)}, u32[]{:S(2)}) async-start(bf16[16,4,16,640]{3,2,1,0:T(8,128)(2,1)} %project.1), calls=%async_computation | async-start | bytes 2621440 | tf_op jit(solution)/shard_map/all_to_all | solution.py:387
  81.4 36.1 %collective-permute-start.15 = (bf16[2,128,1280]{2,1,0:T(8,128)(2,1)}, bf16[2,128,1280]{2,1,0:T(8,128)(2,1)S(1)}, u32[]{:S(2)}, u32[]{:S(2)}) collective-permute-start(bf16[2,128,1280]{2,1,0:T(8,128)(2,1)} %pad_maximum_fusion.2), channel_id=1, source_target_pairs={{2,0},{4,2},{6,4},{8,6},{10,8},{12,10},{14,12},{16,14},{18,16},{20... | collective-permute-start | bytes 1966088 | tf_op jit(solution)/shard_map/ppermute | solution.py:21
  117.5 13.2 %collective-permute-start.16 = (bf16[2,128,1280]{2,1,0:T(8,128)(2,1)S(1)}, bf16[2,128,1280]{2,1,0:T(8,128)(2,1)S(1)}, u32[]{:S(2)}, u32[]{:S(2)}) collective-permute-start(bf16[2,128,1280]{2,1,0:T(8,128)(2,1)S(1)} %collective-permute-done.15.qg1_ref), channel_id=1, source_target_pairs={{2,0},{4,2},{6,4},{8,6},{10,8},{12,10},{14,12},{16,14},{18,16},{20... | collective-permute-start | bytes 1966088 | tf_op jit(solution)/shard_map/ppermute | solution.py:21
  122.1 8.4 %collective-permute-start.17 = (f32[2,16,128]{2,1,0:T(8,128)S(1)}, f32[2,16,128]{2,1,0:T(8,128)S(1)}, u32[]{:S(2)}, u32[]{:S(2)}) collective-permute-start(f32[2,16,128]{2,1,0:T(8,128)S(1)} %get-tuple-element.54.st0_ref), channel_id=1, source_target_pairs={{2,0},{4,2},{6,4},{8,6},{10,8},{12,10},{14,12},{16,14},{18,16},{20... | collective-permute-start | bytes 49160 | tf_op jit(solution)/shard_map/ppermute | solution.py:21
  124.0 6.7 %collective-permute-start.18 = (f32[2,16,128]{2,1,0:T(8,128)S(1)}, f32[2,16,128]{2,1,0:T(8,128)S(1)}, u32[]{:S(2)}, u32[]{:S(2)}) collective-permute-start(f32[2,16,128]{2,1,0:T(8,128)S(1)} %get-tuple-element.54.st0_ref), channel_id=1, source_target_pairs={{4,0},{6,2},{8,4},{10,6},{12,8},{14,10},{16,12},{18,14},{20,16},{2... | collective-permute-start | bytes 49160 | tf_op jit(solution)/shard_map/ppermute | solution.py:21

commit v7 on v3

--- a/solution.py
+++ b/solution.py
@@ -330,21 +330,20 @@
         )
         row1, other0 = ring_step(cache), swapped(cache, "head", 1)
         own, row1, other0, cache = lax.optimization_barrier((own, row1, other0, cache))
-        across = swapped(own, "p", 2)
-        beside = swapped(own, "p", 1)
+        across, beside = swapped(own, "p", 2), swapped(own, "p", 1)
         row2, row3, other1 = ring_step(row1), ring_step(cache, back=True), swapped(row1, "head", 1)
-        beside, stream, back = lax.optimization_barrier((beside, stream, back))
-        near, back1 = shifted(stream, 1), shifted(back, -1)
-        row2, row3, other1 = lax.optimization_barrier((row2, row3, other1))
-        other2, other3 = swapped(row2, "head", 1), swapped(row3, "head", 1)
-        across, other2, other3, near, back1 = lax.optimization_barrier(
-            (across, other2, other3, near, back1)
+        beside, stream = lax.optimization_barrier((beside, stream))
+        near = shifted(stream, 1)
+        row2, row3, other0, other1 = lax.optimization_barrier((row2, row3, other0, other1))
+        other2, other3 = swapped(row2, "head", 1), ring_step(other0, back=True)
+        across, other2, other3, near, back = lax.optimization_barrier(
+            (across, other2, other3, near, back)
         )
         pieces = [own, beside, across, swapped(across, "p", 1)]
-        far = shifted(near, 1)
+        far, back1 = shifted(near, 1), shifted(back, -1)
         rows = [cache, row1, row2, row3, other0, other1, other2, other3]
         slots = project(place, rows, pieces, devices, capacity)
-        slots, far = lax.optimization_barrier((slots, far))
+        slots, far, back1 = lax.optimization_barrier((slots, far, back1))
         return slots, near, far, back1
     near, back1 = shifted(stream, 1), shifted(back, -1)
     far = shifted(near, 1)

time: 135 us -> 136 us (level)
  waiting for transfers between devices: 72.1 us -> 76.5 us
  starting transfers between devices: 45.9 us -> 42.8 us
    ppermute x3 -> x4, waiting for transfers between devices: 6.79 us -> 19.8 us  [ring_step(): lax.ppermute(value, 'z', [(b, a) for a, b in pairs] if back else pairs)]
    ppermute x10 -> x9, waiting for transfers between devices: 28 us -> 17.9 us  [swapped(): lax.ppermute(value, axis, [(i, i ^ mask) for i in range(lax.axis_size(axi...]
    ppermute x6, starting transfers between devices: 21.5 us -> 16.5 us  [shifted(): return lax.ppermute(value, SEQ, pairs)]
    ppermute x10 -> x9, starting transfers between devices: 12.6 us -> 9.83 us  [swapped(): lax.ppermute(value, axis, [(i, i ^ mask) for i in range(lax.axis_size(axi...]
    ppermute x3 -> x4, starting transfers between devices: 4.63 us -> 7.28 us  [ring_step(): lax.ppermute(value, 'z', [(b, a) for a, b in pairs] if back else pairs)]
    all_to_all x1, starting transfers between devices: 7.14 us -> 9.22 us  [body(): memory = lax.all_to_all(slots, SEQ, split_axis=0, concat_axis=0, tiled=True)]
    ppermute x6, waiting for transfers between devices: 9.68 us -> 11.1 us  [shifted(): return lax.ppermute(value, SEQ, pairs)]
  transfers between devices with their start and end apart: 20 -> 20, of which waited for: 10 -> 14; matrix products, arithmetic and copies ran while one was open for 0% -> 0% of each run, Pallas kernels for 7% -> 7%
where the time goes in v7:
time: 136 us; the launch traced here: 135 us
  waiting for transfers between devices  76.5 us (56%)
  starting transfers between devices  42.8 us (31%)
  Pallas kernels  13.6 us (10%)
  local copies, waits for them, and re-layouts  1.42 us (1%)
    all_to_all x1, waiting for transfers between devices, body(): memory = lax.all_to_all(slots, SEQ, split_axis=0, concat_axis=0, tiled=True)  27.7 us
    ppermute x4, waiting for transfers between devices, ring_step(): lax.ppermute(value, 'z', [(b, a) for a, b in pairs] if back else pairs)  19.8 us
    ppermute x9, waiting for transfers between devices, swapped(): lax.ppermute(value, axis, [(i, i ^ mask) for i in range(lax.axis_size(axi...  17.9 us
    ppermute x6, starting transfers between devices, shifted(): return lax.ppermute(value, SEQ, pairs)  16.5 us
    ppermute x6, waiting for transfers between devices, shifted(): return lax.ppermute(value, SEQ, pairs)  11.1 us
    ppermute x9, starting transfers between devices, swapped(): lax.ppermute(value, axis, [(i, i ^ mask) for i in range(lax.axis_size(axi...  9.83 us
    all_to_all x1, starting transfers between devices, body(): memory = lax.all_to_all(slots, SEQ, split_axis=0, concat_axis=0, tiled=True)  9.22 us
    ppermute x4, starting transfers between devices, ring_step(): lax.ppermute(value, 'z', [(b, a) for a, b in pairs] if back else pairs)  7.28 us
  transfers between devices with their start and end apart: 20, of which 14 were waited for; matrix products, arithmetic and copies ran while one was open for 0% of the time, Pallas kernels for 7%

profile of v7, /device:TPU:16, one launch (start us, length us, event | category | flops | bytes accessed | tf_op | source)
XLA Modules:
  0.0 135.3 jit_solution(12357874139885501367)
XLA Ops:
  0.6 0.0 copy-start.4
  0.7 0.0 copy-start.2
  0.7 0.0 copy-start.3
  0.7 1.4 %constant_dynamic-slice_fusion = (bf16[1,160,640]{2,1,0:T(8,128)(2,1)S(1)}, bf16[160,640]{1,0:T(8,128)(2,1)S(1)}, bf16[160,640]{1,0:T(8,128)(2,1)S(1)}, bf16[160,640]{1,0:T(8,128)(2,1)S(1)}) fusion(bf16[2,160,1280]{2,1,0:T(8,128)(2,1)} %param.13, s32[]{:T(128)S(6)} %select_n.24, s32[]{:T(128)S(6)} %select_n.25, s32[]{:T(128)S(6)} %select_n.26, ...), kind=kLoop, calls=%fused_computation.6 | loop fusion | bytes 1638432 | tf_op jit(solution)/shard_map/dynamic_slice | solution.py:312
  2.1 1.6 %collective-permute-start = (bf16[160,640]{1,0:T(8,128)(2,1)S(1)}, bf16[160,640]{1,0:T(8,128)(2,1)S(1)}, u32[]{:S(2)}, u32[]{:S(2)}) collective-permute-start(bf16[160,640]{1,0:T(8,128)(2,1)S(1)} %get-tuple-element.57), channel_id=1, source_target_pairs={{0,8},{8,0},{16,24},{24,16},{1,9},{9,1},{17,25},{25,17},{2,10},{10... | collective-permute-start | bytes 614408 | tf_op jit(solution)/shard_map/ppermute | solution.py:25
  3.7 0.3 collective-permute-start.1
  4.1 1.6 %collective-permute-start.2 = (bf16[160,640]{1,0:T(8,128)(2,1)S(1)}, bf16[160,640]{1,0:T(8,128)(2,1)S(1)}, u32[]{:S(2)}, u32[]{:S(2)}) collective-permute-start(bf16[160,640]{1,0:T(8,128)(2,1)S(1)} %get-tuple-element.58), channel_id=1, source_target_pairs={{0,24},{8,16},{16,8},{24,0},{1,25},{9,17},{17,9},{25,1},{2,26},{10... | collective-permute-start | bytes 614408 | tf_op jit(solution)/shard_map/ppermute | solution.py:25
  5.6 0.0 copy-done.4
  5.6 1.0 collective-permute-start.3
  6.6 1.7 %collective-permute-start.4 = (bf16[128,1280]{1,0:T(8,128)(2,1)S(1)}, bf16[128,1280]{1,0:T(8,128)(2,1)S(1)}, u32[]{:S(2)}, u32[]{:S(2)}) collective-permute-start(bf16[128,1280]{1,0:T(8,128)(2,1)S(1)} %copy-done.4), channel_id=1, source_target_pairs={{0,1},{1,0},{2,3},{3,2},{4,5},{5,4},{6,7},{7,6},{8,9},{9,8},{10,11... | collective-permute-start | bytes 983048 | tf_op jit(solution)/shard_map/ppermute | solution.py:25
  8.4 2.7 %collective-permute-done = bf16[160,640]{1,0:T(8,128)(2,1)S(1)} collective-permute-done((bf16[160,640]{1,0:T(8,128)(2,1)S(1)}, bf16[160,640]{1,0:T(8,128)(2,1)S(1)}, u32[]{:S(2)}, u32[]{:S(2)}) %collective-permute-start) | collective-permute-done | bytes 204832 | tf_op jit(solution)/shard_map/ppermute | solution.py:25
  11.1 7.1 %collective-permute-done.1 = bf16[160,640]{1,0:T(8,128)(2,1)S(1)} collective-permute-done((bf16[160,640]{1,0:T(8,128)(2,1)S(1)}, bf16[160,640]{1,0:T(8,128)(2,1)S(1)}, u32[]{:S(2)}, u32[]{:S(2)}) %collective-permute-start.1) | collective-permute-done | bytes 204832 | tf_op jit(solution)/shard_map/ppermute | solution.py:25
  18.2 6.6 %collective-permute-done.2 = bf16[160,640]{1,0:T(8,128)(2,1)S(1)} collective-permute-done((bf16[160,640]{1,0:T(8,128)(2,1)S(1)}, bf16[160,640]{1,0:T(8,128)(2,1)S(1)}, u32[]{:S(2)}, u32[]{:S(2)}) %collective-permute-start.2) | collective-permute-done | bytes 204832 | tf_op jit(solution)/shard_map/ppermute | solution.py:25
  24.8 0.0 copy-start
  24.8 0.0 copy-start.1
  24.8 0.1 pad_maximum_fusion.refs_8_
  24.9 3.4 %collective-permute-done.3.refs_1_ = bf16[128,1280]{1,0:T(8,128)(2,1)S(1)} collective-permute-done((bf16[128,1280]{1,0:T(8,128)(2,1)S(1)}, bf16[128,1280]{1,0:T(8,128)(2,1)S(1)}, u32[]{:S(2)}, u32[]{:S(2)}) %collective-permute-start.3) | collective-permute-done | bytes 327712 | tf_op jit(solution)/shard_map/ppermute | solution.py:317
  28.3 0.0 collective-permute-done.4.refs_4_
  28.3 0.0 collective-permute-start.11
  28.4 3.4 %collective-permute-start.6 = (bf16[128,1280]{1,0:T(8,128)(2,1)S(1)}, bf16[128,1280]{1,0:T(8,128)(2,1)S(1)}, u32[]{:S(2)}, u32[]{:S(2)}) collective-permute-start(bf16[128,1280]{1,0:T(8,128)(2,1)S(1)} %collective-permute-done.3.refs_1_), channel_id=1, source_target_pairs={{0,8},{8,24},{24,16},{16,0},{1,9},{9,25},{25,17},{17,1},{2,10},{10... | collective-permute-start | bytes 983048 | tf_op jit(solution)/shard_map/ppermute | solution.py:317
  31.7 1.5 %collective-permute-start.8 = (bf16[128,1280]{1,0:T(8,128)(2,1)S(1)}, bf16[128,1280]{1,0:T(8,128)(2,1)S(1)}, u32[]{:S(2)}, u32[]{:S(2)}) collective-permute-start(bf16[128,1280]{1,0:T(8,128)(2,1)S(1)} %collective-permute-done.3.refs_1_), channel_id=1, source_target_pairs={{0,1},{1,0},{2,3},{3,2},{4,5},{5,4},{6,7},{7,6},{8,9},{9,8},{10,11... | collective-permute-start | bytes 983048 | tf_op jit(solution)/shard_map/ppermute | solution.py:25
  33.3 1.5 %collective-permute-start.5 = (bf16[4,160,640]{2,1,0:T(8,128)(2,1)S(1)}, bf16[4,160,640]{2,1,0:T(8,128)(2,1)S(1)}, u32[]{:S(2)}, u32[]{:S(2)}) collective-permute-start(bf16[4,160,640]{2,1,0:T(8,128)(2,1)S(1)} %pad_maximum_fusion.refs_8_), channel_id=1, source_target_pairs={{0,4},{2,6},{4,0},{6,2},{1,5},{3,7},{5,1},{7,3},{8,12},{10,14},{12... | collective-permute-start | bytes 2457608 | tf_op jit(solution)/shard_map/ppermute | solution.py:25
  34.7 0.2 collective-permute-start.7
  34.9 0.0 copy-done.2
  34.9 0.0 copy-done.3
  34.9 0.0 copy-start.6
  34.9 0.1 pad_maximum_fusion.1
  35.0 0.0 collective-permute-done.11.refs_9_
  35.0 1.9 %collective-permute-start.12 = (bf16[2,128,1280]{2,1,0:T(8,128)(2,1)S(1)}, bf16[2,128,1280]{2,1,0:T(8,128)(2,1)S(1)}, u32[]{:S(2)}, u32[]{:S(2)}) collective-permute-start(bf16[2,128,1280]{2,1,0:T(8,128)(2,1)S(1)} %pad_maximum_fusion.1), channel_id=1, source_target_pairs={{0,2},{2,4},{4,6},{6,8},{8,10},{10,12},{12,14},{14,16},{16,18},{18... | collective-permute-start | bytes 1966088 | tf_op jit(solution)/shard_map/ppermute | solution.py:21
  37.0 3.5 %collective-permute-done.6.refs_2_ = bf16[128,1280]{1,0:T(8,128)(2,1)S(1)} collective-permute-done((bf16[128,1280]{1,0:T(8,128)(2,1)S(1)}, bf16[128,1280]{1,0:T(8,128)(2,1)S(1)}, u32[]{:S(2)}, u32[]{:S(2)}) %collective-permute-start.6) | collective-permute-done | bytes 327712 | tf_op jit(solution)/shard_map/ppermute | solution.py:317
  40.4 6.8 %collective-permute-done.7.refs_3_ = bf16[128,1280]{1,0:T(8,128)(2,1)S(1)} collective-permute-done((bf16[128,1280]{1,0:T(8,128)(2,1)S(1)}, bf16[128,1280]{1,0:T(8,128)(2,1)S(1)}, u32[]{:S(2)}, u32[]{:S(2)}) %collective-permute-start.7) | collective-permute-done | bytes 327712 | tf_op jit(solution)/shard_map/ppermute | solution.py:317
  47.2 0.0 collective-permute-done.8.refs_5_
  47.2 2.7 %collective-permute-start.10 = (bf16[128,1280]{1,0:T(8,128)(2,1)S(1)}, bf16[128,1280]{1,0:T(8,128)(2,1)S(1)}, u32[]{:S(2)}, u32[]{:S(2)}) collective-permute-start(bf16[128,1280]{1,0:T(8,128)(2,1)S(1)} %collective-permute-done.4.refs_4_), channel_id=1, source_target_pairs={{8,0},{24,8},{16,24},{0,16},{9,1},{25,9},{17,25},{1,17},{10,2},{26... | collective-permute-start | bytes 983048 | tf_op jit(solution)/shard_map/ppermute | solution.py:317
  49.9 1.5 %collective-permute-start.9 = (bf16[128,1280]{1,0:T(8,128)(2,1)S(1)}, bf16[128,1280]{1,0:T(8,128)(2,1)S(1)}, u32[]{:S(2)}, u32[]{:S(2)}) collective-permute-start(bf16[128,1280]{1,0:T(8,128)(2,1)S(1)} %collective-permute-done.6.refs_2_), channel_id=1, source_target_pairs={{0,1},{1,0},{2,3},{3,2},{4,5},{5,4},{6,7},{7,6},{8,9},{9,8},{10,11... | collective-permute-start | bytes 983048 | tf_op jit(solution)/shard_map/ppermute | solution.py:25
  51.5 0.0 copy-done
  51.5 0.0 copy-done.1
  51.5 0.1 pad_maximum_fusion.2
  51.5 6.1 %collective-permute-done.10.refs_7_ = bf16[128,1280]{1,0:T(8,128)(2,1)S(1)} collective-permute-done((bf16[128,1280]{1,0:T(8,128)(2,1)S(1)}, bf16[128,1280]{1,0:T(8,128)(2,1)S(1)}, u32[]{:S(2)}, u32[]{:S(2)}) %collective-permute-start.10) | collective-permute-done | bytes 327712 | tf_op jit(solution)/shard_map/ppermute | solution.py:317
  57.6 1.4 %collective-permute-done.9.refs_6_ = bf16[128,1280]{1,0:T(8,128)(2,1)S(1)} collective-permute-done((bf16[128,1280]{1,0:T(8,128)(2,1)S(1)}, bf16[128,1280]{1,0:T(8,128)(2,1)S(1)}, u32[]{:S(2)}, u32[]{:S(2)}) %collective-permute-start.9) | collective-permute-done | bytes 327712 | tf_op jit(solution)/shard_map/ppermute | solution.py:25
  59.0 0.2 collective-permute-done.5.refs_10_
  59.2 4.3 %collective-permute-done.12.kv1_ref = bf16[2,128,1280]{2,1,0:T(8,128)(2,1)S(1)} collective-permute-done((bf16[2,128,1280]{2,1,0:T(8,128)(2,1)S(1)}, bf16[2,128,1280]{2,1,0:T(8,128)(2,1)S(1)}, u32[]{:S(2)}, u32[]{:S(2)}) %collective-permute-start.12) | collective-permute-done | bytes 655392 | tf_op jit(solution)/shard_map/ppermute | solution.py:21
  63.5 0.0 collective-permute-start.13
  63.5 2.4 %collective-permute-start.14 = (bf16[2,128,1280]{2,1,0:T(8,128)(2,1)S(1)}, bf16[2,128,1280]{2,1,0:T(8,128)(2,1)S(1)}, u32[]{:S(2)}, u32[]{:S(2)}) collective-permute-start(bf16[2,128,1280]{2,1,0:T(8,128)(2,1)S(1)} %collective-permute-done.12.kv1_ref), channel_id=1, source_target_pairs={{0,2},{2,4},{4,6},{6,8},{8,10},{10,12},{12,14},{14,16},{16,18},{18... | collective-permute-start | bytes 1966088 | tf_op jit(solution)/shard_map/ppermute | solution.py:21
  65.9 4.0 %collective-permute-start.15 = (bf16[2,128,1280]{2,1,0:T(8,128)(2,1)S(1)}, bf16[2,128,1280]{2,1,0:T(8,128)(2,1)S(1)}, u32[]{:S(2)}, u32[]{:S(2)}) collective-permute-start(bf16[2,128,1280]{2,1,0:T(8,128)(2,1)S(1)} %pad_maximum_fusion.2), channel_id=1, source_target_pairs={{2,0},{4,2},{6,4},{8,6},{10,8},{12,10},{14,12},{16,14},{18,16},{20... | collective-permute-start | bytes 1966088 | tf_op jit(solution)/shard_map/ppermute | solution.py:21
  70.0 0.0 copy-done.6
  70.0 0.0 copy-done.7
  70.0 0.3 prepare.1
  70.2 0.0 collective-permute-done.13.refs_11_
  70.2 4.6 %project.1 = bf16[16,4,16,640]{3,2,1,0:T(8,128)(2,1)} custom-call(s32[4,1,128]{2,1,0:T(1,128)S(1)} %get-tuple-element.38.place_ref, bf16[128,1280]{1,0:T(8,128)(2,1)S(1)} %copy-done.4, bf16[128,1280]{1,0:T(8,128)(2,1)S(1)} %collective-permute-done.3.refs_1_, bf16[128,1280]{1,0:T(8,128)(2,1)S(1)} %collective-permute-done.6.refs_2_, ...), custom_call_target="tpu_custom_call" | custom-call | flops 1677721600 | bytes 8388608 | tf_op jit(solution)/shard_map/project/pallas_call | solution.py:225
  74.8 0.0 copy-done.8
  74.8 0.0 copy-done.5
  74.8 1.5 %collective-permute-done.14.kv2_ref = bf16[2,128,1280]{2,1,0:T(8,128)(2,1)S(1)} collective-permute-done((bf16[2,128,1280]{2,1,0:T(8,128)(2,1)S(1)}, bf16[2,128,1280]{2,1,0:T(8,128)(2,1)S(1)}, u32[]{:S(2)}, u32[]{:S(2)}) %collective-permute-start.14) | collective-permute-done | bytes 655392 | tf_op jit(solution)/shard_map/ppermute | solution.py:21
  76.4 1.7 %collective-permute-done.15.qg1_ref = bf16[2,128,1280]{2,1,0:T(8,128)(2,1)S(1)} collective-permute-done((bf16[2,128,1280]{2,1,0:T(8,128)(2,1)S(1)}, bf16[2,128,1280]{2,1,0:T(8,128)(2,1)S(1)}, u32[]{:S(2)}, u32[]{:S(2)}) %collective-permute-start.15) | collective-permute-done | bytes 655392 | tf_op jit(solution)/shard_map/ppermute | solution.py:21
  78.1 0.0 copy-done.9
  78.1 9.2 %all-to-all-start = ((bf16[16,4,16,640]{3,2,1,0:T(8,128)(2,1)}), bf16[16,4,16,640]{3,2,1,0:T(8,128)(2,1)S(1)}, u32[]{:S(2)}, u32[]{:S(2)}) async-start(bf16[16,4,16,640]{3,2,1,0:T(8,128)(2,1)} %project.1), calls=%async_computation | async-start | bytes 2621440 | tf_op jit(solution)/shard_map/all_to_all | solution.py:390
  87.3 3.1 %collective-permute-start.16 = (bf16[2,128,1280]{2,1,0:T(8,128)(2,1)S(1)}, bf16[2,128,1280]{2,1,0:T(8,128)(2,1)}, u32[]{:S(2)}, u32[]{:S(2)}) collective-permute-start(bf16[2,128,1280]{2,1,0:T(8,128)(2,1)S(1)} %collective-permute-done.15.qg1_ref), channel_id=1, source_target_pairs={{2,0},{4,2},{6,4},{8,6},{10,8},{12,10},{14,12},{16,14},{18,16},{20... | collective-permute-start | bytes 1966088 | tf_op jit(solution)/shard_map/ppermute | solution.py:21
  90.4 27.7 %all-to-all-done = bf16[16,4,16,640]{3,2,1,0:T(8,128)(2,1)S(1)} async-done(((bf16[16,4,16,640]{3,2,1,0:T(8,128)(2,1)}), bf16[16,4,16,640]{3,2,1,0:T(8,128)(2,1)S(1)}, u32[]{:S(2)}, u32[]{:S(2)}) %all-to-all-start) | async-done | bytes 1310752 | tf_op jit(solution)/shard_map/all_to_all | solution.py:390
  118.1 5.0 %attend.1 = (bf16[128,1280]{1,0:T(8,128)(2,1)}, bf16[128,1280]{1,0:T(8,128)(2,1)}, f32[2,16,128]{2,1,0:T(8,128)S(1)}) custom-call(bf16[128,1280]{1,0:T(8,128)(2,1)S(1)} %copy-done, bf16[128,1280]{1,0:T(8,128)(2,1)S(1)} %copy-done.1, bf16[128,1280]{1,0:T(8,128)(2,1)S(1)} %copy-done.2, bf16[128,1280]{1,0:T(8,128)(2,1)S(1)} %copy-done.3, ...), custom_call_target="tpu_custom_call" | custom-call | flops 838860800 | bytes 6291456 | tf_op jit(solution)/shard_map/attend/pallas_call | solution.py:103
  123.1 2.9 %collective-permute-start.17 = (f32[2,16,128]{2,1,0:T(8,128)S(1)}, f32[2,16,128]{2,1,0:T(8,128)S(1)}, u32[]{:S(2)}, u32[]{:S(2)}) collective-permute-start(f32[2,16,128]{2,1,0:T(8,128)S(1)} %get-tuple-element.52.st0_ref), channel_id=1, source_target_pairs={{2,0},{4,2},{6,4},{8,6},{10,8},{12,10},{14,12},{16,14},{18,16},{20... | collective-permute-start | bytes 49160 | tf_op jit(solution)/shard_map/ppermute | solution.py:21
  126.0 2.1 %collective-permute-start.18 = (f32[2,16,128]{2,1,0:T(8,128)S(1)}, f32[2,16,128]{2,1,0:T(8,128)S(1)}, u32[]{:S(2)}, u32[]{:S(2)}) collective-permute-start(f32[2,16,128]{2,1,0:T(8,128)S(1)} %get-tuple-element.52.st0_ref), channel_id=1, source_target_pairs={{4,0},{6,2},{8,4},{10,6},{12,8},{14,10},{16,12},{18,14},{20,16},{2... | collective-permute-start | bytes 49160 | tf_op jit(solution)/shard_map/ppermute | solution.py:21
  128.1 0.0 collective-permute-done.16.qg2_ref
  128.1 0.0 collective-permute-done.17.st1_ref
  128.1 3.5 %collective-permute-done.18.st2_ref = f32[2,16,128]{2,1,0:T(8,128)S(1)} collective-permute-done((f32[2,16,128]{2,1,0:T(8,128)S(1)}, f32[2,16,128]{2,1,0:T(8,128)S(1)}, u32[]{:S(2)}, u32[]{:S(2)}) %collective-permute-start.18) | collective-permute-done | bytes 16416 | tf_op jit(solution)/shard_map/ppermute | solution.py:21
  131.6 3.7 %key_grads.1 = (bf16[128,1280]{1,0:T(8,128)(2,1)}, bf16[128,1280]{1,0:T(8,128)(2,1)}) custom-call(bf16[128,1280]{1,0:T(8,128)(2,1)S(1)} %copy-done.2, bf16[128,1280]{1,0:T(8,128)(2,1)S(1)} %copy-done.3, bf16[128,1280]{1,0:T(8,128)(2,1)S(1)} %copy-done, bf16[128,1280]{1,0:T(8,128)(2,1)S(1)} %copy-done.1, ...), custom_call_target="tpu_custom_call" | custom-call | flops 503316480 | bytes 4194304 | tf_op jit(solution)/shard_map/key_grads/pallas_call | solution.py:166
  (4 shorter events, 0.0 us)
Async XLA Ops:
  0.6 5.0 %copy-start.4 = (bf16[128,1280]{1,0:T(8,128)(2,1)S(1)}, bf16[128,1280]{1,0:T(8,128)(2,1)}, u32[]{:S(2)}) copy-start(bf16[128,1280]{1,0:T(8,128)(2,1)} %refs_0_) | copy-start | bytes 983044
  0.7 34.3 %copy-start.2 = (bf16[128,1280]{1,0:T(8,128)(2,1)S(1)}, bf16[128,1280]{1,0:T(8,128)(2,1)}, u32[]{:S(2)}) copy-start(bf16[128,1280]{1,0:T(8,128)(2,1)} %k_ref.3) | copy-start | bytes 983044
  0.7 34.3 %copy-start.3 = (bf16[128,1280]{1,0:T(8,128)(2,1)S(1)}, bf16[128,1280]{1,0:T(8,128)(2,1)}, u32[]{:S(2)}) copy-start(bf16[128,1280]{1,0:T(8,128)(2,1)} %v_ref.3) | copy-start | bytes 983044
  2.1 9.0 %collective-permute-start = (bf16[160,640]{1,0:T(8,128)(2,1)S(1)}, bf16[160,640]{1,0:T(8,128)(2,1)S(1)}, u32[]{:S(2)}, u32[]{:S(2)}) collective-permute-start(bf16[160,640]{1,0:T(8,128)(2,1)S(1)} %get-tuple-element.57), channel_id=1, source_target_pairs={{0,8},{8,0},{16,24},{24,16},{1,9},{9,1},{17,25},{25,17},{2,10},{10... | collective-permute-start | bytes 614408 | tf_op jit(solution)/shard_map/ppermute | solution.py:25
  3.7 14.5 %collective-permute-start.1 = (bf16[160,640]{1,0:T(8,128)(2,1)S(1)}, bf16[160,640]{1,0:T(8,128)(2,1)S(1)}, u32[]{:S(2)}, u32[]{:S(2)}) collective-permute-start(bf16[160,640]{1,0:T(8,128)(2,1)S(1)} %get-tuple-element.59), channel_id=1, source_target_pairs={{0,16},{8,24},{16,0},{24,8},{1,17},{9,25},{17,1},{25,9},{2,18},{10... | collective-permute-start | bytes 614408 | tf_op jit(solution)/shard_map/ppermute | solution.py:25
  4.1 20.7 %collective-permute-start.2 = (bf16[160,640]{1,0:T(8,128)(2,1)S(1)}, bf16[160,640]{1,0:T(8,128)(2,1)S(1)}, u32[]{:S(2)}, u32[]{:S(2)}) collective-permute-start(bf16[160,640]{1,0:T(8,128)(2,1)S(1)} %get-tuple-element.58), channel_id=1, source_target_pairs={{0,24},{8,16},{16,8},{24,0},{1,25},{9,17},{17,9},{25,1},{2,26},{10... | collective-permute-start | bytes 614408 | tf_op jit(solution)/shard_map/ppermute | solution.py:25
  5.6 22.7 %collective-permute-start.3 = (bf16[128,1280]{1,0:T(8,128)(2,1)S(1)}, bf16[128,1280]{1,0:T(8,128)(2,1)S(1)}, u32[]{:S(2)}, u32[]{:S(2)}) collective-permute-start(bf16[128,1280]{1,0:T(8,128)(2,1)S(1)} %copy-done.4), channel_id=1, source_target_pairs={{0,8},{8,24},{24,16},{16,0},{1,9},{9,25},{25,17},{17,1},{2,10},{10... | collective-permute-start | bytes 983048 | tf_op jit(solution)/shard_map/ppermute | solution.py:317
  6.6 21.7 %collective-permute-start.4 = (bf16[128,1280]{1,0:T(8,128)(2,1)S(1)}, bf16[128,1280]{1,0:T(8,128)(2,1)S(1)}, u32[]{:S(2)}, u32[]{:S(2)}) collective-permute-start(bf16[128,1280]{1,0:T(8,128)(2,1)S(1)} %copy-done.4), channel_id=1, source_target_pairs={{0,1},{1,0},{2,3},{3,2},{4,5},{5,4},{6,7},{7,6},{8,9},{9,8},{10,11... | collective-permute-start | bytes 983048 | tf_op jit(solution)/shard_map/ppermute | solution.py:25
  24.8 26.7 %copy-start = (bf16[128,1280]{1,0:T(8,128)(2,1)S(1)}, bf16[128,1280]{1,0:T(8,128)(2,1)}, u32[]{:S(2)}) copy-start(bf16[128,1280]{1,0:T(8,128)(2,1)} %q_ref.3) | copy-start | bytes 983044
  24.8 26.7 %copy-start.1 = (bf16[128,1280]{1,0:T(8,128)(2,1)S(1)}, bf16[128,1280]{1,0:T(8,128)(2,1)}, u32[]{:S(2)}) copy-start(bf16[128,1280]{1,0:T(8,128)(2,1)} %g_ref.3) | copy-start | bytes 983044
  28.3 6.7 %collective-permute-start.11 = (bf16[4,160,640]{2,1,0:T(8,128)(2,1)S(1)}, bf16[4,160,640]{2,1,0:T(8,128)(2,1)S(1)}, u32[]{:S(2)}, u32[]{:S(2)}) collective-permute-start(bf16[4,160,640]{2,1,0:T(8,128)(2,1)S(1)} %pad_maximum_fusion.refs_8_), channel_id=1, source_target_pairs={{0,2},{2,0},{4,6},{6,4},{1,3},{3,1},{5,7},{7,5},{8,10},{10,8},{12,... | collective-permute-start | bytes 2457608 | tf_op jit(solution)/shard_map/ppermute | solution.py:25
  28.4 12.1 %collective-permute-start.6 = (bf16[128,1280]{1,0:T(8,128)(2,1)S(1)}, bf16[128,1280]{1,0:T(8,128)(2,1)S(1)}, u32[]{:S(2)}, u32[]{:S(2)}) collective-permute-start(bf16[128,1280]{1,0:T(8,128)(2,1)S(1)} %collective-permute-done.3.refs_1_), channel_id=1, source_target_pairs={{0,8},{8,24},{24,16},{16,0},{1,9},{9,25},{25,17},{17,1},{2,10},{10... | collective-permute-start | bytes 983048 | tf_op jit(solution)/shard_map/ppermute | solution.py:317
  31.7 15.5 %collective-permute-start.8 = (bf16[128,1280]{1,0:T(8,128)(2,1)S(1)}, bf16[128,1280]{1,0:T(8,128)(2,1)S(1)}, u32[]{:S(2)}, u32[]{:S(2)}) collective-permute-start(bf16[128,1280]{1,0:T(8,128)(2,1)S(1)} %collective-permute-done.3.refs_1_), channel_id=1, source_target_pairs={{0,1},{1,0},{2,3},{3,2},{4,5},{5,4},{6,7},{7,6},{8,9},{9,8},{10,11... | collective-permute-start | bytes 983048 | tf_op jit(solution)/shard_map/ppermute | solution.py:25
  33.3 25.9 %collective-permute-start.5 = (bf16[4,160,640]{2,1,0:T(8,128)(2,1)S(1)}, bf16[4,160,640]{2,1,0:T(8,128)(2,1)S(1)}, u32[]{:S(2)}, u32[]{:S(2)}) collective-permute-start(bf16[4,160,640]{2,1,0:T(8,128)(2,1)S(1)} %pad_maximum_fusion.refs_8_), channel_id=1, source_target_pairs={{0,4},{2,6},{4,0},{6,2},{1,5},{3,7},{5,1},{7,3},{8,12},{10,14},{12... | collective-permute-start | bytes 2457608 | tf_op jit(solution)/shard_map/ppermute | solution.py:25
  34.7 12.5 %collective-permute-start.7 = (bf16[128,1280]{1,0:T(8,128)(2,1)S(1)}, bf16[128,1280]{1,0:T(8,128)(2,1)S(1)}, u32[]{:S(2)}, u32[]{:S(2)}) collective-permute-start(bf16[128,1280]{1,0:T(8,128)(2,1)S(1)} %copy-done.4), channel_id=1, source_target_pairs={{8,0},{24,8},{16,24},{0,16},{9,1},{25,9},{17,25},{1,17},{10,2},{26... | collective-permute-start | bytes 983048 | tf_op jit(solution)/shard_map/ppermute | solution.py:317
  34.9 35.0 %copy-start.6 = (s32[2048]{0:T(1024)S(1)}, s32[2048]{0:T(1024)}, u32[]{:S(2)}) copy-start(s32[2048]{0:T(1024)} %param.15) | copy-start | bytes 24580
  34.9 35.0 %copy-start.7 = (s32[2048]{0:T(1024)S(1)}, s32[2048]{0:T(1024)}, u32[]{:S(2)}) copy-start(s32[2048]{0:T(1024)} %param.14) | copy-start | bytes 24580
  35.0 28.5 %collective-permute-start.12 = (bf16[2,128,1280]{2,1,0:T(8,128)(2,1)S(1)}, bf16[2,128,1280]{2,1,0:T(8,128)(2,1)S(1)}, u32[]{:S(2)}, u32[]{:S(2)}) collective-permute-start(bf16[2,128,1280]{2,1,0:T(8,128)(2,1)S(1)} %pad_maximum_fusion.1), channel_id=1, source_target_pairs={{0,2},{2,4},{4,6},{6,8},{8,10},{10,12},{12,14},{14,16},{16,18},{18... | collective-permute-start | bytes 1966088 | tf_op jit(solution)/shard_map/ppermute | solution.py:21
  47.2 10.4 %collective-permute-start.10 = (bf16[128,1280]{1,0:T(8,128)(2,1)S(1)}, bf16[128,1280]{1,0:T(8,128)(2,1)S(1)}, u32[]{:S(2)}, u32[]{:S(2)}) collective-permute-start(bf16[128,1280]{1,0:T(8,128)(2,1)S(1)} %collective-permute-done.4.refs_4_), channel_id=1, source_target_pairs={{8,0},{24,8},{16,24},{0,16},{9,1},{25,9},{17,25},{1,17},{10,2},{26... | collective-permute-start | bytes 983048 | tf_op jit(solution)/shard_map/ppermute | solution.py:317
  49.9 9.1 %collective-permute-start.9 = (bf16[128,1280]{1,0:T(8,128)(2,1)S(1)}, bf16[128,1280]{1,0:T(8,128)(2,1)S(1)}, u32[]{:S(2)}, u32[]{:S(2)}) collective-permute-start(bf16[128,1280]{1,0:T(8,128)(2,1)S(1)} %collective-permute-done.6.refs_2_), channel_id=1, source_target_pairs={{0,1},{1,0},{2,3},{3,2},{4,5},{5,4},{6,7},{7,6},{8,9},{9,8},{10,11... | collective-permute-start | bytes 983048 | tf_op jit(solution)/shard_map/ppermute | solution.py:25
  63.5 11.4 %copy-start.8 = (bf16[2,128,1280]{2,1,0:T(8,128)(2,1)}, bf16[2,128,1280]{2,1,0:T(8,128)(2,1)S(1)}, u32[]{:S(2)}) copy-start(bf16[2,128,1280]{2,1,0:T(8,128)(2,1)S(1)} %collective-permute-done.12.kv1_ref) | copy-start | bytes 1966084
  63.5 6.7 %collective-permute-start.13 = (bf16[4,160,640]{2,1,0:T(8,128)(2,1)S(1)}, bf16[4,160,640]{2,1,0:T(8,128)(2,1)S(1)}, u32[]{:S(2)}, u32[]{:S(2)}) collective-permute-start(bf16[4,160,640]{2,1,0:T(8,128)(2,1)S(1)} %collective-permute-done.5.refs_10_), channel_id=1, source_target_pairs={{0,2},{2,0},{4,6},{6,4},{1,3},{3,1},{5,7},{7,5},{8,10},{10,8},{12,... | collective-permute-start | bytes 2457608 | tf_op jit(solution)/shard_map/ppermute | solution.py:25
  63.5 12.9 %collective-permute-start.14 = (bf16[2,128,1280]{2,1,0:T(8,128)(2,1)S(1)}, bf16[2,128,1280]{2,1,0:T(8,128)(2,1)S(1)}, u32[]{:S(2)}, u32[]{:S(2)}) collective-permute-start(bf16[2,128,1280]{2,1,0:T(8,128)(2,1)S(1)} %collective-permute-done.12.kv1_ref), channel_id=1, source_target_pairs={{0,2},{2,4},{4,6},{6,8},{8,10},{10,12},{12,14},{14,16},{16,18},{18... | collective-permute-start | bytes 1966088 | tf_op jit(solution)/shard_map/ppermute | solution.py:21
  65.9 12.2 %collective-permute-start.15 = (bf16[2,128,1280]{2,1,0:T(8,128)(2,1)S(1)}, bf16[2,128,1280]{2,1,0:T(8,128)(2,1)S(1)}, u32[]{:S(2)}, u32[]{:S(2)}) collective-permute-start(bf16[2,128,1280]{2,1,0:T(8,128)(2,1)S(1)} %pad_maximum_fusion.2), channel_id=1, source_target_pairs={{2,0},{4,2},{6,4},{8,6},{10,8},{12,10},{14,12},{16,14},{18,16},{20... | collective-permute-start | bytes 1966088 | tf_op jit(solution)/shard_map/ppermute | solution.py:21
  70.2 4.6 %copy-start.5 = (bf16[128,640]{1,0:T(8,128)(2,1)}, bf16[128,640]{1,0:T(8,128)(2,1)S(1)}, u32[]{:S(2)}) copy-start(bf16[128,640]{1,0:T(8,128)(2,1)S(1)} %get-tuple-element.48.bias_ref) | copy-start | bytes 491524
  76.4 1.7 %copy-start.9 = (bf16[2,128,1280]{2,1,0:T(8,128)(2,1)}, bf16[2,128,1280]{2,1,0:T(8,128)(2,1)S(1)}, u32[]{:S(2)}) copy-start(bf16[2,128,1280]{2,1,0:T(8,128)(2,1)S(1)} %collective-permute-done.14.kv2_ref) | copy-start | bytes 1966084
  78.1 40.0 %all-to-all-start = ((bf16[16,4,16,640]{3,2,1,0:T(8,128)(2,1)}), bf16[16,4,16,640]{3,2,1,0:T(8,128)(2,1)S(1)}, u32[]{:S(2)}, u32[]{:S(2)}) async-start(bf16[16,4,16,640]{3,2,1,0:T(8,128)(2,1)} %project.1), calls=%async_computation | async-start | bytes 2621440 | tf_op jit(solution)/shard_map/all_to_all | solution.py:390
  87.3 40.8 %collective-permute-start.16 = (bf16[2,128,1280]{2,1,0:T(8,128)(2,1)S(1)}, bf16[2,128,1280]{2,1,0:T(8,128)(2,1)}, u32[]{:S(2)}, u32[]{:S(2)}) collective-permute-start(bf16[2,128,1280]{2,1,0:T(8,128)(2,1)S(1)} %collective-permute-done.15.qg1_ref), channel_id=1, source_target_pairs={{2,0},{4,2},{6,4},{8,6},{10,8},{12,10},{14,12},{16,14},{18,16},{20... | collective-permute-start | bytes 1966088 | tf_op jit(solution)/shard_map/ppermute | solution.py:21
  123.1 5.0 %collective-permute-start.17 = (f32[2,16,128]{2,1,0:T(8,128)S(1)}, f32[2,16,128]{2,1,0:T(8,128)S(1)}, u32[]{:S(2)}, u32[]{:S(2)}) collective-permute-start(f32[2,16,128]{2,1,0:T(8,128)S(1)} %get-tuple-element.52.st0_ref), channel_id=1, source_target_pairs={{2,0},{4,2},{6,4},{8,6},{10,8},{12,10},{14,12},{16,14},{18,16},{20... | collective-permute-start | bytes 49160 | tf_op jit(solution)/shard_map/ppermute | solution.py:21
  126.0 5.6 %collective-permute-start.18 = (f32[2,16,128]{2,1,0:T(8,128)S(1)}, f32[2,16,128]{2,1,0:T(8,128)S(1)}, u32[]{:S(2)}, u32[]{:S(2)}) collective-permute-start(f32[2,16,128]{2,1,0:T(8,128)S(1)} %get-tuple-element.52.st0_ref), channel_id=1, source_target_pairs={{4,0},{6,2},{8,4},{10,6},{12,8},{14,10},{16,12},{18,14},{20,16},{2... | collective-permute-start | bytes 49160 | tf_op jit(solution)/shard_map/ppermute | solution.py:21

commit v8 on v5

--- a/solution.py
+++ b/solution.py
@@ -1,3 +1,5 @@
+import functools
+
 import jax
 import jax.numpy as jnp
 from jax import lax
@@ -181,11 +183,11 @@
     )(keys, values, queries, grad_out, *in_vmem(qg1, qg2), *stats, *in_vmem(bias))
 
 
-def project_kernel(place_ref, *refs):
+def project_kernel(layout, place_ref, *refs):
     n_z, _, cache_rows = place_ref.shape
     out_ref, w_ref, a_ref = refs[-3:]
     rows, pieces = refs[: 2 * n_z], refs[2 * n_z : -3]
-    n_p, (_, w_rows, block) = len(pieces), pieces[0].shape
+    w_rows, block = pieces[0].shape[1:]
     depth = rows[0].shape[1]
     devices, _, capacity, _ = out_ref.shape
     z, p, y = (lax.axis_index(name) for name in ("z", "p", "head"))
@@ -193,9 +195,9 @@
     for i, ref in enumerate(rows):
         source = (place_in_ring - i % n_z + n_z) & (n_z - 1)
         a_ref[y ^ (i // n_z), source ^ (source >> 1)] = ref[...]
-    for m in range(n_p):
-        for k in range(n_z):
-            w_ref[z ^ k, p ^ m] = pieces[m][k]
+    for (m, first), piece in zip(layout, pieces):
+        for k in range(piece.shape[0]):
+            w_ref[z ^ (first + k), p ^ m] = piece[k]
     half = n_z // 2
     proj = sum(
         jnp.dot(
@@ -219,12 +221,13 @@
 def project(place, rows, pieces, devices, capacity):
     n_z, _, cache_rows = place.shape
     depth = rows[0].shape[1]
-    n_p = len(pieces)
-    _, w_rows, block = pieces[0].shape
+    layout, pieces = [piece[:2] for piece in pieces], [piece[2] for piece in pieces]
+    n_p = devices // n_z
+    w_rows, block = pieces[0].shape[1:]
     whole = pl.BlockSpec(memory_space=pltpu.VMEM)
     return pl.pallas_call(
-        project_kernel,
-        in_specs=[whole] * (1 + len(rows) + n_p),
+        functools.partial(project_kernel, layout),
+        in_specs=[whole] * (1 + len(rows) + len(pieces)),
         out_specs=whole,
         out_shape=pltpu.VMEM((devices, n_z, capacity, block), jnp.bfloat16),
         scratch_shapes=[
@@ -325,24 +328,38 @@
     z = lax.axis_index("z")
     if n_p == 4 and capacity % ROW_TILE == 0 and w_rows % ROW_TILE == 0:
         blocks = [column_block(w_kv, z ^ mask) for mask in range(n_z)]
-        arrived = [blocks[0]] + [swapped(blocks[mask], "z", mask) for mask in range(1, n_z)]
+        arrived = swapped(blocks[1], "z", 1)
         row1, other0 = ring_step(cache), swapped(cache, "head", 1)
-        row1, arrived[1], arrived[2] = lax.optimization_barrier((row1, arrived[1], arrived[2]))
+        arrived, row1, other0, blocks = lax.optimization_barrier((arrived, row1, other0, blocks))
+        own_lo = jnp.stack([blocks[0], arrived], 0)
+        across_lo = swapped(own_lo, "p", 2)
+        own_hi = jnp.stack([swapped(blocks[mask], "z", mask) for mask in (2, 3)], 0)
         row2, other1 = ring_step(row1), swapped(row1, "head", 1)
-        own, row2, other0, other1 = lax.optimization_barrier(
-            (jnp.stack(arrived, 0), row2, other0, other1)
-        )
-        across, beside = swapped(own, "p", 2), swapped(own, "p", 1)
+        own_lo, own_hi, across_lo, row2, other1 = lax.optimization_barrier(
+            (own_lo, own_hi, across_lo, row2, other1)
+        )
+        across_hi = swapped(own_hi, "p", 2)
+        beside_lo, beside_hi, beyond_lo = (
+            swapped(block, "p", 1) for block in (own_lo, own_hi, across_lo)
+        )
         row3, other2 = ring_step(row2), swapped(row2, "head", 1)
-        row3, other2, beside = lax.optimization_barrier((row3, other2, beside))
+        beside_hi, stream, back = lax.optimization_barrier((beside_hi, stream, back))
+        near, back1 = shifted(stream, 1), shifted(back, -1)
+        row3, other2 = lax.optimization_barrier((row3, other2))
         other3 = swapped(row3, "head", 1)
-        across, other3, stream, back = lax.optimization_barrier((across, other3, stream, back))
-        pieces = [own, beside, across, swapped(across, "p", 1)]
-        near, back1 = shifted(stream, 1), shifted(back, -1)
+        across_hi, other3, near, back1, beside_lo, beyond_lo = lax.optimization_barrier(
+            (across_hi, other3, near, back1, beside_lo, beyond_lo)
+        )
+        pieces = [
+            (0, 0, own_lo), (0, 2, own_hi), (1, 0, beside_lo), (1, 2, beside_hi),
+            (2, 0, across_lo), (2, 2, across_hi),
+            (3, 0, beyond_lo), (3, 2, swapped(across_hi, "p", 1)),
+        ]
+        far = shifted(near, 1)
         rows = [cache, row1, row2, row3, other0, other1, other2, other3]
         slots = project(place, rows, pieces, devices, capacity)
-        slots, near, back1 = lax.optimization_barrier((slots, near, back1))
-        return slots, near, shifted(near, 1), back1
+        slots, far, back1 = lax.optimization_barrier((slots, far, back1))
+        return slots, near, far, back1
     near, back1 = shifted(stream, 1), shifted(back, -1)
     far = shifted(near, 1)
     targets = [column_block(w_kv, jnp.int32(i)) for i in range(n_z)]

time: 137 us -> 144 us (1.051)
  waiting for transfers between devices: 75.5 us -> 89.8 us
  starting transfers between devices: 43.3 us -> 35 us
    ppermute x6, waiting for transfers between devices: 36.6 us -> 5.51 us  [shifted(): return lax.ppermute(value, SEQ, pairs)]
    all_to_all x1, waiting for transfers between devices: 0.01 us -> 27.7 us  [body(): memory = lax.all_to_all(slots, SEQ, split_axis=0, concat_axis=0, tiled=True)]
    ppermute x10 -> x13, waiting for transfers between devices: 32.2 us -> 56.4 us  [swapped(): lax.ppermute(value, axis, [(i, i ^ mask) for i in range(lax.axis_size(axi...]
    ppermute x3, waiting for transfers between devices: 6.69 us -> 0.23 us  [ring_step(): lax.ppermute(value, 'z', [(b, a) for a, b in pairs] if back else pairs)]
    all_to_all x1, starting transfers between devices: 10.6 us -> 5 us  [body(): memory = lax.all_to_all(slots, SEQ, split_axis=0, concat_axis=0, tiled=True)]
    ppermute x3, starting transfers between devices: 5.83 us -> 1.3 us  [ring_step(): lax.ppermute(value, 'z', [(b, a) for a, b in pairs] if back else pairs)]
    ppermute x10 -> x13, starting transfers between devices: 10.1 us -> 12.3 us  [swapped(): lax.ppermute(value, axis, [(i, i ^ mask) for i in range(lax.axis_size(axi...]
  transfers between devices with their start and end apart: 20 -> 23, of which waited for: 12 -> 12; matrix products, arithmetic and copies ran while one was open for 1% -> 1% of each run, Pallas kernels for 7% -> 7%
where the time goes in v8:
time: 144 us; the launch traced here: 142 us
  waiting for transfers between devices  89.8 us (62%)
  starting transfers between devices  35 us (24%)
  Pallas kernels  13.6 us (9%)
  local copies, waits for them, and re-layouts  2.12 us (1%)
    ppermute x13, waiting for transfers between devices, swapped(): lax.ppermute(value, axis, [(i, i ^ mask) for i in range(lax.axis_size(axi...  56.4 us
    all_to_all x1, waiting for transfers between devices, body(): memory = lax.all_to_all(slots, SEQ, split_axis=0, concat_axis=0, tiled=True)  27.7 us
    ppermute x6, starting transfers between devices, shifted(): return lax.ppermute(value, SEQ, pairs)  16.4 us
    ppermute x13, starting transfers between devices, swapped(): lax.ppermute(value, axis, [(i, i ^ mask) for i in range(lax.axis_size(axi...  12.3 us
    ppermute x6, waiting for transfers between devices, shifted(): return lax.ppermute(value, SEQ, pairs)  5.51 us
    all_to_all x1, starting transfers between devices, body(): memory = lax.all_to_all(slots, SEQ, split_axis=0, concat_axis=0, tiled=True)  5 us
    pallas_call x1, Pallas kernels, attend(): pl.pallas_call(attend_kernel, grid=(steps,), in_specs=[flat, flat, flat,...  4.98 us
    pallas_call x1, Pallas kernels, project(): pl.pallas_call(functools.partial(project_kernel, layout), in_specs=[whole...  4.59 us
  transfers between devices with their start and end apart: 23, of which 12 were waited for; matrix products, arithmetic and copies ran while one was open for 1% of the time, Pallas kernels for 7%

profile of v8, /device:TPU:16, one launch (start us, length us, event | category | flops | bytes accessed | tf_op | source)
XLA Modules:
  0.0 141.6 jit_solution(96425385984591898)
XLA Ops:
  0.6 0.1 collective-permute-start.1
  0.7 1.8 %collective-permute-start.2 = (bf16[128,1280]{1,0:T(8,128)(2,1)}, bf16[128,1280]{1,0:T(8,128)(2,1)S(1)}, u32[]{:S(2)}, u32[]{:S(2)}) collective-permute-start(bf16[128,1280]{1,0:T(8,128)(2,1)} %refs_0_.1), channel_id=1, source_target_pairs={{0,1},{1,0},{2,3},{3,2},{4,5},{5,4},{6,7},{7,6},{8,9},{9,8},{10,11... | collective-permute-start | bytes 983048 | tf_op jit(solution)/shard_map/ppermute | solution.py:27
  2.6 1.4 dynamic-slice_bitcast_fusion
  4.0 1.8 %collective-permute-start = (bf16[160,640]{1,0:T(8,128)(2,1)S(1)}, bf16[160,640]{1,0:T(8,128)(2,1)S(1)}, u32[]{:S(2)}, u32[]{:S(2)}) collective-permute-start(bf16[160,640]{1,0:T(8,128)(2,1)S(1)} %get-tuple-element.72), channel_id=1, source_target_pairs={{0,8},{8,0},{16,24},{24,16},{1,9},{9,1},{17,25},{25,17},{2,10},{10... | collective-permute-start | bytes 614408 | tf_op jit(solution)/shard_map/ppermute | solution.py:27
  5.7 9.0 %collective-permute-done = bf16[160,640]{1,0:T(8,128)(2,1)S(1)} collective-permute-done((bf16[160,640]{1,0:T(8,128)(2,1)S(1)}, bf16[160,640]{1,0:T(8,128)(2,1)S(1)}, u32[]{:S(2)}, u32[]{:S(2)}) %collective-permute-start) | collective-permute-done | bytes 204832 | tf_op jit(solution)/shard_map/ppermute | solution.py:27
  14.7 0.0 collective-permute-done.1.refs_1_
  14.7 0.0 collective-permute-done.2.refs_4_
  14.8 1.6 %collective-permute-start.5 = (bf16[2,160,640]{2,1,0:T(8,128)(2,1)S(1)}, bf16[2,160,640]{2,1,0:T(8,128)(2,1)S(1)}, u32[]{:S(2)}, u32[]{:S(2)}) collective-permute-start(bf16[2,160,640]{2,1,0:T(8,128)(2,1)S(1)} %pad_maximum_fusion.2.refs_8_), channel_id=1, source_target_pairs={{0,4},{2,6},{4,0},{6,2},{1,5},{3,7},{5,1},{7,3},{8,12},{10,14},{12... | collective-permute-start | bytes 1228808 | tf_op jit(solution)/shard_map/ppermute | solution.py:27
  16.4 1.5 %collective-permute-start.7 = (bf16[128,1280]{1,0:T(8,128)(2,1)S(1)}, bf16[128,1280]{1,0:T(8,128)(2,1)S(1)}, u32[]{:S(2)}, u32[]{:S(2)}) collective-permute-start(bf16[128,1280]{1,0:T(8,128)(2,1)S(1)} %collective-permute-done.1.refs_1_), channel_id=1, source_target_pairs={{0,1},{1,0},{2,3},{3,2},{4,5},{5,4},{6,7},{7,6},{8,9},{9,8},{10,11... | collective-permute-start | bytes 983048 | tf_op jit(solution)/shard_map/ppermute | solution.py:27
  17.9 1.2 collective-permute-start.6
  19.1 0.7 collective-permute-start.3
  19.8 2.1 %collective-permute-start.4 = (bf16[160,640]{1,0:T(8,128)(2,1)S(1)}, bf16[160,640]{1,0:T(8,128)(2,1)S(1)}, u32[]{:S(2)}, u32[]{:S(2)}) collective-permute-start(bf16[160,640]{1,0:T(8,128)(2,1)S(1)} %get-tuple-element.40), channel_id=1, source_target_pairs={{0,24},{8,16},{16,8},{24,0},{1,25},{9,17},{17,9},{25,1},{2,26},{10... | collective-permute-start | bytes 614408 | tf_op jit(solution)/shard_map/ppermute | solution.py:27
  21.8 18.6 %collective-permute-done.3 = bf16[160,640]{1,0:T(8,128)(2,1)S(1)} collective-permute-done((bf16[160,640]{1,0:T(8,128)(2,1)S(1)}, bf16[160,640]{1,0:T(8,128)(2,1)S(1)}, u32[]{:S(2)}, u32[]{:S(2)}) %collective-permute-start.3) | collective-permute-done | bytes 204832 | tf_op jit(solution)/shard_map/ppermute | solution.py:27
  40.4 6.0 %collective-permute-done.4 = bf16[160,640]{1,0:T(8,128)(2,1)S(1)} collective-permute-done((bf16[160,640]{1,0:T(8,128)(2,1)S(1)}, bf16[160,640]{1,0:T(8,128)(2,1)S(1)}, u32[]{:S(2)}, u32[]{:S(2)}) %collective-permute-start.4) | collective-permute-done | bytes 204832 | tf_op jit(solution)/shard_map/ppermute | solution.py:27
  46.5 0.0 collective-permute-done.7.refs_5_
  46.5 0.0 collective-permute-done.6.refs_2_
  46.5 0.0 collective-permute-done.5.refs_12_
  46.5 0.1 collective-permute-start.12
  46.6 0.6 collective-permute-start.10
  47.1 0.0 collective-permute-start.9
  47.1 0.2 collective-permute-start.15
  47.3 0.0 copy-done
  47.3 0.0 copy-done.1
  47.3 0.0 copy-done.2
  47.3 0.0 copy-done.3
  47.3 0.0 copy-start.6
  47.3 0.0 copy-start.7
  47.4 0.0 copy-start.4
  47.4 0.1 pad_maximum_fusion
  47.5 0.8 collective-permute-done.12.refs_11_
  48.3 2.0 %collective-permute-start.13 = (bf16[2,128,1280]{2,1,0:T(8,128)(2,1)S(1)}, bf16[2,128,1280]{2,1,0:T(8,128)(2,1)S(1)}, u32[]{:S(2)}, u32[]{:S(2)}) collective-permute-start(bf16[2,128,1280]{2,1,0:T(8,128)(2,1)S(1)} %get-tuple-element.45), channel_id=1, source_target_pairs={{0,2},{2,4},{4,6},{6,8},{8,10},{10,12},{12,14},{14,16},{16,18},{18... | collective-permute-start | bytes 1966088 | tf_op jit(solution)/shard_map/ppermute | solution.py:23
  50.3 4.4 %collective-permute-start.14 = (bf16[2,128,1280]{2,1,0:T(8,128)(2,1)S(1)}, bf16[2,128,1280]{2,1,0:T(8,128)(2,1)S(1)}, u32[]{:S(2)}, u32[]{:S(2)}) collective-permute-start(bf16[2,128,1280]{2,1,0:T(8,128)(2,1)S(1)} %get-tuple-element.46), channel_id=1, source_target_pairs={{2,0},{4,2},{6,4},{8,6},{10,8},{12,10},{14,12},{16,14},{18,16},{20... | collective-permute-start | bytes 1966088 | tf_op jit(solution)/shard_map/ppermute | solution.py:23
  54.8 1.9 %collective-permute-done.10.refs_6_ = bf16[128,1280]{1,0:T(8,128)(2,1)S(1)} collective-permute-done((bf16[128,1280]{1,0:T(8,128)(2,1)S(1)}, bf16[128,1280]{1,0:T(8,128)(2,1)S(1)}, u32[]{:S(2)}, u32[]{:S(2)}) %collective-permute-start.10) | collective-permute-done | bytes 327712 | tf_op jit(solution)/shard_map/ppermute | solution.py:27
  56.7 0.0 collective-permute-start.16
  56.7 0.2 collective-permute-done.9.refs_3_
  56.9 0.5 collective-permute-start.8
  57.5 0.0 collective-permute-done.15.refs_10_
  57.5 1.5 %collective-permute-start.11 = (bf16[128,1280]{1,0:T(8,128)(2,1)S(1)}, bf16[128,1280]{1,0:T(8,128)(2,1)S(1)}, u32[]{:S(2)}, u32[]{:S(2)}) collective-permute-start(bf16[128,1280]{1,0:T(8,128)(2,1)S(1)} %collective-permute-done.9.refs_3_), channel_id=1, source_target_pairs={{0,1},{1,0},{2,3},{3,2},{4,5},{5,4},{6,7},{7,6},{8,9},{9,8},{10,11... | collective-permute-start | bytes 983048 | tf_op jit(solution)/shard_map/ppermute | solution.py:27
  59.0 0.0 collective-permute-done.16.refs_14_
  59.0 18.8 %collective-permute-done.8.refs_13_ = bf16[2,160,640]{2,1,0:T(8,128)(2,1)S(1)} collective-permute-done((bf16[2,160,640]{2,1,0:T(8,128)(2,1)S(1)}, bf16[2,160,640]{2,1,0:T(8,128)(2,1)S(1)}, u32[]{:S(2)}, u32[]{:S(2)}) %collective-permute-start.8) | collective-permute-done | bytes 409632 | tf_op jit(solution)/shard_map/ppermute | solution.py:27
  77.8 0.0 collective-permute-done.11.refs_7_
  77.8 0.0 collective-permute-done.13.kv1_ref
  77.8 0.0 collective-permute-done.14.qg1_ref
  77.8 1.9 %collective-permute-start.18 = (bf16[2,128,1280]{2,1,0:T(8,128)(2,1)S(1)}, bf16[2,128,1280]{2,1,0:T(8,128)(2,1)}, u32[]{:S(2)}, u32[]{:S(2)}) collective-permute-start(bf16[2,128,1280]{2,1,0:T(8,128)(2,1)S(1)} %collective-permute-done.13.kv1_ref), channel_id=1, source_target_pairs={{0,2},{2,4},{4,6},{6,8},{8,10},{10,12},{12,14},{14,16},{16,18},{18... | collective-permute-start | bytes 1966088 | tf_op jit(solution)/shard_map/ppermute | solution.py:23
  79.8 0.1 collective-permute-start.17
  79.8 0.0 copy-done.6
  79.8 0.0 copy-done.7
  79.9 0.3 prepare.1
  80.1 0.7 copy-done.5
  80.8 1.3 collective-permute-done.17.refs_15_
  82.0 0.0 copy-done.4
  82.0 4.6 %project.1 = bf16[16,4,16,640]{3,2,1,0:T(8,128)(2,1)} custom-call(s32[4,1,128]{2,1,0:T(1,128)S(1)} %get-tuple-element.50.place_ref, bf16[128,1280]{1,0:T(8,128)(2,1)S(1)} %copy-done.4, bf16[128,1280]{1,0:T(8,128)(2,1)S(1)} %collective-permute-done.1.refs_1_, bf16[128,1280]{1,0:T(8,128)(2,1)S(1)} %collective-permute-done.6.refs_2_, ...), custom_call_target="tpu_custom_call" | custom-call | flops 1677721600 | bytes 8388608 | tf_op jit(solution)/shard_map/project/pallas_call | solution.py:228
  86.6 0.0 copy-done.8
  86.6 4.1 %collective-permute-done.18.kv2_ref = bf16[2,128,1280]{2,1,0:T(8,128)(2,1)} collective-permute-done((bf16[2,128,1280]{2,1,0:T(8,128)(2,1)S(1)}, bf16[2,128,1280]{2,1,0:T(8,128)(2,1)}, u32[]{:S(2)}, u32[]{:S(2)}) %collective-permute-start.18) | collective-permute-done | bytes 655392 | tf_op jit(solution)/shard_map/ppermute | solution.py:23
  90.7 5.0 %all-to-all-start = ((bf16[16,4,16,640]{3,2,1,0:T(8,128)(2,1)}), bf16[16,4,16,640]{3,2,1,0:T(8,128)(2,1)S(1)}, u32[]{:S(2)}, u32[]{:S(2)}) async-start(bf16[16,4,16,640]{3,2,1,0:T(8,128)(2,1)} %project.1), calls=%async_computation | async-start | bytes 2621440 | tf_op jit(solution)/shard_map/all_to_all | solution.py:405
  95.7 3.1 %collective-permute-start.19 = (bf16[2,128,1280]{2,1,0:T(8,128)(2,1)S(1)}, bf16[2,128,1280]{2,1,0:T(8,128)(2,1)}, u32[]{:S(2)}, u32[]{:S(2)}) collective-permute-start(bf16[2,128,1280]{2,1,0:T(8,128)(2,1)S(1)} %collective-permute-done.14.qg1_ref), channel_id=1, source_target_pairs={{2,0},{4,2},{6,4},{8,6},{10,8},{12,10},{14,12},{16,14},{18,16},{20... | collective-permute-start | bytes 1966088 | tf_op jit(solution)/shard_map/ppermute | solution.py:23
  98.9 27.7 %all-to-all-done = bf16[16,4,16,640]{3,2,1,0:T(8,128)(2,1)S(1)} async-done(((bf16[16,4,16,640]{3,2,1,0:T(8,128)(2,1)}), bf16[16,4,16,640]{3,2,1,0:T(8,128)(2,1)S(1)}, u32[]{:S(2)}, u32[]{:S(2)}) %all-to-all-start) | async-done | bytes 1310752 | tf_op jit(solution)/shard_map/all_to_all | solution.py:405
  126.5 5.0 %attend.1 = (bf16[128,1280]{1,0:T(8,128)(2,1)}, bf16[128,1280]{1,0:T(8,128)(2,1)}, f32[2,16,128]{2,1,0:T(8,128)S(1)}) custom-call(bf16[128,1280]{1,0:T(8,128)(2,1)S(1)} %copy-done, bf16[128,1280]{1,0:T(8,128)(2,1)S(1)} %copy-done.1, bf16[128,1280]{1,0:T(8,128)(2,1)S(1)} %copy-done.2, bf16[128,1280]{1,0:T(8,128)(2,1)S(1)} %copy-done.3, ...), custom_call_target="tpu_custom_call" | custom-call | flops 838860800 | bytes 6291456 | tf_op jit(solution)/shard_map/attend/pallas_call | solution.py:105
  131.5 3.0 %collective-permute-start.21 = (f32[2,16,128]{2,1,0:T(8,128)S(1)}, f32[2,16,128]{2,1,0:T(8,128)S(1)}, u32[]{:S(2)}, u32[]{:S(2)}) collective-permute-start(f32[2,16,128]{2,1,0:T(8,128)S(1)} %get-tuple-element.66.st0_ref), channel_id=1, source_target_pairs={{4,0},{6,2},{8,4},{10,6},{12,8},{14,10},{16,12},{18,14},{20,16},{2... | collective-permute-start | bytes 49160 | tf_op jit(solution)/shard_map/ppermute | solution.py:23
  134.5 1.9 %collective-permute-start.20 = (f32[2,16,128]{2,1,0:T(8,128)S(1)}, f32[2,16,128]{2,1,0:T(8,128)S(1)}, u32[]{:S(2)}, u32[]{:S(2)}) collective-permute-start(f32[2,16,128]{2,1,0:T(8,128)S(1)} %get-tuple-element.66.st0_ref), channel_id=1, source_target_pairs={{2,0},{4,2},{6,4},{8,6},{10,8},{12,10},{14,12},{16,14},{18,16},{20... | collective-permute-start | bytes 49160 | tf_op jit(solution)/shard_map/ppermute | solution.py:23
  136.4 0.0 collective-permute-done.19.qg2_ref
  136.5 0.7 collective-permute-done.21.st2_ref
  137.1 0.7 collective-permute-done.20.st1_ref
  137.9 3.7 %key_grads.1 = (bf16[128,1280]{1,0:T(8,128)(2,1)}, bf16[128,1280]{1,0:T(8,128)(2,1)}) custom-call(bf16[128,1280]{1,0:T(8,128)(2,1)S(1)} %copy-done.2, bf16[128,1280]{1,0:T(8,128)(2,1)S(1)} %copy-done.3, bf16[128,1280]{1,0:T(8,128)(2,1)S(1)} %copy-done, bf16[128,1280]{1,0:T(8,128)(2,1)S(1)} %copy-done.1, ...), custom_call_target="tpu_custom_call" | custom-call | flops 503316480 | bytes 4194304 | tf_op jit(solution)/shard_map/key_grads/pallas_call | solution.py:168
  (8 shorter events, 0.1 us)
Async XLA Ops:
  0.6 14.1 %collective-permute-start.1 = (bf16[128,1280]{1,0:T(8,128)(2,1)}, bf16[128,1280]{1,0:T(8,128)(2,1)S(1)}, u32[]{:S(2)}, u32[]{:S(2)}) collective-permute-start(bf16[128,1280]{1,0:T(8,128)(2,1)} %refs_0_.1), channel_id=1, source_target_pairs={{0,8},{8,24},{24,16},{16,0},{1,9},{9,25},{25,17},{17,1},{2,10},{10... | collective-permute-start | bytes 983048 | tf_op jit(solution)/shard_map/ppermute | solution.py:320
  0.7 14.0 %collective-permute-start.2 = (bf16[128,1280]{1,0:T(8,128)(2,1)}, bf16[128,1280]{1,0:T(8,128)(2,1)S(1)}, u32[]{:S(2)}, u32[]{:S(2)}) collective-permute-start(bf16[128,1280]{1,0:T(8,128)(2,1)} %refs_0_.1), channel_id=1, source_target_pairs={{0,1},{1,0},{2,3},{3,2},{4,5},{5,4},{6,7},{7,6},{8,9},{9,8},{10,11... | collective-permute-start | bytes 983048 | tf_op jit(solution)/shard_map/ppermute | solution.py:27
  2.5 44.8 %copy-start = (bf16[128,1280]{1,0:T(8,128)(2,1)S(1)}, bf16[128,1280]{1,0:T(8,128)(2,1)}, u32[]{:S(2)}) copy-start(bf16[128,1280]{1,0:T(8,128)(2,1)} %q_ref.3) | copy-start | bytes 983044
  2.5 44.8 %copy-start.1 = (bf16[128,1280]{1,0:T(8,128)(2,1)S(1)}, bf16[128,1280]{1,0:T(8,128)(2,1)}, u32[]{:S(2)}) copy-start(bf16[128,1280]{1,0:T(8,128)(2,1)} %g_ref.3) | copy-start | bytes 983044
  2.5 44.8 %copy-start.2 = (bf16[128,1280]{1,0:T(8,128)(2,1)S(1)}, bf16[128,1280]{1,0:T(8,128)(2,1)}, u32[]{:S(2)}) copy-start(bf16[128,1280]{1,0:T(8,128)(2,1)} %k_ref.3) | copy-start | bytes 983044
  2.5 44.8 %copy-start.3 = (bf16[128,1280]{1,0:T(8,128)(2,1)S(1)}, bf16[128,1280]{1,0:T(8,128)(2,1)}, u32[]{:S(2)}) copy-start(bf16[128,1280]{1,0:T(8,128)(2,1)} %v_ref.3) | copy-start | bytes 983044
  4.0 10.8 %collective-permute-start = (bf16[160,640]{1,0:T(8,128)(2,1)S(1)}, bf16[160,640]{1,0:T(8,128)(2,1)S(1)}, u32[]{:S(2)}, u32[]{:S(2)}) collective-permute-start(bf16[160,640]{1,0:T(8,128)(2,1)S(1)} %get-tuple-element.72), channel_id=1, source_target_pairs={{0,8},{8,0},{16,24},{24,16},{1,9},{9,1},{17,25},{25,17},{2,10},{10... | collective-permute-start | bytes 614408 | tf_op jit(solution)/shard_map/ppermute | solution.py:27
  14.8 31.7 %collective-permute-start.5 = (bf16[2,160,640]{2,1,0:T(8,128)(2,1)S(1)}, bf16[2,160,640]{2,1,0:T(8,128)(2,1)S(1)}, u32[]{:S(2)}, u32[]{:S(2)}) collective-permute-start(bf16[2,160,640]{2,1,0:T(8,128)(2,1)S(1)} %pad_maximum_fusion.2.refs_8_), channel_id=1, source_target_pairs={{0,4},{2,6},{4,0},{6,2},{1,5},{3,7},{5,1},{7,3},{8,12},{10,14},{12... | collective-permute-start | bytes 1228808 | tf_op jit(solution)/shard_map/ppermute | solution.py:27
  16.4 30.1 %collective-permute-start.7 = (bf16[128,1280]{1,0:T(8,128)(2,1)S(1)}, bf16[128,1280]{1,0:T(8,128)(2,1)S(1)}, u32[]{:S(2)}, u32[]{:S(2)}) collective-permute-start(bf16[128,1280]{1,0:T(8,128)(2,1)S(1)} %collective-permute-done.1.refs_1_), channel_id=1, source_target_pairs={{0,1},{1,0},{2,3},{3,2},{4,5},{5,4},{6,7},{7,6},{8,9},{9,8},{10,11... | collective-permute-start | bytes 983048 | tf_op jit(solution)/shard_map/ppermute | solution.py:27
  17.9 28.6 %collective-permute-start.6 = (bf16[128,1280]{1,0:T(8,128)(2,1)S(1)}, bf16[128,1280]{1,0:T(8,128)(2,1)S(1)}, u32[]{:S(2)}, u32[]{:S(2)}) collective-permute-start(bf16[128,1280]{1,0:T(8,128)(2,1)S(1)} %collective-permute-done.1.refs_1_), channel_id=1, source_target_pairs={{0,8},{8,24},{24,16},{16,0},{1,9},{9,25},{25,17},{17,1},{2,10},{10... | collective-permute-start | bytes 983048 | tf_op jit(solution)/shard_map/ppermute | solution.py:320
  19.1 21.3 %collective-permute-start.3 = (bf16[160,640]{1,0:T(8,128)(2,1)S(1)}, bf16[160,640]{1,0:T(8,128)(2,1)S(1)}, u32[]{:S(2)}, u32[]{:S(2)}) collective-permute-start(bf16[160,640]{1,0:T(8,128)(2,1)S(1)} %get-tuple-element.39), channel_id=1, source_target_pairs={{0,16},{8,24},{16,0},{24,8},{1,17},{9,25},{17,1},{25,9},{2,18},{10... | collective-permute-start | bytes 614408 | tf_op jit(solution)/shard_map/ppermute | solution.py:27
  19.8 26.6 %collective-permute-start.4 = (bf16[160,640]{1,0:T(8,128)(2,1)S(1)}, bf16[160,640]{1,0:T(8,128)(2,1)S(1)}, u32[]{:S(2)}, u32[]{:S(2)}) collective-permute-start(bf16[160,640]{1,0:T(8,128)(2,1)S(1)} %get-tuple-element.40), channel_id=1, source_target_pairs={{0,24},{8,16},{16,8},{24,0},{1,25},{9,17},{17,9},{25,1},{2,26},{10... | collective-permute-start | bytes 614408 | tf_op jit(solution)/shard_map/ppermute | solution.py:27
  46.5 1.8 %collective-permute-start.12 = (bf16[2,160,640]{2,1,0:T(8,128)(2,1)S(1)}, bf16[2,160,640]{2,1,0:T(8,128)(2,1)S(1)}, u32[]{:S(2)}, u32[]{:S(2)}) collective-permute-start(bf16[2,160,640]{2,1,0:T(8,128)(2,1)S(1)} %pad_maximum_fusion.3.refs_9_), channel_id=1, source_target_pairs={{0,2},{2,0},{4,6},{6,4},{1,3},{3,1},{5,7},{7,5},{8,10},{10,8},{12,... | collective-permute-start | bytes 1228808 | tf_op jit(solution)/shard_map/ppermute | solution.py:27
  46.6 10.1 %collective-permute-start.10 = (bf16[128,1280]{1,0:T(8,128)(2,1)S(1)}, bf16[128,1280]{1,0:T(8,128)(2,1)S(1)}, u32[]{:S(2)}, u32[]{:S(2)}) collective-permute-start(bf16[128,1280]{1,0:T(8,128)(2,1)S(1)} %collective-permute-done.6.refs_2_), channel_id=1, source_target_pairs={{0,1},{1,0},{2,3},{3,2},{4,5},{5,4},{6,7},{7,6},{8,9},{9,8},{10,11... | collective-permute-start | bytes 983048 | tf_op jit(solution)/shard_map/ppermute | solution.py:27
  47.1 9.8 %collective-permute-start.9 = (bf16[128,1280]{1,0:T(8,128)(2,1)S(1)}, bf16[128,1280]{1,0:T(8,128)(2,1)S(1)}, u32[]{:S(2)}, u32[]{:S(2)}) collective-permute-start(bf16[128,1280]{1,0:T(8,128)(2,1)S(1)} %collective-permute-done.6.refs_2_), channel_id=1, source_target_pairs={{0,8},{8,24},{24,16},{16,0},{1,9},{9,25},{25,17},{17,1},{2,10},{10... | collective-permute-start | bytes 983048 | tf_op jit(solution)/shard_map/ppermute | solution.py:320
  47.1 10.3 %collective-permute-start.15 = (bf16[2,160,640]{2,1,0:T(8,128)(2,1)S(1)}, bf16[2,160,640]{2,1,0:T(8,128)(2,1)S(1)}, u32[]{:S(2)}, u32[]{:S(2)}) collective-permute-start(bf16[2,160,640]{2,1,0:T(8,128)(2,1)S(1)} %pad_maximum_fusion.2.refs_8_), channel_id=1, source_target_pairs={{0,2},{2,0},{4,6},{6,4},{1,3},{3,1},{5,7},{7,5},{8,10},{10,8},{12,... | collective-permute-start | bytes 1228808 | tf_op jit(solution)/shard_map/ppermute | solution.py:27
  47.3 32.5 %copy-start.6 = (s32[2048]{0:T(1024)S(1)}, s32[2048]{0:T(1024)}, u32[]{:S(2)}) copy-start(s32[2048]{0:T(1024)} %param.15) | copy-start | bytes 24580
  47.3 32.5 %copy-start.7 = (s32[2048]{0:T(1024)S(1)}, s32[2048]{0:T(1024)}, u32[]{:S(2)}) copy-start(s32[2048]{0:T(1024)} %param.14) | copy-start | bytes 24580
  47.4 34.7 %copy-start.4 = (bf16[128,1280]{1,0:T(8,128)(2,1)S(1)}, bf16[128,1280]{1,0:T(8,128)(2,1)}, u32[]{:S(2)}) copy-start(bf16[128,1280]{1,0:T(8,128)(2,1)} %refs_0_.1) | copy-start | bytes 983044
  48.3 29.5 %collective-permute-start.13 = (bf16[2,128,1280]{2,1,0:T(8,128)(2,1)S(1)}, bf16[2,128,1280]{2,1,0:T(8,128)(2,1)S(1)}, u32[]{:S(2)}, u32[]{:S(2)}) collective-permute-start(bf16[2,128,1280]{2,1,0:T(8,128)(2,1)S(1)} %get-tuple-element.45), channel_id=1, source_target_pairs={{0,2},{2,4},{4,6},{6,8},{8,10},{10,12},{12,14},{14,16},{16,18},{18... | collective-permute-start | bytes 1966088 | tf_op jit(solution)/shard_map/ppermute | solution.py:23
  50.3 27.5 %collective-permute-start.14 = (bf16[2,128,1280]{2,1,0:T(8,128)(2,1)S(1)}, bf16[2,128,1280]{2,1,0:T(8,128)(2,1)S(1)}, u32[]{:S(2)}, u32[]{:S(2)}) collective-permute-start(bf16[2,128,1280]{2,1,0:T(8,128)(2,1)S(1)} %get-tuple-element.46), channel_id=1, source_target_pairs={{2,0},{4,2},{6,4},{8,6},{10,8},{12,10},{14,12},{16,14},{18,16},{20... | collective-permute-start | bytes 1966088 | tf_op jit(solution)/shard_map/ppermute | solution.py:23
  56.7 2.3 %collective-permute-start.16 = (bf16[2,160,640]{2,1,0:T(8,128)(2,1)S(1)}, bf16[2,160,640]{2,1,0:T(8,128)(2,1)S(1)}, u32[]{:S(2)}, u32[]{:S(2)}) collective-permute-start(bf16[2,160,640]{2,1,0:T(8,128)(2,1)S(1)} %collective-permute-done.5.refs_12_), channel_id=1, source_target_pairs={{0,2},{2,0},{4,6},{6,4},{1,3},{3,1},{5,7},{7,5},{8,10},{10,8},{12,... | collective-permute-start | bytes 1228808 | tf_op jit(solution)/shard_map/ppermute | solution.py:27
  56.9 20.9 %collective-permute-start.8 = (bf16[2,160,640]{2,1,0:T(8,128)(2,1)S(1)}, bf16[2,160,640]{2,1,0:T(8,128)(2,1)S(1)}, u32[]{:S(2)}, u32[]{:S(2)}) collective-permute-start(bf16[2,160,640]{2,1,0:T(8,128)(2,1)S(1)} %pad_maximum_fusion.3.refs_9_), channel_id=1, source_target_pairs={{0,4},{2,6},{4,0},{6,2},{1,5},{3,7},{5,1},{7,3},{8,12},{10,14},{12... | collective-permute-start | bytes 1228808 | tf_op jit(solution)/shard_map/ppermute | solution.py:27
  57.5 20.3 %collective-permute-start.11 = (bf16[128,1280]{1,0:T(8,128)(2,1)S(1)}, bf16[128,1280]{1,0:T(8,128)(2,1)S(1)}, u32[]{:S(2)}, u32[]{:S(2)}) collective-permute-start(bf16[128,1280]{1,0:T(8,128)(2,1)S(1)} %collective-permute-done.9.refs_3_), channel_id=1, source_target_pairs={{0,1},{1,0},{2,3},{3,2},{4,5},{5,4},{6,7},{7,6},{8,9},{9,8},{10,11... | collective-permute-start | bytes 983048 | tf_op jit(solution)/shard_map/ppermute | solution.py:27
  77.8 8.8 %copy-start.8 = (bf16[2,128,1280]{2,1,0:T(8,128)(2,1)}, bf16[2,128,1280]{2,1,0:T(8,128)(2,1)S(1)}, u32[]{:S(2)}) copy-start(bf16[2,128,1280]{2,1,0:T(8,128)(2,1)S(1)} %collective-permute-done.13.kv1_ref) | copy-start | bytes 1966084
  77.8 12.9 %collective-permute-start.18 = (bf16[2,128,1280]{2,1,0:T(8,128)(2,1)S(1)}, bf16[2,128,1280]{2,1,0:T(8,128)(2,1)}, u32[]{:S(2)}, u32[]{:S(2)}) collective-permute-start(bf16[2,128,1280]{2,1,0:T(8,128)(2,1)S(1)} %collective-permute-done.13.kv1_ref), channel_id=1, source_target_pairs={{0,2},{2,4},{4,6},{6,8},{8,10},{10,12},{12,14},{14,16},{16,18},{18... | collective-permute-start | bytes 1966088 | tf_op jit(solution)/shard_map/ppermute | solution.py:23
  79.8 2.3 %collective-permute-start.17 = (bf16[2,160,640]{2,1,0:T(8,128)(2,1)S(1)}, bf16[2,160,640]{2,1,0:T(8,128)(2,1)S(1)}, u32[]{:S(2)}, u32[]{:S(2)}) collective-permute-start(bf16[2,160,640]{2,1,0:T(8,128)(2,1)S(1)} %collective-permute-done.8.refs_13_), channel_id=1, source_target_pairs={{0,2},{2,0},{4,6},{6,4},{1,3},{3,1},{5,7},{7,5},{8,10},{10,8},{12,... | collective-permute-start | bytes 1228808 | tf_op jit(solution)/shard_map/ppermute | solution.py:27
  80.1 0.7 copy-start.5
  90.7 35.8 %all-to-all-start = ((bf16[16,4,16,640]{3,2,1,0:T(8,128)(2,1)}), bf16[16,4,16,640]{3,2,1,0:T(8,128)(2,1)S(1)}, u32[]{:S(2)}, u32[]{:S(2)}) async-start(bf16[16,4,16,640]{3,2,1,0:T(8,128)(2,1)} %project.1), calls=%async_computation | async-start | bytes 2621440 | tf_op jit(solution)/shard_map/all_to_all | solution.py:405
  95.7 40.7 %collective-permute-start.19 = (bf16[2,128,1280]{2,1,0:T(8,128)(2,1)S(1)}, bf16[2,128,1280]{2,1,0:T(8,128)(2,1)}, u32[]{:S(2)}, u32[]{:S(2)}) collective-permute-start(bf16[2,128,1280]{2,1,0:T(8,128)(2,1)S(1)} %collective-permute-done.14.qg1_ref), channel_id=1, source_target_pairs={{2,0},{4,2},{6,4},{8,6},{10,8},{12,10},{14,12},{16,14},{18,16},{20... | collective-permute-start | bytes 1966088 | tf_op jit(solution)/shard_map/ppermute | solution.py:23
  131.5 5.6 %collective-permute-start.21 = (f32[2,16,128]{2,1,0:T(8,128)S(1)}, f32[2,16,128]{2,1,0:T(8,128)S(1)}, u32[]{:S(2)}, u32[]{:S(2)}) collective-permute-start(f32[2,16,128]{2,1,0:T(8,128)S(1)} %get-tuple-element.66.st0_ref), channel_id=1, source_target_pairs={{4,0},{6,2},{8,4},{10,6},{12,8},{14,10},{16,12},{18,14},{20,16},{2... | collective-permute-start | bytes 49160 | tf_op jit(solution)/shard_map/ppermute | solution.py:23
  134.5 3.4 %collective-permute-start.20 = (f32[2,16,128]{2,1,0:T(8,128)S(1)}, f32[2,16,128]{2,1,0:T(8,128)S(1)}, u32[]{:S(2)}, u32[]{:S(2)}) collective-permute-start(f32[2,16,128]{2,1,0:T(8,128)S(1)} %get-tuple-element.66.st0_ref), channel_id=1, source_target_pairs={{2,0},{4,2},{6,4},{8,6},{10,8},{12,10},{14,12},{16,14},{18,16},{20... | collective-permute-start | bytes 49160 | tf_op jit(solution)/shard_map/ppermute | solution.py:23

commit v9 on v3

--- a/solution.py
+++ b/solution.py
@@ -332,20 +332,21 @@
         own, row1, other0, cache = lax.optimization_barrier((own, row1, other0, cache))
         across = swapped(own, "p", 2)
         beside = swapped(own, "p", 1)
-        row2, row3, other1 = ring_step(row1), ring_step(cache, back=True), swapped(row1, "head", 1)
-        beside, stream, back = lax.optimization_barrier((beside, stream, back))
-        near, back1 = shifted(stream, 1), shifted(back, -1)
-        row2, row3, other1 = lax.optimization_barrier((row2, row3, other1))
-        other2, other3 = swapped(row2, "head", 1), swapped(row3, "head", 1)
-        across, other2, other3, near, back1 = lax.optimization_barrier(
-            (across, other2, other3, near, back1)
+        row2, other1 = ring_step(row1), swapped(row1, "head", 1)
+        row2, other1, beside, cache, other0 = lax.optimization_barrier(
+            (row2, other1, beside, cache, other0)
+        )
+        row3, other3 = ring_step(cache, back=True), ring_step(other0, back=True)
+        other2 = swapped(row2, "head", 1)
+        across, row3, other2, other3, stream = lax.optimization_barrier(
+            (across, row3, other2, other3, stream)
         )
         pieces = [own, beside, across, swapped(across, "p", 1)]
-        far = shifted(near, 1)
+        near = shifted(stream, 1)
         rows = [cache, row1, row2, row3, other0, other1, other2, other3]
         slots = project(place, rows, pieces, devices, capacity)
-        slots, far = lax.optimization_barrier((slots, far))
-        return slots, near, far, back1
+        slots, near, back = lax.optimization_barrier((slots, near, back))
+        return slots, near, shifted(near, 1), shifted(back, -1)
     near, back1 = shifted(stream, 1), shifted(back, -1)
     far = shifted(near, 1)
     targets = [column_block(w_kv, jnp.int32(i)) for i in range(n_z)]
@@ -391,8 +392,9 @@
     memory = lax.all_to_all(slots, SEQ, split_axis=0, concat_axis=0, tiled=True)
     memory = memory.reshape(n_z, slot_count, slots.shape[-1])
 
+    output, grad_q, stats = attend(queries, grad_out, keys, values, kv1, kv2, memory, bias)
+    qg1, stats = lax.optimization_barrier((qg1, stats))
     qg2 = shifted(qg1, -1)
-    output, grad_q, stats = attend(queries, grad_out, keys, values, kv1, kv2, memory, bias)
     all_stats = [stats, shifted(stats, -1), shifted(stats, -2)]
     grad_k, grad_v = key_grads(
         keys, values, queries, grad_out, qg1, qg2, all_stats, back_bias

time: 135 us -> 137 us (1.015); the launches traced: 135 us -> 134 us
  waiting for transfers between devices: 72.1 us -> 82.1 us
  starting transfers between devices: 45.9 us -> 36.2 us
    ppermute x6, waiting for transfers between devices: 9.68 us -> 41 us  [shifted(): return lax.ppermute(value, SEQ, pairs)]
    all_to_all x1, waiting for transfers between devices: 27.7 us -> 0.01 us  [body(): memory = lax.all_to_all(slots, SEQ, split_axis=0, concat_axis=0, tiled=True)]
    ppermute x3 -> x4, waiting for transfers between devices: 6.79 us -> 19.3 us  [ring_step(): lax.ppermute(value, 'z', [(b, a) for a, b in pairs] if back else pairs)]
    ppermute x6, starting transfers between devices: 21.5 us -> 14.6 us  [shifted(): return lax.ppermute(value, SEQ, pairs)]
    ppermute x10 -> x9, waiting for transfers between devices: 28 us -> 21.8 us  [swapped(): lax.ppermute(value, axis, [(i, i ^ mask) for i in range(lax.axis_size(axi...]
    ppermute x3 -> x4, starting transfers between devices: 4.63 us -> 7.43 us  [ring_step(): lax.ppermute(value, 'z', [(b, a) for a, b in pairs] if back else pairs)]
    all_to_all x1, starting transfers between devices: 7.14 us -> 4.37 us  [body(): memory = lax.all_to_all(slots, SEQ, split_axis=0, concat_axis=0, tiled=True)]
    ppermute x10 -> x9, starting transfers between devices: 12.6 us -> 9.83 us  [swapped(): lax.ppermute(value, axis, [(i, i ^ mask) for i in range(lax.axis_size(axi...]
  transfers between devices with their start and end apart: 20 -> 20, of which waited for: 10 -> 14; matrix products, arithmetic and copies ran while one was open for 0% -> 1% of each run, Pallas kernels for 7% -> 7%
where the time goes in v9:
time: 137 us; the launch traced here: 134 us
  waiting for transfers between devices  82.1 us (60%)
  starting transfers between devices  36.2 us (26%)
  Pallas kernels  12.5 us (9%)
  local copies, waits for them, and re-layouts  1.41 us (1%)
    ppermute x6, waiting for transfers between devices, shifted(): return lax.ppermute(value, SEQ, pairs)  41 us
    ppermute x9, waiting for transfers between devices, swapped(): lax.ppermute(value, axis, [(i, i ^ mask) for i in range(lax.axis_size(axi...  21.8 us
    ppermute x4, waiting for transfers between devices, ring_step(): lax.ppermute(value, 'z', [(b, a) for a, b in pairs] if back else pairs)  19.3 us
    ppermute x6, starting transfers between devices, shifted(): return lax.ppermute(value, SEQ, pairs)  14.6 us
    ppermute x9, starting transfers between devices, swapped(): lax.ppermute(value, axis, [(i, i ^ mask) for i in range(lax.axis_size(axi...  9.83 us
    ppermute x4, starting transfers between devices, ring_step(): lax.ppermute(value, 'z', [(b, a) for a, b in pairs] if back else pairs)  7.43 us
    pallas_call x1, Pallas kernels, attend(): pl.pallas_call(attend_kernel, grid=(steps,), in_specs=[flat, flat, flat,...  5 us
    pallas_call x1, Pallas kernels, project(): pl.pallas_call(project_kernel, in_specs=[whole] * (1 + len(rows) + n_p),...  4.59 us
  transfers between devices with their start and end apart: 20, of which 14 were waited for; matrix products, arithmetic and copies ran while one was open for 1% of the time, Pallas kernels for 7%

profile of v9, /device:TPU:16, one launch (start us, length us, event | category | flops | bytes accessed | tf_op | source)
XLA Modules:
  0.0 134.1 jit_solution(10699421936257034095)
XLA Ops:
  0.6 0.0 copy-start.4
  0.7 0.0 copy-start.2
  0.7 0.0 copy-start.3
  0.7 1.4 %constant_dynamic-slice_fusion = (bf16[1,160,640]{2,1,0:T(8,128)(2,1)S(1)}, bf16[160,640]{1,0:T(8,128)(2,1)S(1)}, bf16[160,640]{1,0:T(8,128)(2,1)S(1)}, bf16[160,640]{1,0:T(8,128)(2,1)S(1)}) fusion(bf16[2,160,1280]{2,1,0:T(8,128)(2,1)} %param.13, s32[]{:T(128)S(6)} %select_n.24, s32[]{:T(128)S(6)} %select_n.25, s32[]{:T(128)S(6)} %select_n.26, ...), kind=kLoop, calls=%fused_computation.6 | loop fusion | bytes 1638432 | tf_op jit(solution)/shard_map/dynamic_slice | solution.py:312
  2.1 1.6 %collective-permute-start = (bf16[160,640]{1,0:T(8,128)(2,1)S(1)}, bf16[160,640]{1,0:T(8,128)(2,1)S(1)}, u32[]{:S(2)}, u32[]{:S(2)}) collective-permute-start(bf16[160,640]{1,0:T(8,128)(2,1)S(1)} %get-tuple-element.59), channel_id=1, source_target_pairs={{0,8},{8,0},{16,24},{24,16},{1,9},{9,1},{17,25},{25,17},{2,10},{10... | collective-permute-start | bytes 614408 | tf_op jit(solution)/shard_map/ppermute | solution.py:25
  3.7 0.3 collective-permute-start.1
  4.1 1.6 %collective-permute-start.2 = (bf16[160,640]{1,0:T(8,128)(2,1)S(1)}, bf16[160,640]{1,0:T(8,128)(2,1)S(1)}, u32[]{:S(2)}, u32[]{:S(2)}) collective-permute-start(bf16[160,640]{1,0:T(8,128)(2,1)S(1)} %get-tuple-element.60), channel_id=1, source_target_pairs={{0,24},{8,16},{16,8},{24,0},{1,25},{9,17},{17,9},{25,1},{2,26},{10... | collective-permute-start | bytes 614408 | tf_op jit(solution)/shard_map/ppermute | solution.py:25
  5.6 0.0 copy-done.4
  5.6 1.0 collective-permute-start.3
  6.6 1.7 %collective-permute-start.4 = (bf16[128,1280]{1,0:T(8,128)(2,1)S(1)}, bf16[128,1280]{1,0:T(8,128)(2,1)S(1)}, u32[]{:S(2)}, u32[]{:S(2)}) collective-permute-start(bf16[128,1280]{1,0:T(8,128)(2,1)S(1)} %copy-done.4), channel_id=1, source_target_pairs={{0,1},{1,0},{2,3},{3,2},{4,5},{5,4},{6,7},{7,6},{8,9},{9,8},{10,11... | collective-permute-start | bytes 983048 | tf_op jit(solution)/shard_map/ppermute | solution.py:25
  8.4 2.7 %collective-permute-done = bf16[160,640]{1,0:T(8,128)(2,1)S(1)} collective-permute-done((bf16[160,640]{1,0:T(8,128)(2,1)S(1)}, bf16[160,640]{1,0:T(8,128)(2,1)S(1)}, u32[]{:S(2)}, u32[]{:S(2)}) %collective-permute-start) | collective-permute-done | bytes 204832 | tf_op jit(solution)/shard_map/ppermute | solution.py:25
  11.1 7.1 %collective-permute-done.1 = bf16[160,640]{1,0:T(8,128)(2,1)S(1)} collective-permute-done((bf16[160,640]{1,0:T(8,128)(2,1)S(1)}, bf16[160,640]{1,0:T(8,128)(2,1)S(1)}, u32[]{:S(2)}, u32[]{:S(2)}) %collective-permute-start.1) | collective-permute-done | bytes 204832 | tf_op jit(solution)/shard_map/ppermute | solution.py:25
  18.2 6.6 %collective-permute-done.2 = bf16[160,640]{1,0:T(8,128)(2,1)S(1)} collective-permute-done((bf16[160,640]{1,0:T(8,128)(2,1)S(1)}, bf16[160,640]{1,0:T(8,128)(2,1)S(1)}, u32[]{:S(2)}, u32[]{:S(2)}) %collective-permute-start.2) | collective-permute-done | bytes 204832 | tf_op jit(solution)/shard_map/ppermute | solution.py:25
  24.8 0.0 copy-start.6
  24.8 0.0 copy-start.7
  24.8 0.0 copy-start
  24.8 0.0 copy-start.1
  24.8 0.1 pad_maximum_fusion.refs_8_
  24.9 3.4 %collective-permute-done.3.refs_1_ = bf16[128,1280]{1,0:T(8,128)(2,1)S(1)} collective-permute-done((bf16[128,1280]{1,0:T(8,128)(2,1)S(1)}, bf16[128,1280]{1,0:T(8,128)(2,1)S(1)}, u32[]{:S(2)}, u32[]{:S(2)}) %collective-permute-start.3) | collective-permute-done | bytes 327712 | tf_op jit(solution)/shard_map/ppermute | solution.py:317
  28.3 0.0 collective-permute-done.4.refs_4_
  28.3 0.0 collective-permute-start.7
  28.4 1.5 %collective-permute-start.8 = (bf16[4,160,640]{2,1,0:T(8,128)(2,1)S(1)}, bf16[4,160,640]{2,1,0:T(8,128)(2,1)S(1)}, u32[]{:S(2)}, u32[]{:S(2)}) collective-permute-start(bf16[4,160,640]{2,1,0:T(8,128)(2,1)S(1)} %pad_maximum_fusion.refs_8_), channel_id=1, source_target_pairs={{0,4},{2,6},{4,0},{6,2},{1,5},{3,7},{5,1},{7,3},{8,12},{10,14},{12... | collective-permute-start | bytes 2457608 | tf_op jit(solution)/shard_map/ppermute | solution.py:25
  29.8 3.4 %collective-permute-start.5 = (bf16[128,1280]{1,0:T(8,128)(2,1)S(1)}, bf16[128,1280]{1,0:T(8,128)(2,1)S(1)}, u32[]{:S(2)}, u32[]{:S(2)}) collective-permute-start(bf16[128,1280]{1,0:T(8,128)(2,1)S(1)} %collective-permute-done.3.refs_1_), channel_id=1, source_target_pairs={{0,8},{8,24},{24,16},{16,0},{1,9},{9,25},{25,17},{17,1},{2,10},{10... | collective-permute-start | bytes 983048 | tf_op jit(solution)/shard_map/ppermute | solution.py:317
  33.2 1.5 %collective-permute-start.6 = (bf16[128,1280]{1,0:T(8,128)(2,1)S(1)}, bf16[128,1280]{1,0:T(8,128)(2,1)S(1)}, u32[]{:S(2)}, u32[]{:S(2)}) collective-permute-start(bf16[128,1280]{1,0:T(8,128)(2,1)S(1)} %collective-permute-done.3.refs_1_), channel_id=1, source_target_pairs={{0,1},{1,0},{2,3},{3,2},{4,5},{5,4},{6,7},{7,6},{8,9},{9,8},{10,11... | collective-permute-start | bytes 983048 | tf_op jit(solution)/shard_map/ppermute | solution.py:25
  34.7 6.7 %collective-permute-done.5.refs_2_ = bf16[128,1280]{1,0:T(8,128)(2,1)S(1)} collective-permute-done((bf16[128,1280]{1,0:T(8,128)(2,1)S(1)}, bf16[128,1280]{1,0:T(8,128)(2,1)S(1)}, u32[]{:S(2)}, u32[]{:S(2)}) %collective-permute-start.5) | collective-permute-done | bytes 327712 | tf_op jit(solution)/shard_map/ppermute | solution.py:317
  41.4 1.4 %collective-permute-done.6.refs_5_ = bf16[128,1280]{1,0:T(8,128)(2,1)S(1)} collective-permute-done((bf16[128,1280]{1,0:T(8,128)(2,1)S(1)}, bf16[128,1280]{1,0:T(8,128)(2,1)S(1)}, u32[]{:S(2)}, u32[]{:S(2)}) %collective-permute-start.6) | collective-permute-done | bytes 327712 | tf_op jit(solution)/shard_map/ppermute | solution.py:25
  42.8 0.0 collective-permute-done.7.refs_9_
  42.8 1.5 %collective-permute-start.10 = (bf16[128,1280]{1,0:T(8,128)(2,1)S(1)}, bf16[128,1280]{1,0:T(8,128)(2,1)S(1)}, u32[]{:S(2)}, u32[]{:S(2)}) collective-permute-start(bf16[128,1280]{1,0:T(8,128)(2,1)S(1)} %collective-permute-done.5.refs_2_), channel_id=1, source_target_pairs={{0,1},{1,0},{2,3},{3,2},{4,5},{5,4},{6,7},{7,6},{8,9},{9,8},{10,11... | collective-permute-start | bytes 983048 | tf_op jit(solution)/shard_map/ppermute | solution.py:25
  44.3 1.3 collective-permute-start.11
  45.6 1.7 %collective-permute-start.9 = (bf16[128,1280]{1,0:T(8,128)(2,1)S(1)}, bf16[128,1280]{1,0:T(8,128)(2,1)S(1)}, u32[]{:S(2)}, u32[]{:S(2)}) collective-permute-start(bf16[128,1280]{1,0:T(8,128)(2,1)S(1)} %copy-done.4), channel_id=1, source_target_pairs={{8,0},{24,8},{16,24},{0,16},{9,1},{25,9},{17,25},{1,17},{10,2},{26... | collective-permute-start | bytes 983048 | tf_op jit(solution)/shard_map/ppermute | solution.py:317
  47.3 0.0 copy-done.2
  47.4 0.0 copy-done.3
  47.4 0.1 pad_maximum_fusion.1
  47.4 1.6 %collective-permute-done.8.refs_10_ = bf16[4,160,640]{2,1,0:T(8,128)(2,1)S(1)} collective-permute-done((bf16[4,160,640]{2,1,0:T(8,128)(2,1)S(1)}, bf16[4,160,640]{2,1,0:T(8,128)(2,1)S(1)}, u32[]{:S(2)}, u32[]{:S(2)}) %collective-permute-start.8) | collective-permute-done | bytes 819232 | tf_op jit(solution)/shard_map/ppermute | solution.py:25
  49.0 2.5 %collective-permute-done.10.refs_6_ = bf16[128,1280]{1,0:T(8,128)(2,1)S(1)} collective-permute-done((bf16[128,1280]{1,0:T(8,128)(2,1)S(1)}, bf16[128,1280]{1,0:T(8,128)(2,1)S(1)}, u32[]{:S(2)}, u32[]{:S(2)}) %collective-permute-start.10) | collective-permute-done | bytes 327712 | tf_op jit(solution)/shard_map/ppermute | solution.py:25
  51.5 4.4 %collective-permute-done.11.refs_7_ = bf16[128,1280]{1,0:T(8,128)(2,1)S(1)} collective-permute-done((bf16[128,1280]{1,0:T(8,128)(2,1)S(1)}, bf16[128,1280]{1,0:T(8,128)(2,1)S(1)}, u32[]{:S(2)}, u32[]{:S(2)}) %collective-permute-start.11) | collective-permute-done | bytes 327712 | tf_op jit(solution)/shard_map/ppermute | solution.py:317
  55.9 4.8 %collective-permute-done.9.refs_3_ = bf16[128,1280]{1,0:T(8,128)(2,1)S(1)} collective-permute-done((bf16[128,1280]{1,0:T(8,128)(2,1)S(1)}, bf16[128,1280]{1,0:T(8,128)(2,1)S(1)}, u32[]{:S(2)}, u32[]{:S(2)}) %collective-permute-start.9) | collective-permute-done | bytes 327712 | tf_op jit(solution)/shard_map/ppermute | solution.py:317
  60.7 0.0 collective-permute-start.12
  60.7 2.4 %collective-permute-start.13 = (bf16[2,128,1280]{2,1,0:T(8,128)(2,1)S(1)}, bf16[2,128,1280]{2,1,0:T(8,128)(2,1)}, u32[]{:S(2)}, u32[]{:S(2)}) collective-permute-start(bf16[2,128,1280]{2,1,0:T(8,128)(2,1)S(1)} %pad_maximum_fusion.1), channel_id=1, source_target_pairs={{0,2},{2,4},{4,6},{6,8},{8,10},{10,12},{12,14},{14,16},{16,18},{18... | collective-permute-start | bytes 1966088 | tf_op jit(solution)/shard_map/ppermute | solution.py:21
  63.1 0.0 copy-done.6
  63.1 0.0 copy-done.7
  63.1 0.3 prepare.1
  63.3 0.0 copy-start.5
  63.3 0.0 copy-done
  63.4 0.0 copy-done.1
  63.4 0.9 pad_maximum_fusion.2
  64.3 0.0 collective-permute-done.12.refs_11_
  64.3 4.6 %project.1 = bf16[16,4,16,640]{3,2,1,0:T(8,128)(2,1)} custom-call(s32[4,1,128]{2,1,0:T(1,128)S(1)} %get-tuple-element.31.place_ref, bf16[128,1280]{1,0:T(8,128)(2,1)S(1)} %copy-done.4, bf16[128,1280]{1,0:T(8,128)(2,1)S(1)} %collective-permute-done.3.refs_1_, bf16[128,1280]{1,0:T(8,128)(2,1)S(1)} %collective-permute-done.5.refs_2_, ...), custom_call_target="tpu_custom_call" | custom-call | flops 1677721600 | bytes 8388608 | tf_op jit(solution)/shard_map/project/pallas_call | solution.py:225
  68.9 0.0 copy-done.5
  68.9 4.7 %collective-permute-done.13.kv1_ref = bf16[2,128,1280]{2,1,0:T(8,128)(2,1)} collective-permute-done((bf16[2,128,1280]{2,1,0:T(8,128)(2,1)S(1)}, bf16[2,128,1280]{2,1,0:T(8,128)(2,1)}, u32[]{:S(2)}, u32[]{:S(2)}) %collective-permute-start.13) | collective-permute-done | bytes 655392 | tf_op jit(solution)/shard_map/ppermute | solution.py:21
  73.6 4.4 %all-to-all-start = ((bf16[16,4,16,640]{3,2,1,0:T(8,128)(2,1)}), bf16[16,4,16,640]{3,2,1,0:T(8,128)(2,1)S(1)}, u32[]{:S(2)}, u32[]{:S(2)}) async-start(bf16[16,4,16,640]{3,2,1,0:T(8,128)(2,1)} %project.1), calls=%async_computation | async-start | bytes 2621440 | tf_op jit(solution)/shard_map/all_to_all | solution.py:392
  77.9 2.0 %collective-permute-start.14 = (bf16[2,128,1280]{2,1,0:T(8,128)(2,1)}, bf16[2,128,1280]{2,1,0:T(8,128)(2,1)}, u32[]{:S(2)}, u32[]{:S(2)}) collective-permute-start(bf16[2,128,1280]{2,1,0:T(8,128)(2,1)} %collective-permute-done.13.kv1_ref), channel_id=1, source_target_pairs={{0,2},{2,4},{4,6},{6,8},{8,10},{10,12},{12,14},{14,16},{16,18},{18... | collective-permute-start | bytes 1966088 | tf_op jit(solution)/shard_map/ppermute | solution.py:21
  80.0 4.4 %collective-permute-start.15 = (bf16[2,128,1280]{2,1,0:T(8,128)(2,1)}, bf16[2,128,1280]{2,1,0:T(8,128)(2,1)S(1)}, u32[]{:S(2)}, u32[]{:S(2)}) collective-permute-start(bf16[2,128,1280]{2,1,0:T(8,128)(2,1)} %pad_maximum_fusion.2), channel_id=1, source_target_pairs={{2,0},{4,2},{6,4},{8,6},{10,8},{12,10},{14,12},{16,14},{18,16},{20... | collective-permute-start | bytes 1966088 | tf_op jit(solution)/shard_map/ppermute | solution.py:21
  84.4 31.5 %collective-permute-done.14.kv2_ref = bf16[2,128,1280]{2,1,0:T(8,128)(2,1)} collective-permute-done((bf16[2,128,1280]{2,1,0:T(8,128)(2,1)}, bf16[2,128,1280]{2,1,0:T(8,128)(2,1)}, u32[]{:S(2)}, u32[]{:S(2)}) %collective-permute-start.14) | collective-permute-done | bytes 655392 | tf_op jit(solution)/shard_map/ppermute | solution.py:21
  115.9 0.0 all-to-all-done
  115.9 5.0 %attend.1 = (bf16[128,1280]{1,0:T(8,128)(2,1)}, bf16[128,1280]{1,0:T(8,128)(2,1)}, f32[2,16,128]{2,1,0:T(8,128)S(1)}) custom-call(bf16[128,1280]{1,0:T(8,128)(2,1)S(1)} %copy-done, bf16[128,1280]{1,0:T(8,128)(2,1)S(1)} %copy-done.1, bf16[128,1280]{1,0:T(8,128)(2,1)S(1)} %copy-done.2, bf16[128,1280]{1,0:T(8,128)(2,1)S(1)} %copy-done.3, ...), custom_call_target="tpu_custom_call" | custom-call | flops 838860800 | bytes 6291456 | tf_op jit(solution)/shard_map/attend/pallas_call | solution.py:103
  120.9 0.0 collective-permute-done.15.qg1_ref
  120.9 1.9 %collective-permute-start.16 = (bf16[2,128,1280]{2,1,0:T(8,128)(2,1)S(1)}, bf16[2,128,1280]{2,1,0:T(8,128)(2,1)S(1)}, u32[]{:S(2)}, u32[]{:S(2)}) collective-permute-start(bf16[2,128,1280]{2,1,0:T(8,128)(2,1)S(1)} %collective-permute-done.15.qg1_ref), channel_id=1, source_target_pairs={{2,0},{4,2},{6,4},{8,6},{10,8},{12,10},{14,12},{16,14},{18,16},{20... | collective-permute-start | bytes 1966088 | tf_op jit(solution)/shard_map/ppermute | solution.py:21
  122.9 1.9 %collective-permute-start.17 = (f32[2,16,128]{2,1,0:T(8,128)S(1)}, f32[2,16,128]{2,1,0:T(8,128)S(1)}, u32[]{:S(2)}, u32[]{:S(2)}) collective-permute-start(f32[2,16,128]{2,1,0:T(8,128)S(1)} %get-tuple-element.54.st0_ref), channel_id=1, source_target_pairs={{2,0},{4,2},{6,4},{8,6},{10,8},{12,10},{14,12},{16,14},{18,16},{20... | collective-permute-start | bytes 49160 | tf_op jit(solution)/shard_map/ppermute | solution.py:21
  124.8 1.9 %collective-permute-start.18 = (f32[2,16,128]{2,1,0:T(8,128)S(1)}, f32[2,16,128]{2,1,0:T(8,128)S(1)}, u32[]{:S(2)}, u32[]{:S(2)}) collective-permute-start(f32[2,16,128]{2,1,0:T(8,128)S(1)} %get-tuple-element.54.st0_ref), channel_id=1, source_target_pairs={{4,0},{6,2},{8,4},{10,6},{12,8},{14,10},{16,12},{18,14},{20,16},{2... | collective-permute-start | bytes 49160 | tf_op jit(solution)/shard_map/ppermute | solution.py:21
  126.7 4.6 %collective-permute-done.17.st1_ref = f32[2,16,128]{2,1,0:T(8,128)S(1)} collective-permute-done((f32[2,16,128]{2,1,0:T(8,128)S(1)}, f32[2,16,128]{2,1,0:T(8,128)S(1)}, u32[]{:S(2)}, u32[]{:S(2)}) %collective-permute-start.17) | collective-permute-done | bytes 16416 | tf_op jit(solution)/shard_map/ppermute | solution.py:21
  131.3 0.2 collective-permute-done.18.st2_ref
  131.5 0.0 collective-permute-done.16.qg2_ref
  131.5 2.7 %key_grads.1 = (bf16[128,1280]{1,0:T(8,128)(2,1)}, bf16[128,1280]{1,0:T(8,128)(2,1)}) custom-call(bf16[128,1280]{1,0:T(8,128)(2,1)S(1)} %copy-done.2, bf16[128,1280]{1,0:T(8,128)(2,1)S(1)} %copy-done.3, bf16[128,1280]{1,0:T(8,128)(2,1)S(1)} %copy-done, bf16[128,1280]{1,0:T(8,128)(2,1)S(1)} %copy-done.1, ...), custom_call_target="tpu_custom_call" | custom-call | flops 503316480 | bytes 4194304 | tf_op jit(solution)/shard_map/key_grads/pallas_call | solution.py:166
Async XLA Ops:
  0.6 5.0 %copy-start.4 = (bf16[128,1280]{1,0:T(8,128)(2,1)S(1)}, bf16[128,1280]{1,0:T(8,128)(2,1)}, u32[]{:S(2)}) copy-start(bf16[128,1280]{1,0:T(8,128)(2,1)} %refs_0_) | copy-start | bytes 983044
  0.7 46.7 %copy-start.2 = (bf16[128,1280]{1,0:T(8,128)(2,1)S(1)}, bf16[128,1280]{1,0:T(8,128)(2,1)}, u32[]{:S(2)}) copy-start(bf16[128,1280]{1,0:T(8,128)(2,1)} %k_ref.3) | copy-start | bytes 983044
  0.7 46.7 %copy-start.3 = (bf16[128,1280]{1,0:T(8,128)(2,1)S(1)}, bf16[128,1280]{1,0:T(8,128)(2,1)}, u32[]{:S(2)}) copy-start(bf16[128,1280]{1,0:T(8,128)(2,1)} %v_ref.3) | copy-start | bytes 983044
  2.1 9.0 %collective-permute-start = (bf16[160,640]{1,0:T(8,128)(2,1)S(1)}, bf16[160,640]{1,0:T(8,128)(2,1)S(1)}, u32[]{:S(2)}, u32[]{:S(2)}) collective-permute-start(bf16[160,640]{1,0:T(8,128)(2,1)S(1)} %get-tuple-element.59), channel_id=1, source_target_pairs={{0,8},{8,0},{16,24},{24,16},{1,9},{9,1},{17,25},{25,17},{2,10},{10... | collective-permute-start | bytes 614408 | tf_op jit(solution)/shard_map/ppermute | solution.py:25
  3.7 14.5 %collective-permute-start.1 = (bf16[160,640]{1,0:T(8,128)(2,1)S(1)}, bf16[160,640]{1,0:T(8,128)(2,1)S(1)}, u32[]{:S(2)}, u32[]{:S(2)}) collective-permute-start(bf16[160,640]{1,0:T(8,128)(2,1)S(1)} %get-tuple-element.61), channel_id=1, source_target_pairs={{0,16},{8,24},{16,0},{24,8},{1,17},{9,25},{17,1},{25,9},{2,18},{10... | collective-permute-start | bytes 614408 | tf_op jit(solution)/shard_map/ppermute | solution.py:25
  4.1 20.7 %collective-permute-start.2 = (bf16[160,640]{1,0:T(8,128)(2,1)S(1)}, bf16[160,640]{1,0:T(8,128)(2,1)S(1)}, u32[]{:S(2)}, u32[]{:S(2)}) collective-permute-start(bf16[160,640]{1,0:T(8,128)(2,1)S(1)} %get-tuple-element.60), channel_id=1, source_target_pairs={{0,24},{8,16},{16,8},{24,0},{1,25},{9,17},{17,9},{25,1},{2,26},{10... | collective-permute-start | bytes 614408 | tf_op jit(solution)/shard_map/ppermute | solution.py:25
  5.6 22.7 %collective-permute-start.3 = (bf16[128,1280]{1,0:T(8,128)(2,1)S(1)}, bf16[128,1280]{1,0:T(8,128)(2,1)S(1)}, u32[]{:S(2)}, u32[]{:S(2)}) collective-permute-start(bf16[128,1280]{1,0:T(8,128)(2,1)S(1)} %copy-done.4), channel_id=1, source_target_pairs={{0,8},{8,24},{24,16},{16,0},{1,9},{9,25},{25,17},{17,1},{2,10},{10... | collective-permute-start | bytes 983048 | tf_op jit(solution)/shard_map/ppermute | solution.py:317
  6.6 21.7 %collective-permute-start.4 = (bf16[128,1280]{1,0:T(8,128)(2,1)S(1)}, bf16[128,1280]{1,0:T(8,128)(2,1)S(1)}, u32[]{:S(2)}, u32[]{:S(2)}) collective-permute-start(bf16[128,1280]{1,0:T(8,128)(2,1)S(1)} %copy-done.4), channel_id=1, source_target_pairs={{0,1},{1,0},{2,3},{3,2},{4,5},{5,4},{6,7},{7,6},{8,9},{9,8},{10,11... | collective-permute-start | bytes 983048 | tf_op jit(solution)/shard_map/ppermute | solution.py:25
  24.8 38.3 %copy-start.6 = (s32[2048]{0:T(1024)S(1)}, s32[2048]{0:T(1024)}, u32[]{:S(2)}) copy-start(s32[2048]{0:T(1024)} %param.15) | copy-start | bytes 24580
  24.8 38.3 %copy-start.7 = (s32[2048]{0:T(1024)S(1)}, s32[2048]{0:T(1024)}, u32[]{:S(2)}) copy-start(s32[2048]{0:T(1024)} %param.14) | copy-start | bytes 24580
  24.8 38.6 %copy-start = (bf16[128,1280]{1,0:T(8,128)(2,1)S(1)}, bf16[128,1280]{1,0:T(8,128)(2,1)}, u32[]{:S(2)}) copy-start(bf16[128,1280]{1,0:T(8,128)(2,1)} %q_ref.3) | copy-start | bytes 983044
  24.8 38.6 %copy-start.1 = (bf16[128,1280]{1,0:T(8,128)(2,1)S(1)}, bf16[128,1280]{1,0:T(8,128)(2,1)}, u32[]{:S(2)}) copy-start(bf16[128,1280]{1,0:T(8,128)(2,1)} %g_ref.3) | copy-start | bytes 983044
  28.3 14.4 %collective-permute-start.7 = (bf16[4,160,640]{2,1,0:T(8,128)(2,1)S(1)}, bf16[4,160,640]{2,1,0:T(8,128)(2,1)S(1)}, u32[]{:S(2)}, u32[]{:S(2)}) collective-permute-start(bf16[4,160,640]{2,1,0:T(8,128)(2,1)S(1)} %pad_maximum_fusion.refs_8_), channel_id=1, source_target_pairs={{0,2},{2,0},{4,6},{6,4},{1,3},{3,1},{5,7},{7,5},{8,10},{10,8},{12,... | collective-permute-start | bytes 2457608 | tf_op jit(solution)/shard_map/ppermute | solution.py:25
  28.4 20.7 %collective-permute-start.8 = (bf16[4,160,640]{2,1,0:T(8,128)(2,1)S(1)}, bf16[4,160,640]{2,1,0:T(8,128)(2,1)S(1)}, u32[]{:S(2)}, u32[]{:S(2)}) collective-permute-start(bf16[4,160,640]{2,1,0:T(8,128)(2,1)S(1)} %pad_maximum_fusion.refs_8_), channel_id=1, source_target_pairs={{0,4},{2,6},{4,0},{6,2},{1,5},{3,7},{5,1},{7,3},{8,12},{10,14},{12... | collective-permute-start | bytes 2457608 | tf_op jit(solution)/shard_map/ppermute | solution.py:25
  29.8 11.6 %collective-permute-start.5 = (bf16[128,1280]{1,0:T(8,128)(2,1)S(1)}, bf16[128,1280]{1,0:T(8,128)(2,1)S(1)}, u32[]{:S(2)}, u32[]{:S(2)}) collective-permute-start(bf16[128,1280]{1,0:T(8,128)(2,1)S(1)} %collective-permute-done.3.refs_1_), channel_id=1, source_target_pairs={{0,8},{8,24},{24,16},{16,0},{1,9},{9,25},{25,17},{17,1},{2,10},{10... | collective-permute-start | bytes 983048 | tf_op jit(solution)/shard_map/ppermute | solution.py:317
  33.2 9.6 %collective-permute-start.6 = (bf16[128,1280]{1,0:T(8,128)(2,1)S(1)}, bf16[128,1280]{1,0:T(8,128)(2,1)S(1)}, u32[]{:S(2)}, u32[]{:S(2)}) collective-permute-start(bf16[128,1280]{1,0:T(8,128)(2,1)S(1)} %collective-permute-done.3.refs_1_), channel_id=1, source_target_pairs={{0,1},{1,0},{2,3},{3,2},{4,5},{5,4},{6,7},{7,6},{8,9},{9,8},{10,11... | collective-permute-start | bytes 983048 | tf_op jit(solution)/shard_map/ppermute | solution.py:25
  42.8 8.7 %collective-permute-start.10 = (bf16[128,1280]{1,0:T(8,128)(2,1)S(1)}, bf16[128,1280]{1,0:T(8,128)(2,1)S(1)}, u32[]{:S(2)}, u32[]{:S(2)}) collective-permute-start(bf16[128,1280]{1,0:T(8,128)(2,1)S(1)} %collective-permute-done.5.refs_2_), channel_id=1, source_target_pairs={{0,1},{1,0},{2,3},{3,2},{4,5},{5,4},{6,7},{7,6},{8,9},{9,8},{10,11... | collective-permute-start | bytes 983048 | tf_op jit(solution)/shard_map/ppermute | solution.py:25
  44.3 11.5 %collective-permute-start.11 = (bf16[128,1280]{1,0:T(8,128)(2,1)S(1)}, bf16[128,1280]{1,0:T(8,128)(2,1)S(1)}, u32[]{:S(2)}, u32[]{:S(2)}) collective-permute-start(bf16[128,1280]{1,0:T(8,128)(2,1)S(1)} %collective-permute-done.4.refs_4_), channel_id=1, source_target_pairs={{8,0},{24,8},{16,24},{0,16},{9,1},{25,9},{17,25},{1,17},{10,2},{26... | collective-permute-start | bytes 983048 | tf_op jit(solution)/shard_map/ppermute | solution.py:317
  45.6 15.1 %collective-permute-start.9 = (bf16[128,1280]{1,0:T(8,128)(2,1)S(1)}, bf16[128,1280]{1,0:T(8,128)(2,1)S(1)}, u32[]{:S(2)}, u32[]{:S(2)}) collective-permute-start(bf16[128,1280]{1,0:T(8,128)(2,1)S(1)} %copy-done.4), channel_id=1, source_target_pairs={{8,0},{24,8},{16,24},{0,16},{9,1},{25,9},{17,25},{1,17},{10,2},{26... | collective-permute-start | bytes 983048 | tf_op jit(solution)/shard_map/ppermute | solution.py:317
  60.7 3.6 %collective-permute-start.12 = (bf16[4,160,640]{2,1,0:T(8,128)(2,1)S(1)}, bf16[4,160,640]{2,1,0:T(8,128)(2,1)S(1)}, u32[]{:S(2)}, u32[]{:S(2)}) collective-permute-start(bf16[4,160,640]{2,1,0:T(8,128)(2,1)S(1)} %collective-permute-done.8.refs_10_), channel_id=1, source_target_pairs={{0,2},{2,0},{4,6},{6,4},{1,3},{3,1},{5,7},{7,5},{8,10},{10,8},{12,... | collective-permute-start | bytes 2457608 | tf_op jit(solution)/shard_map/ppermute | solution.py:25
  60.7 12.9 %collective-permute-start.13 = (bf16[2,128,1280]{2,1,0:T(8,128)(2,1)S(1)}, bf16[2,128,1280]{2,1,0:T(8,128)(2,1)}, u32[]{:S(2)}, u32[]{:S(2)}) collective-permute-start(bf16[2,128,1280]{2,1,0:T(8,128)(2,1)S(1)} %pad_maximum_fusion.1), channel_id=1, source_target_pairs={{0,2},{2,4},{4,6},{6,8},{8,10},{10,12},{12,14},{14,16},{16,18},{18... | collective-permute-start | bytes 1966088 | tf_op jit(solution)/shard_map/ppermute | solution.py:21
  63.3 5.5 %copy-start.5 = (bf16[128,640]{1,0:T(8,128)(2,1)}, bf16[128,640]{1,0:T(8,128)(2,1)S(1)}, u32[]{:S(2)}) copy-start(bf16[128,640]{1,0:T(8,128)(2,1)S(1)} %get-tuple-element.48.bias_ref) | copy-start | bytes 491524
  73.6 42.4 %all-to-all-start = ((bf16[16,4,16,640]{3,2,1,0:T(8,128)(2,1)}), bf16[16,4,16,640]{3,2,1,0:T(8,128)(2,1)S(1)}, u32[]{:S(2)}, u32[]{:S(2)}) async-start(bf16[16,4,16,640]{3,2,1,0:T(8,128)(2,1)} %project.1), calls=%async_computation | async-start | bytes 2621440 | tf_op jit(solution)/shard_map/all_to_all | solution.py:392
  77.9 38.0 %collective-permute-start.14 = (bf16[2,128,1280]{2,1,0:T(8,128)(2,1)}, bf16[2,128,1280]{2,1,0:T(8,128)(2,1)}, u32[]{:S(2)}, u32[]{:S(2)}) collective-permute-start(bf16[2,128,1280]{2,1,0:T(8,128)(2,1)} %collective-permute-done.13.kv1_ref), channel_id=1, source_target_pairs={{0,2},{2,4},{4,6},{6,8},{8,10},{10,12},{12,14},{14,16},{16,18},{18... | collective-permute-start | bytes 1966088 | tf_op jit(solution)/shard_map/ppermute | solution.py:21
  80.0 41.0 %collective-permute-start.15 = (bf16[2,128,1280]{2,1,0:T(8,128)(2,1)}, bf16[2,128,1280]{2,1,0:T(8,128)(2,1)S(1)}, u32[]{:S(2)}, u32[]{:S(2)}) collective-permute-start(bf16[2,128,1280]{2,1,0:T(8,128)(2,1)} %pad_maximum_fusion.2), channel_id=1, source_target_pairs={{2,0},{4,2},{6,4},{8,6},{10,8},{12,10},{14,12},{16,14},{18,16},{20... | collective-permute-start | bytes 1966088 | tf_op jit(solution)/shard_map/ppermute | solution.py:21
  120.9 10.5 %collective-permute-start.16 = (bf16[2,128,1280]{2,1,0:T(8,128)(2,1)S(1)}, bf16[2,128,1280]{2,1,0:T(8,128)(2,1)S(1)}, u32[]{:S(2)}, u32[]{:S(2)}) collective-permute-start(bf16[2,128,1280]{2,1,0:T(8,128)(2,1)S(1)} %collective-permute-done.15.qg1_ref), channel_id=1, source_target_pairs={{2,0},{4,2},{6,4},{8,6},{10,8},{12,10},{14,12},{16,14},{18,16},{20... | collective-permute-start | bytes 1966088 | tf_op jit(solution)/shard_map/ppermute | solution.py:21
  122.9 8.4 %collective-permute-start.17 = (f32[2,16,128]{2,1,0:T(8,128)S(1)}, f32[2,16,128]{2,1,0:T(8,128)S(1)}, u32[]{:S(2)}, u32[]{:S(2)}) collective-permute-start(f32[2,16,128]{2,1,0:T(8,128)S(1)} %get-tuple-element.54.st0_ref), channel_id=1, source_target_pairs={{2,0},{4,2},{6,4},{8,6},{10,8},{12,10},{14,12},{16,14},{18,16},{20... | collective-permute-start | bytes 49160 | tf_op jit(solution)/shard_map/ppermute | solution.py:21
  124.8 6.7 %collective-permute-start.18 = (f32[2,16,128]{2,1,0:T(8,128)S(1)}, f32[2,16,128]{2,1,0:T(8,128)S(1)}, u32[]{:S(2)}, u32[]{:S(2)}) collective-permute-start(f32[2,16,128]{2,1,0:T(8,128)S(1)} %get-tuple-element.54.st0_ref), channel_id=1, source_target_pairs={{4,0},{6,2},{8,4},{10,6},{12,8},{14,10},{16,12},{18,14},{20,16},{2... | collective-permute-start | bytes 49160 | tf_op jit(solution)/shard_map/ppermute | solution.py:21

commit v10 on v3

--- a/solution.py
+++ b/solution.py
@@ -332,19 +332,19 @@
         own, row1, other0, cache = lax.optimization_barrier((own, row1, other0, cache))
         across = swapped(own, "p", 2)
         beside = swapped(own, "p", 1)
-        row2, row3, other1 = ring_step(row1), ring_step(cache, back=True), swapped(row1, "head", 1)
-        beside, stream, back = lax.optimization_barrier((beside, stream, back))
+        row2, other1 = ring_step(row1), swapped(row1, "head", 1)
+        row2, other1, beside, cache, other0, stream, back = lax.optimization_barrier(
+            (row2, other1, beside, cache, other0, stream, back)
+        )
+        row3, other3 = ring_step(cache, back=True), ring_step(other0, back=True)
+        other2 = swapped(row2, "head", 1)
         near, back1 = shifted(stream, 1), shifted(back, -1)
-        row2, row3, other1 = lax.optimization_barrier((row2, row3, other1))
-        other2, other3 = swapped(row2, "head", 1), swapped(row3, "head", 1)
-        across, other2, other3, near, back1 = lax.optimization_barrier(
-            (across, other2, other3, near, back1)
-        )
+        across, row3, other2, other3 = lax.optimization_barrier((across, row3, other2, other3))
         pieces = [own, beside, across, swapped(across, "p", 1)]
         far = shifted(near, 1)
         rows = [cache, row1, row2, row3, other0, other1, other2, other3]
         slots = project(place, rows, pieces, devices, capacity)
-        slots, far = lax.optimization_barrier((slots, far))
+        slots, far, back1 = lax.optimization_barrier((slots, far, back1))
         return slots, near, far, back1
     near, back1 = shifted(stream, 1), shifted(back, -1)
     far = shifted(near, 1)

time: 135 us -> 143 us (1.059)
  waiting for transfers between devices: 72.1 us -> 78.7 us
  starting transfers between devices: 45.9 us -> 47.7 us
    ppermute x3 -> x4, waiting for transfers between devices: 6.79 us -> 23.1 us  [ring_step(): lax.ppermute(value, 'z', [(b, a) for a, b in pairs] if back else pairs)]
    ppermute x10 -> x9, waiting for transfers between devices: 28 us -> 18.2 us  [swapped(): lax.ppermute(value, axis, [(i, i ^ mask) for i in range(lax.axis_size(axi...]
    all_to_all x1, starting transfers between devices: 7.14 us -> 15 us  [body(): memory = lax.all_to_all(slots, SEQ, split_axis=0, concat_axis=0, tiled=True)]
    ppermute x6, starting transfers between devices: 21.5 us -> 15.3 us  [shifted(): return lax.ppermute(value, SEQ, pairs)]
    ppermute x3 -> x4, starting transfers between devices: 4.63 us -> 7.48 us  [ring_step(): lax.ppermute(value, 'z', [(b, a) for a, b in pairs] if back else pairs)]
    ppermute x10 -> x9, starting transfers between devices: 12.6 us -> 9.84 us  [swapped(): lax.ppermute(value, axis, [(i, i ^ mask) for i in range(lax.axis_size(axi...]
  transfers between devices with their start and end apart: 20 -> 20, of which waited for: 10 -> 13; matrix products, arithmetic and copies ran while one was open for 0% -> 0% of each run, Pallas kernels for 7% -> 7%
where the time goes in v10:
time: 143 us; the launch traced here: 142 us
  waiting for transfers between devices  78.7 us (55%)
  starting transfers between devices  47.7 us (33%)
  Pallas kernels  13.6 us (10%)
  local copies, waits for them, and re-layouts  1.46 us (1%)
    all_to_all x1, waiting for transfers between devices, body(): memory = lax.all_to_all(slots, SEQ, split_axis=0, concat_axis=0, tiled=True)  27.7 us
    ppermute x4, waiting for transfers between devices, ring_step(): lax.ppermute(value, 'z', [(b, a) for a, b in pairs] if back else pairs)  23.1 us
    ppermute x9, waiting for transfers between devices, swapped(): lax.ppermute(value, axis, [(i, i ^ mask) for i in range(lax.axis_size(axi...  18.2 us
    ppermute x6, starting transfers between devices, shifted(): return lax.ppermute(value, SEQ, pairs)  15.3 us
    all_to_all x1, starting transfers between devices, body(): memory = lax.all_to_all(slots, SEQ, split_axis=0, concat_axis=0, tiled=True)  15 us
    ppermute x9, starting transfers between devices, swapped(): lax.ppermute(value, axis, [(i, i ^ mask) for i in range(lax.axis_size(axi...  9.84 us
    ppermute x6, waiting for transfers between devices, shifted(): return lax.ppermute(value, SEQ, pairs)  9.72 us
    ppermute x4, starting transfers between devices, ring_step(): lax.ppermute(value, 'z', [(b, a) for a, b in pairs] if back else pairs)  7.48 us
  transfers between devices with their start and end apart: 20, of which 13 were waited for; matrix products, arithmetic and copies ran while one was open for 0% of the time, Pallas kernels for 7%

profile of v10, /device:TPU:16, one launch (start us, length us, event | category | flops | bytes accessed | tf_op | source)
XLA Modules:
  0.0 142.5 jit_solution(13098602981940470826)
XLA Ops:
  0.6 0.0 copy-start.4
  0.7 0.0 copy-start
  0.7 0.0 copy-start.1
  0.7 0.0 copy-start.2
  0.7 0.0 copy-start.3
  0.7 1.4 constant_dynamic-slice_fusion
  2.1 1.6 %collective-permute-start = (bf16[160,640]{1,0:T(8,128)(2,1)S(1)}, bf16[160,640]{1,0:T(8,128)(2,1)S(1)}, u32[]{:S(2)}, u32[]{:S(2)}) collective-permute-start(bf16[160,640]{1,0:T(8,128)(2,1)S(1)} %get-tuple-element.57), channel_id=1, source_target_pairs={{0,8},{8,0},{16,24},{24,16},{1,9},{9,1},{17,25},{25,17},{2,10},{10... | collective-permute-start | bytes 614408 | tf_op jit(solution)/shard_map/ppermute | solution.py:25
  3.8 0.3 collective-permute-start.1
  4.1 1.6 %collective-permute-start.2 = (bf16[160,640]{1,0:T(8,128)(2,1)S(1)}, bf16[160,640]{1,0:T(8,128)(2,1)S(1)}, u32[]{:S(2)}, u32[]{:S(2)}) collective-permute-start(bf16[160,640]{1,0:T(8,128)(2,1)S(1)} %get-tuple-element.58), channel_id=1, source_target_pairs={{0,24},{8,16},{16,8},{24,0},{1,25},{9,17},{17,9},{25,1},{2,26},{10... | collective-permute-start | bytes 614408 | tf_op jit(solution)/shard_map/ppermute | solution.py:25
  5.7 0.0 copy-done.4
  5.7 1.0 collective-permute-start.3
  6.7 1.7 %collective-permute-start.4 = (bf16[128,1280]{1,0:T(8,128)(2,1)S(1)}, bf16[128,1280]{1,0:T(8,128)(2,1)S(1)}, u32[]{:S(2)}, u32[]{:S(2)}) collective-permute-start(bf16[128,1280]{1,0:T(8,128)(2,1)S(1)} %copy-done.4), channel_id=1, source_target_pairs={{0,1},{1,0},{2,3},{3,2},{4,5},{5,4},{6,7},{7,6},{8,9},{9,8},{10,11... | collective-permute-start | bytes 983048 | tf_op jit(solution)/shard_map/ppermute | solution.py:25
  8.4 2.7 %collective-permute-done = bf16[160,640]{1,0:T(8,128)(2,1)S(1)} collective-permute-done((bf16[160,640]{1,0:T(8,128)(2,1)S(1)}, bf16[160,640]{1,0:T(8,128)(2,1)S(1)}, u32[]{:S(2)}, u32[]{:S(2)}) %collective-permute-start) | collective-permute-done | bytes 204832 | tf_op jit(solution)/shard_map/ppermute | solution.py:25
  11.2 7.1 %collective-permute-done.1 = bf16[160,640]{1,0:T(8,128)(2,1)S(1)} collective-permute-done((bf16[160,640]{1,0:T(8,128)(2,1)S(1)}, bf16[160,640]{1,0:T(8,128)(2,1)S(1)}, u32[]{:S(2)}, u32[]{:S(2)}) %collective-permute-start.1) | collective-permute-done | bytes 204832 | tf_op jit(solution)/shard_map/ppermute | solution.py:25
  18.3 6.6 %collective-permute-done.2 = bf16[160,640]{1,0:T(8,128)(2,1)S(1)} collective-permute-done((bf16[160,640]{1,0:T(8,128)(2,1)S(1)}, bf16[160,640]{1,0:T(8,128)(2,1)S(1)}, u32[]{:S(2)}, u32[]{:S(2)}) %collective-permute-start.2) | collective-permute-done | bytes 204832 | tf_op jit(solution)/shard_map/ppermute | solution.py:25
  24.8 0.1 pad_maximum_fusion.refs_8_
  25.0 3.4 %collective-permute-done.3.refs_1_ = bf16[128,1280]{1,0:T(8,128)(2,1)S(1)} collective-permute-done((bf16[128,1280]{1,0:T(8,128)(2,1)S(1)}, bf16[128,1280]{1,0:T(8,128)(2,1)S(1)}, u32[]{:S(2)}, u32[]{:S(2)}) %collective-permute-start.3) | collective-permute-done | bytes 327712 | tf_op jit(solution)/shard_map/ppermute | solution.py:317
  28.4 0.0 collective-permute-done.4.refs_4_
  28.4 0.0 collective-permute-start.7
  28.4 1.5 %collective-permute-start.9 = (bf16[4,160,640]{2,1,0:T(8,128)(2,1)S(1)}, bf16[4,160,640]{2,1,0:T(8,128)(2,1)S(1)}, u32[]{:S(2)}, u32[]{:S(2)}) collective-permute-start(bf16[4,160,640]{2,1,0:T(8,128)(2,1)S(1)} %pad_maximum_fusion.refs_8_), channel_id=1, source_target_pairs={{0,4},{2,6},{4,0},{6,2},{1,5},{3,7},{5,1},{7,3},{8,12},{10,14},{12... | collective-permute-start | bytes 2457608 | tf_op jit(solution)/shard_map/ppermute | solution.py:25
  29.9 3.4 %collective-permute-start.5 = (bf16[128,1280]{1,0:T(8,128)(2,1)S(1)}, bf16[128,1280]{1,0:T(8,128)(2,1)S(1)}, u32[]{:S(2)}, u32[]{:S(2)}) collective-permute-start(bf16[128,1280]{1,0:T(8,128)(2,1)S(1)} %collective-permute-done.3.refs_1_), channel_id=1, source_target_pairs={{0,8},{8,24},{24,16},{16,0},{1,9},{9,25},{25,17},{17,1},{2,10},{10... | collective-permute-start | bytes 983048 | tf_op jit(solution)/shard_map/ppermute | solution.py:317
  33.3 1.5 %collective-permute-start.6 = (bf16[128,1280]{1,0:T(8,128)(2,1)S(1)}, bf16[128,1280]{1,0:T(8,128)(2,1)S(1)}, u32[]{:S(2)}, u32[]{:S(2)}) collective-permute-start(bf16[128,1280]{1,0:T(8,128)(2,1)S(1)} %collective-permute-done.3.refs_1_), channel_id=1, source_target_pairs={{0,1},{1,0},{2,3},{3,2},{4,5},{5,4},{6,7},{7,6},{8,9},{9,8},{10,11... | collective-permute-start | bytes 983048 | tf_op jit(solution)/shard_map/ppermute | solution.py:25
  34.8 0.0 copy-done
  34.8 0.0 copy-done.1
  34.8 0.0 copy-done.2
  34.8 0.0 copy-done.3
  34.8 0.0 copy-start.6
  34.8 0.0 copy-start.7
  34.8 0.1 pad_maximum_fusion.1
  35.0 6.5 %collective-permute-done.5.refs_2_ = bf16[128,1280]{1,0:T(8,128)(2,1)S(1)} collective-permute-done((bf16[128,1280]{1,0:T(8,128)(2,1)S(1)}, bf16[128,1280]{1,0:T(8,128)(2,1)S(1)}, u32[]{:S(2)}, u32[]{:S(2)}) %collective-permute-start.5) | collective-permute-done | bytes 327712 | tf_op jit(solution)/shard_map/ppermute | solution.py:317
  41.5 1.4 collective-permute-done.6.refs_5_
  42.8 0.0 collective-permute-done.7.refs_9_
  42.8 1.9 %collective-permute-start.8 = (bf16[2,128,1280]{2,1,0:T(8,128)(2,1)S(1)}, bf16[2,128,1280]{2,1,0:T(8,128)(2,1)S(1)}, u32[]{:S(2)}, u32[]{:S(2)}) collective-permute-start(bf16[2,128,1280]{2,1,0:T(8,128)(2,1)S(1)} %get-tuple-element.34), channel_id=1, source_target_pairs={{0,2},{2,4},{4,6},{6,8},{8,10},{10,12},{12,14},{14,16},{16,18},{18... | collective-permute-start | bytes 1966088 | tf_op jit(solution)/shard_map/ppermute | solution.py:21
  44.8 1.3 collective-permute-start.10
  46.1 1.5 %collective-permute-start.11 = (bf16[128,1280]{1,0:T(8,128)(2,1)S(1)}, bf16[128,1280]{1,0:T(8,128)(2,1)S(1)}, u32[]{:S(2)}, u32[]{:S(2)}) collective-permute-start(bf16[128,1280]{1,0:T(8,128)(2,1)S(1)} %collective-permute-done.5.refs_2_), channel_id=1, source_target_pairs={{0,1},{1,0},{2,3},{3,2},{4,5},{5,4},{6,7},{7,6},{8,9},{9,8},{10,11... | collective-permute-start | bytes 983048 | tf_op jit(solution)/shard_map/ppermute | solution.py:25
  47.6 1.7 %collective-permute-start.12 = (bf16[128,1280]{1,0:T(8,128)(2,1)S(1)}, bf16[128,1280]{1,0:T(8,128)(2,1)S(1)}, u32[]{:S(2)}, u32[]{:S(2)}) collective-permute-start(bf16[128,1280]{1,0:T(8,128)(2,1)S(1)} %collective-permute-done.4.refs_4_), channel_id=1, source_target_pairs={{8,0},{24,8},{16,24},{0,16},{9,1},{25,9},{17,25},{1,17},{10,2},{26... | collective-permute-start | bytes 983048 | tf_op jit(solution)/shard_map/ppermute | solution.py:317
  49.4 0.5 collective-permute-done.9.refs_10_
  49.9 6.4 %collective-permute-done.10.refs_3_ = bf16[128,1280]{1,0:T(8,128)(2,1)S(1)} collective-permute-done((bf16[128,1280]{1,0:T(8,128)(2,1)S(1)}, bf16[128,1280]{1,0:T(8,128)(2,1)S(1)}, u32[]{:S(2)}, u32[]{:S(2)}) %collective-permute-start.10) | collective-permute-done | bytes 327712 | tf_op jit(solution)/shard_map/ppermute | solution.py:317
  56.3 0.0 collective-permute-done.11.refs_6_
  56.3 6.7 %collective-permute-done.12.refs_7_ = bf16[128,1280]{1,0:T(8,128)(2,1)S(1)} collective-permute-done((bf16[128,1280]{1,0:T(8,128)(2,1)S(1)}, bf16[128,1280]{1,0:T(8,128)(2,1)S(1)}, u32[]{:S(2)}, u32[]{:S(2)}) %collective-permute-start.12) | collective-permute-done | bytes 327712 | tf_op jit(solution)/shard_map/ppermute | solution.py:317
  63.0 0.0 collective-permute-start.13
  63.0 3.4 %collective-permute-start.15 = (bf16[2,128,1280]{2,1,0:T(8,128)(2,1)S(1)}, bf16[2,128,1280]{2,1,0:T(8,128)(2,1)S(1)}, u32[]{:S(2)}, u32[]{:S(2)}) collective-permute-start(bf16[2,128,1280]{2,1,0:T(8,128)(2,1)S(1)} %get-tuple-element.45), channel_id=1, source_target_pairs={{2,0},{4,2},{6,4},{8,6},{10,8},{12,10},{14,12},{16,14},{18,16},{20... | collective-permute-start | bytes 1966088 | tf_op jit(solution)/shard_map/ppermute | solution.py:21
  66.4 0.0 collective-permute-done.8.kv1_ref
  66.5 0.0 copy-start.8
  66.5 1.9 %collective-permute-start.14 = (bf16[2,128,1280]{2,1,0:T(8,128)(2,1)S(1)}, bf16[2,128,1280]{2,1,0:T(8,128)(2,1)}, u32[]{:S(2)}, u32[]{:S(2)}) collective-permute-start(bf16[2,128,1280]{2,1,0:T(8,128)(2,1)S(1)} %collective-permute-done.8.kv1_ref), channel_id=1, source_target_pairs={{0,2},{2,4},{4,6},{6,8},{8,10},{10,12},{12,14},{14,16},{16,18},{18... | collective-permute-start | bytes 1966088 | tf_op jit(solution)/shard_map/ppermute | solution.py:21
  68.4 0.0 copy-done.6
  68.4 0.0 copy-done.7
  68.4 0.3 prepare.1
  68.7 0.0 collective-permute-done.13.refs_11_
  68.7 4.6 %project.1 = bf16[16,4,16,640]{3,2,1,0:T(8,128)(2,1)} custom-call(s32[4,1,128]{2,1,0:T(1,128)S(1)} %get-tuple-element.35.place_ref, bf16[128,1280]{1,0:T(8,128)(2,1)S(1)} %copy-done.4, bf16[128,1280]{1,0:T(8,128)(2,1)S(1)} %collective-permute-done.3.refs_1_, bf16[128,1280]{1,0:T(8,128)(2,1)S(1)} %collective-permute-done.5.refs_2_, ...), custom_call_target="tpu_custom_call" | custom-call | flops 1677721600 | bytes 8388608 | tf_op jit(solution)/shard_map/project/pallas_call | solution.py:225
  73.3 0.0 copy-done.8
  73.3 0.0 copy-done.5
  73.3 1.3 collective-permute-done.15.qg1_ref
  74.6 4.9 %collective-permute-done.14.kv2_ref = bf16[2,128,1280]{2,1,0:T(8,128)(2,1)} collective-permute-done((bf16[2,128,1280]{2,1,0:T(8,128)(2,1)S(1)}, bf16[2,128,1280]{2,1,0:T(8,128)(2,1)}, u32[]{:S(2)}, u32[]{:S(2)}) %collective-permute-start.14) | collective-permute-done | bytes 655392 | tf_op jit(solution)/shard_map/ppermute | solution.py:21
  79.5 15.0 %all-to-all-start = ((bf16[16,4,16,640]{3,2,1,0:T(8,128)(2,1)}), bf16[16,4,16,640]{3,2,1,0:T(8,128)(2,1)S(1)}, u32[]{:S(2)}, u32[]{:S(2)}) async-start(bf16[16,4,16,640]{3,2,1,0:T(8,128)(2,1)} %project.1), calls=%async_computation | async-start | bytes 2621440 | tf_op jit(solution)/shard_map/all_to_all | solution.py:391
  94.5 3.1 %collective-permute-start.16 = (bf16[2,128,1280]{2,1,0:T(8,128)(2,1)S(1)}, bf16[2,128,1280]{2,1,0:T(8,128)(2,1)}, u32[]{:S(2)}, u32[]{:S(2)}) collective-permute-start(bf16[2,128,1280]{2,1,0:T(8,128)(2,1)S(1)} %collective-permute-done.15.qg1_ref), channel_id=1, source_target_pairs={{2,0},{4,2},{6,4},{8,6},{10,8},{12,10},{14,12},{16,14},{18,16},{20... | collective-permute-start | bytes 1966088 | tf_op jit(solution)/shard_map/ppermute | solution.py:21
  97.6 27.7 %all-to-all-done = bf16[16,4,16,640]{3,2,1,0:T(8,128)(2,1)S(1)} async-done(((bf16[16,4,16,640]{3,2,1,0:T(8,128)(2,1)}), bf16[16,4,16,640]{3,2,1,0:T(8,128)(2,1)S(1)}, u32[]{:S(2)}, u32[]{:S(2)}) %all-to-all-start) | async-done | bytes 1310752 | tf_op jit(solution)/shard_map/all_to_all | solution.py:391
  125.3 5.0 %attend.1 = (bf16[128,1280]{1,0:T(8,128)(2,1)}, bf16[128,1280]{1,0:T(8,128)(2,1)}, f32[2,16,128]{2,1,0:T(8,128)S(1)}) custom-call(bf16[128,1280]{1,0:T(8,128)(2,1)S(1)} %copy-done, bf16[128,1280]{1,0:T(8,128)(2,1)S(1)} %copy-done.1, bf16[128,1280]{1,0:T(8,128)(2,1)S(1)} %copy-done.2, bf16[128,1280]{1,0:T(8,128)(2,1)S(1)} %copy-done.3, ...), custom_call_target="tpu_custom_call" | custom-call | flops 838860800 | bytes 6291456 | tf_op jit(solution)/shard_map/attend/pallas_call | solution.py:103
  130.2 2.9 %collective-permute-start.17 = (f32[2,16,128]{2,1,0:T(8,128)S(1)}, f32[2,16,128]{2,1,0:T(8,128)S(1)}, u32[]{:S(2)}, u32[]{:S(2)}) collective-permute-start(f32[2,16,128]{2,1,0:T(8,128)S(1)} %get-tuple-element.52.st0_ref), channel_id=1, source_target_pairs={{2,0},{4,2},{6,4},{8,6},{10,8},{12,10},{14,12},{16,14},{18,16},{20... | collective-permute-start | bytes 49160 | tf_op jit(solution)/shard_map/ppermute | solution.py:21
  133.1 2.1 %collective-permute-start.18 = (f32[2,16,128]{2,1,0:T(8,128)S(1)}, f32[2,16,128]{2,1,0:T(8,128)S(1)}, u32[]{:S(2)}, u32[]{:S(2)}) collective-permute-start(f32[2,16,128]{2,1,0:T(8,128)S(1)} %get-tuple-element.52.st0_ref), channel_id=1, source_target_pairs={{4,0},{6,2},{8,4},{10,6},{12,8},{14,10},{16,12},{18,14},{20,16},{2... | collective-permute-start | bytes 49160 | tf_op jit(solution)/shard_map/ppermute | solution.py:21
  135.2 0.0 collective-permute-done.16.qg2_ref
  135.2 0.0 collective-permute-done.17.st1_ref
  135.2 3.5 %collective-permute-done.18.st2_ref = f32[2,16,128]{2,1,0:T(8,128)S(1)} collective-permute-done((f32[2,16,128]{2,1,0:T(8,128)S(1)}, f32[2,16,128]{2,1,0:T(8,128)S(1)}, u32[]{:S(2)}, u32[]{:S(2)}) %collective-permute-start.18) | collective-permute-done | bytes 16416 | tf_op jit(solution)/shard_map/ppermute | solution.py:21
  138.8 3.7 %key_grads.1 = (bf16[128,1280]{1,0:T(8,128)(2,1)}, bf16[128,1280]{1,0:T(8,128)(2,1)}) custom-call(bf16[128,1280]{1,0:T(8,128)(2,1)S(1)} %copy-done.2, bf16[128,1280]{1,0:T(8,128)(2,1)S(1)} %copy-done.3, bf16[128,1280]{1,0:T(8,128)(2,1)S(1)} %copy-done, bf16[128,1280]{1,0:T(8,128)(2,1)S(1)} %copy-done.1, ...), custom_call_target="tpu_custom_call" | custom-call | flops 503316480 | bytes 4194304 | tf_op jit(solution)/shard_map/key_grads/pallas_call | solution.py:166
  (1 shorter events, 0.0 us)
Async XLA Ops:
  0.6 5.1 %copy-start.4 = (bf16[128,1280]{1,0:T(8,128)(2,1)S(1)}, bf16[128,1280]{1,0:T(8,128)(2,1)}, u32[]{:S(2)}) copy-start(bf16[128,1280]{1,0:T(8,128)(2,1)} %refs_0_) | copy-start | bytes 983044
  0.7 34.1 %copy-start = (bf16[128,1280]{1,0:T(8,128)(2,1)S(1)}, bf16[128,1280]{1,0:T(8,128)(2,1)}, u32[]{:S(2)}) copy-start(bf16[128,1280]{1,0:T(8,128)(2,1)} %q_ref.3) | copy-start | bytes 983044
  0.7 34.1 %copy-start.1 = (bf16[128,1280]{1,0:T(8,128)(2,1)S(1)}, bf16[128,1280]{1,0:T(8,128)(2,1)}, u32[]{:S(2)}) copy-start(bf16[128,1280]{1,0:T(8,128)(2,1)} %g_ref.3) | copy-start | bytes 983044
  0.7 34.1 %copy-start.2 = (bf16[128,1280]{1,0:T(8,128)(2,1)S(1)}, bf16[128,1280]{1,0:T(8,128)(2,1)}, u32[]{:S(2)}) copy-start(bf16[128,1280]{1,0:T(8,128)(2,1)} %k_ref.3) | copy-start | bytes 983044
  0.7 34.1 %copy-start.3 = (bf16[128,1280]{1,0:T(8,128)(2,1)S(1)}, bf16[128,1280]{1,0:T(8,128)(2,1)}, u32[]{:S(2)}) copy-start(bf16[128,1280]{1,0:T(8,128)(2,1)} %v_ref.3) | copy-start | bytes 983044
  2.1 9.0 %collective-permute-start = (bf16[160,640]{1,0:T(8,128)(2,1)S(1)}, bf16[160,640]{1,0:T(8,128)(2,1)S(1)}, u32[]{:S(2)}, u32[]{:S(2)}) collective-permute-start(bf16[160,640]{1,0:T(8,128)(2,1)S(1)} %get-tuple-element.57), channel_id=1, source_target_pairs={{0,8},{8,0},{16,24},{24,16},{1,9},{9,1},{17,25},{25,17},{2,10},{10... | collective-permute-start | bytes 614408 | tf_op jit(solution)/shard_map/ppermute | solution.py:25
  3.8 14.5 %collective-permute-start.1 = (bf16[160,640]{1,0:T(8,128)(2,1)S(1)}, bf16[160,640]{1,0:T(8,128)(2,1)S(1)}, u32[]{:S(2)}, u32[]{:S(2)}) collective-permute-start(bf16[160,640]{1,0:T(8,128)(2,1)S(1)} %get-tuple-element.59), channel_id=1, source_target_pairs={{0,16},{8,24},{16,0},{24,8},{1,17},{9,25},{17,1},{25,9},{2,18},{10... | collective-permute-start | bytes 614408 | tf_op jit(solution)/shard_map/ppermute | solution.py:25
  4.1 20.7 %collective-permute-start.2 = (bf16[160,640]{1,0:T(8,128)(2,1)S(1)}, bf16[160,640]{1,0:T(8,128)(2,1)S(1)}, u32[]{:S(2)}, u32[]{:S(2)}) collective-permute-start(bf16[160,640]{1,0:T(8,128)(2,1)S(1)} %get-tuple-element.58), channel_id=1, source_target_pairs={{0,24},{8,16},{16,8},{24,0},{1,25},{9,17},{17,9},{25,1},{2,26},{10... | collective-permute-start | bytes 614408 | tf_op jit(solution)/shard_map/ppermute | solution.py:25
  5.7 22.7 %collective-permute-start.3 = (bf16[128,1280]{1,0:T(8,128)(2,1)S(1)}, bf16[128,1280]{1,0:T(8,128)(2,1)S(1)}, u32[]{:S(2)}, u32[]{:S(2)}) collective-permute-start(bf16[128,1280]{1,0:T(8,128)(2,1)S(1)} %copy-done.4), channel_id=1, source_target_pairs={{0,8},{8,24},{24,16},{16,0},{1,9},{9,25},{25,17},{17,1},{2,10},{10... | collective-permute-start | bytes 983048 | tf_op jit(solution)/shard_map/ppermute | solution.py:317
  6.7 21.7 %collective-permute-start.4 = (bf16[128,1280]{1,0:T(8,128)(2,1)S(1)}, bf16[128,1280]{1,0:T(8,128)(2,1)S(1)}, u32[]{:S(2)}, u32[]{:S(2)}) collective-permute-start(bf16[128,1280]{1,0:T(8,128)(2,1)S(1)} %copy-done.4), channel_id=1, source_target_pairs={{0,1},{1,0},{2,3},{3,2},{4,5},{5,4},{6,7},{7,6},{8,9},{9,8},{10,11... | collective-permute-start | bytes 983048 | tf_op jit(solution)/shard_map/ppermute | solution.py:25
  28.4 14.4 %collective-permute-start.7 = (bf16[4,160,640]{2,1,0:T(8,128)(2,1)S(1)}, bf16[4,160,640]{2,1,0:T(8,128)(2,1)S(1)}, u32[]{:S(2)}, u32[]{:S(2)}) collective-permute-start(bf16[4,160,640]{2,1,0:T(8,128)(2,1)S(1)} %pad_maximum_fusion.refs_8_), channel_id=1, source_target_pairs={{0,2},{2,0},{4,6},{6,4},{1,3},{3,1},{5,7},{7,5},{8,10},{10,8},{12,... | collective-permute-start | bytes 2457608 | tf_op jit(solution)/shard_map/ppermute | solution.py:25
  28.4 21.4 %collective-permute-start.9 = (bf16[4,160,640]{2,1,0:T(8,128)(2,1)S(1)}, bf16[4,160,640]{2,1,0:T(8,128)(2,1)S(1)}, u32[]{:S(2)}, u32[]{:S(2)}) collective-permute-start(bf16[4,160,640]{2,1,0:T(8,128)(2,1)S(1)} %pad_maximum_fusion.refs_8_), channel_id=1, source_target_pairs={{0,4},{2,6},{4,0},{6,2},{1,5},{3,7},{5,1},{7,3},{8,12},{10,14},{12... | collective-permute-start | bytes 2457608 | tf_op jit(solution)/shard_map/ppermute | solution.py:25
  29.9 11.6 %collective-permute-start.5 = (bf16[128,1280]{1,0:T(8,128)(2,1)S(1)}, bf16[128,1280]{1,0:T(8,128)(2,1)S(1)}, u32[]{:S(2)}, u32[]{:S(2)}) collective-permute-start(bf16[128,1280]{1,0:T(8,128)(2,1)S(1)} %collective-permute-done.3.refs_1_), channel_id=1, source_target_pairs={{0,8},{8,24},{24,16},{16,0},{1,9},{9,25},{25,17},{17,1},{2,10},{10... | collective-permute-start | bytes 983048 | tf_op jit(solution)/shard_map/ppermute | solution.py:317
  33.3 9.6 %collective-permute-start.6 = (bf16[128,1280]{1,0:T(8,128)(2,1)S(1)}, bf16[128,1280]{1,0:T(8,128)(2,1)S(1)}, u32[]{:S(2)}, u32[]{:S(2)}) collective-permute-start(bf16[128,1280]{1,0:T(8,128)(2,1)S(1)} %collective-permute-done.3.refs_1_), channel_id=1, source_target_pairs={{0,1},{1,0},{2,3},{3,2},{4,5},{5,4},{6,7},{7,6},{8,9},{9,8},{10,11... | collective-permute-start | bytes 983048 | tf_op jit(solution)/shard_map/ppermute | solution.py:25
  34.8 33.6 %copy-start.6 = (s32[2048]{0:T(1024)S(1)}, s32[2048]{0:T(1024)}, u32[]{:S(2)}) copy-start(s32[2048]{0:T(1024)} %param.15) | copy-start | bytes 24580
  34.8 33.6 %copy-start.7 = (s32[2048]{0:T(1024)S(1)}, s32[2048]{0:T(1024)}, u32[]{:S(2)}) copy-start(s32[2048]{0:T(1024)} %param.14) | copy-start | bytes 24580
  42.8 23.6 %collective-permute-start.8 = (bf16[2,128,1280]{2,1,0:T(8,128)(2,1)S(1)}, bf16[2,128,1280]{2,1,0:T(8,128)(2,1)S(1)}, u32[]{:S(2)}, u32[]{:S(2)}) collective-permute-start(bf16[2,128,1280]{2,1,0:T(8,128)(2,1)S(1)} %get-tuple-element.34), channel_id=1, source_target_pairs={{0,2},{2,4},{4,6},{6,8},{8,10},{10,12},{12,14},{14,16},{16,18},{18... | collective-permute-start | bytes 1966088 | tf_op jit(solution)/shard_map/ppermute | solution.py:21
  44.8 11.5 %collective-permute-start.10 = (bf16[128,1280]{1,0:T(8,128)(2,1)S(1)}, bf16[128,1280]{1,0:T(8,128)(2,1)S(1)}, u32[]{:S(2)}, u32[]{:S(2)}) collective-permute-start(bf16[128,1280]{1,0:T(8,128)(2,1)S(1)} %copy-done.4), channel_id=1, source_target_pairs={{8,0},{24,8},{16,24},{0,16},{9,1},{25,9},{17,25},{1,17},{10,2},{26... | collective-permute-start | bytes 983048 | tf_op jit(solution)/shard_map/ppermute | solution.py:317
  46.1 10.2 %collective-permute-start.11 = (bf16[128,1280]{1,0:T(8,128)(2,1)S(1)}, bf16[128,1280]{1,0:T(8,128)(2,1)S(1)}, u32[]{:S(2)}, u32[]{:S(2)}) collective-permute-start(bf16[128,1280]{1,0:T(8,128)(2,1)S(1)} %collective-permute-done.5.refs_2_), channel_id=1, source_target_pairs={{0,1},{1,0},{2,3},{3,2},{4,5},{5,4},{6,7},{7,6},{8,9},{9,8},{10,11... | collective-permute-start | bytes 983048 | tf_op jit(solution)/shard_map/ppermute | solution.py:25
  47.6 15.3 %collective-permute-start.12 = (bf16[128,1280]{1,0:T(8,128)(2,1)S(1)}, bf16[128,1280]{1,0:T(8,128)(2,1)S(1)}, u32[]{:S(2)}, u32[]{:S(2)}) collective-permute-start(bf16[128,1280]{1,0:T(8,128)(2,1)S(1)} %collective-permute-done.4.refs_4_), channel_id=1, source_target_pairs={{8,0},{24,8},{16,24},{0,16},{9,1},{25,9},{17,25},{1,17},{10,2},{26... | collective-permute-start | bytes 983048 | tf_op jit(solution)/shard_map/ppermute | solution.py:317
  63.0 5.7 %collective-permute-start.13 = (bf16[4,160,640]{2,1,0:T(8,128)(2,1)S(1)}, bf16[4,160,640]{2,1,0:T(8,128)(2,1)S(1)}, u32[]{:S(2)}, u32[]{:S(2)}) collective-permute-start(bf16[4,160,640]{2,1,0:T(8,128)(2,1)S(1)} %collective-permute-done.9.refs_10_), channel_id=1, source_target_pairs={{0,2},{2,0},{4,6},{6,4},{1,3},{3,1},{5,7},{7,5},{8,10},{10,8},{12,... | collective-permute-start | bytes 2457608 | tf_op jit(solution)/shard_map/ppermute | solution.py:25
  63.0 11.6 %collective-permute-start.15 = (bf16[2,128,1280]{2,1,0:T(8,128)(2,1)S(1)}, bf16[2,128,1280]{2,1,0:T(8,128)(2,1)S(1)}, u32[]{:S(2)}, u32[]{:S(2)}) collective-permute-start(bf16[2,128,1280]{2,1,0:T(8,128)(2,1)S(1)} %get-tuple-element.45), channel_id=1, source_target_pairs={{2,0},{4,2},{6,4},{8,6},{10,8},{12,10},{14,12},{16,14},{18,16},{20... | collective-permute-start | bytes 1966088 | tf_op jit(solution)/shard_map/ppermute | solution.py:21
  66.5 6.8 %copy-start.8 = (bf16[2,128,1280]{2,1,0:T(8,128)(2,1)}, bf16[2,128,1280]{2,1,0:T(8,128)(2,1)S(1)}, u32[]{:S(2)}) copy-start(bf16[2,128,1280]{2,1,0:T(8,128)(2,1)S(1)} %collective-permute-done.8.kv1_ref) | copy-start | bytes 1966084
  66.5 13.0 %collective-permute-start.14 = (bf16[2,128,1280]{2,1,0:T(8,128)(2,1)S(1)}, bf16[2,128,1280]{2,1,0:T(8,128)(2,1)}, u32[]{:S(2)}, u32[]{:S(2)}) collective-permute-start(bf16[2,128,1280]{2,1,0:T(8,128)(2,1)S(1)} %collective-permute-done.8.kv1_ref), channel_id=1, source_target_pairs={{0,2},{2,4},{4,6},{6,8},{8,10},{10,12},{12,14},{14,16},{16,18},{18... | collective-permute-start | bytes 1966088 | tf_op jit(solution)/shard_map/ppermute | solution.py:21
  68.7 4.6 %copy-start.5 = (bf16[128,640]{1,0:T(8,128)(2,1)}, bf16[128,640]{1,0:T(8,128)(2,1)S(1)}, u32[]{:S(2)}) copy-start(bf16[128,640]{1,0:T(8,128)(2,1)S(1)} %get-tuple-element.48.bias_ref) | copy-start | bytes 491524
  79.5 45.8 %all-to-all-start = ((bf16[16,4,16,640]{3,2,1,0:T(8,128)(2,1)}), bf16[16,4,16,640]{3,2,1,0:T(8,128)(2,1)S(1)}, u32[]{:S(2)}, u32[]{:S(2)}) async-start(bf16[16,4,16,640]{3,2,1,0:T(8,128)(2,1)} %project.1), calls=%async_computation | async-start | bytes 2621440 | tf_op jit(solution)/shard_map/all_to_all | solution.py:391
  94.5 40.8 %collective-permute-start.16 = (bf16[2,128,1280]{2,1,0:T(8,128)(2,1)S(1)}, bf16[2,128,1280]{2,1,0:T(8,128)(2,1)}, u32[]{:S(2)}, u32[]{:S(2)}) collective-permute-start(bf16[2,128,1280]{2,1,0:T(8,128)(2,1)S(1)} %collective-permute-done.15.qg1_ref), channel_id=1, source_target_pairs={{2,0},{4,2},{6,4},{8,6},{10,8},{12,10},{14,12},{16,14},{18,16},{20... | collective-permute-start | bytes 1966088 | tf_op jit(solution)/shard_map/ppermute | solution.py:21
  130.2 5.0 %collective-permute-start.17 = (f32[2,16,128]{2,1,0:T(8,128)S(1)}, f32[2,16,128]{2,1,0:T(8,128)S(1)}, u32[]{:S(2)}, u32[]{:S(2)}) collective-permute-start(f32[2,16,128]{2,1,0:T(8,128)S(1)} %get-tuple-element.52.st0_ref), channel_id=1, source_target_pairs={{2,0},{4,2},{6,4},{8,6},{10,8},{12,10},{14,12},{16,14},{18,16},{20... | collective-permute-start | bytes 49160 | tf_op jit(solution)/shard_map/ppermute | solution.py:21
  133.1 5.6 %collective-permute-start.18 = (f32[2,16,128]{2,1,0:T(8,128)S(1)}, f32[2,16,128]{2,1,0:T(8,128)S(1)}, u32[]{:S(2)}, u32[]{:S(2)}) collective-permute-start(f32[2,16,128]{2,1,0:T(8,128)S(1)} %get-tuple-element.52.st0_ref), channel_id=1, source_target_pairs={{4,0},{6,2},{8,4},{10,6},{12,8},{14,10},{16,12},{18,14},{20,16},{2... | collective-permute-start | bytes 49160 | tf_op jit(solution)/shard_map/ppermute | solution.py:21

commit v11 on v4

--- a/solution.py
+++ b/solution.py
@@ -334,17 +334,18 @@
         row1, row3 = ring_step(cache), ring_step(cache, back=True)
         beside, stream, back = lax.optimization_barrier((beside, stream, back))
         near, back1 = shifted(stream, 1), shifted(back, -1)
-        row1, row3 = lax.optimization_barrier((row1, row3))
-        row2 = ring_step(row1)
-        others13 = swapped(jnp.stack([row1, row3], 0), "head", 1)
+        row1 = lax.optimization_barrier(row1)
+        row2, other1 = ring_step(row1), swapped(row1, "head", 1)
+        row3, other1 = lax.optimization_barrier((row3, other1))
+        other3 = swapped(row3, "head", 1)
         row2 = lax.optimization_barrier(row2)
         other2 = swapped(row2, "head", 1)
-        across, others13, other2, near, back1 = lax.optimization_barrier(
-            (across, others13, other2, near, back1)
+        across, other2, other3, near, back1 = lax.optimization_barrier(
+            (across, other2, other3, near, back1)
         )
         pieces = [own, beside, across, swapped(across, "p", 1)]
         far = shifted(near, 1)
-        rows = [cache, row1, row2, row3, other0, others13[0], other2, others13[1]]
+        rows = [cache, row1, row2, row3, other0, other1, other2, other3]
         slots = project(place, rows, pieces, devices, capacity)
         slots, far = lax.optimization_barrier((slots, far))
         return slots, near, far, back1

time: 132 us -> 127 us (0.962)
  waiting for transfers between devices: 79.5 us -> 75.2 us
    ppermute x9 -> x10, waiting for transfers between devices: 30.2 us -> 27.1 us  [swapped(): lax.ppermute(value, axis, [(i, i ^ mask) for i in range(lax.axis_size(axi...]
    ppermute x3, waiting for transfers between devices: 13.2 us -> 11.4 us  [ring_step(): lax.ppermute(value, 'z', [(b, a) for a, b in pairs] if back else pairs)]
    ppermute x9 -> x10, starting transfers between devices: 9.73 us -> 11.3 us  [swapped(): lax.ppermute(value, axis, [(i, i ^ mask) for i in range(lax.axis_size(axi...]
    ppermute x6, starting transfers between devices: 16.9 us -> 15.6 us  [shifted(): return lax.ppermute(value, SEQ, pairs)]
  transfers between devices with their start and end apart: 19 -> 20, of which waited for: 10 -> 11; matrix products, arithmetic and copies ran while one was open for 0% -> 0% of each run, Pallas kernels for 7% -> 8%
where the time goes in v11:
time: 127 us; the launch traced here: 126 us
  waiting for transfers between devices  75.2 us (59%)
  starting transfers between devices  34.2 us (27%)
  Pallas kernels  13.6 us (11%)
  local copies, waits for them, and re-layouts  2.31 us (2%)
    all_to_all x1, waiting for transfers between devices, body(): memory = lax.all_to_all(slots, SEQ, split_axis=0, concat_axis=0, tiled=True)  27.7 us
    ppermute x10, waiting for transfers between devices, swapped(): lax.ppermute(value, axis, [(i, i ^ mask) for i in range(lax.axis_size(axi...  27.1 us
    ppermute x6, starting transfers between devices, shifted(): return lax.ppermute(value, SEQ, pairs)  15.6 us
    ppermute x3, waiting for transfers between devices, ring_step(): lax.ppermute(value, 'z', [(b, a) for a, b in pairs] if back else pairs)  11.4 us
    ppermute x10, starting transfers between devices, swapped(): lax.ppermute(value, axis, [(i, i ^ mask) for i in range(lax.axis_size(axi...  11.3 us
    ppermute x6, waiting for transfers between devices, shifted(): return lax.ppermute(value, SEQ, pairs)  9.04 us
    pallas_call x1, Pallas kernels, attend(): pl.pallas_call(attend_kernel, grid=(steps,), in_specs=[flat, flat, flat,...  4.98 us
    pallas_call x1, Pallas kernels, project(): pl.pallas_call(project_kernel, in_specs=[whole] * (1 + len(rows) + n_p),...  4.6 us
  transfers between devices with their start and end apart: 20, of which 11 were waited for; matrix products, arithmetic and copies ran while one was open for 0% of the time, Pallas kernels for 8%

profile of v11, /device:TPU:16, one launch (start us, length us, event | category | flops | bytes accessed | tf_op | source)
XLA Modules:
  0.0 126.4 jit_solution(16694860796844854834)
XLA Ops:
  0.6 0.0 copy-start.4
  0.7 0.0 copy-start
  0.7 0.0 copy-start.1
  0.7 0.0 copy-start.2
  0.7 0.0 copy-start.3
  0.7 1.4 %constant_dynamic-slice_fusion = (bf16[1,160,640]{2,1,0:T(8,128)(2,1)S(1)}, bf16[160,640]{1,0:T(8,128)(2,1)S(1)}, bf16[160,640]{1,0:T(8,128)(2,1)S(1)}, bf16[160,640]{1,0:T(8,128)(2,1)S(1)}) fusion(bf16[2,160,1280]{2,1,0:T(8,128)(2,1)} %param.13, s32[]{:T(128)S(6)} %select_n.24, s32[]{:T(128)S(6)} %select_n.25, s32[]{:T(128)S(6)} %select_n.26, ...), kind=kLoop, calls=%fused_computation.6 | loop fusion | bytes 1638432 | tf_op jit(solution)/shard_map/dynamic_slice | solution.py:312
  2.1 1.6 %collective-permute-start = (bf16[160,640]{1,0:T(8,128)(2,1)S(1)}, bf16[160,640]{1,0:T(8,128)(2,1)S(1)}, u32[]{:S(2)}, u32[]{:S(2)}) collective-permute-start(bf16[160,640]{1,0:T(8,128)(2,1)S(1)} %get-tuple-element.51), channel_id=1, source_target_pairs={{0,8},{8,0},{16,24},{24,16},{1,9},{9,1},{17,25},{25,17},{2,10},{10... | collective-permute-start | bytes 614408 | tf_op jit(solution)/shard_map/ppermute | solution.py:25
  3.8 0.3 collective-permute-start.1
  4.1 1.6 %collective-permute-start.2 = (bf16[160,640]{1,0:T(8,128)(2,1)S(1)}, bf16[160,640]{1,0:T(8,128)(2,1)S(1)}, u32[]{:S(2)}, u32[]{:S(2)}) collective-permute-start(bf16[160,640]{1,0:T(8,128)(2,1)S(1)} %get-tuple-element.52), channel_id=1, source_target_pairs={{0,24},{8,16},{16,8},{24,0},{1,25},{9,17},{17,9},{25,1},{2,26},{10... | collective-permute-start | bytes 614408 | tf_op jit(solution)/shard_map/ppermute | solution.py:25
  5.7 0.0 copy-done.4
  5.7 1.5 %collective-permute-start.3 = (bf16[128,1280]{1,0:T(8,128)(2,1)S(1)}, bf16[128,1280]{1,0:T(8,128)(2,1)S(1)}, u32[]{:S(2)}, u32[]{:S(2)}) collective-permute-start(bf16[128,1280]{1,0:T(8,128)(2,1)S(1)} %copy-done.4), channel_id=1, source_target_pairs={{0,1},{1,0},{2,3},{3,2},{4,5},{5,4},{6,7},{7,6},{8,9},{9,8},{10,11... | collective-permute-start | bytes 983048 | tf_op jit(solution)/shard_map/ppermute | solution.py:25
  7.2 4.0 %collective-permute-done = bf16[160,640]{1,0:T(8,128)(2,1)S(1)} collective-permute-done((bf16[160,640]{1,0:T(8,128)(2,1)S(1)}, bf16[160,640]{1,0:T(8,128)(2,1)S(1)}, u32[]{:S(2)}, u32[]{:S(2)}) %collective-permute-start) | collective-permute-done | bytes 204832 | tf_op jit(solution)/shard_map/ppermute | solution.py:25
  11.2 7.2 %collective-permute-done.1 = bf16[160,640]{1,0:T(8,128)(2,1)S(1)} collective-permute-done((bf16[160,640]{1,0:T(8,128)(2,1)S(1)}, bf16[160,640]{1,0:T(8,128)(2,1)S(1)}, u32[]{:S(2)}, u32[]{:S(2)}) %collective-permute-start.1) | collective-permute-done | bytes 204832 | tf_op jit(solution)/shard_map/ppermute | solution.py:25
  18.4 5.0 %collective-permute-done.2 = bf16[160,640]{1,0:T(8,128)(2,1)S(1)} collective-permute-done((bf16[160,640]{1,0:T(8,128)(2,1)S(1)}, bf16[160,640]{1,0:T(8,128)(2,1)S(1)}, u32[]{:S(2)}, u32[]{:S(2)}) %collective-permute-start.2) | collective-permute-done | bytes 204832 | tf_op jit(solution)/shard_map/ppermute | solution.py:25
  23.4 0.1 pad_maximum_fusion.refs_8_
  23.5 0.0 collective-permute-done.3.refs_4_
  23.5 0.1 collective-permute-start.11
  23.6 0.1 collective-permute-start.5
  23.7 2.0 %collective-permute-start.8 = (bf16[128,1280]{1,0:T(8,128)(2,1)S(1)}, bf16[128,1280]{1,0:T(8,128)(2,1)S(1)}, u32[]{:S(2)}, u32[]{:S(2)}) collective-permute-start(bf16[128,1280]{1,0:T(8,128)(2,1)S(1)} %copy-done.4), channel_id=1, source_target_pairs={{8,0},{24,8},{16,24},{0,16},{9,1},{25,9},{17,25},{1,17},{10,2},{26... | collective-permute-start | bytes 983048 | tf_op jit(solution)/shard_map/ppermute | solution.py:317
  25.7 1.5 %collective-permute-start.4 = (bf16[4,160,640]{2,1,0:T(8,128)(2,1)S(1)}, bf16[4,160,640]{2,1,0:T(8,128)(2,1)S(1)}, u32[]{:S(2)}, u32[]{:S(2)}) collective-permute-start(bf16[4,160,640]{2,1,0:T(8,128)(2,1)S(1)} %pad_maximum_fusion.refs_8_), channel_id=1, source_target_pairs={{0,4},{2,6},{4,0},{6,2},{1,5},{3,7},{5,1},{7,3},{8,12},{10,14},{12... | collective-permute-start | bytes 2457608 | tf_op jit(solution)/shard_map/ppermute | solution.py:25
  27.2 0.0 copy-done
  27.2 0.0 copy-done.1
  27.2 0.0 copy-done.2
  27.2 0.0 copy-done.3
  27.2 0.0 copy-start.6
  27.2 0.0 copy-start.7
  27.2 0.1 pad_maximum_fusion.1
  27.4 6.8 %collective-permute-done.5.refs_1_ = bf16[128,1280]{1,0:T(8,128)(2,1)S(1)} collective-permute-done((bf16[128,1280]{1,0:T(8,128)(2,1)S(1)}, bf16[128,1280]{1,0:T(8,128)(2,1)S(1)}, u32[]{:S(2)}, u32[]{:S(2)}) %collective-permute-start.5) | collective-permute-done | bytes 327712 | tf_op jit(solution)/shard_map/ppermute | solution.py:317
  34.2 1.5 %collective-permute-start.9 = (bf16[128,1280]{1,0:T(8,128)(2,1)S(1)}, bf16[128,1280]{1,0:T(8,128)(2,1)S(1)}, u32[]{:S(2)}, u32[]{:S(2)}) collective-permute-start(bf16[128,1280]{1,0:T(8,128)(2,1)S(1)} %collective-permute-done.5.refs_1_), channel_id=1, source_target_pairs={{0,1},{1,0},{2,3},{3,2},{4,5},{5,4},{6,7},{7,6},{8,9},{9,8},{10,11... | collective-permute-start | bytes 983048 | tf_op jit(solution)/shard_map/ppermute | solution.py:25
  35.7 0.8 collective-permute-start.6
  36.5 0.0 collective-permute-done.11.refs_9_
  36.5 1.9 %collective-permute-start.12 = (bf16[2,128,1280]{2,1,0:T(8,128)(2,1)S(1)}, bf16[2,128,1280]{2,1,0:T(8,128)(2,1)S(1)}, u32[]{:S(2)}, u32[]{:S(2)}) collective-permute-start(bf16[2,128,1280]{2,1,0:T(8,128)(2,1)S(1)} %get-tuple-element.30), channel_id=1, source_target_pairs={{0,2},{2,4},{4,6},{6,8},{8,10},{10,12},{12,14},{14,16},{16,18},{18... | collective-permute-start | bytes 1966088 | tf_op jit(solution)/shard_map/ppermute | solution.py:21
  38.5 2.7 %collective-permute-done.8.refs_3_ = bf16[128,1280]{1,0:T(8,128)(2,1)S(1)} collective-permute-done((bf16[128,1280]{1,0:T(8,128)(2,1)S(1)}, bf16[128,1280]{1,0:T(8,128)(2,1)S(1)}, u32[]{:S(2)}, u32[]{:S(2)}) %collective-permute-start.8) | collective-permute-done | bytes 327712 | tf_op jit(solution)/shard_map/ppermute | solution.py:317
  41.1 3.2 %collective-permute-start.13 = (bf16[2,128,1280]{2,1,0:T(8,128)(2,1)S(1)}, bf16[2,128,1280]{2,1,0:T(8,128)(2,1)S(1)}, u32[]{:S(2)}, u32[]{:S(2)}) collective-permute-start(bf16[2,128,1280]{2,1,0:T(8,128)(2,1)S(1)} %get-tuple-element.31), channel_id=1, source_target_pairs={{2,0},{4,2},{6,4},{8,6},{10,8},{12,10},{14,12},{16,14},{18,16},{20... | collective-permute-start | bytes 1966088 | tf_op jit(solution)/shard_map/ppermute | solution.py:21
  44.4 0.0 collective-permute-done.9.refs_5_
  44.4 1.6 %collective-permute-start.10 = (bf16[128,1280]{1,0:T(8,128)(2,1)S(1)}, bf16[128,1280]{1,0:T(8,128)(2,1)S(1)}, u32[]{:S(2)}, u32[]{:S(2)}) collective-permute-start(bf16[128,1280]{1,0:T(8,128)(2,1)S(1)} %collective-permute-done.8.refs_3_), channel_id=1, source_target_pairs={{0,1},{1,0},{2,3},{3,2},{4,5},{5,4},{6,7},{7,6},{8,9},{9,8},{10,11... | collective-permute-start | bytes 983048 | tf_op jit(solution)/shard_map/ppermute | solution.py:25
  46.0 1.9 %collective-permute-done.6.refs_2_ = bf16[128,1280]{1,0:T(8,128)(2,1)S(1)} collective-permute-done((bf16[128,1280]{1,0:T(8,128)(2,1)S(1)}, bf16[128,1280]{1,0:T(8,128)(2,1)S(1)}, u32[]{:S(2)}, u32[]{:S(2)}) %collective-permute-start.6) | collective-permute-done | bytes 327712 | tf_op jit(solution)/shard_map/ppermute | solution.py:317
  47.8 1.5 %collective-permute-start.7 = (bf16[128,1280]{1,0:T(8,128)(2,1)S(1)}, bf16[128,1280]{1,0:T(8,128)(2,1)S(1)}, u32[]{:S(2)}, u32[]{:S(2)}) collective-permute-start(bf16[128,1280]{1,0:T(8,128)(2,1)S(1)} %collective-permute-done.6.refs_2_), channel_id=1, source_target_pairs={{0,1},{1,0},{2,3},{3,2},{4,5},{5,4},{6,7},{7,6},{8,9},{9,8},{10,11... | collective-permute-start | bytes 983048 | tf_op jit(solution)/shard_map/ppermute | solution.py:25
  49.3 0.0 collective-permute-done.4.refs_10_
  49.3 5.7 %collective-permute-done.10.refs_7_ = bf16[128,1280]{1,0:T(8,128)(2,1)S(1)} collective-permute-done((bf16[128,1280]{1,0:T(8,128)(2,1)S(1)}, bf16[128,1280]{1,0:T(8,128)(2,1)S(1)}, u32[]{:S(2)}, u32[]{:S(2)}) %collective-permute-start.10) | collective-permute-done | bytes 327712 | tf_op jit(solution)/shard_map/ppermute | solution.py:25
  55.1 5.2 %collective-permute-done.7.refs_6_ = bf16[128,1280]{1,0:T(8,128)(2,1)S(1)} collective-permute-done((bf16[128,1280]{1,0:T(8,128)(2,1)S(1)}, bf16[128,1280]{1,0:T(8,128)(2,1)S(1)}, u32[]{:S(2)}, u32[]{:S(2)}) %collective-permute-start.7) | collective-permute-done | bytes 327712 | tf_op jit(solution)/shard_map/ppermute | solution.py:25
  60.3 0.0 collective-permute-done.12.kv1_ref
  60.3 0.0 collective-permute-done.13.qg1_ref
  60.3 0.1 collective-permute-start.14
  60.4 2.4 %collective-permute-start.15 = (bf16[2,128,1280]{2,1,0:T(8,128)(2,1)S(1)}, bf16[2,128,1280]{2,1,0:T(8,128)(2,1)S(1)}, u32[]{:S(2)}, u32[]{:S(2)}) collective-permute-start(bf16[2,128,1280]{2,1,0:T(8,128)(2,1)S(1)} %collective-permute-done.12.kv1_ref), channel_id=1, source_target_pairs={{0,2},{2,4},{4,6},{6,8},{8,10},{10,12},{12,14},{14,16},{16,18},{18... | collective-permute-start | bytes 1966088 | tf_op jit(solution)/shard_map/ppermute | solution.py:21
  62.8 0.0 copy-done.6
  62.8 0.0 copy-done.7
  62.8 0.3 prepare.1
  63.0 0.0 collective-permute-done.14.refs_11_
  63.0 4.6 %project.1 = bf16[16,4,16,640]{3,2,1,0:T(8,128)(2,1)} custom-call(s32[4,1,128]{2,1,0:T(1,128)S(1)} %get-tuple-element.33.place_ref, bf16[128,1280]{1,0:T(8,128)(2,1)S(1)} %copy-done.4, bf16[128,1280]{1,0:T(8,128)(2,1)S(1)} %collective-permute-done.5.refs_1_, bf16[128,1280]{1,0:T(8,128)(2,1)S(1)} %collective-permute-done.6.refs_2_, ...), custom_call_target="tpu_custom_call" | custom-call | flops 1677721600 | bytes 8388608 | tf_op jit(solution)/shard_map/project/pallas_call | solution.py:225
  67.6 0.0 copy-done.8
  67.6 0.0 copy-done.5
  67.6 5.5 %collective-permute-done.15.kv2_ref = bf16[2,128,1280]{2,1,0:T(8,128)(2,1)S(1)} collective-permute-done((bf16[2,128,1280]{2,1,0:T(8,128)(2,1)S(1)}, bf16[2,128,1280]{2,1,0:T(8,128)(2,1)S(1)}, u32[]{:S(2)}, u32[]{:S(2)}) %collective-permute-start.15) | collective-permute-done | bytes 655392 | tf_op jit(solution)/shard_map/ppermute | solution.py:21
  73.2 0.8 copy-done.9
  74.0 4.4 %all-to-all-start = ((bf16[16,4,16,640]{3,2,1,0:T(8,128)(2,1)}), bf16[16,4,16,640]{3,2,1,0:T(8,128)(2,1)S(1)}, u32[]{:S(2)}, u32[]{:S(2)}) async-start(bf16[16,4,16,640]{3,2,1,0:T(8,128)(2,1)} %project.1), calls=%async_computation | async-start | bytes 2621440 | tf_op jit(solution)/shard_map/all_to_all | solution.py:394
  78.4 3.1 %collective-permute-start.16 = (bf16[2,128,1280]{2,1,0:T(8,128)(2,1)S(1)}, bf16[2,128,1280]{2,1,0:T(8,128)(2,1)}, u32[]{:S(2)}, u32[]{:S(2)}) collective-permute-start(bf16[2,128,1280]{2,1,0:T(8,128)(2,1)S(1)} %collective-permute-done.13.qg1_ref), channel_id=1, source_target_pairs={{2,0},{4,2},{6,4},{8,6},{10,8},{12,10},{14,12},{16,14},{18,16},{20... | collective-permute-start | bytes 1966088 | tf_op jit(solution)/shard_map/ppermute | solution.py:21
  81.5 27.7 %all-to-all-done = bf16[16,4,16,640]{3,2,1,0:T(8,128)(2,1)S(1)} async-done(((bf16[16,4,16,640]{3,2,1,0:T(8,128)(2,1)}), bf16[16,4,16,640]{3,2,1,0:T(8,128)(2,1)S(1)}, u32[]{:S(2)}, u32[]{:S(2)}) %all-to-all-start) | async-done | bytes 1310752 | tf_op jit(solution)/shard_map/all_to_all | solution.py:394
  109.2 5.0 %attend.1 = (bf16[128,1280]{1,0:T(8,128)(2,1)}, bf16[128,1280]{1,0:T(8,128)(2,1)}, f32[2,16,128]{2,1,0:T(8,128)S(1)}) custom-call(bf16[128,1280]{1,0:T(8,128)(2,1)S(1)} %copy-done, bf16[128,1280]{1,0:T(8,128)(2,1)S(1)} %copy-done.1, bf16[128,1280]{1,0:T(8,128)(2,1)S(1)} %copy-done.2, bf16[128,1280]{1,0:T(8,128)(2,1)S(1)} %copy-done.3, ...), custom_call_target="tpu_custom_call" | custom-call | flops 838860800 | bytes 6291456 | tf_op jit(solution)/shard_map/attend/pallas_call | solution.py:103
  114.1 2.9 %collective-permute-start.17 = (f32[2,16,128]{2,1,0:T(8,128)S(1)}, f32[2,16,128]{2,1,0:T(8,128)S(1)}, u32[]{:S(2)}, u32[]{:S(2)}) collective-permute-start(f32[2,16,128]{2,1,0:T(8,128)S(1)} %get-tuple-element.46.st0_ref), channel_id=1, source_target_pairs={{2,0},{4,2},{6,4},{8,6},{10,8},{12,10},{14,12},{16,14},{18,16},{20... | collective-permute-start | bytes 49160 | tf_op jit(solution)/shard_map/ppermute | solution.py:21
  117.0 2.1 %collective-permute-start.18 = (f32[2,16,128]{2,1,0:T(8,128)S(1)}, f32[2,16,128]{2,1,0:T(8,128)S(1)}, u32[]{:S(2)}, u32[]{:S(2)}) collective-permute-start(f32[2,16,128]{2,1,0:T(8,128)S(1)} %get-tuple-element.46.st0_ref), channel_id=1, source_target_pairs={{4,0},{6,2},{8,4},{10,6},{12,8},{14,10},{16,12},{18,14},{20,16},{2... | collective-permute-start | bytes 49160 | tf_op jit(solution)/shard_map/ppermute | solution.py:21
  119.1 0.0 collective-permute-done.16.qg2_ref
  119.1 0.0 collective-permute-done.17.st1_ref
  119.2 3.5 %collective-permute-done.18.st2_ref = f32[2,16,128]{2,1,0:T(8,128)S(1)} collective-permute-done((f32[2,16,128]{2,1,0:T(8,128)S(1)}, f32[2,16,128]{2,1,0:T(8,128)S(1)}, u32[]{:S(2)}, u32[]{:S(2)}) %collective-permute-start.18) | collective-permute-done | bytes 16416 | tf_op jit(solution)/shard_map/ppermute | solution.py:21
  122.7 3.7 %key_grads.1 = (bf16[128,1280]{1,0:T(8,128)(2,1)}, bf16[128,1280]{1,0:T(8,128)(2,1)}) custom-call(bf16[128,1280]{1,0:T(8,128)(2,1)S(1)} %copy-done.2, bf16[128,1280]{1,0:T(8,128)(2,1)S(1)} %copy-done.3, bf16[128,1280]{1,0:T(8,128)(2,1)S(1)} %copy-done, bf16[128,1280]{1,0:T(8,128)(2,1)S(1)} %copy-done.1, ...), custom_call_target="tpu_custom_call" | custom-call | flops 503316480 | bytes 4194304 | tf_op jit(solution)/shard_map/key_grads/pallas_call | solution.py:166
  (3 shorter events, 0.0 us)
Async XLA Ops:
  0.6 5.1 %copy-start.4 = (bf16[128,1280]{1,0:T(8,128)(2,1)S(1)}, bf16[128,1280]{1,0:T(8,128)(2,1)}, u32[]{:S(2)}) copy-start(bf16[128,1280]{1,0:T(8,128)(2,1)} %refs_0_) | copy-start | bytes 983044
  0.7 26.5 %copy-start = (bf16[128,1280]{1,0:T(8,128)(2,1)S(1)}, bf16[128,1280]{1,0:T(8,128)(2,1)}, u32[]{:S(2)}) copy-start(bf16[128,1280]{1,0:T(8,128)(2,1)} %q_ref.3) | copy-start | bytes 983044
  0.7 26.5 %copy-start.1 = (bf16[128,1280]{1,0:T(8,128)(2,1)S(1)}, bf16[128,1280]{1,0:T(8,128)(2,1)}, u32[]{:S(2)}) copy-start(bf16[128,1280]{1,0:T(8,128)(2,1)} %g_ref.3) | copy-start | bytes 983044
  0.7 26.5 %copy-start.2 = (bf16[128,1280]{1,0:T(8,128)(2,1)S(1)}, bf16[128,1280]{1,0:T(8,128)(2,1)}, u32[]{:S(2)}) copy-start(bf16[128,1280]{1,0:T(8,128)(2,1)} %k_ref.3) | copy-start | bytes 983044
  0.7 26.5 %copy-start.3 = (bf16[128,1280]{1,0:T(8,128)(2,1)S(1)}, bf16[128,1280]{1,0:T(8,128)(2,1)}, u32[]{:S(2)}) copy-start(bf16[128,1280]{1,0:T(8,128)(2,1)} %v_ref.3) | copy-start | bytes 983044
  2.1 9.0 %collective-permute-start = (bf16[160,640]{1,0:T(8,128)(2,1)S(1)}, bf16[160,640]{1,0:T(8,128)(2,1)S(1)}, u32[]{:S(2)}, u32[]{:S(2)}) collective-permute-start(bf16[160,640]{1,0:T(8,128)(2,1)S(1)} %get-tuple-element.51), channel_id=1, source_target_pairs={{0,8},{8,0},{16,24},{24,16},{1,9},{9,1},{17,25},{25,17},{2,10},{10... | collective-permute-start | bytes 614408 | tf_op jit(solution)/shard_map/ppermute | solution.py:25
  3.8 14.6 %collective-permute-start.1 = (bf16[160,640]{1,0:T(8,128)(2,1)S(1)}, bf16[160,640]{1,0:T(8,128)(2,1)S(1)}, u32[]{:S(2)}, u32[]{:S(2)}) collective-permute-start(bf16[160,640]{1,0:T(8,128)(2,1)S(1)} %get-tuple-element.53), channel_id=1, source_target_pairs={{0,16},{8,24},{16,0},{24,8},{1,17},{9,25},{17,1},{25,9},{2,18},{10... | collective-permute-start | bytes 614408 | tf_op jit(solution)/shard_map/ppermute | solution.py:25
  4.1 19.3 %collective-permute-start.2 = (bf16[160,640]{1,0:T(8,128)(2,1)S(1)}, bf16[160,640]{1,0:T(8,128)(2,1)S(1)}, u32[]{:S(2)}, u32[]{:S(2)}) collective-permute-start(bf16[160,640]{1,0:T(8,128)(2,1)S(1)} %get-tuple-element.52), channel_id=1, source_target_pairs={{0,24},{8,16},{16,8},{24,0},{1,25},{9,17},{17,9},{25,1},{2,26},{10... | collective-permute-start | bytes 614408 | tf_op jit(solution)/shard_map/ppermute | solution.py:25
  5.7 17.8 %collective-permute-start.3 = (bf16[128,1280]{1,0:T(8,128)(2,1)S(1)}, bf16[128,1280]{1,0:T(8,128)(2,1)S(1)}, u32[]{:S(2)}, u32[]{:S(2)}) collective-permute-start(bf16[128,1280]{1,0:T(8,128)(2,1)S(1)} %copy-done.4), channel_id=1, source_target_pairs={{0,1},{1,0},{2,3},{3,2},{4,5},{5,4},{6,7},{7,6},{8,9},{9,8},{10,11... | collective-permute-start | bytes 983048 | tf_op jit(solution)/shard_map/ppermute | solution.py:25
  23.5 13.0 %collective-permute-start.11 = (bf16[4,160,640]{2,1,0:T(8,128)(2,1)S(1)}, bf16[4,160,640]{2,1,0:T(8,128)(2,1)S(1)}, u32[]{:S(2)}, u32[]{:S(2)}) collective-permute-start(bf16[4,160,640]{2,1,0:T(8,128)(2,1)S(1)} %pad_maximum_fusion.refs_8_), channel_id=1, source_target_pairs={{0,2},{2,0},{4,6},{6,4},{1,3},{3,1},{5,7},{7,5},{8,10},{10,8},{12,... | collective-permute-start | bytes 2457608 | tf_op jit(solution)/shard_map/ppermute | solution.py:25
  23.6 10.6 %collective-permute-start.5 = (bf16[128,1280]{1,0:T(8,128)(2,1)S(1)}, bf16[128,1280]{1,0:T(8,128)(2,1)S(1)}, u32[]{:S(2)}, u32[]{:S(2)}) collective-permute-start(bf16[128,1280]{1,0:T(8,128)(2,1)S(1)} %copy-done.4), channel_id=1, source_target_pairs={{0,8},{8,24},{24,16},{16,0},{1,9},{9,25},{25,17},{17,1},{2,10},{10... | collective-permute-start | bytes 983048 | tf_op jit(solution)/shard_map/ppermute | solution.py:317
  23.7 17.5 %collective-permute-start.8 = (bf16[128,1280]{1,0:T(8,128)(2,1)S(1)}, bf16[128,1280]{1,0:T(8,128)(2,1)S(1)}, u32[]{:S(2)}, u32[]{:S(2)}) collective-permute-start(bf16[128,1280]{1,0:T(8,128)(2,1)S(1)} %copy-done.4), channel_id=1, source_target_pairs={{8,0},{24,8},{16,24},{0,16},{9,1},{25,9},{17,25},{1,17},{10,2},{26... | collective-permute-start | bytes 983048 | tf_op jit(solution)/shard_map/ppermute | solution.py:317
  25.7 23.6 %collective-permute-start.4 = (bf16[4,160,640]{2,1,0:T(8,128)(2,1)S(1)}, bf16[4,160,640]{2,1,0:T(8,128)(2,1)S(1)}, u32[]{:S(2)}, u32[]{:S(2)}) collective-permute-start(bf16[4,160,640]{2,1,0:T(8,128)(2,1)S(1)} %pad_maximum_fusion.refs_8_), channel_id=1, source_target_pairs={{0,4},{2,6},{4,0},{6,2},{1,5},{3,7},{5,1},{7,3},{8,12},{10,14},{12... | collective-permute-start | bytes 2457608 | tf_op jit(solution)/shard_map/ppermute | solution.py:25
  27.2 35.6 %copy-start.6 = (s32[2048]{0:T(1024)S(1)}, s32[2048]{0:T(1024)}, u32[]{:S(2)}) copy-start(s32[2048]{0:T(1024)} %param.15) | copy-start | bytes 24580
  27.2 35.6 %copy-start.7 = (s32[2048]{0:T(1024)S(1)}, s32[2048]{0:T(1024)}, u32[]{:S(2)}) copy-start(s32[2048]{0:T(1024)} %param.14) | copy-start | bytes 24580
  34.2 10.2 %collective-permute-start.9 = (bf16[128,1280]{1,0:T(8,128)(2,1)S(1)}, bf16[128,1280]{1,0:T(8,128)(2,1)S(1)}, u32[]{:S(2)}, u32[]{:S(2)}) collective-permute-start(bf16[128,1280]{1,0:T(8,128)(2,1)S(1)} %collective-permute-done.5.refs_1_), channel_id=1, source_target_pairs={{0,1},{1,0},{2,3},{3,2},{4,5},{5,4},{6,7},{7,6},{8,9},{9,8},{10,11... | collective-permute-start | bytes 983048 | tf_op jit(solution)/shard_map/ppermute | solution.py:25
  35.7 12.1 %collective-permute-start.6 = (bf16[128,1280]{1,0:T(8,128)(2,1)S(1)}, bf16[128,1280]{1,0:T(8,128)(2,1)S(1)}, u32[]{:S(2)}, u32[]{:S(2)}) collective-permute-start(bf16[128,1280]{1,0:T(8,128)(2,1)S(1)} %collective-permute-done.5.refs_1_), channel_id=1, source_target_pairs={{0,8},{8,24},{24,16},{16,0},{1,9},{9,25},{25,17},{17,1},{2,10},{10... | collective-permute-start | bytes 983048 | tf_op jit(solution)/shard_map/ppermute | solution.py:317
  36.5 23.7 %collective-permute-start.12 = (bf16[2,128,1280]{2,1,0:T(8,128)(2,1)S(1)}, bf16[2,128,1280]{2,1,0:T(8,128)(2,1)S(1)}, u32[]{:S(2)}, u32[]{:S(2)}) collective-permute-start(bf16[2,128,1280]{2,1,0:T(8,128)(2,1)S(1)} %get-tuple-element.30), channel_id=1, source_target_pairs={{0,2},{2,4},{4,6},{6,8},{8,10},{10,12},{12,14},{14,16},{16,18},{18... | collective-permute-start | bytes 1966088 | tf_op jit(solution)/shard_map/ppermute | solution.py:21
  41.1 19.1 %collective-permute-start.13 = (bf16[2,128,1280]{2,1,0:T(8,128)(2,1)S(1)}, bf16[2,128,1280]{2,1,0:T(8,128)(2,1)S(1)}, u32[]{:S(2)}, u32[]{:S(2)}) collective-permute-start(bf16[2,128,1280]{2,1,0:T(8,128)(2,1)S(1)} %get-tuple-element.31), channel_id=1, source_target_pairs={{2,0},{4,2},{6,4},{8,6},{10,8},{12,10},{14,12},{16,14},{18,16},{20... | collective-permute-start | bytes 1966088 | tf_op jit(solution)/shard_map/ppermute | solution.py:21
  44.4 10.7 %collective-permute-start.10 = (bf16[128,1280]{1,0:T(8,128)(2,1)S(1)}, bf16[128,1280]{1,0:T(8,128)(2,1)S(1)}, u32[]{:S(2)}, u32[]{:S(2)}) collective-permute-start(bf16[128,1280]{1,0:T(8,128)(2,1)S(1)} %collective-permute-done.8.refs_3_), channel_id=1, source_target_pairs={{0,1},{1,0},{2,3},{3,2},{4,5},{5,4},{6,7},{7,6},{8,9},{9,8},{10,11... | collective-permute-start | bytes 983048 | tf_op jit(solution)/shard_map/ppermute | solution.py:25
  47.8 12.4 %collective-permute-start.7 = (bf16[128,1280]{1,0:T(8,128)(2,1)S(1)}, bf16[128,1280]{1,0:T(8,128)(2,1)S(1)}, u32[]{:S(2)}, u32[]{:S(2)}) collective-permute-start(bf16[128,1280]{1,0:T(8,128)(2,1)S(1)} %collective-permute-done.6.refs_2_), channel_id=1, source_target_pairs={{0,1},{1,0},{2,3},{3,2},{4,5},{5,4},{6,7},{7,6},{8,9},{9,8},{10,11... | collective-permute-start | bytes 983048 | tf_op jit(solution)/shard_map/ppermute | solution.py:25
  60.3 7.4 %copy-start.8 = (bf16[2,128,1280]{2,1,0:T(8,128)(2,1)}, bf16[2,128,1280]{2,1,0:T(8,128)(2,1)S(1)}, u32[]{:S(2)}) copy-start(bf16[2,128,1280]{2,1,0:T(8,128)(2,1)S(1)} %collective-permute-done.12.kv1_ref) | copy-start | bytes 1966084
  60.3 2.8 %collective-permute-start.14 = (bf16[4,160,640]{2,1,0:T(8,128)(2,1)S(1)}, bf16[4,160,640]{2,1,0:T(8,128)(2,1)S(1)}, u32[]{:S(2)}, u32[]{:S(2)}) collective-permute-start(bf16[4,160,640]{2,1,0:T(8,128)(2,1)S(1)} %collective-permute-done.4.refs_10_), channel_id=1, source_target_pairs={{0,2},{2,0},{4,6},{6,4},{1,3},{3,1},{5,7},{7,5},{8,10},{10,8},{12,... | collective-permute-start | bytes 2457608 | tf_op jit(solution)/shard_map/ppermute | solution.py:25
  60.4 12.8 %collective-permute-start.15 = (bf16[2,128,1280]{2,1,0:T(8,128)(2,1)S(1)}, bf16[2,128,1280]{2,1,0:T(8,128)(2,1)S(1)}, u32[]{:S(2)}, u32[]{:S(2)}) collective-permute-start(bf16[2,128,1280]{2,1,0:T(8,128)(2,1)S(1)} %collective-permute-done.12.kv1_ref), channel_id=1, source_target_pairs={{0,2},{2,4},{4,6},{6,8},{8,10},{10,12},{12,14},{14,16},{16,18},{18... | collective-permute-start | bytes 1966088 | tf_op jit(solution)/shard_map/ppermute | solution.py:21
  63.0 4.6 %copy-start.5 = (bf16[128,640]{1,0:T(8,128)(2,1)}, bf16[128,640]{1,0:T(8,128)(2,1)S(1)}, u32[]{:S(2)}) copy-start(bf16[128,640]{1,0:T(8,128)(2,1)S(1)} %get-tuple-element.42.bias_ref) | copy-start | bytes 491524
  73.2 0.9 copy-start.9
  74.0 35.1 %all-to-all-start = ((bf16[16,4,16,640]{3,2,1,0:T(8,128)(2,1)}), bf16[16,4,16,640]{3,2,1,0:T(8,128)(2,1)S(1)}, u32[]{:S(2)}, u32[]{:S(2)}) async-start(bf16[16,4,16,640]{3,2,1,0:T(8,128)(2,1)} %project.1), calls=%async_computation | async-start | bytes 2621440 | tf_op jit(solution)/shard_map/all_to_all | solution.py:394
  78.4 40.8 %collective-permute-start.16 = (bf16[2,128,1280]{2,1,0:T(8,128)(2,1)S(1)}, bf16[2,128,1280]{2,1,0:T(8,128)(2,1)}, u32[]{:S(2)}, u32[]{:S(2)}) collective-permute-start(bf16[2,128,1280]{2,1,0:T(8,128)(2,1)S(1)} %collective-permute-done.13.qg1_ref), channel_id=1, source_target_pairs={{2,0},{4,2},{6,4},{8,6},{10,8},{12,10},{14,12},{16,14},{18,16},{20... | collective-permute-start | bytes 1966088 | tf_op jit(solution)/shard_map/ppermute | solution.py:21
  114.1 5.0 %collective-permute-start.17 = (f32[2,16,128]{2,1,0:T(8,128)S(1)}, f32[2,16,128]{2,1,0:T(8,128)S(1)}, u32[]{:S(2)}, u32[]{:S(2)}) collective-permute-start(f32[2,16,128]{2,1,0:T(8,128)S(1)} %get-tuple-element.46.st0_ref), channel_id=1, source_target_pairs={{2,0},{4,2},{6,4},{8,6},{10,8},{12,10},{14,12},{16,14},{18,16},{20... | collective-permute-start | bytes 49160 | tf_op jit(solution)/shard_map/ppermute | solution.py:21
  117.0 5.6 %collective-permute-start.18 = (f32[2,16,128]{2,1,0:T(8,128)S(1)}, f32[2,16,128]{2,1,0:T(8,128)S(1)}, u32[]{:S(2)}, u32[]{:S(2)}) collective-permute-start(f32[2,16,128]{2,1,0:T(8,128)S(1)} %get-tuple-element.46.st0_ref), channel_id=1, source_target_pairs={{4,0},{6,2},{8,4},{10,6},{12,8},{14,10},{16,12},{18,14},{20,16},{2... | collective-permute-start | bytes 49160 | tf_op jit(solution)/shard_map/ppermute | solution.py:21

commit v12 on v3

--- a/solution.py
+++ b/solution.py
@@ -9,7 +9,6 @@
 GROUPS = 4
 SEQ = ("z", "p")
 ROW_TILE = 16
-RING = [0, 1, 3, 2]
 VMEM = 24 * 1024 * 1024
 SMALL_VMEM = 4 * 1024 * 1024
 STATS = 16
@@ -189,10 +188,8 @@
     depth = rows[0].shape[1]
     devices, _, capacity, _ = out_ref.shape
     z, p, y = (lax.axis_index(name) for name in ("z", "p", "head"))
-    place_in_ring = z ^ (z >> 1)
     for i, ref in enumerate(rows):
-        source = (place_in_ring - i % n_z + n_z) & (n_z - 1)
-        a_ref[y ^ (i // n_z), source ^ (source >> 1)] = ref[...]
+        a_ref[y ^ (i // n_z), z ^ (i % n_z)] = ref[...]
     for m in range(n_p):
         for k in range(n_z):
             w_ref[z ^ k, p ^ m] = pieces[m][k]
@@ -312,11 +309,6 @@
     return lax.dynamic_slice(w_kv, start, (1, w_rows, half))[0]
 
 
-def ring_step(value, back=False):
-    pairs = list(zip(RING, RING[1:] + RING[:1]))
-    return lax.ppermute(value, "z", [(b, a) for a, b in pairs] if back else pairs)
-
-
 def memory_slots(cache, w_kv, place, capacity, stream, back):
     n_z, n_p = lax.axis_size("z"), lax.axis_size("p")
     devices = n_z * n_p
@@ -328,15 +320,16 @@
         own = jnp.stack(
             [blocks[0]] + [swapped(blocks[mask], "z", mask) for mask in range(1, n_z)], 0
         )
-        row1, other0 = ring_step(cache), swapped(cache, "head", 1)
+        row1, other0 = swapped(cache, "z", 1), swapped(cache, "head", 1)
         own, row1, other0, cache = lax.optimization_barrier((own, row1, other0, cache))
-        across = swapped(own, "p", 2)
-        beside = swapped(own, "p", 1)
-        row2, row3, other1 = ring_step(row1), ring_step(cache, back=True), swapped(row1, "head", 1)
+        across, beside = swapped(own, "p", 2), swapped(own, "p", 1)
+        row2, other1 = swapped(cache, "z", 2), swapped(row1, "head", 1)
         beside, stream, back = lax.optimization_barrier((beside, stream, back))
         near, back1 = shifted(stream, 1), shifted(back, -1)
-        row2, row3, other1 = lax.optimization_barrier((row2, row3, other1))
-        other2, other3 = swapped(row2, "head", 1), swapped(row3, "head", 1)
+        row2, other1 = lax.optimization_barrier((row2, other1))
+        row3, other2 = swapped(row2, "z", 1), swapped(row2, "head", 1)
+        row3, other2 = lax.optimization_barrier((row3, other2))
+        other3 = swapped(row3, "head", 1)
         across, other2, other3, near, back1 = lax.optimization_barrier(
             (across, other2, other3, near, back1)
         )

time: 135 us -> 134 us (level)
  starting transfers between devices: 45.9 us -> 44.3 us
    ppermute x10 -> x13, starting transfers between devices: 12.6 us -> 21.6 us  [swapped(): lax.ppermute(value, axis, [(i, i ^ mask) for i in range(lax.axis_size(axi...]
    ppermute x10 -> x13, waiting for transfers between devices: 28 us -> 35.1 us  [swapped(): lax.ppermute(value, axis, [(i, i ^ mask) for i in range(lax.axis_size(axi...]
    ppermute x3 -> x0, waiting for transfers between devices: 6.79 us -> none  [ring_step(): lax.ppermute(value, 'z', [(b, a) for a, b in pairs] if back else pairs)]
    ppermute x6, starting transfers between devices: 21.5 us -> 16.4 us  [shifted(): return lax.ppermute(value, SEQ, pairs)]
    ppermute x3 -> x0, starting transfers between devices: 4.63 us -> none  [ring_step(): lax.ppermute(value, 'z', [(b, a) for a, b in pairs] if back else pairs)]
where the time goes in v12:
time: 134 us
  waiting for transfers between devices  72.2 us (54%)
  starting transfers between devices  44.3 us (33%)
  Pallas kernels  13.6 us (10%)
  local copies, waits for them, and re-layouts  2.31 us (2%)
    ppermute x13, waiting for transfers between devices, swapped(): lax.ppermute(value, axis, [(i, i ^ mask) for i in range(lax.axis_size(axi...  35.1 us
    all_to_all x1, waiting for transfers between devices, body(): memory = lax.all_to_all(slots, SEQ, split_axis=0, concat_axis=0, tiled=True)  27.7 us
    ppermute x13, starting transfers between devices, swapped(): lax.ppermute(value, axis, [(i, i ^ mask) for i in range(lax.axis_size(axi...  21.6 us
    ppermute x6, starting transfers between devices, shifted(): return lax.ppermute(value, SEQ, pairs)  16.4 us
    ppermute x6, waiting for transfers between devices, shifted(): return lax.ppermute(value, SEQ, pairs)  9.51 us
    all_to_all x1, starting transfers between devices, body(): memory = lax.all_to_all(slots, SEQ, split_axis=0, concat_axis=0, tiled=True)  6.28 us
    pallas_call x1, Pallas kernels, attend(): pl.pallas_call(attend_kernel, grid=(steps,), in_specs=[flat, flat, flat,...  4.98 us
    pallas_call x1, Pallas kernels, project(): pl.pallas_call(project_kernel, in_specs=[whole] * (1 + len(rows) + n_p),...  4.6 us
  transfers between devices with their start and end apart: 20, of which 10 were waited for; matrix products, arithmetic and copies ran while one was open for 0% of the time, Pallas kernels for 7%

profile of v12, /device:TPU:16, one launch (start us, length us, event | category | flops | bytes accessed | tf_op | source)
XLA Modules:
  0.0 133.5 jit_solution(4132114098674094240)
XLA Ops:
  0.6 0.0 copy-start.4
  0.7 0.0 copy-start
  0.7 0.0 copy-start.1
  0.7 0.0 copy-start.2
  0.7 0.0 copy-start.3
  0.7 1.4 %constant_dynamic-slice_fusion = (bf16[1,160,640]{2,1,0:T(8,128)(2,1)S(1)}, bf16[160,640]{1,0:T(8,128)(2,1)S(1)}, bf16[160,640]{1,0:T(8,128)(2,1)S(1)}, bf16[160,640]{1,0:T(8,128)(2,1)S(1)}) fusion(bf16[2,160,1280]{2,1,0:T(8,128)(2,1)} %param.13, s32[]{:T(128)S(6)} %select_n.24, s32[]{:T(128)S(6)} %select_n.25, s32[]{:T(128)S(6)} %select_n.26, ...), kind=kLoop, calls=%fused_computation.6 | loop fusion | bytes 1638432 | tf_op jit(solution)/shard_map/dynamic_slice | solution.py:309
  2.1 1.6 %collective-permute-start = (bf16[160,640]{1,0:T(8,128)(2,1)S(1)}, bf16[160,640]{1,0:T(8,128)(2,1)S(1)}, u32[]{:S(2)}, u32[]{:S(2)}) collective-permute-start(bf16[160,640]{1,0:T(8,128)(2,1)S(1)} %get-tuple-element.57), channel_id=1, source_target_pairs={{0,8},{8,0},{16,24},{24,16},{1,9},{9,1},{17,25},{25,17},{2,10},{10... | collective-permute-start | bytes 614408 | tf_op jit(solution)/shard_map/ppermute | solution.py:24
  3.8 0.3 collective-permute-start.1
  4.1 1.6 %collective-permute-start.2 = (bf16[160,640]{1,0:T(8,128)(2,1)S(1)}, bf16[160,640]{1,0:T(8,128)(2,1)S(1)}, u32[]{:S(2)}, u32[]{:S(2)}) collective-permute-start(bf16[160,640]{1,0:T(8,128)(2,1)S(1)} %get-tuple-element.58), channel_id=1, source_target_pairs={{0,24},{8,16},{16,8},{24,0},{1,25},{9,17},{17,9},{25,1},{2,26},{10... | collective-permute-start | bytes 614408 | tf_op jit(solution)/shard_map/ppermute | solution.py:24
  5.7 0.0 copy-done.4
  5.7 2.5 %collective-permute-start.3 = (bf16[128,1280]{1,0:T(8,128)(2,1)S(1)}, bf16[128,1280]{1,0:T(8,128)(2,1)S(1)}, u32[]{:S(2)}, u32[]{:S(2)}) collective-permute-start(bf16[128,1280]{1,0:T(8,128)(2,1)S(1)} %copy-done.4), channel_id=1, source_target_pairs={{0,8},{8,0},{16,24},{24,16},{1,9},{9,1},{17,25},{25,17},{2,10},{10... | collective-permute-start | bytes 983048 | tf_op jit(solution)/shard_map/ppermute | solution.py:24
  8.2 1.5 %collective-permute-start.4 = (bf16[128,1280]{1,0:T(8,128)(2,1)S(1)}, bf16[128,1280]{1,0:T(8,128)(2,1)S(1)}, u32[]{:S(2)}, u32[]{:S(2)}) collective-permute-start(bf16[128,1280]{1,0:T(8,128)(2,1)S(1)} %copy-done.4), channel_id=1, source_target_pairs={{0,1},{1,0},{2,3},{3,2},{4,5},{5,4},{6,7},{7,6},{8,9},{9,8},{10,11... | collective-permute-start | bytes 983048 | tf_op jit(solution)/shard_map/ppermute | solution.py:24
  9.7 3.2 %collective-permute-done = bf16[160,640]{1,0:T(8,128)(2,1)S(1)} collective-permute-done((bf16[160,640]{1,0:T(8,128)(2,1)S(1)}, bf16[160,640]{1,0:T(8,128)(2,1)S(1)}, u32[]{:S(2)}, u32[]{:S(2)}) %collective-permute-start) | collective-permute-done | bytes 204832 | tf_op jit(solution)/shard_map/ppermute | solution.py:24
  12.9 5.4 %collective-permute-done.1 = bf16[160,640]{1,0:T(8,128)(2,1)S(1)} collective-permute-done((bf16[160,640]{1,0:T(8,128)(2,1)S(1)}, bf16[160,640]{1,0:T(8,128)(2,1)S(1)}, u32[]{:S(2)}, u32[]{:S(2)}) %collective-permute-start.1) | collective-permute-done | bytes 204832 | tf_op jit(solution)/shard_map/ppermute | solution.py:24
  18.3 5.1 %collective-permute-done.2 = bf16[160,640]{1,0:T(8,128)(2,1)S(1)} collective-permute-done((bf16[160,640]{1,0:T(8,128)(2,1)S(1)}, bf16[160,640]{1,0:T(8,128)(2,1)S(1)}, u32[]{:S(2)}, u32[]{:S(2)}) %collective-permute-start.2) | collective-permute-done | bytes 204832 | tf_op jit(solution)/shard_map/ppermute | solution.py:24
  23.4 0.1 pad_maximum_fusion.refs_8_
  23.6 1.3 collective-permute-done.3.refs_1_
  24.9 0.0 collective-permute-done.4.refs_4_
  24.9 0.0 collective-permute-start.11
  24.9 0.1 collective-permute-start.6
  25.0 1.7 %collective-permute-start.7 = (bf16[128,1280]{1,0:T(8,128)(2,1)S(1)}, bf16[128,1280]{1,0:T(8,128)(2,1)S(1)}, u32[]{:S(2)}, u32[]{:S(2)}) collective-permute-start(bf16[128,1280]{1,0:T(8,128)(2,1)S(1)} %collective-permute-done.3.refs_1_), channel_id=1, source_target_pairs={{0,1},{1,0},{2,3},{3,2},{4,5},{5,4},{6,7},{7,6},{8,9},{9,8},{10,11... | collective-permute-start | bytes 983048 | tf_op jit(solution)/shard_map/ppermute | solution.py:24
  26.7 1.5 %collective-permute-start.5 = (bf16[4,160,640]{2,1,0:T(8,128)(2,1)S(1)}, bf16[4,160,640]{2,1,0:T(8,128)(2,1)S(1)}, u32[]{:S(2)}, u32[]{:S(2)}) collective-permute-start(bf16[4,160,640]{2,1,0:T(8,128)(2,1)S(1)} %pad_maximum_fusion.refs_8_), channel_id=1, source_target_pairs={{0,4},{2,6},{4,0},{6,2},{1,5},{3,7},{5,1},{7,3},{8,12},{10,14},{12... | collective-permute-start | bytes 2457608 | tf_op jit(solution)/shard_map/ppermute | solution.py:24
  28.2 0.0 copy-done
  28.2 0.0 copy-done.1
  28.2 0.0 copy-done.2
  28.2 0.0 copy-done.3
  28.2 0.0 copy-start.6
  28.2 0.0 copy-start.7
  28.2 0.1 pad_maximum_fusion.1
  28.3 11.5 %collective-permute-done.6.refs_2_ = bf16[128,1280]{1,0:T(8,128)(2,1)S(1)} collective-permute-done((bf16[128,1280]{1,0:T(8,128)(2,1)S(1)}, bf16[128,1280]{1,0:T(8,128)(2,1)S(1)}, u32[]{:S(2)}, u32[]{:S(2)}) %collective-permute-start.6) | collective-permute-done | bytes 327712 | tf_op jit(solution)/shard_map/ppermute | solution.py:24
  39.9 0.0 collective-permute-done.7.refs_5_
  39.9 4.6 %collective-permute-start.8 = (bf16[128,1280]{1,0:T(8,128)(2,1)S(1)}, bf16[128,1280]{1,0:T(8,128)(2,1)S(1)}, u32[]{:S(2)}, u32[]{:S(2)}) collective-permute-start(bf16[128,1280]{1,0:T(8,128)(2,1)S(1)} %collective-permute-done.6.refs_2_), channel_id=1, source_target_pairs={{0,8},{8,0},{16,24},{24,16},{1,9},{9,1},{17,25},{25,17},{2,10},{10... | collective-permute-start | bytes 983048 | tf_op jit(solution)/shard_map/ppermute | solution.py:24
  44.4 1.5 %collective-permute-start.9 = (bf16[128,1280]{1,0:T(8,128)(2,1)S(1)}, bf16[128,1280]{1,0:T(8,128)(2,1)S(1)}, u32[]{:S(2)}, u32[]{:S(2)}) collective-permute-start(bf16[128,1280]{1,0:T(8,128)(2,1)S(1)} %collective-permute-done.6.refs_2_), channel_id=1, source_target_pairs={{0,1},{1,0},{2,3},{3,2},{4,5},{5,4},{6,7},{7,6},{8,9},{9,8},{10,11... | collective-permute-start | bytes 983048 | tf_op jit(solution)/shard_map/ppermute | solution.py:24
  45.9 0.0 collective-permute-done.11.refs_9_
  45.9 1.9 %collective-permute-start.12 = (bf16[2,128,1280]{2,1,0:T(8,128)(2,1)S(1)}, bf16[2,128,1280]{2,1,0:T(8,128)(2,1)S(1)}, u32[]{:S(2)}, u32[]{:S(2)}) collective-permute-start(bf16[2,128,1280]{2,1,0:T(8,128)(2,1)S(1)} %get-tuple-element.36), channel_id=1, source_target_pairs={{0,2},{2,4},{4,6},{6,8},{8,10},{10,12},{12,14},{14,16},{16,18},{18... | collective-permute-start | bytes 1966088 | tf_op jit(solution)/shard_map/ppermute | solution.py:20
  47.9 4.5 %collective-permute-start.13 = (bf16[2,128,1280]{2,1,0:T(8,128)(2,1)S(1)}, bf16[2,128,1280]{2,1,0:T(8,128)(2,1)S(1)}, u32[]{:S(2)}, u32[]{:S(2)}) collective-permute-start(bf16[2,128,1280]{2,1,0:T(8,128)(2,1)S(1)} %get-tuple-element.37), channel_id=1, source_target_pairs={{2,0},{4,2},{6,4},{8,6},{10,8},{12,10},{14,12},{16,14},{18,16},{20... | collective-permute-start | bytes 1966088 | tf_op jit(solution)/shard_map/ppermute | solution.py:20
  52.4 0.0 collective-permute-done.8.refs_3_
  52.4 1.4 %collective-permute-done.9.refs_6_ = bf16[128,1280]{1,0:T(8,128)(2,1)S(1)} collective-permute-done((bf16[128,1280]{1,0:T(8,128)(2,1)S(1)}, bf16[128,1280]{1,0:T(8,128)(2,1)S(1)}, u32[]{:S(2)}, u32[]{:S(2)}) %collective-permute-start.9) | collective-permute-done | bytes 327712 | tf_op jit(solution)/shard_map/ppermute | solution.py:24
  53.8 1.5 %collective-permute-start.10 = (bf16[128,1280]{1,0:T(8,128)(2,1)S(1)}, bf16[128,1280]{1,0:T(8,128)(2,1)S(1)}, u32[]{:S(2)}, u32[]{:S(2)}) collective-permute-start(bf16[128,1280]{1,0:T(8,128)(2,1)S(1)} %collective-permute-done.8.refs_3_), channel_id=1, source_target_pairs={{0,1},{1,0},{2,3},{3,2},{4,5},{5,4},{6,7},{7,6},{8,9},{9,8},{10,11... | collective-permute-start | bytes 983048 | tf_op jit(solution)/shard_map/ppermute | solution.py:24
  55.3 0.0 collective-permute-done.5.refs_10_
  55.4 7.0 %collective-permute-done.10.refs_7_ = bf16[128,1280]{1,0:T(8,128)(2,1)S(1)} collective-permute-done((bf16[128,1280]{1,0:T(8,128)(2,1)S(1)}, bf16[128,1280]{1,0:T(8,128)(2,1)S(1)}, u32[]{:S(2)}, u32[]{:S(2)}) %collective-permute-start.10) | collective-permute-done | bytes 327712 | tf_op jit(solution)/shard_map/ppermute | solution.py:24
  62.4 0.0 collective-permute-done.12.kv1_ref
  62.4 0.0 collective-permute-done.13.qg1_ref
  62.4 3.2 %collective-permute-start.14 = (bf16[4,160,640]{2,1,0:T(8,128)(2,1)S(1)}, bf16[4,160,640]{2,1,0:T(8,128)(2,1)S(1)}, u32[]{:S(2)}, u32[]{:S(2)}) collective-permute-start(bf16[4,160,640]{2,1,0:T(8,128)(2,1)S(1)} %collective-permute-done.5.refs_10_), channel_id=1, source_target_pairs={{0,2},{2,0},{4,6},{6,4},{1,3},{3,1},{5,7},{7,5},{8,10},{10,8},{12,... | collective-permute-start | bytes 2457608 | tf_op jit(solution)/shard_map/ppermute | solution.py:24
  65.6 1.9 %collective-permute-start.15 = (bf16[2,128,1280]{2,1,0:T(8,128)(2,1)S(1)}, bf16[2,128,1280]{2,1,0:T(8,128)(2,1)S(1)}, u32[]{:S(2)}, u32[]{:S(2)}) collective-permute-start(bf16[2,128,1280]{2,1,0:T(8,128)(2,1)S(1)} %collective-permute-done.12.kv1_ref), channel_id=1, source_target_pairs={{0,2},{2,4},{4,6},{6,8},{8,10},{10,12},{12,14},{14,16},{16,18},{18... | collective-permute-start | bytes 1966088 | tf_op jit(solution)/shard_map/ppermute | solution.py:20
  67.5 0.0 copy-done.6
  67.5 0.0 copy-done.7
  67.5 0.3 prepare.1
  67.8 0.0 collective-permute-done.14.refs_11_
  67.8 4.6 %project.1 = bf16[16,4,16,640]{3,2,1,0:T(8,128)(2,1)} custom-call(s32[4,1,128]{2,1,0:T(1,128)S(1)} %get-tuple-element.39.place_ref, bf16[128,1280]{1,0:T(8,128)(2,1)S(1)} %copy-done.4, bf16[128,1280]{1,0:T(8,128)(2,1)S(1)} %collective-permute-done.3.refs_1_, bf16[128,1280]{1,0:T(8,128)(2,1)S(1)} %collective-permute-done.6.refs_2_, ...), custom_call_target="tpu_custom_call" | custom-call | flops 1677721600 | bytes 8388608 | tf_op jit(solution)/shard_map/project/pallas_call | solution.py:222
  72.4 0.0 copy-done.8
  72.4 0.0 copy-done.5
  72.4 6.0 %collective-permute-done.15.kv2_ref = bf16[2,128,1280]{2,1,0:T(8,128)(2,1)S(1)} collective-permute-done((bf16[2,128,1280]{2,1,0:T(8,128)(2,1)S(1)}, bf16[2,128,1280]{2,1,0:T(8,128)(2,1)S(1)}, u32[]{:S(2)}, u32[]{:S(2)}) %collective-permute-start.15) | collective-permute-done | bytes 655392 | tf_op jit(solution)/shard_map/ppermute | solution.py:20
  78.4 0.8 copy-done.9
  79.2 6.3 %all-to-all-start = ((bf16[16,4,16,640]{3,2,1,0:T(8,128)(2,1)}), bf16[16,4,16,640]{3,2,1,0:T(8,128)(2,1)S(1)}, u32[]{:S(2)}, u32[]{:S(2)}) async-start(bf16[16,4,16,640]{3,2,1,0:T(8,128)(2,1)} %project.1), calls=%async_computation | async-start | bytes 2621440 | tf_op jit(solution)/shard_map/all_to_all | solution.py:384
  85.5 3.1 %collective-permute-start.16 = (bf16[2,128,1280]{2,1,0:T(8,128)(2,1)S(1)}, bf16[2,128,1280]{2,1,0:T(8,128)(2,1)}, u32[]{:S(2)}, u32[]{:S(2)}) collective-permute-start(bf16[2,128,1280]{2,1,0:T(8,128)(2,1)S(1)} %collective-permute-done.13.qg1_ref), channel_id=1, source_target_pairs={{2,0},{4,2},{6,4},{8,6},{10,8},{12,10},{14,12},{16,14},{18,16},{20... | collective-permute-start | bytes 1966088 | tf_op jit(solution)/shard_map/ppermute | solution.py:20
  88.6 27.7 %all-to-all-done = bf16[16,4,16,640]{3,2,1,0:T(8,128)(2,1)S(1)} async-done(((bf16[16,4,16,640]{3,2,1,0:T(8,128)(2,1)}), bf16[16,4,16,640]{3,2,1,0:T(8,128)(2,1)S(1)}, u32[]{:S(2)}, u32[]{:S(2)}) %all-to-all-start) | async-done | bytes 1310752 | tf_op jit(solution)/shard_map/all_to_all | solution.py:384
  116.3 5.0 %attend.1 = (bf16[128,1280]{1,0:T(8,128)(2,1)}, bf16[128,1280]{1,0:T(8,128)(2,1)}, f32[2,16,128]{2,1,0:T(8,128)S(1)}) custom-call(bf16[128,1280]{1,0:T(8,128)(2,1)S(1)} %copy-done, bf16[128,1280]{1,0:T(8,128)(2,1)S(1)} %copy-done.1, bf16[128,1280]{1,0:T(8,128)(2,1)S(1)} %copy-done.2, bf16[128,1280]{1,0:T(8,128)(2,1)S(1)} %copy-done.3, ...), custom_call_target="tpu_custom_call" | custom-call | flops 838860800 | bytes 6291456 | tf_op jit(solution)/shard_map/attend/pallas_call | solution.py:102
  121.3 2.9 %collective-permute-start.17 = (f32[2,16,128]{2,1,0:T(8,128)S(1)}, f32[2,16,128]{2,1,0:T(8,128)S(1)}, u32[]{:S(2)}, u32[]{:S(2)}) collective-permute-start(f32[2,16,128]{2,1,0:T(8,128)S(1)} %get-tuple-element.52.st0_ref), channel_id=1, source_target_pairs={{2,0},{4,2},{6,4},{8,6},{10,8},{12,10},{14,12},{16,14},{18,16},{20... | collective-permute-start | bytes 49160 | tf_op jit(solution)/shard_map/ppermute | solution.py:20
  124.2 2.1 %collective-permute-start.18 = (f32[2,16,128]{2,1,0:T(8,128)S(1)}, f32[2,16,128]{2,1,0:T(8,128)S(1)}, u32[]{:S(2)}, u32[]{:S(2)}) collective-permute-start(f32[2,16,128]{2,1,0:T(8,128)S(1)} %get-tuple-element.52.st0_ref), channel_id=1, source_target_pairs={{4,0},{6,2},{8,4},{10,6},{12,8},{14,10},{16,12},{18,14},{20,16},{2... | collective-permute-start | bytes 49160 | tf_op jit(solution)/shard_map/ppermute | solution.py:20
  126.3 0.0 collective-permute-done.16.qg2_ref
  126.3 0.0 collective-permute-done.17.st1_ref
  126.3 3.5 %collective-permute-done.18.st2_ref = f32[2,16,128]{2,1,0:T(8,128)S(1)} collective-permute-done((f32[2,16,128]{2,1,0:T(8,128)S(1)}, f32[2,16,128]{2,1,0:T(8,128)S(1)}, u32[]{:S(2)}, u32[]{:S(2)}) %collective-permute-start.18) | collective-permute-done | bytes 16416 | tf_op jit(solution)/shard_map/ppermute | solution.py:20
  129.8 3.7 %key_grads.1 = (bf16[128,1280]{1,0:T(8,128)(2,1)}, bf16[128,1280]{1,0:T(8,128)(2,1)}) custom-call(bf16[128,1280]{1,0:T(8,128)(2,1)S(1)} %copy-done.2, bf16[128,1280]{1,0:T(8,128)(2,1)S(1)} %copy-done.3, bf16[128,1280]{1,0:T(8,128)(2,1)S(1)} %copy-done, bf16[128,1280]{1,0:T(8,128)(2,1)S(1)} %copy-done.1, ...), custom_call_target="tpu_custom_call" | custom-call | flops 503316480 | bytes 4194304 | tf_op jit(solution)/shard_map/key_grads/pallas_call | solution.py:165
  (3 shorter events, 0.0 us)
Async XLA Ops:
  0.6 5.1 %copy-start.4 = (bf16[128,1280]{1,0:T(8,128)(2,1)S(1)}, bf16[128,1280]{1,0:T(8,128)(2,1)}, u32[]{:S(2)}) copy-start(bf16[128,1280]{1,0:T(8,128)(2,1)} %refs_0_) | copy-start | bytes 983044
  0.7 27.5 %copy-start = (bf16[128,1280]{1,0:T(8,128)(2,1)S(1)}, bf16[128,1280]{1,0:T(8,128)(2,1)}, u32[]{:S(2)}) copy-start(bf16[128,1280]{1,0:T(8,128)(2,1)} %q_ref.3) | copy-start | bytes 983044
  0.7 27.5 %copy-start.1 = (bf16[128,1280]{1,0:T(8,128)(2,1)S(1)}, bf16[128,1280]{1,0:T(8,128)(2,1)}, u32[]{:S(2)}) copy-start(bf16[128,1280]{1,0:T(8,128)(2,1)} %g_ref.3) | copy-start | bytes 983044
  0.7 27.5 %copy-start.2 = (bf16[128,1280]{1,0:T(8,128)(2,1)S(1)}, bf16[128,1280]{1,0:T(8,128)(2,1)}, u32[]{:S(2)}) copy-start(bf16[128,1280]{1,0:T(8,128)(2,1)} %k_ref.3) | copy-start | bytes 983044
  0.7 27.5 %copy-start.3 = (bf16[128,1280]{1,0:T(8,128)(2,1)S(1)}, bf16[128,1280]{1,0:T(8,128)(2,1)}, u32[]{:S(2)}) copy-start(bf16[128,1280]{1,0:T(8,128)(2,1)} %v_ref.3) | copy-start | bytes 983044
  2.1 10.8 %collective-permute-start = (bf16[160,640]{1,0:T(8,128)(2,1)S(1)}, bf16[160,640]{1,0:T(8,128)(2,1)S(1)}, u32[]{:S(2)}, u32[]{:S(2)}) collective-permute-start(bf16[160,640]{1,0:T(8,128)(2,1)S(1)} %get-tuple-element.57), channel_id=1, source_target_pairs={{0,8},{8,0},{16,24},{24,16},{1,9},{9,1},{17,25},{25,17},{2,10},{10... | collective-permute-start | bytes 614408 | tf_op jit(solution)/shard_map/ppermute | solution.py:24
  3.8 14.5 %collective-permute-start.1 = (bf16[160,640]{1,0:T(8,128)(2,1)S(1)}, bf16[160,640]{1,0:T(8,128)(2,1)S(1)}, u32[]{:S(2)}, u32[]{:S(2)}) collective-permute-start(bf16[160,640]{1,0:T(8,128)(2,1)S(1)} %get-tuple-element.59), channel_id=1, source_target_pairs={{0,16},{8,24},{16,0},{24,8},{1,17},{9,25},{17,1},{25,9},{2,18},{10... | collective-permute-start | bytes 614408 | tf_op jit(solution)/shard_map/ppermute | solution.py:24
  4.1 19.3 %collective-permute-start.2 = (bf16[160,640]{1,0:T(8,128)(2,1)S(1)}, bf16[160,640]{1,0:T(8,128)(2,1)S(1)}, u32[]{:S(2)}, u32[]{:S(2)}) collective-permute-start(bf16[160,640]{1,0:T(8,128)(2,1)S(1)} %get-tuple-element.58), channel_id=1, source_target_pairs={{0,24},{8,16},{16,8},{24,0},{1,25},{9,17},{17,9},{25,1},{2,26},{10... | collective-permute-start | bytes 614408 | tf_op jit(solution)/shard_map/ppermute | solution.py:24
  5.7 19.2 %collective-permute-start.3 = (bf16[128,1280]{1,0:T(8,128)(2,1)S(1)}, bf16[128,1280]{1,0:T(8,128)(2,1)S(1)}, u32[]{:S(2)}, u32[]{:S(2)}) collective-permute-start(bf16[128,1280]{1,0:T(8,128)(2,1)S(1)} %copy-done.4), channel_id=1, source_target_pairs={{0,8},{8,0},{16,24},{24,16},{1,9},{9,1},{17,25},{25,17},{2,10},{10... | collective-permute-start | bytes 983048 | tf_op jit(solution)/shard_map/ppermute | solution.py:24
  8.2 16.7 %collective-permute-start.4 = (bf16[128,1280]{1,0:T(8,128)(2,1)S(1)}, bf16[128,1280]{1,0:T(8,128)(2,1)S(1)}, u32[]{:S(2)}, u32[]{:S(2)}) collective-permute-start(bf16[128,1280]{1,0:T(8,128)(2,1)S(1)} %copy-done.4), channel_id=1, source_target_pairs={{0,1},{1,0},{2,3},{3,2},{4,5},{5,4},{6,7},{7,6},{8,9},{9,8},{10,11... | collective-permute-start | bytes 983048 | tf_op jit(solution)/shard_map/ppermute | solution.py:24
  24.9 21.0 %collective-permute-start.11 = (bf16[4,160,640]{2,1,0:T(8,128)(2,1)S(1)}, bf16[4,160,640]{2,1,0:T(8,128)(2,1)S(1)}, u32[]{:S(2)}, u32[]{:S(2)}) collective-permute-start(bf16[4,160,640]{2,1,0:T(8,128)(2,1)S(1)} %pad_maximum_fusion.refs_8_), channel_id=1, source_target_pairs={{0,2},{2,0},{4,6},{6,4},{1,3},{3,1},{5,7},{7,5},{8,10},{10,8},{12,... | collective-permute-start | bytes 2457608 | tf_op jit(solution)/shard_map/ppermute | solution.py:24
  24.9 14.9 %collective-permute-start.6 = (bf16[128,1280]{1,0:T(8,128)(2,1)S(1)}, bf16[128,1280]{1,0:T(8,128)(2,1)S(1)}, u32[]{:S(2)}, u32[]{:S(2)}) collective-permute-start(bf16[128,1280]{1,0:T(8,128)(2,1)S(1)} %copy-done.4), channel_id=1, source_target_pairs={{0,16},{8,24},{16,0},{24,8},{1,17},{9,25},{17,1},{25,9},{2,18},{10... | collective-permute-start | bytes 983048 | tf_op jit(solution)/shard_map/ppermute | solution.py:24
  25.0 14.9 %collective-permute-start.7 = (bf16[128,1280]{1,0:T(8,128)(2,1)S(1)}, bf16[128,1280]{1,0:T(8,128)(2,1)S(1)}, u32[]{:S(2)}, u32[]{:S(2)}) collective-permute-start(bf16[128,1280]{1,0:T(8,128)(2,1)S(1)} %collective-permute-done.3.refs_1_), channel_id=1, source_target_pairs={{0,1},{1,0},{2,3},{3,2},{4,5},{5,4},{6,7},{7,6},{8,9},{9,8},{10,11... | collective-permute-start | bytes 983048 | tf_op jit(solution)/shard_map/ppermute | solution.py:24
  26.7 28.7 %collective-permute-start.5 = (bf16[4,160,640]{2,1,0:T(8,128)(2,1)S(1)}, bf16[4,160,640]{2,1,0:T(8,128)(2,1)S(1)}, u32[]{:S(2)}, u32[]{:S(2)}) collective-permute-start(bf16[4,160,640]{2,1,0:T(8,128)(2,1)S(1)} %pad_maximum_fusion.refs_8_), channel_id=1, source_target_pairs={{0,4},{2,6},{4,0},{6,2},{1,5},{3,7},{5,1},{7,3},{8,12},{10,14},{12... | collective-permute-start | bytes 2457608 | tf_op jit(solution)/shard_map/ppermute | solution.py:24
  28.2 39.3 %copy-start.6 = (s32[2048]{0:T(1024)S(1)}, s32[2048]{0:T(1024)}, u32[]{:S(2)}) copy-start(s32[2048]{0:T(1024)} %param.15) | copy-start | bytes 24580
  28.2 39.3 %copy-start.7 = (s32[2048]{0:T(1024)S(1)}, s32[2048]{0:T(1024)}, u32[]{:S(2)}) copy-start(s32[2048]{0:T(1024)} %param.14) | copy-start | bytes 24580
  39.9 12.6 %collective-permute-start.8 = (bf16[128,1280]{1,0:T(8,128)(2,1)S(1)}, bf16[128,1280]{1,0:T(8,128)(2,1)S(1)}, u32[]{:S(2)}, u32[]{:S(2)}) collective-permute-start(bf16[128,1280]{1,0:T(8,128)(2,1)S(1)} %collective-permute-done.6.refs_2_), channel_id=1, source_target_pairs={{0,8},{8,0},{16,24},{24,16},{1,9},{9,1},{17,25},{25,17},{2,10},{10... | collective-permute-start | bytes 983048 | tf_op jit(solution)/shard_map/ppermute | solution.py:24
  44.4 9.4 %collective-permute-start.9 = (bf16[128,1280]{1,0:T(8,128)(2,1)S(1)}, bf16[128,1280]{1,0:T(8,128)(2,1)S(1)}, u32[]{:S(2)}, u32[]{:S(2)}) collective-permute-start(bf16[128,1280]{1,0:T(8,128)(2,1)S(1)} %collective-permute-done.6.refs_2_), channel_id=1, source_target_pairs={{0,1},{1,0},{2,3},{3,2},{4,5},{5,4},{6,7},{7,6},{8,9},{9,8},{10,11... | collective-permute-start | bytes 983048 | tf_op jit(solution)/shard_map/ppermute | solution.py:24
  45.9 16.4 %collective-permute-start.12 = (bf16[2,128,1280]{2,1,0:T(8,128)(2,1)S(1)}, bf16[2,128,1280]{2,1,0:T(8,128)(2,1)S(1)}, u32[]{:S(2)}, u32[]{:S(2)}) collective-permute-start(bf16[2,128,1280]{2,1,0:T(8,128)(2,1)S(1)} %get-tuple-element.36), channel_id=1, source_target_pairs={{0,2},{2,4},{4,6},{6,8},{8,10},{10,12},{12,14},{14,16},{16,18},{18... | collective-permute-start | bytes 1966088 | tf_op jit(solution)/shard_map/ppermute | solution.py:20
  47.9 14.5 %collective-permute-start.13 = (bf16[2,128,1280]{2,1,0:T(8,128)(2,1)S(1)}, bf16[2,128,1280]{2,1,0:T(8,128)(2,1)S(1)}, u32[]{:S(2)}, u32[]{:S(2)}) collective-permute-start(bf16[2,128,1280]{2,1,0:T(8,128)(2,1)S(1)} %get-tuple-element.37), channel_id=1, source_target_pairs={{2,0},{4,2},{6,4},{8,6},{10,8},{12,10},{14,12},{16,14},{18,16},{20... | collective-permute-start | bytes 1966088 | tf_op jit(solution)/shard_map/ppermute | solution.py:20
  53.8 8.5 %collective-permute-start.10 = (bf16[128,1280]{1,0:T(8,128)(2,1)S(1)}, bf16[128,1280]{1,0:T(8,128)(2,1)S(1)}, u32[]{:S(2)}, u32[]{:S(2)}) collective-permute-start(bf16[128,1280]{1,0:T(8,128)(2,1)S(1)} %collective-permute-done.8.refs_3_), channel_id=1, source_target_pairs={{0,1},{1,0},{2,3},{3,2},{4,5},{5,4},{6,7},{7,6},{8,9},{9,8},{10,11... | collective-permute-start | bytes 983048 | tf_op jit(solution)/shard_map/ppermute | solution.py:24
  62.4 10.0 %copy-start.8 = (bf16[2,128,1280]{2,1,0:T(8,128)(2,1)}, bf16[2,128,1280]{2,1,0:T(8,128)(2,1)S(1)}, u32[]{:S(2)}) copy-start(bf16[2,128,1280]{2,1,0:T(8,128)(2,1)S(1)} %collective-permute-done.12.kv1_ref) | copy-start | bytes 1966084
  62.4 5.4 %collective-permute-start.14 = (bf16[4,160,640]{2,1,0:T(8,128)(2,1)S(1)}, bf16[4,160,640]{2,1,0:T(8,128)(2,1)S(1)}, u32[]{:S(2)}, u32[]{:S(2)}) collective-permute-start(bf16[4,160,640]{2,1,0:T(8,128)(2,1)S(1)} %collective-permute-done.5.refs_10_), channel_id=1, source_target_pairs={{0,2},{2,0},{4,6},{6,4},{1,3},{3,1},{5,7},{7,5},{8,10},{10,8},{12,... | collective-permute-start | bytes 2457608 | tf_op jit(solution)/shard_map/ppermute | solution.py:24
  65.6 12.8 %collective-permute-start.15 = (bf16[2,128,1280]{2,1,0:T(8,128)(2,1)S(1)}, bf16[2,128,1280]{2,1,0:T(8,128)(2,1)S(1)}, u32[]{:S(2)}, u32[]{:S(2)}) collective-permute-start(bf16[2,128,1280]{2,1,0:T(8,128)(2,1)S(1)} %collective-permute-done.12.kv1_ref), channel_id=1, source_target_pairs={{0,2},{2,4},{4,6},{6,8},{8,10},{10,12},{12,14},{14,16},{16,18},{18... | collective-permute-start | bytes 1966088 | tf_op jit(solution)/shard_map/ppermute | solution.py:20
  67.8 4.6 %copy-start.5 = (bf16[128,640]{1,0:T(8,128)(2,1)}, bf16[128,640]{1,0:T(8,128)(2,1)S(1)}, u32[]{:S(2)}) copy-start(bf16[128,640]{1,0:T(8,128)(2,1)S(1)} %get-tuple-element.48.bias_ref) | copy-start | bytes 491524
  78.4 0.9 copy-start.9
  79.2 37.1 %all-to-all-start = ((bf16[16,4,16,640]{3,2,1,0:T(8,128)(2,1)}), bf16[16,4,16,640]{3,2,1,0:T(8,128)(2,1)S(1)}, u32[]{:S(2)}, u32[]{:S(2)}) async-start(bf16[16,4,16,640]{3,2,1,0:T(8,128)(2,1)} %project.1), calls=%async_computation | async-start | bytes 2621440 | tf_op jit(solution)/shard_map/all_to_all | solution.py:384
  85.5 40.8 %collective-permute-start.16 = (bf16[2,128,1280]{2,1,0:T(8,128)(2,1)S(1)}, bf16[2,128,1280]{2,1,0:T(8,128)(2,1)}, u32[]{:S(2)}, u32[]{:S(2)}) collective-permute-start(bf16[2,128,1280]{2,1,0:T(8,128)(2,1)S(1)} %collective-permute-done.13.qg1_ref), channel_id=1, source_target_pairs={{2,0},{4,2},{6,4},{8,6},{10,8},{12,10},{14,12},{16,14},{18,16},{20... | collective-permute-start | bytes 1966088 | tf_op jit(solution)/shard_map/ppermute | solution.py:20
  121.3 5.0 %collective-permute-start.17 = (f32[2,16,128]{2,1,0:T(8,128)S(1)}, f32[2,16,128]{2,1,0:T(8,128)S(1)}, u32[]{:S(2)}, u32[]{:S(2)}) collective-permute-start(f32[2,16,128]{2,1,0:T(8,128)S(1)} %get-tuple-element.52.st0_ref), channel_id=1, source_target_pairs={{2,0},{4,2},{6,4},{8,6},{10,8},{12,10},{14,12},{16,14},{18,16},{20... | collective-permute-start | bytes 49160 | tf_op jit(solution)/shard_map/ppermute | solution.py:20
  124.2 5.6 %collective-permute-start.18 = (f32[2,16,128]{2,1,0:T(8,128)S(1)}, f32[2,16,128]{2,1,0:T(8,128)S(1)}, u32[]{:S(2)}, u32[]{:S(2)}) collective-permute-start(f32[2,16,128]{2,1,0:T(8,128)S(1)} %get-tuple-element.52.st0_ref), channel_id=1, source_target_pairs={{4,0},{6,2},{8,4},{10,6},{12,8},{14,10},{16,12},{18,14},{20,16},{2... | collective-permute-start | bytes 49160 | tf_op jit(solution)/shard_map/ppermute | solution.py:20

commit v13 on v11

--- a/solution.py
+++ b/solution.py
@@ -40,10 +40,11 @@
 def attend_kernel(
     q_ref, g_ref, k_ref, v_ref, kv1_ref, kv2_ref, mem_ref, bias_ref, out_ref, gq_ref, stats_ref
 ):
-    rows, width = q_ref.shape
+    rows, width = out_ref.shape
     scaling = HD ** (-0.5)
     bias = bias_ref[...].astype(jnp.float32)
     step = pl.program_id(0)
+    picked = [pl.ds(pl.multiple_of(step * width + i * HD, HD), HD) for i in range(width // HD)]
     heads = [slice(i * HD, (i + 1) * HD) for i in range(width // HD)]
     ks, vs = (
         [
@@ -52,16 +53,16 @@
                     mem_ref[2 * step + which, :, cols],
                     kv2_ref[which, :, cols],
                     kv1_ref[which, :, cols],
-                    own_ref[:, cols],
+                    own_ref[:, wide],
                 ],
                 0,
             )
-            for cols in heads
+            for cols, wide in zip(heads, picked)
         ]
         for which, own_ref in enumerate((k_ref, v_ref))
     )
-    scores = [dot_t(q_ref[:, cols], kh, ((1,), (1,))) + bias for cols, kh in zip(heads, ks)]
-    dprobs = [dot_t(g_ref[:, cols], vh, ((1,), (1,))) for cols, vh in zip(heads, vs)]
+    scores = [dot_t(q_ref[:, wide], kh, ((1,), (1,))) + bias for wide, kh in zip(picked, ks)]
+    dprobs = [dot_t(g_ref[:, wide], vh, ((1,), (1,))) for wide, vh in zip(picked, vs)]
     tops, shares, probs = [], [], []
     for score in scores:
         top = jnp.max(score, axis=-1, keepdims=True)
@@ -75,10 +76,10 @@
         for prob, vh in zip(probs, vs)
     ]
     deltas, dscores = [], []
-    for cols, out_b, prob, dprob in zip(heads, outs, probs, dprobs):
+    for cols, wide, out_b, prob, dprob in zip(heads, picked, outs, probs, dprobs):
         out_ref[:, cols] = out_b
         delta = jnp.sum(
-            g_ref[:, cols].astype(jnp.float32) * out_b.astype(jnp.float32), axis=-1, keepdims=True
+            g_ref[:, wide].astype(jnp.float32) * out_b.astype(jnp.float32), axis=-1, keepdims=True
         )
         deltas.append(delta)
         dscores.append((prob * ((dprob - delta) * scaling)).astype(jnp.bfloat16))
@@ -104,7 +105,7 @@
         attend_kernel,
         grid=(steps,),
         in_specs=[
-            flat, flat, flat, flat, pair, pair, whole,
+            whole, whole, whole, whole, pair, pair, whole,
             pl.BlockSpec((rows, keys_all), lambda i: (0, 0)),
         ],
         out_specs=[flat, flat, pl.BlockSpec((1, STATS, rows), lambda i: (i, 0, 0))],
@@ -120,14 +121,19 @@
             transcendentals=rows * keys_all * heads,
         ),
         name="attend",
-    )(queries, grad_out, keys, values, *in_hbm(kv1, kv2), *in_vmem(memory), *in_hbm(bias))
+    )(
+        *in_vmem(queries, grad_out, keys, values),
+        *in_hbm(kv1, kv2),
+        *in_vmem(memory),
+        *in_hbm(bias),
+    )
 
 
 def key_grads_kernel(
     k_ref, v_ref, q_ref, g_ref, qg1_ref, qg2_ref, st0_ref, st1_ref, st2_ref, bias_ref,
     gk_ref, gv_ref,
 ):
-    width = k_ref.shape[1]
+    width = gk_ref.shape[1]
     scaling = HD ** (-0.5)
     bias = bias_ref[...]
     heads = [slice(i * HD, (i + 1) * HD) for i in range(width // HD)]
@@ -135,15 +141,15 @@
     picked = [pl.ds(pl.multiple_of(start + i * HD, HD), HD) for i in range(len(heads))]
     stats = jnp.concatenate([st0_ref[0], st1_ref[0], st2_ref[0]], 1)
     qs = [
-        jnp.concatenate([q_ref[:, cols], qg1_ref[0, :, wide], qg2_ref[0, :, wide]], 0)
+        jnp.concatenate([q_ref[:, wide], qg1_ref[0, :, cols], qg2_ref[0, :, wide]], 0)
         for cols, wide in zip(heads, picked)
     ]
     gs = [
-        jnp.concatenate([g_ref[:, cols], qg1_ref[1, :, wide], qg2_ref[1, :, wide]], 0)
+        jnp.concatenate([g_ref[:, wide], qg1_ref[1, :, cols], qg2_ref[1, :, wide]], 0)
         for cols, wide in zip(heads, picked)
     ]
-    scores = [dot_t(k_ref[:, cols], qh, ((1,), (1,))) + bias for cols, qh in zip(heads, qs)]
-    dprobs = [dot_t(v_ref[:, cols], gh, ((1,), (1,))) for cols, gh in zip(heads, gs)]
+    scores = [dot_t(k_ref[:, wide], qh, ((1,), (1,))) + bias for wide, qh in zip(picked, qs)]
+    dprobs = [dot_t(v_ref[:, wide], gh, ((1,), (1,))) for wide, gh in zip(picked, gs)]
     probs, dscores = [], []
     for i, (score, dprob) in enumerate(zip(scores, dprobs)):
         top, share, delta = (stats[i + j * len(heads) : i + j * len(heads) + 1] for j in range(3))
@@ -160,6 +166,7 @@
     steps = stats[0].shape[0]
     block = features // steps
     flat = pl.BlockSpec((rows, block), lambda i: (0, i))
+    pair = pl.BlockSpec((2, rows, block), lambda i: (0, 0, i))
     whole = pl.BlockSpec(memory_space=pltpu.VMEM)
     stat = pl.BlockSpec((1, STATS, rows), lambda i: (i, 0, 0))
     heads = features // HD
@@ -167,7 +174,7 @@
         key_grads_kernel,
         grid=(steps,),
         in_specs=[
-            flat, flat, flat, flat, whole, whole, stat, stat, stat, whole,
+            whole, whole, whole, whole, pair, whole, stat, stat, stat, whole,
         ],
         out_specs=[flat, flat],
         out_shape=[jax.ShapeDtypeStruct((rows, features), jnp.bfloat16)] * 2,
@@ -178,7 +185,13 @@
             transcendentals=rows * 3 * rows * heads,
         ),
         name="key_grads",
-    )(keys, values, queries, grad_out, *in_vmem(qg1, qg2), *stats, *in_vmem(bias))
+    )(
+        *in_vmem(keys, values, queries, grad_out),
+        *in_hbm(qg1),
+        *in_vmem(qg2),
+        *stats,
+        *in_vmem(bias),
+    )
 
 
 def project_kernel(place_ref, *refs):

time: 127 us -> 126 us (level)
  no operation moved by 1% of the time
where the time goes in v13:
time: 126 us; the launch traced here: 125 us
  waiting for transfers between devices  75.3 us (60%)
  starting transfers between devices  34.2 us (27%)
  Pallas kernels  13.4 us (11%)
  local copies, waits for them, and re-layouts  1.46 us (1%)
    all_to_all x1, waiting for transfers between devices, body(): memory = lax.all_to_all(slots, SEQ, split_axis=0, concat_axis=0, tiled=True)  27.7 us
    ppermute x10, waiting for transfers between devices, swapped(): lax.ppermute(value, axis, [(i, i ^ mask) for i in range(lax.axis_size(axi...  27.1 us
    ppermute x6, starting transfers between devices, shifted(): return lax.ppermute(value, SEQ, pairs)  15.6 us
    ppermute x3, waiting for transfers between devices, ring_step(): lax.ppermute(value, 'z', [(b, a) for a, b in pairs] if back else pairs)  11.4 us
    ppermute x10, starting transfers between devices, swapped(): lax.ppermute(value, axis, [(i, i ^ mask) for i in range(lax.axis_size(axi...  11.3 us
    ppermute x6, waiting for transfers between devices, shifted(): return lax.ppermute(value, SEQ, pairs)  9.15 us
    pallas_call x1, Pallas kernels, attend(): pl.pallas_call(attend_kernel, grid=(steps,), in_specs=[whole, whole, whol...  5.02 us
    pallas_call x1, Pallas kernels, project(): pl.pallas_call(project_kernel, in_specs=[whole] * (1 + len(rows) + n_p),...  4.6 us
  transfers between devices with their start and end apart: 20, of which 11 were waited for; matrix products, arithmetic and copies ran while one was open for 0% of the time, Pallas kernels for 8%

profile of v13, /device:TPU:16, one launch (start us, length us, event | category | flops | bytes accessed | tf_op | source)
XLA Modules:
  0.0 125.5 jit_solution(14116345308494614617)
XLA Ops:
  0.6 0.0 copy-start.4
  0.7 0.0 copy-start
  0.7 0.0 copy-start.1
  0.7 0.0 copy-start.2
  0.7 0.0 copy-start.3
  0.7 1.4 %constant_dynamic-slice_fusion = (bf16[1,160,640]{2,1,0:T(8,128)(2,1)S(1)}, bf16[160,640]{1,0:T(8,128)(2,1)S(1)}, bf16[160,640]{1,0:T(8,128)(2,1)S(1)}, bf16[160,640]{1,0:T(8,128)(2,1)S(1)}) fusion(bf16[2,160,1280]{2,1,0:T(8,128)(2,1)} %param.13, s32[]{:T(128)S(6)} %select_n.24, s32[]{:T(128)S(6)} %select_n.25, s32[]{:T(128)S(6)} %select_n.26, ...), kind=kLoop, calls=%fused_computation.6 | loop fusion | bytes 1638432 | tf_op jit(solution)/shard_map/dynamic_slice | solution.py:325
  2.1 1.6 %collective-permute-start = (bf16[160,640]{1,0:T(8,128)(2,1)S(1)}, bf16[160,640]{1,0:T(8,128)(2,1)S(1)}, u32[]{:S(2)}, u32[]{:S(2)}) collective-permute-start(bf16[160,640]{1,0:T(8,128)(2,1)S(1)} %get-tuple-element.51), channel_id=1, source_target_pairs={{0,8},{8,0},{16,24},{24,16},{1,9},{9,1},{17,25},{25,17},{2,10},{10... | collective-permute-start | bytes 614408 | tf_op jit(solution)/shard_map/ppermute | solution.py:25
  3.8 0.3 collective-permute-start.1
  4.1 1.6 %collective-permute-start.2 = (bf16[160,640]{1,0:T(8,128)(2,1)S(1)}, bf16[160,640]{1,0:T(8,128)(2,1)S(1)}, u32[]{:S(2)}, u32[]{:S(2)}) collective-permute-start(bf16[160,640]{1,0:T(8,128)(2,1)S(1)} %get-tuple-element.52), channel_id=1, source_target_pairs={{0,24},{8,16},{16,8},{24,0},{1,25},{9,17},{17,9},{25,1},{2,26},{10... | collective-permute-start | bytes 614408 | tf_op jit(solution)/shard_map/ppermute | solution.py:25
  5.7 0.0 copy-done.4
  5.7 1.5 %collective-permute-start.3 = (bf16[128,1280]{1,0:T(8,128)(2,1)S(1)}, bf16[128,1280]{1,0:T(8,128)(2,1)S(1)}, u32[]{:S(2)}, u32[]{:S(2)}) collective-permute-start(bf16[128,1280]{1,0:T(8,128)(2,1)S(1)} %copy-done.4), channel_id=1, source_target_pairs={{0,1},{1,0},{2,3},{3,2},{4,5},{5,4},{6,7},{7,6},{8,9},{9,8},{10,11... | collective-permute-start | bytes 983048 | tf_op jit(solution)/shard_map/ppermute | solution.py:25
  7.2 4.0 %collective-permute-done = bf16[160,640]{1,0:T(8,128)(2,1)S(1)} collective-permute-done((bf16[160,640]{1,0:T(8,128)(2,1)S(1)}, bf16[160,640]{1,0:T(8,128)(2,1)S(1)}, u32[]{:S(2)}, u32[]{:S(2)}) %collective-permute-start) | collective-permute-done | bytes 204832 | tf_op jit(solution)/shard_map/ppermute | solution.py:25
  11.2 7.2 %collective-permute-done.1 = bf16[160,640]{1,0:T(8,128)(2,1)S(1)} collective-permute-done((bf16[160,640]{1,0:T(8,128)(2,1)S(1)}, bf16[160,640]{1,0:T(8,128)(2,1)S(1)}, u32[]{:S(2)}, u32[]{:S(2)}) %collective-permute-start.1) | collective-permute-done | bytes 204832 | tf_op jit(solution)/shard_map/ppermute | solution.py:25
  18.4 5.0 %collective-permute-done.2 = bf16[160,640]{1,0:T(8,128)(2,1)S(1)} collective-permute-done((bf16[160,640]{1,0:T(8,128)(2,1)S(1)}, bf16[160,640]{1,0:T(8,128)(2,1)S(1)}, u32[]{:S(2)}, u32[]{:S(2)}) %collective-permute-start.2) | collective-permute-done | bytes 204832 | tf_op jit(solution)/shard_map/ppermute | solution.py:25
  23.4 0.1 pad_maximum_fusion.refs_8_
  23.5 0.0 collective-permute-done.3.refs_4_
  23.5 0.1 collective-permute-start.11
  23.6 0.1 collective-permute-start.5
  23.7 2.0 %collective-permute-start.8 = (bf16[128,1280]{1,0:T(8,128)(2,1)S(1)}, bf16[128,1280]{1,0:T(8,128)(2,1)S(1)}, u32[]{:S(2)}, u32[]{:S(2)}) collective-permute-start(bf16[128,1280]{1,0:T(8,128)(2,1)S(1)} %copy-done.4), channel_id=1, source_target_pairs={{8,0},{24,8},{16,24},{0,16},{9,1},{25,9},{17,25},{1,17},{10,2},{26... | collective-permute-start | bytes 983048 | tf_op jit(solution)/shard_map/ppermute | solution.py:330
  25.7 1.5 %collective-permute-start.4 = (bf16[4,160,640]{2,1,0:T(8,128)(2,1)S(1)}, bf16[4,160,640]{2,1,0:T(8,128)(2,1)S(1)}, u32[]{:S(2)}, u32[]{:S(2)}) collective-permute-start(bf16[4,160,640]{2,1,0:T(8,128)(2,1)S(1)} %pad_maximum_fusion.refs_8_), channel_id=1, source_target_pairs={{0,4},{2,6},{4,0},{6,2},{1,5},{3,7},{5,1},{7,3},{8,12},{10,14},{12... | collective-permute-start | bytes 2457608 | tf_op jit(solution)/shard_map/ppermute | solution.py:25
  27.2 0.0 copy-done
  27.2 0.0 copy-done.1
  27.2 0.0 copy-done.2
  27.2 0.0 copy-done.3
  27.2 0.0 copy-start.6
  27.2 0.0 copy-start.7
  27.2 0.1 pad_maximum_fusion.1
  27.4 6.8 %collective-permute-done.5.refs_1_ = bf16[128,1280]{1,0:T(8,128)(2,1)S(1)} collective-permute-done((bf16[128,1280]{1,0:T(8,128)(2,1)S(1)}, bf16[128,1280]{1,0:T(8,128)(2,1)S(1)}, u32[]{:S(2)}, u32[]{:S(2)}) %collective-permute-start.5) | collective-permute-done | bytes 327712 | tf_op jit(solution)/shard_map/ppermute | solution.py:330
  34.2 1.5 %collective-permute-start.9 = (bf16[128,1280]{1,0:T(8,128)(2,1)S(1)}, bf16[128,1280]{1,0:T(8,128)(2,1)S(1)}, u32[]{:S(2)}, u32[]{:S(2)}) collective-permute-start(bf16[128,1280]{1,0:T(8,128)(2,1)S(1)} %collective-permute-done.5.refs_1_), channel_id=1, source_target_pairs={{0,1},{1,0},{2,3},{3,2},{4,5},{5,4},{6,7},{7,6},{8,9},{9,8},{10,11... | collective-permute-start | bytes 983048 | tf_op jit(solution)/shard_map/ppermute | solution.py:25
  35.7 0.8 collective-permute-start.6
  36.5 0.0 collective-permute-done.11.refs_9_
  36.5 1.9 %collective-permute-start.12 = (bf16[2,128,1280]{2,1,0:T(8,128)(2,1)S(1)}, bf16[2,128,1280]{2,1,0:T(8,128)(2,1)S(1)}, u32[]{:S(2)}, u32[]{:S(2)}) collective-permute-start(bf16[2,128,1280]{2,1,0:T(8,128)(2,1)S(1)} %get-tuple-element.30), channel_id=1, source_target_pairs={{0,2},{2,4},{4,6},{6,8},{8,10},{10,12},{12,14},{14,16},{16,18},{18... | collective-permute-start | bytes 1966088 | tf_op jit(solution)/shard_map/ppermute | solution.py:21
  38.5 2.7 %collective-permute-done.8.refs_3_ = bf16[128,1280]{1,0:T(8,128)(2,1)S(1)} collective-permute-done((bf16[128,1280]{1,0:T(8,128)(2,1)S(1)}, bf16[128,1280]{1,0:T(8,128)(2,1)S(1)}, u32[]{:S(2)}, u32[]{:S(2)}) %collective-permute-start.8) | collective-permute-done | bytes 327712 | tf_op jit(solution)/shard_map/ppermute | solution.py:330
  41.1 3.2 %collective-permute-start.13 = (bf16[2,128,1280]{2,1,0:T(8,128)(2,1)S(1)}, bf16[2,128,1280]{2,1,0:T(8,128)(2,1)}, u32[]{:S(2)}, u32[]{:S(2)}) collective-permute-start(bf16[2,128,1280]{2,1,0:T(8,128)(2,1)S(1)} %get-tuple-element.31), channel_id=1, source_target_pairs={{2,0},{4,2},{6,4},{8,6},{10,8},{12,10},{14,12},{16,14},{18,16},{20... | collective-permute-start | bytes 1966088 | tf_op jit(solution)/shard_map/ppermute | solution.py:21
  44.4 0.0 collective-permute-done.9.refs_5_
  44.4 1.6 %collective-permute-start.10 = (bf16[128,1280]{1,0:T(8,128)(2,1)S(1)}, bf16[128,1280]{1,0:T(8,128)(2,1)S(1)}, u32[]{:S(2)}, u32[]{:S(2)}) collective-permute-start(bf16[128,1280]{1,0:T(8,128)(2,1)S(1)} %collective-permute-done.8.refs_3_), channel_id=1, source_target_pairs={{0,1},{1,0},{2,3},{3,2},{4,5},{5,4},{6,7},{7,6},{8,9},{9,8},{10,11... | collective-permute-start | bytes 983048 | tf_op jit(solution)/shard_map/ppermute | solution.py:25
  46.0 1.9 %collective-permute-done.6.refs_2_ = bf16[128,1280]{1,0:T(8,128)(2,1)S(1)} collective-permute-done((bf16[128,1280]{1,0:T(8,128)(2,1)S(1)}, bf16[128,1280]{1,0:T(8,128)(2,1)S(1)}, u32[]{:S(2)}, u32[]{:S(2)}) %collective-permute-start.6) | collective-permute-done | bytes 327712 | tf_op jit(solution)/shard_map/ppermute | solution.py:330
  47.8 1.5 %collective-permute-start.7 = (bf16[128,1280]{1,0:T(8,128)(2,1)S(1)}, bf16[128,1280]{1,0:T(8,128)(2,1)S(1)}, u32[]{:S(2)}, u32[]{:S(2)}) collective-permute-start(bf16[128,1280]{1,0:T(8,128)(2,1)S(1)} %collective-permute-done.6.refs_2_), channel_id=1, source_target_pairs={{0,1},{1,0},{2,3},{3,2},{4,5},{5,4},{6,7},{7,6},{8,9},{9,8},{10,11... | collective-permute-start | bytes 983048 | tf_op jit(solution)/shard_map/ppermute | solution.py:25
  49.3 0.0 collective-permute-done.4.refs_10_
  49.3 5.7 %collective-permute-done.10.refs_7_ = bf16[128,1280]{1,0:T(8,128)(2,1)S(1)} collective-permute-done((bf16[128,1280]{1,0:T(8,128)(2,1)S(1)}, bf16[128,1280]{1,0:T(8,128)(2,1)S(1)}, u32[]{:S(2)}, u32[]{:S(2)}) %collective-permute-start.10) | collective-permute-done | bytes 327712 | tf_op jit(solution)/shard_map/ppermute | solution.py:25
  55.1 5.2 %collective-permute-done.7.refs_6_ = bf16[128,1280]{1,0:T(8,128)(2,1)S(1)} collective-permute-done((bf16[128,1280]{1,0:T(8,128)(2,1)S(1)}, bf16[128,1280]{1,0:T(8,128)(2,1)S(1)}, u32[]{:S(2)}, u32[]{:S(2)}) %collective-permute-start.7) | collective-permute-done | bytes 327712 | tf_op jit(solution)/shard_map/ppermute | solution.py:25
  60.3 0.0 collective-permute-done.12.kv1_ref
  60.3 0.0 copy-start.8
  60.3 0.0 collective-permute-done.13.qg1_ref
  60.3 0.1 collective-permute-start.14
  60.4 2.4 %collective-permute-start.15 = (bf16[2,128,1280]{2,1,0:T(8,128)(2,1)S(1)}, bf16[2,128,1280]{2,1,0:T(8,128)(2,1)}, u32[]{:S(2)}, u32[]{:S(2)}) collective-permute-start(bf16[2,128,1280]{2,1,0:T(8,128)(2,1)S(1)} %collective-permute-done.12.kv1_ref), channel_id=1, source_target_pairs={{0,2},{2,4},{4,6},{6,8},{8,10},{10,12},{12,14},{14,16},{16,18},{18... | collective-permute-start | bytes 1966088 | tf_op jit(solution)/shard_map/ppermute | solution.py:21
  62.8 0.0 copy-done.6
  62.8 0.0 copy-done.7
  62.8 0.3 prepare.1
  63.0 0.0 collective-permute-done.14.refs_11_
  63.0 4.6 %project.1 = bf16[16,4,16,640]{3,2,1,0:T(8,128)(2,1)} custom-call(s32[4,1,128]{2,1,0:T(1,128)S(1)} %get-tuple-element.33.place_ref, bf16[128,1280]{1,0:T(8,128)(2,1)S(1)} %copy-done.4, bf16[128,1280]{1,0:T(8,128)(2,1)S(1)} %collective-permute-done.5.refs_1_, bf16[128,1280]{1,0:T(8,128)(2,1)S(1)} %collective-permute-done.6.refs_2_, ...), custom_call_target="tpu_custom_call" | custom-call | flops 1677721600 | bytes 8388608 | tf_op jit(solution)/shard_map/project/pallas_call | solution.py:238
  67.6 0.0 copy-done.8
  67.7 0.0 copy-done.5
  67.7 5.6 %collective-permute-done.15.kv2_ref = bf16[2,128,1280]{2,1,0:T(8,128)(2,1)} collective-permute-done((bf16[2,128,1280]{2,1,0:T(8,128)(2,1)S(1)}, bf16[2,128,1280]{2,1,0:T(8,128)(2,1)}, u32[]{:S(2)}, u32[]{:S(2)}) %collective-permute-start.15) | collective-permute-done | bytes 655392 | tf_op jit(solution)/shard_map/ppermute | solution.py:21
  73.3 4.4 %all-to-all-start = ((bf16[16,4,16,640]{3,2,1,0:T(8,128)(2,1)}), bf16[16,4,16,640]{3,2,1,0:T(8,128)(2,1)S(1)}, u32[]{:S(2)}, u32[]{:S(2)}) async-start(bf16[16,4,16,640]{3,2,1,0:T(8,128)(2,1)} %project.1), calls=%async_computation | async-start | bytes 2621440 | tf_op jit(solution)/shard_map/all_to_all | solution.py:407
  77.6 3.1 %collective-permute-start.16 = (bf16[2,128,1280]{2,1,0:T(8,128)(2,1)}, bf16[2,128,1280]{2,1,0:T(8,128)(2,1)S(1)}, u32[]{:S(2)}, u32[]{:S(2)}) collective-permute-start(bf16[2,128,1280]{2,1,0:T(8,128)(2,1)} %collective-permute-done.13.qg1_ref), channel_id=1, source_target_pairs={{2,0},{4,2},{6,4},{8,6},{10,8},{12,10},{14,12},{16,14},{18,16},{20... | collective-permute-start | bytes 1966088 | tf_op jit(solution)/shard_map/ppermute | solution.py:21
  80.7 27.7 %all-to-all-done = bf16[16,4,16,640]{3,2,1,0:T(8,128)(2,1)S(1)} async-done(((bf16[16,4,16,640]{3,2,1,0:T(8,128)(2,1)}), bf16[16,4,16,640]{3,2,1,0:T(8,128)(2,1)S(1)}, u32[]{:S(2)}, u32[]{:S(2)}) %all-to-all-start) | async-done | bytes 1310752 | tf_op jit(solution)/shard_map/all_to_all | solution.py:407
  108.4 5.0 %attend.1 = (bf16[128,1280]{1,0:T(8,128)(2,1)}, bf16[128,1280]{1,0:T(8,128)(2,1)}, f32[2,16,128]{2,1,0:T(8,128)S(1)}) custom-call(bf16[128,1280]{1,0:T(8,128)(2,1)S(1)} %copy-done, bf16[128,1280]{1,0:T(8,128)(2,1)S(1)} %copy-done.1, bf16[128,1280]{1,0:T(8,128)(2,1)S(1)} %copy-done.2, bf16[128,1280]{1,0:T(8,128)(2,1)S(1)} %copy-done.3, ...), custom_call_target="tpu_custom_call" | custom-call | flops 838860800 | bytes 6291456 | tf_op jit(solution)/shard_map/attend/pallas_call | solution.py:104
  113.4 2.9 %collective-permute-start.17 = (f32[2,16,128]{2,1,0:T(8,128)S(1)}, f32[2,16,128]{2,1,0:T(8,128)S(1)}, u32[]{:S(2)}, u32[]{:S(2)}) collective-permute-start(f32[2,16,128]{2,1,0:T(8,128)S(1)} %get-tuple-element.46.st0_ref), channel_id=1, source_target_pairs={{2,0},{4,2},{6,4},{8,6},{10,8},{12,10},{14,12},{16,14},{18,16},{20... | collective-permute-start | bytes 49160 | tf_op jit(solution)/shard_map/ppermute | solution.py:21
  116.3 2.1 %collective-permute-start.18 = (f32[2,16,128]{2,1,0:T(8,128)S(1)}, f32[2,16,128]{2,1,0:T(8,128)S(1)}, u32[]{:S(2)}, u32[]{:S(2)}) collective-permute-start(f32[2,16,128]{2,1,0:T(8,128)S(1)} %get-tuple-element.46.st0_ref), channel_id=1, source_target_pairs={{4,0},{6,2},{8,4},{10,6},{12,8},{14,10},{16,12},{18,14},{20,16},{2... | collective-permute-start | bytes 49160 | tf_op jit(solution)/shard_map/ppermute | solution.py:21
  118.4 0.0 collective-permute-done.16.qg2_ref
  118.4 0.0 collective-permute-done.17.st1_ref
  118.5 3.5 %collective-permute-done.18.st2_ref = f32[2,16,128]{2,1,0:T(8,128)S(1)} collective-permute-done((f32[2,16,128]{2,1,0:T(8,128)S(1)}, f32[2,16,128]{2,1,0:T(8,128)S(1)}, u32[]{:S(2)}, u32[]{:S(2)}) %collective-permute-start.18) | collective-permute-done | bytes 16416 | tf_op jit(solution)/shard_map/ppermute | solution.py:21
  122.0 3.5 %key_grads.1 = (bf16[128,1280]{1,0:T(8,128)(2,1)}, bf16[128,1280]{1,0:T(8,128)(2,1)}) custom-call(bf16[128,1280]{1,0:T(8,128)(2,1)S(1)} %copy-done.2, bf16[128,1280]{1,0:T(8,128)(2,1)S(1)} %copy-done.3, bf16[128,1280]{1,0:T(8,128)(2,1)S(1)} %copy-done, bf16[128,1280]{1,0:T(8,128)(2,1)S(1)} %copy-done.1, ...), custom_call_target="tpu_custom_call" | custom-call | flops 503316480 | bytes 4194304 | tf_op jit(solution)/shard_map/key_grads/pallas_call | solution.py:173
  (1 shorter events, 0.0 us)
Async XLA Ops:
  0.6 5.1 %copy-start.4 = (bf16[128,1280]{1,0:T(8,128)(2,1)S(1)}, bf16[128,1280]{1,0:T(8,128)(2,1)}, u32[]{:S(2)}) copy-start(bf16[128,1280]{1,0:T(8,128)(2,1)} %refs_0_) | copy-start | bytes 983044
  0.7 26.5 %copy-start = (bf16[128,1280]{1,0:T(8,128)(2,1)S(1)}, bf16[128,1280]{1,0:T(8,128)(2,1)}, u32[]{:S(2)}) copy-start(bf16[128,1280]{1,0:T(8,128)(2,1)} %q_ref.3) | copy-start | bytes 983044
  0.7 26.5 %copy-start.1 = (bf16[128,1280]{1,0:T(8,128)(2,1)S(1)}, bf16[128,1280]{1,0:T(8,128)(2,1)}, u32[]{:S(2)}) copy-start(bf16[128,1280]{1,0:T(8,128)(2,1)} %g_ref.3) | copy-start | bytes 983044
  0.7 26.5 %copy-start.2 = (bf16[128,1280]{1,0:T(8,128)(2,1)S(1)}, bf16[128,1280]{1,0:T(8,128)(2,1)}, u32[]{:S(2)}) copy-start(bf16[128,1280]{1,0:T(8,128)(2,1)} %k_ref.3) | copy-start | bytes 983044
  0.7 26.5 %copy-start.3 = (bf16[128,1280]{1,0:T(8,128)(2,1)S(1)}, bf16[128,1280]{1,0:T(8,128)(2,1)}, u32[]{:S(2)}) copy-start(bf16[128,1280]{1,0:T(8,128)(2,1)} %v_ref.3) | copy-start | bytes 983044
  2.1 9.0 %collective-permute-start = (bf16[160,640]{1,0:T(8,128)(2,1)S(1)}, bf16[160,640]{1,0:T(8,128)(2,1)S(1)}, u32[]{:S(2)}, u32[]{:S(2)}) collective-permute-start(bf16[160,640]{1,0:T(8,128)(2,1)S(1)} %get-tuple-element.51), channel_id=1, source_target_pairs={{0,8},{8,0},{16,24},{24,16},{1,9},{9,1},{17,25},{25,17},{2,10},{10... | collective-permute-start | bytes 614408 | tf_op jit(solution)/shard_map/ppermute | solution.py:25
  3.8 14.6 %collective-permute-start.1 = (bf16[160,640]{1,0:T(8,128)(2,1)S(1)}, bf16[160,640]{1,0:T(8,128)(2,1)S(1)}, u32[]{:S(2)}, u32[]{:S(2)}) collective-permute-start(bf16[160,640]{1,0:T(8,128)(2,1)S(1)} %get-tuple-element.53), channel_id=1, source_target_pairs={{0,16},{8,24},{16,0},{24,8},{1,17},{9,25},{17,1},{25,9},{2,18},{10... | collective-permute-start | bytes 614408 | tf_op jit(solution)/shard_map/ppermute | solution.py:25
  4.1 19.3 %collective-permute-start.2 = (bf16[160,640]{1,0:T(8,128)(2,1)S(1)}, bf16[160,640]{1,0:T(8,128)(2,1)S(1)}, u32[]{:S(2)}, u32[]{:S(2)}) collective-permute-start(bf16[160,640]{1,0:T(8,128)(2,1)S(1)} %get-tuple-element.52), channel_id=1, source_target_pairs={{0,24},{8,16},{16,8},{24,0},{1,25},{9,17},{17,9},{25,1},{2,26},{10... | collective-permute-start | bytes 614408 | tf_op jit(solution)/shard_map/ppermute | solution.py:25
  5.7 17.8 %collective-permute-start.3 = (bf16[128,1280]{1,0:T(8,128)(2,1)S(1)}, bf16[128,1280]{1,0:T(8,128)(2,1)S(1)}, u32[]{:S(2)}, u32[]{:S(2)}) collective-permute-start(bf16[128,1280]{1,0:T(8,128)(2,1)S(1)} %copy-done.4), channel_id=1, source_target_pairs={{0,1},{1,0},{2,3},{3,2},{4,5},{5,4},{6,7},{7,6},{8,9},{9,8},{10,11... | collective-permute-start | bytes 983048 | tf_op jit(solution)/shard_map/ppermute | solution.py:25
  23.5 13.0 %collective-permute-start.11 = (bf16[4,160,640]{2,1,0:T(8,128)(2,1)S(1)}, bf16[4,160,640]{2,1,0:T(8,128)(2,1)S(1)}, u32[]{:S(2)}, u32[]{:S(2)}) collective-permute-start(bf16[4,160,640]{2,1,0:T(8,128)(2,1)S(1)} %pad_maximum_fusion.refs_8_), channel_id=1, source_target_pairs={{0,2},{2,0},{4,6},{6,4},{1,3},{3,1},{5,7},{7,5},{8,10},{10,8},{12,... | collective-permute-start | bytes 2457608 | tf_op jit(solution)/shard_map/ppermute | solution.py:25
  23.6 10.6 %collective-permute-start.5 = (bf16[128,1280]{1,0:T(8,128)(2,1)S(1)}, bf16[128,1280]{1,0:T(8,128)(2,1)S(1)}, u32[]{:S(2)}, u32[]{:S(2)}) collective-permute-start(bf16[128,1280]{1,0:T(8,128)(2,1)S(1)} %copy-done.4), channel_id=1, source_target_pairs={{0,8},{8,24},{24,16},{16,0},{1,9},{9,25},{25,17},{17,1},{2,10},{10... | collective-permute-start | bytes 983048 | tf_op jit(solution)/shard_map/ppermute | solution.py:330
  23.7 17.5 %collective-permute-start.8 = (bf16[128,1280]{1,0:T(8,128)(2,1)S(1)}, bf16[128,1280]{1,0:T(8,128)(2,1)S(1)}, u32[]{:S(2)}, u32[]{:S(2)}) collective-permute-start(bf16[128,1280]{1,0:T(8,128)(2,1)S(1)} %copy-done.4), channel_id=1, source_target_pairs={{8,0},{24,8},{16,24},{0,16},{9,1},{25,9},{17,25},{1,17},{10,2},{26... | collective-permute-start | bytes 983048 | tf_op jit(solution)/shard_map/ppermute | solution.py:330
  25.7 23.6 %collective-permute-start.4 = (bf16[4,160,640]{2,1,0:T(8,128)(2,1)S(1)}, bf16[4,160,640]{2,1,0:T(8,128)(2,1)S(1)}, u32[]{:S(2)}, u32[]{:S(2)}) collective-permute-start(bf16[4,160,640]{2,1,0:T(8,128)(2,1)S(1)} %pad_maximum_fusion.refs_8_), channel_id=1, source_target_pairs={{0,4},{2,6},{4,0},{6,2},{1,5},{3,7},{5,1},{7,3},{8,12},{10,14},{12... | collective-permute-start | bytes 2457608 | tf_op jit(solution)/shard_map/ppermute | solution.py:25
  27.2 35.6 %copy-start.6 = (s32[2048]{0:T(1024)S(1)}, s32[2048]{0:T(1024)}, u32[]{:S(2)}) copy-start(s32[2048]{0:T(1024)} %param.15) | copy-start | bytes 24580
  27.2 35.6 %copy-start.7 = (s32[2048]{0:T(1024)S(1)}, s32[2048]{0:T(1024)}, u32[]{:S(2)}) copy-start(s32[2048]{0:T(1024)} %param.14) | copy-start | bytes 24580
  34.2 10.2 %collective-permute-start.9 = (bf16[128,1280]{1,0:T(8,128)(2,1)S(1)}, bf16[128,1280]{1,0:T(8,128)(2,1)S(1)}, u32[]{:S(2)}, u32[]{:S(2)}) collective-permute-start(bf16[128,1280]{1,0:T(8,128)(2,1)S(1)} %collective-permute-done.5.refs_1_), channel_id=1, source_target_pairs={{0,1},{1,0},{2,3},{3,2},{4,5},{5,4},{6,7},{7,6},{8,9},{9,8},{10,11... | collective-permute-start | bytes 983048 | tf_op jit(solution)/shard_map/ppermute | solution.py:25
  35.7 12.1 %collective-permute-start.6 = (bf16[128,1280]{1,0:T(8,128)(2,1)S(1)}, bf16[128,1280]{1,0:T(8,128)(2,1)S(1)}, u32[]{:S(2)}, u32[]{:S(2)}) collective-permute-start(bf16[128,1280]{1,0:T(8,128)(2,1)S(1)} %collective-permute-done.5.refs_1_), channel_id=1, source_target_pairs={{0,8},{8,24},{24,16},{16,0},{1,9},{9,25},{25,17},{17,1},{2,10},{10... | collective-permute-start | bytes 983048 | tf_op jit(solution)/shard_map/ppermute | solution.py:330
  36.5 23.7 %collective-permute-start.12 = (bf16[2,128,1280]{2,1,0:T(8,128)(2,1)S(1)}, bf16[2,128,1280]{2,1,0:T(8,128)(2,1)S(1)}, u32[]{:S(2)}, u32[]{:S(2)}) collective-permute-start(bf16[2,128,1280]{2,1,0:T(8,128)(2,1)S(1)} %get-tuple-element.30), channel_id=1, source_target_pairs={{0,2},{2,4},{4,6},{6,8},{8,10},{10,12},{12,14},{14,16},{16,18},{18... | collective-permute-start | bytes 1966088 | tf_op jit(solution)/shard_map/ppermute | solution.py:21
  41.1 19.1 %collective-permute-start.13 = (bf16[2,128,1280]{2,1,0:T(8,128)(2,1)S(1)}, bf16[2,128,1280]{2,1,0:T(8,128)(2,1)}, u32[]{:S(2)}, u32[]{:S(2)}) collective-permute-start(bf16[2,128,1280]{2,1,0:T(8,128)(2,1)S(1)} %get-tuple-element.31), channel_id=1, source_target_pairs={{2,0},{4,2},{6,4},{8,6},{10,8},{12,10},{14,12},{16,14},{18,16},{20... | collective-permute-start | bytes 1966088 | tf_op jit(solution)/shard_map/ppermute | solution.py:21
  44.4 10.7 %collective-permute-start.10 = (bf16[128,1280]{1,0:T(8,128)(2,1)S(1)}, bf16[128,1280]{1,0:T(8,128)(2,1)S(1)}, u32[]{:S(2)}, u32[]{:S(2)}) collective-permute-start(bf16[128,1280]{1,0:T(8,128)(2,1)S(1)} %collective-permute-done.8.refs_3_), channel_id=1, source_target_pairs={{0,1},{1,0},{2,3},{3,2},{4,5},{5,4},{6,7},{7,6},{8,9},{9,8},{10,11... | collective-permute-start | bytes 983048 | tf_op jit(solution)/shard_map/ppermute | solution.py:25
  47.8 12.4 %collective-permute-start.7 = (bf16[128,1280]{1,0:T(8,128)(2,1)S(1)}, bf16[128,1280]{1,0:T(8,128)(2,1)S(1)}, u32[]{:S(2)}, u32[]{:S(2)}) collective-permute-start(bf16[128,1280]{1,0:T(8,128)(2,1)S(1)} %collective-permute-done.6.refs_2_), channel_id=1, source_target_pairs={{0,1},{1,0},{2,3},{3,2},{4,5},{5,4},{6,7},{7,6},{8,9},{9,8},{10,11... | collective-permute-start | bytes 983048 | tf_op jit(solution)/shard_map/ppermute | solution.py:25
  60.3 7.4 %copy-start.8 = (bf16[2,128,1280]{2,1,0:T(8,128)(2,1)}, bf16[2,128,1280]{2,1,0:T(8,128)(2,1)S(1)}, u32[]{:S(2)}) copy-start(bf16[2,128,1280]{2,1,0:T(8,128)(2,1)S(1)} %collective-permute-done.12.kv1_ref) | copy-start | bytes 1966084
  60.3 2.8 %collective-permute-start.14 = (bf16[4,160,640]{2,1,0:T(8,128)(2,1)S(1)}, bf16[4,160,640]{2,1,0:T(8,128)(2,1)S(1)}, u32[]{:S(2)}, u32[]{:S(2)}) collective-permute-start(bf16[4,160,640]{2,1,0:T(8,128)(2,1)S(1)} %collective-permute-done.4.refs_10_), channel_id=1, source_target_pairs={{0,2},{2,0},{4,6},{6,4},{1,3},{3,1},{5,7},{7,5},{8,10},{10,8},{12,... | collective-permute-start | bytes 2457608 | tf_op jit(solution)/shard_map/ppermute | solution.py:25
  60.4 12.9 %collective-permute-start.15 = (bf16[2,128,1280]{2,1,0:T(8,128)(2,1)S(1)}, bf16[2,128,1280]{2,1,0:T(8,128)(2,1)}, u32[]{:S(2)}, u32[]{:S(2)}) collective-permute-start(bf16[2,128,1280]{2,1,0:T(8,128)(2,1)S(1)} %collective-permute-done.12.kv1_ref), channel_id=1, source_target_pairs={{0,2},{2,4},{4,6},{6,8},{8,10},{10,12},{12,14},{14,16},{16,18},{18... | collective-permute-start | bytes 1966088 | tf_op jit(solution)/shard_map/ppermute | solution.py:21
  63.0 4.6 %copy-start.5 = (bf16[128,640]{1,0:T(8,128)(2,1)}, bf16[128,640]{1,0:T(8,128)(2,1)S(1)}, u32[]{:S(2)}) copy-start(bf16[128,640]{1,0:T(8,128)(2,1)S(1)} %get-tuple-element.42.bias_ref) | copy-start | bytes 491524
  73.3 35.1 %all-to-all-start = ((bf16[16,4,16,640]{3,2,1,0:T(8,128)(2,1)}), bf16[16,4,16,640]{3,2,1,0:T(8,128)(2,1)S(1)}, u32[]{:S(2)}, u32[]{:S(2)}) async-start(bf16[16,4,16,640]{3,2,1,0:T(8,128)(2,1)} %project.1), calls=%async_computation | async-start | bytes 2621440 | tf_op jit(solution)/shard_map/all_to_all | solution.py:407
  77.6 40.8 %collective-permute-start.16 = (bf16[2,128,1280]{2,1,0:T(8,128)(2,1)}, bf16[2,128,1280]{2,1,0:T(8,128)(2,1)S(1)}, u32[]{:S(2)}, u32[]{:S(2)}) collective-permute-start(bf16[2,128,1280]{2,1,0:T(8,128)(2,1)} %collective-permute-done.13.qg1_ref), channel_id=1, source_target_pairs={{2,0},{4,2},{6,4},{8,6},{10,8},{12,10},{14,12},{16,14},{18,16},{20... | collective-permute-start | bytes 1966088 | tf_op jit(solution)/shard_map/ppermute | solution.py:21
  113.4 5.0 %collective-permute-start.17 = (f32[2,16,128]{2,1,0:T(8,128)S(1)}, f32[2,16,128]{2,1,0:T(8,128)S(1)}, u32[]{:S(2)}, u32[]{:S(2)}) collective-permute-start(f32[2,16,128]{2,1,0:T(8,128)S(1)} %get-tuple-element.46.st0_ref), channel_id=1, source_target_pairs={{2,0},{4,2},{6,4},{8,6},{10,8},{12,10},{14,12},{16,14},{18,16},{20... | collective-permute-start | bytes 49160 | tf_op jit(solution)/shard_map/ppermute | solution.py:21
  116.3 5.6 %collective-permute-start.18 = (f32[2,16,128]{2,1,0:T(8,128)S(1)}, f32[2,16,128]{2,1,0:T(8,128)S(1)}, u32[]{:S(2)}, u32[]{:S(2)}) collective-permute-start(f32[2,16,128]{2,1,0:T(8,128)S(1)} %get-tuple-element.46.st0_ref), channel_id=1, source_target_pairs={{4,0},{6,2},{8,4},{10,6},{12,8},{14,10},{16,12},{18,14},{20,16},{2... | collective-permute-start | bytes 49160 | tf_op jit(solution)/shard_map/ppermute | solution.py:21

commit v14 on v13

--- a/solution.py
+++ b/solution.py
@@ -1,3 +1,5 @@
+import functools
+
 import jax
 import jax.numpy as jnp
 from jax import lax
@@ -194,11 +196,11 @@
     )
 
 
-def project_kernel(place_ref, *refs):
+def project_kernel(layout, place_ref, *refs):
     n_z, _, cache_rows = place_ref.shape
     out_ref, w_ref, a_ref = refs[-3:]
     rows, pieces = refs[: 2 * n_z], refs[2 * n_z : -3]
-    n_p, (_, w_rows, block) = len(pieces), pieces[0].shape
+    w_rows, block = pieces[0].shape[1:]
     depth = rows[0].shape[1]
     devices, _, capacity, _ = out_ref.shape
     z, p, y = (lax.axis_index(name) for name in ("z", "p", "head"))
@@ -206,9 +208,9 @@
     for i, ref in enumerate(rows):
         source = (place_in_ring - i % n_z + n_z) & (n_z - 1)
         a_ref[y ^ (i // n_z), source ^ (source >> 1)] = ref[...]
-    for m in range(n_p):
-        for k in range(n_z):
-            w_ref[z ^ k, p ^ m] = pieces[m][k]
+    for (m, first), piece in zip(layout, pieces):
+        for k in range(piece.shape[0]):
+            w_ref[z ^ (first + k), p ^ m] = piece[k]
     half = n_z // 2
     proj = sum(
         jnp.dot(
@@ -232,12 +234,13 @@
 def project(place, rows, pieces, devices, capacity):
     n_z, _, cache_rows = place.shape
     depth = rows[0].shape[1]
-    n_p = len(pieces)
-    _, w_rows, block = pieces[0].shape
+    layout, pieces = [piece[:2] for piece in pieces], [piece[2] for piece in pieces]
+    n_p = devices // n_z
+    w_rows, block = pieces[0].shape[1:]
     whole = pl.BlockSpec(memory_space=pltpu.VMEM)
     return pl.pallas_call(
-        project_kernel,
-        in_specs=[whole] * (1 + len(rows) + n_p),
+        functools.partial(project_kernel, layout),
+        in_specs=[whole] * (1 + len(rows) + len(pieces)),
         out_specs=whole,
         out_shape=pltpu.VMEM((devices, n_z, capacity, block), jnp.bfloat16),
         scratch_shapes=[
@@ -247,7 +250,7 @@
         compiler_params=pltpu.CompilerParams(vmem_limit_bytes=VMEM),
         cost_estimate=pl.CostEstimate(
             flops=4 * n_z * cache_rows * depth * block,
-            bytes_accessed=8 * 1024 * 1024,
+            bytes_accessed=1024 * 1024,
             transcendentals=0,
         ),
         name="project",
@@ -353,11 +356,14 @@
         other3 = swapped(row3, "head", 1)
         row2 = lax.optimization_barrier(row2)
         other2 = swapped(row2, "head", 1)
-        across, other2, other3, near, back1 = lax.optimization_barrier(
-            (across, other2, other3, near, back1)
-        )
-        pieces = [own, beside, across, swapped(across, "p", 1)]
+        near, other3 = lax.optimization_barrier((near, other3))
         far = shifted(near, 1)
+        parts = [across[k : k + 1] for k in range(n_z)]
+        parts, other2, other3, back1 = lax.optimization_barrier((parts, other2, other3, back1))
+        pieces = [
+            (0, 0, own), (1, 0, beside), (2, 0, across),
+            *((3, k, swapped(part, "p", 1)) for k, part in enumerate(parts)),
+        ]
         rows = [cache, row1, row2, row3, other0, other1, other2, other3]
         slots = project(place, rows, pieces, devices, capacity)
         slots, far = lax.optimization_barrier((slots, far))

time: 126 us -> 129 us (1.024)
  starting transfers between devices: 34.2 us -> 45.7 us
  waiting for transfers between devices: 75.3 us -> 65.9 us
    ppermute x3, starting transfers between devices: 2.91 us -> 12.4 us  [ring_step(): lax.ppermute(value, 'z', [(b, a) for a, b in pairs] if back else pairs)]
    ppermute x6, waiting for transfers between devices: 9.15 us -> 3.53 us  [shifted(): return lax.ppermute(value, SEQ, pairs)]
    ppermute x10 -> x13, waiting for transfers between devices: 27.1 us -> 23.2 us  [swapped(): lax.ppermute(value, axis, [(i, i ^ mask) for i in range(lax.axis_size(axi...]
    all_to_all x1, starting transfers between devices: 4.35 us -> 7.62 us  [body(): memory = lax.all_to_all(slots, SEQ, split_axis=0, concat_axis=0, tiled=True)]
    ppermute x10 -> x13, starting transfers between devices: 11.3 us -> 10.7 us  [swapped(): lax.ppermute(value, axis, [(i, i ^ mask) for i in range(lax.axis_size(axi...]
  transfers between devices with their start and end apart: 20 -> 23, of which waited for: 11 -> 12; matrix products, arithmetic and copies ran while one was open for 0% -> 0% of each run, Pallas kernels for 8% -> 8%
where the time goes in v14:
time: 129 us
  waiting for transfers between devices  65.9 us (51%)
  starting transfers between devices  45.7 us (35%)
  Pallas kernels  13.4 us (10%)
  local copies, waits for them, and re-layouts  2.37 us (2%)
    all_to_all x1, waiting for transfers between devices, body(): memory = lax.all_to_all(slots, SEQ, split_axis=0, concat_axis=0, tiled=True)  27.7 us
    ppermute x13, waiting for transfers between devices, swapped(): lax.ppermute(value, axis, [(i, i ^ mask) for i in range(lax.axis_size(axi...  23.2 us
    ppermute x6, starting transfers between devices, shifted(): return lax.ppermute(value, SEQ, pairs)  15 us
    ppermute x3, starting transfers between devices, ring_step(): lax.ppermute(value, 'z', [(b, a) for a, b in pairs] if back else pairs)  12.4 us
    ppermute x3, waiting for transfers between devices, ring_step(): lax.ppermute(value, 'z', [(b, a) for a, b in pairs] if back else pairs)  11.5 us
    ppermute x13, starting transfers between devices, swapped(): lax.ppermute(value, axis, [(i, i ^ mask) for i in range(lax.axis_size(axi...  10.7 us
    all_to_all x1, starting transfers between devices, body(): memory = lax.all_to_all(slots, SEQ, split_axis=0, concat_axis=0, tiled=True)  7.62 us
    pallas_call x1, Pallas kernels, attend(): pl.pallas_call(attend_kernel, grid=(steps,), in_specs=[whole, whole, whol...  5.02 us
  transfers between devices with their start and end apart: 23, of which 12 were waited for; matrix products, arithmetic and copies ran while one was open for 0% of the time, Pallas kernels for 8%

profile of v14, /device:TPU:16, one launch (start us, length us, event | category | flops | bytes accessed | tf_op | source)
XLA Modules:
  0.0 128.5 jit_solution(8764970990598969348)
XLA Ops:
  0.6 0.0 copy-start.4
  0.7 0.0 copy-start
  0.7 0.0 copy-start.1
  0.7 0.0 copy-start.2
  0.7 0.0 copy-start.3
  0.7 1.4 %constant_dynamic-slice_fusion = (bf16[1,160,640]{2,1,0:T(8,128)(2,1)S(1)}, bf16[160,640]{1,0:T(8,128)(2,1)S(1)}, bf16[160,640]{1,0:T(8,128)(2,1)S(1)}, bf16[160,640]{1,0:T(8,128)(2,1)S(1)}) fusion(bf16[2,160,1280]{2,1,0:T(8,128)(2,1)} %param.13, s32[]{:T(128)S(6)} %select_n.24, s32[]{:T(128)S(6)} %select_n.25, s32[]{:T(128)S(6)} %select_n.26, ...), kind=kLoop, calls=%fused_computation.6 | loop fusion | bytes 1638432 | tf_op jit(solution)/shard_map/dynamic_slice | solution.py:328
  2.1 0.5 collective-permute-start.2
  2.6 3.5 %collective-permute-start.1 = (bf16[160,640]{1,0:T(8,128)(2,1)S(1)}, bf16[160,640]{1,0:T(8,128)(2,1)S(1)}, u32[]{:S(2)}, u32[]{:S(2)}) collective-permute-start(bf16[160,640]{1,0:T(8,128)(2,1)S(1)} %get-tuple-element.65), channel_id=1, source_target_pairs={{0,16},{8,24},{16,0},{24,8},{1,17},{9,25},{17,1},{25,9},{2,18},{10... | collective-permute-start | bytes 614408 | tf_op jit(solution)/shard_map/ppermute | solution.py:27
  6.1 0.0 collective-permute-start
  6.1 0.0 copy-done.4
  6.1 1.5 %collective-permute-start.3 = (bf16[128,1280]{1,0:T(8,128)(2,1)S(1)}, bf16[128,1280]{1,0:T(8,128)(2,1)S(1)}, u32[]{:S(2)}, u32[]{:S(2)}) collective-permute-start(bf16[128,1280]{1,0:T(8,128)(2,1)S(1)} %copy-done.4), channel_id=1, source_target_pairs={{0,1},{1,0},{2,3},{3,2},{4,5},{5,4},{6,7},{7,6},{8,9},{9,8},{10,11... | collective-permute-start | bytes 983048 | tf_op jit(solution)/shard_map/ppermute | solution.py:27
  7.7 11.3 %collective-permute-done.2 = bf16[160,640]{1,0:T(8,128)(2,1)S(1)} collective-permute-done((bf16[160,640]{1,0:T(8,128)(2,1)S(1)}, bf16[160,640]{1,0:T(8,128)(2,1)S(1)}, u32[]{:S(2)}, u32[]{:S(2)}) %collective-permute-start.2) | collective-permute-done | bytes 204832 | tf_op jit(solution)/shard_map/ppermute | solution.py:27
  18.9 1.2 collective-permute-done.1
  20.1 0.0 collective-permute-done
  20.2 0.1 pad_maximum_fusion.refs_8_
  20.3 0.0 collective-permute-done.3.refs_4_
  20.3 0.1 collective-permute-start.4
  20.4 3.4 %collective-permute-start.7 = (bf16[128,1280]{1,0:T(8,128)(2,1)S(1)}, bf16[128,1280]{1,0:T(8,128)(2,1)S(1)}, u32[]{:S(2)}, u32[]{:S(2)}) collective-permute-start(bf16[128,1280]{1,0:T(8,128)(2,1)S(1)} %copy-done.4), channel_id=1, source_target_pairs={{0,8},{8,24},{24,16},{16,0},{1,9},{9,25},{25,17},{17,1},{2,10},{10... | collective-permute-start | bytes 983048 | tf_op jit(solution)/shard_map/ppermute | solution.py:333
  23.8 0.2 collective-permute-start.6
  24.0 1.5 %collective-permute-start.11 = (bf16[4,160,640]{2,1,0:T(8,128)(2,1)S(1)}, bf16[4,160,640]{2,1,0:T(8,128)(2,1)S(1)}, u32[]{:S(2)}, u32[]{:S(2)}) collective-permute-start(bf16[4,160,640]{2,1,0:T(8,128)(2,1)S(1)} %pad_maximum_fusion.refs_8_), channel_id=1, source_target_pairs={{0,4},{2,6},{4,0},{6,2},{1,5},{3,7},{5,1},{7,3},{8,12},{10,14},{12... | collective-permute-start | bytes 2457608 | tf_op jit(solution)/shard_map/ppermute | solution.py:27
  25.5 0.1 pad_maximum_fusion.1
  25.6 0.0 copy-start.6
  25.6 0.0 copy-start.7
  25.7 6.8 %collective-permute-done.7.refs_1_ = bf16[128,1280]{1,0:T(8,128)(2,1)S(1)} collective-permute-done((bf16[128,1280]{1,0:T(8,128)(2,1)S(1)}, bf16[128,1280]{1,0:T(8,128)(2,1)S(1)}, u32[]{:S(2)}, u32[]{:S(2)}) %collective-permute-start.7) | collective-permute-done | bytes 327712 | tf_op jit(solution)/shard_map/ppermute | solution.py:333
  32.5 1.5 %collective-permute-start.8 = (bf16[128,1280]{1,0:T(8,128)(2,1)S(1)}, bf16[128,1280]{1,0:T(8,128)(2,1)S(1)}, u32[]{:S(2)}, u32[]{:S(2)}) collective-permute-start(bf16[128,1280]{1,0:T(8,128)(2,1)S(1)} %collective-permute-done.7.refs_1_), channel_id=1, source_target_pairs={{0,1},{1,0},{2,3},{3,2},{4,5},{5,4},{6,7},{7,6},{8,9},{9,8},{10,11... | collective-permute-start | bytes 983048 | tf_op jit(solution)/shard_map/ppermute | solution.py:27
  34.0 0.0 collective-permute-done.4.refs_9_
  34.0 1.9 %collective-permute-start.5 = (bf16[2,128,1280]{2,1,0:T(8,128)(2,1)S(1)}, bf16[2,128,1280]{2,1,0:T(8,128)(2,1)S(1)}, u32[]{:S(2)}, u32[]{:S(2)}) collective-permute-start(bf16[2,128,1280]{2,1,0:T(8,128)(2,1)S(1)} %get-tuple-element.32), channel_id=1, source_target_pairs={{0,2},{2,4},{4,6},{6,8},{8,10},{10,12},{12,14},{14,16},{16,18},{18... | collective-permute-start | bytes 1966088 | tf_op jit(solution)/shard_map/ppermute | solution.py:23
  35.9 8.8 %collective-permute-start.10 = (bf16[128,1280]{1,0:T(8,128)(2,1)S(1)}, bf16[128,1280]{1,0:T(8,128)(2,1)S(1)}, u32[]{:S(2)}, u32[]{:S(2)}) collective-permute-start(bf16[128,1280]{1,0:T(8,128)(2,1)S(1)} %collective-permute-done.7.refs_1_), channel_id=1, source_target_pairs={{0,8},{8,24},{24,16},{16,0},{1,9},{9,25},{25,17},{17,1},{2,10},{10... | collective-permute-start | bytes 983048 | tf_op jit(solution)/shard_map/ppermute | solution.py:333
  44.7 0.0 collective-permute-done.6.refs_3_
  44.7 3.1 %collective-permute-start.13 = (bf16[2,128,1280]{2,1,0:T(8,128)(2,1)S(1)}, bf16[2,128,1280]{2,1,0:T(8,128)(2,1)}, u32[]{:S(2)}, u32[]{:S(2)}) collective-permute-start(bf16[2,128,1280]{2,1,0:T(8,128)(2,1)S(1)} %get-tuple-element.40), channel_id=1, source_target_pairs={{2,0},{4,2},{6,4},{8,6},{10,8},{12,10},{14,12},{16,14},{18,16},{20... | collective-permute-start | bytes 1966088 | tf_op jit(solution)/shard_map/ppermute | solution.py:23
  47.8 0.0 collective-permute-done.8.refs_5_
  47.8 0.6 collective-permute-start.9
  48.4 4.7 %collective-permute-done.10.refs_2_ = bf16[128,1280]{1,0:T(8,128)(2,1)S(1)} collective-permute-done((bf16[128,1280]{1,0:T(8,128)(2,1)S(1)}, bf16[128,1280]{1,0:T(8,128)(2,1)S(1)}, u32[]{:S(2)}, u32[]{:S(2)}) %collective-permute-start.10) | collective-permute-done | bytes 327712 | tf_op jit(solution)/shard_map/ppermute | solution.py:333
  53.1 0.5 collective-permute-start.12
  53.6 4.8 %collective-permute-done.9.refs_7_ = bf16[128,1280]{1,0:T(8,128)(2,1)S(1)} collective-permute-done((bf16[128,1280]{1,0:T(8,128)(2,1)S(1)}, bf16[128,1280]{1,0:T(8,128)(2,1)S(1)}, u32[]{:S(2)}, u32[]{:S(2)}) %collective-permute-start.9) | collective-permute-done | bytes 327712 | tf_op jit(solution)/shard_map/ppermute | solution.py:27
  58.5 0.0 collective-permute-done.5.kv1_ref
  58.5 1.9 %collective-permute-start.18 = (bf16[2,128,1280]{2,1,0:T(8,128)(2,1)S(1)}, bf16[2,128,1280]{2,1,0:T(8,128)(2,1)S(1)}, u32[]{:S(2)}, u32[]{:S(2)}) collective-permute-start(bf16[2,128,1280]{2,1,0:T(8,128)(2,1)S(1)} %collective-permute-done.5.kv1_ref), channel_id=1, source_target_pairs={{0,2},{2,4},{4,6},{6,8},{8,10},{10,12},{12,14},{14,16},{16,18},{18... | collective-permute-start | bytes 1966088 | tf_op jit(solution)/shard_map/ppermute | solution.py:23
  60.4 0.0 collective-permute-done.11.refs_10_
  60.4 0.1 fusion
  60.5 4.8 %collective-permute-done.12.refs_6_ = bf16[128,1280]{1,0:T(8,128)(2,1)S(1)} collective-permute-done((bf16[128,1280]{1,0:T(8,128)(2,1)S(1)}, bf16[128,1280]{1,0:T(8,128)(2,1)S(1)}, u32[]{:S(2)}, u32[]{:S(2)}) %collective-permute-start.12) | collective-permute-done | bytes 327712 | tf_op jit(solution)/shard_map/ppermute | solution.py:27
  65.3 0.0 collective-permute-done.13.qg1_ref
  65.3 0.0 collective-permute-start.14
  65.3 0.5 collective-permute-start.15
  65.8 0.0 collective-permute-start.16
  65.8 0.5 collective-permute-start.17
  66.3 0.0 copy-done.6
  66.3 0.2 prepare.1
  66.6 0.2 collective-permute-done.14.refs_11_
  66.7 0.3 collective-permute-done.15.refs_12_
  67.0 0.3 collective-permute-done.16.refs_13_
  67.3 0.3 collective-permute-done.17.refs_14_
  67.6 4.6 %project.1 = bf16[16,4,16,640]{3,2,1,0:T(8,128)(2,1)} custom-call(s32[4,1,128]{2,1,0:T(1,128)S(1)} %get-tuple-element.36.place_ref, bf16[128,1280]{1,0:T(8,128)(2,1)S(1)} %copy-done.4, bf16[128,1280]{1,0:T(8,128)(2,1)S(1)} %collective-permute-done.7.refs_1_, bf16[128,1280]{1,0:T(8,128)(2,1)S(1)} %collective-permute-done.10.refs_2_, ...), custom_call_target="tpu_custom_call" | custom-call | flops 1677721600 | bytes 1048576 | tf_op jit(solution)/shard_map/project/pallas_call | solution.py:241
  72.2 0.0 collective-permute-done.18.kv2_ref
  72.2 0.8 copy-done.9
  73.1 7.6 %all-to-all-start = ((bf16[16,4,16,640]{3,2,1,0:T(8,128)(2,1)}), bf16[16,4,16,640]{3,2,1,0:T(8,128)(2,1)S(1)}, u32[]{:S(2)}, u32[]{:S(2)}) async-start(bf16[16,4,16,640]{3,2,1,0:T(8,128)(2,1)} %project.1), calls=%async_computation | async-start | bytes 2621440 | tf_op jit(solution)/shard_map/all_to_all | solution.py:413
  80.7 3.1 %collective-permute-start.19 = (bf16[2,128,1280]{2,1,0:T(8,128)(2,1)}, bf16[2,128,1280]{2,1,0:T(8,128)(2,1)S(1)}, u32[]{:S(2)}, u32[]{:S(2)}) collective-permute-start(bf16[2,128,1280]{2,1,0:T(8,128)(2,1)} %collective-permute-done.13.qg1_ref), channel_id=1, source_target_pairs={{2,0},{4,2},{6,4},{8,6},{10,8},{12,10},{14,12},{16,14},{18,16},{20... | collective-permute-start | bytes 1966088 | tf_op jit(solution)/shard_map/ppermute | solution.py:23
  83.8 27.7 %all-to-all-done = bf16[16,4,16,640]{3,2,1,0:T(8,128)(2,1)S(1)} async-done(((bf16[16,4,16,640]{3,2,1,0:T(8,128)(2,1)}), bf16[16,4,16,640]{3,2,1,0:T(8,128)(2,1)S(1)}, u32[]{:S(2)}, u32[]{:S(2)}) %all-to-all-start) | async-done | bytes 1310752 | tf_op jit(solution)/shard_map/all_to_all | solution.py:413
  111.5 5.0 %attend.1 = (bf16[128,1280]{1,0:T(8,128)(2,1)}, bf16[128,1280]{1,0:T(8,128)(2,1)}, f32[2,16,128]{2,1,0:T(8,128)S(1)}) custom-call(bf16[128,1280]{1,0:T(8,128)(2,1)S(1)} %copy-done, bf16[128,1280]{1,0:T(8,128)(2,1)S(1)} %copy-done.1, bf16[128,1280]{1,0:T(8,128)(2,1)S(1)} %copy-done.2, bf16[128,1280]{1,0:T(8,128)(2,1)S(1)} %copy-done.3, ...), custom_call_target="tpu_custom_call" | custom-call | flops 838860800 | bytes 6291456 | tf_op jit(solution)/shard_map/attend/pallas_call | solution.py:106
  116.5 2.9 %collective-permute-start.20 = (f32[2,16,128]{2,1,0:T(8,128)S(1)}, f32[2,16,128]{2,1,0:T(8,128)S(1)}, u32[]{:S(2)}, u32[]{:S(2)}) collective-permute-start(f32[2,16,128]{2,1,0:T(8,128)S(1)} %get-tuple-element.54.st0_ref), channel_id=1, source_target_pairs={{2,0},{4,2},{6,4},{8,6},{10,8},{12,10},{14,12},{16,14},{18,16},{20... | collective-permute-start | bytes 49160 | tf_op jit(solution)/shard_map/ppermute | solution.py:23
  119.4 2.1 %collective-permute-start.21 = (f32[2,16,128]{2,1,0:T(8,128)S(1)}, f32[2,16,128]{2,1,0:T(8,128)S(1)}, u32[]{:S(2)}, u32[]{:S(2)}) collective-permute-start(f32[2,16,128]{2,1,0:T(8,128)S(1)} %get-tuple-element.54.st0_ref), channel_id=1, source_target_pairs={{4,0},{6,2},{8,4},{10,6},{12,8},{14,10},{16,12},{18,14},{20,16},{2... | collective-permute-start | bytes 49160 | tf_op jit(solution)/shard_map/ppermute | solution.py:23
  121.5 0.0 collective-permute-done.19.qg2_ref
  121.5 0.0 collective-permute-done.20.st1_ref
  121.5 3.5 %collective-permute-done.21.st2_ref = f32[2,16,128]{2,1,0:T(8,128)S(1)} collective-permute-done((f32[2,16,128]{2,1,0:T(8,128)S(1)}, f32[2,16,128]{2,1,0:T(8,128)S(1)}, u32[]{:S(2)}, u32[]{:S(2)}) %collective-permute-start.21) | collective-permute-done | bytes 16416 | tf_op jit(solution)/shard_map/ppermute | solution.py:23
  125.0 3.5 %key_grads.1 = (bf16[128,1280]{1,0:T(8,128)(2,1)}, bf16[128,1280]{1,0:T(8,128)(2,1)}) custom-call(bf16[128,1280]{1,0:T(8,128)(2,1)S(1)} %copy-done.2, bf16[128,1280]{1,0:T(8,128)(2,1)S(1)} %copy-done.3, bf16[128,1280]{1,0:T(8,128)(2,1)S(1)} %copy-done, bf16[128,1280]{1,0:T(8,128)(2,1)S(1)} %copy-done.1, ...), custom_call_target="tpu_custom_call" | custom-call | flops 503316480 | bytes 4194304 | tf_op jit(solution)/shard_map/key_grads/pallas_call | solution.py:175
  (10 shorter events, 0.0 us)
Async XLA Ops:
  0.6 5.5 %copy-start.4 = (bf16[128,1280]{1,0:T(8,128)(2,1)S(1)}, bf16[128,1280]{1,0:T(8,128)(2,1)}, u32[]{:S(2)}) copy-start(bf16[128,1280]{1,0:T(8,128)(2,1)} %refs_0_) | copy-start | bytes 983044
  0.7 24.8 %copy-start = (bf16[128,1280]{1,0:T(8,128)(2,1)S(1)}, bf16[128,1280]{1,0:T(8,128)(2,1)}, u32[]{:S(2)}) copy-start(bf16[128,1280]{1,0:T(8,128)(2,1)} %q_ref.3) | copy-start | bytes 983044
  0.7 24.8 %copy-start.1 = (bf16[128,1280]{1,0:T(8,128)(2,1)S(1)}, bf16[128,1280]{1,0:T(8,128)(2,1)}, u32[]{:S(2)}) copy-start(bf16[128,1280]{1,0:T(8,128)(2,1)} %g_ref.3) | copy-start | bytes 983044
  0.7 24.8 %copy-start.2 = (bf16[128,1280]{1,0:T(8,128)(2,1)S(1)}, bf16[128,1280]{1,0:T(8,128)(2,1)}, u32[]{:S(2)}) copy-start(bf16[128,1280]{1,0:T(8,128)(2,1)} %k_ref.3) | copy-start | bytes 983044
  0.7 24.8 %copy-start.3 = (bf16[128,1280]{1,0:T(8,128)(2,1)S(1)}, bf16[128,1280]{1,0:T(8,128)(2,1)}, u32[]{:S(2)}) copy-start(bf16[128,1280]{1,0:T(8,128)(2,1)} %v_ref.3) | copy-start | bytes 983044
  2.1 16.8 %collective-permute-start.2 = (bf16[160,640]{1,0:T(8,128)(2,1)S(1)}, bf16[160,640]{1,0:T(8,128)(2,1)S(1)}, u32[]{:S(2)}, u32[]{:S(2)}) collective-permute-start(bf16[160,640]{1,0:T(8,128)(2,1)S(1)} %get-tuple-element.64), channel_id=1, source_target_pairs={{0,24},{8,16},{16,8},{24,0},{1,25},{9,17},{17,9},{25,1},{2,26},{10... | collective-permute-start | bytes 614408 | tf_op jit(solution)/shard_map/ppermute | solution.py:27
  2.6 17.5 %collective-permute-start.1 = (bf16[160,640]{1,0:T(8,128)(2,1)S(1)}, bf16[160,640]{1,0:T(8,128)(2,1)S(1)}, u32[]{:S(2)}, u32[]{:S(2)}) collective-permute-start(bf16[160,640]{1,0:T(8,128)(2,1)S(1)} %get-tuple-element.65), channel_id=1, source_target_pairs={{0,16},{8,24},{16,0},{24,8},{1,17},{9,25},{17,1},{25,9},{2,18},{10... | collective-permute-start | bytes 614408 | tf_op jit(solution)/shard_map/ppermute | solution.py:27
  6.1 14.0 %collective-permute-start = (bf16[160,640]{1,0:T(8,128)(2,1)S(1)}, bf16[160,640]{1,0:T(8,128)(2,1)S(1)}, u32[]{:S(2)}, u32[]{:S(2)}) collective-permute-start(bf16[160,640]{1,0:T(8,128)(2,1)S(1)} %get-tuple-element.63), channel_id=1, source_target_pairs={{0,8},{8,0},{16,24},{24,16},{1,9},{9,1},{17,25},{25,17},{2,10},{10... | collective-permute-start | bytes 614408 | tf_op jit(solution)/shard_map/ppermute | solution.py:27
  6.1 14.1 %collective-permute-start.3 = (bf16[128,1280]{1,0:T(8,128)(2,1)S(1)}, bf16[128,1280]{1,0:T(8,128)(2,1)S(1)}, u32[]{:S(2)}, u32[]{:S(2)}) collective-permute-start(bf16[128,1280]{1,0:T(8,128)(2,1)S(1)} %copy-done.4), channel_id=1, source_target_pairs={{0,1},{1,0},{2,3},{3,2},{4,5},{5,4},{6,7},{7,6},{8,9},{9,8},{10,11... | collective-permute-start | bytes 983048 | tf_op jit(solution)/shard_map/ppermute | solution.py:27
  20.3 13.7 %collective-permute-start.4 = (bf16[4,160,640]{2,1,0:T(8,128)(2,1)S(1)}, bf16[4,160,640]{2,1,0:T(8,128)(2,1)S(1)}, u32[]{:S(2)}, u32[]{:S(2)}) collective-permute-start(bf16[4,160,640]{2,1,0:T(8,128)(2,1)S(1)} %pad_maximum_fusion.refs_8_), channel_id=1, source_target_pairs={{0,2},{2,0},{4,6},{6,4},{1,3},{3,1},{5,7},{7,5},{8,10},{10,8},{12,... | collective-permute-start | bytes 2457608 | tf_op jit(solution)/shard_map/ppermute | solution.py:27
  20.4 12.1 %collective-permute-start.7 = (bf16[128,1280]{1,0:T(8,128)(2,1)S(1)}, bf16[128,1280]{1,0:T(8,128)(2,1)S(1)}, u32[]{:S(2)}, u32[]{:S(2)}) collective-permute-start(bf16[128,1280]{1,0:T(8,128)(2,1)S(1)} %copy-done.4), channel_id=1, source_target_pairs={{0,8},{8,24},{24,16},{16,0},{1,9},{9,25},{25,17},{17,1},{2,10},{10... | collective-permute-start | bytes 983048 | tf_op jit(solution)/shard_map/ppermute | solution.py:333
  23.8 20.9 %collective-permute-start.6 = (bf16[128,1280]{1,0:T(8,128)(2,1)S(1)}, bf16[128,1280]{1,0:T(8,128)(2,1)S(1)}, u32[]{:S(2)}, u32[]{:S(2)}) collective-permute-start(bf16[128,1280]{1,0:T(8,128)(2,1)S(1)} %copy-done.4), channel_id=1, source_target_pairs={{8,0},{24,8},{16,24},{0,16},{9,1},{25,9},{17,25},{1,17},{10,2},{26... | collective-permute-start | bytes 983048 | tf_op jit(solution)/shard_map/ppermute | solution.py:333
  24.0 36.4 %collective-permute-start.11 = (bf16[4,160,640]{2,1,0:T(8,128)(2,1)S(1)}, bf16[4,160,640]{2,1,0:T(8,128)(2,1)S(1)}, u32[]{:S(2)}, u32[]{:S(2)}) collective-permute-start(bf16[4,160,640]{2,1,0:T(8,128)(2,1)S(1)} %pad_maximum_fusion.refs_8_), channel_id=1, source_target_pairs={{0,4},{2,6},{4,0},{6,2},{1,5},{3,7},{5,1},{7,3},{8,12},{10,14},{12... | collective-permute-start | bytes 2457608 | tf_op jit(solution)/shard_map/ppermute | solution.py:27
  25.6 40.7 %copy-start.6 = (s32[2048]{0:T(1024)S(1)}, s32[2048]{0:T(1024)}, u32[]{:S(2)}) copy-start(s32[2048]{0:T(1024)} %param.15) | copy-start | bytes 24580
  25.6 40.7 %copy-start.7 = (s32[2048]{0:T(1024)S(1)}, s32[2048]{0:T(1024)}, u32[]{:S(2)}) copy-start(s32[2048]{0:T(1024)} %param.14) | copy-start | bytes 24580
  32.5 15.3 %collective-permute-start.8 = (bf16[128,1280]{1,0:T(8,128)(2,1)S(1)}, bf16[128,1280]{1,0:T(8,128)(2,1)S(1)}, u32[]{:S(2)}, u32[]{:S(2)}) collective-permute-start(bf16[128,1280]{1,0:T(8,128)(2,1)S(1)} %collective-permute-done.7.refs_1_), channel_id=1, source_target_pairs={{0,1},{1,0},{2,3},{3,2},{4,5},{5,4},{6,7},{7,6},{8,9},{9,8},{10,11... | collective-permute-start | bytes 983048 | tf_op jit(solution)/shard_map/ppermute | solution.py:27
  34.0 24.5 %collective-permute-start.5 = (bf16[2,128,1280]{2,1,0:T(8,128)(2,1)S(1)}, bf16[2,128,1280]{2,1,0:T(8,128)(2,1)S(1)}, u32[]{:S(2)}, u32[]{:S(2)}) collective-permute-start(bf16[2,128,1280]{2,1,0:T(8,128)(2,1)S(1)} %get-tuple-element.32), channel_id=1, source_target_pairs={{0,2},{2,4},{4,6},{6,8},{8,10},{10,12},{12,14},{14,16},{16,18},{18... | collective-permute-start | bytes 1966088 | tf_op jit(solution)/shard_map/ppermute | solution.py:23
  35.9 17.2 %collective-permute-start.10 = (bf16[128,1280]{1,0:T(8,128)(2,1)S(1)}, bf16[128,1280]{1,0:T(8,128)(2,1)S(1)}, u32[]{:S(2)}, u32[]{:S(2)}) collective-permute-start(bf16[128,1280]{1,0:T(8,128)(2,1)S(1)} %collective-permute-done.7.refs_1_), channel_id=1, source_target_pairs={{0,8},{8,24},{24,16},{16,0},{1,9},{9,25},{25,17},{17,1},{2,10},{10... | collective-permute-start | bytes 983048 | tf_op jit(solution)/shard_map/ppermute | solution.py:333
  44.7 20.5 %collective-permute-start.13 = (bf16[2,128,1280]{2,1,0:T(8,128)(2,1)S(1)}, bf16[2,128,1280]{2,1,0:T(8,128)(2,1)}, u32[]{:S(2)}, u32[]{:S(2)}) collective-permute-start(bf16[2,128,1280]{2,1,0:T(8,128)(2,1)S(1)} %get-tuple-element.40), channel_id=1, source_target_pairs={{2,0},{4,2},{6,4},{8,6},{10,8},{12,10},{14,12},{16,14},{18,16},{20... | collective-permute-start | bytes 1966088 | tf_op jit(solution)/shard_map/ppermute | solution.py:23
  47.8 10.6 %collective-permute-start.9 = (bf16[128,1280]{1,0:T(8,128)(2,1)S(1)}, bf16[128,1280]{1,0:T(8,128)(2,1)S(1)}, u32[]{:S(2)}, u32[]{:S(2)}) collective-permute-start(bf16[128,1280]{1,0:T(8,128)(2,1)S(1)} %collective-permute-done.6.refs_3_), channel_id=1, source_target_pairs={{0,1},{1,0},{2,3},{3,2},{4,5},{5,4},{6,7},{7,6},{8,9},{9,8},{10,11... | collective-permute-start | bytes 983048 | tf_op jit(solution)/shard_map/ppermute | solution.py:27
  53.1 12.2 %collective-permute-start.12 = (bf16[128,1280]{1,0:T(8,128)(2,1)S(1)}, bf16[128,1280]{1,0:T(8,128)(2,1)S(1)}, u32[]{:S(2)}, u32[]{:S(2)}) collective-permute-start(bf16[128,1280]{1,0:T(8,128)(2,1)S(1)} %collective-permute-done.10.refs_2_), channel_id=1, source_target_pairs={{0,1},{1,0},{2,3},{3,2},{4,5},{5,4},{6,7},{7,6},{8,9},{9,8},{10,11... | collective-permute-start | bytes 983048 | tf_op jit(solution)/shard_map/ppermute | solution.py:27
  58.5 13.7 %copy-start.8 = (bf16[2,128,1280]{2,1,0:T(8,128)(2,1)}, bf16[2,128,1280]{2,1,0:T(8,128)(2,1)S(1)}, u32[]{:S(2)}) copy-start(bf16[2,128,1280]{2,1,0:T(8,128)(2,1)S(1)} %collective-permute-done.5.kv1_ref) | copy-start | bytes 1966084
  58.5 13.7 %collective-permute-start.18 = (bf16[2,128,1280]{2,1,0:T(8,128)(2,1)S(1)}, bf16[2,128,1280]{2,1,0:T(8,128)(2,1)S(1)}, u32[]{:S(2)}, u32[]{:S(2)}) collective-permute-start(bf16[2,128,1280]{2,1,0:T(8,128)(2,1)S(1)} %collective-permute-done.5.kv1_ref), channel_id=1, source_target_pairs={{0,2},{2,4},{4,6},{6,8},{8,10},{10,12},{12,14},{14,16},{16,18},{18... | collective-permute-start | bytes 1966088 | tf_op jit(solution)/shard_map/ppermute | solution.py:23
  65.3 1.5 %collective-permute-start.14 = (bf16[1,160,640]{2,1,0:T(8,128)(2,1)S(1)}, bf16[1,160,640]{2,1,0:T(8,128)(2,1)S(1)}, u32[]{:S(2)}, u32[]{:S(2)}) collective-permute-start(bf16[1,160,640]{2,1,0:T(8,128)(2,1)S(1)} %get-tuple-element.44), channel_id=1, source_target_pairs={{0,2},{2,0},{4,6},{6,4},{1,3},{3,1},{5,7},{7,5},{8,10},{10,8},{12,... | collective-permute-start | bytes 614408 | tf_op jit(solution)/shard_map/ppermute | solution.py:27
  65.3 1.7 %collective-permute-start.15 = (bf16[1,160,640]{2,1,0:T(8,128)(2,1)S(1)}, bf16[1,160,640]{2,1,0:T(8,128)(2,1)S(1)}, u32[]{:S(2)}, u32[]{:S(2)}) collective-permute-start(bf16[1,160,640]{2,1,0:T(8,128)(2,1)S(1)} %get-tuple-element.45), channel_id=1, source_target_pairs={{0,2},{2,0},{4,6},{6,4},{1,3},{3,1},{5,7},{7,5},{8,10},{10,8},{12,... | collective-permute-start | bytes 614408 | tf_op jit(solution)/shard_map/ppermute | solution.py:27
  65.8 1.5 %collective-permute-start.16 = (bf16[1,160,640]{2,1,0:T(8,128)(2,1)S(1)}, bf16[1,160,640]{2,1,0:T(8,128)(2,1)S(1)}, u32[]{:S(2)}, u32[]{:S(2)}) collective-permute-start(bf16[1,160,640]{2,1,0:T(8,128)(2,1)S(1)} %get-tuple-element.46), channel_id=1, source_target_pairs={{0,2},{2,0},{4,6},{6,4},{1,3},{3,1},{5,7},{7,5},{8,10},{10,8},{12,... | collective-permute-start | bytes 614408 | tf_op jit(solution)/shard_map/ppermute | solution.py:27
  65.8 1.8 %collective-permute-start.17 = (bf16[1,160,640]{2,1,0:T(8,128)(2,1)S(1)}, bf16[1,160,640]{2,1,0:T(8,128)(2,1)S(1)}, u32[]{:S(2)}, u32[]{:S(2)}) collective-permute-start(bf16[1,160,640]{2,1,0:T(8,128)(2,1)S(1)} %get-tuple-element.47), channel_id=1, source_target_pairs={{0,2},{2,0},{4,6},{6,4},{1,3},{3,1},{5,7},{7,5},{8,10},{10,8},{12,... | collective-permute-start | bytes 614408 | tf_op jit(solution)/shard_map/ppermute | solution.py:27
  66.5 5.7 %copy-start.5 = (bf16[128,640]{1,0:T(8,128)(2,1)}, bf16[128,640]{1,0:T(8,128)(2,1)S(1)}, u32[]{:S(2)}) copy-start(bf16[128,640]{1,0:T(8,128)(2,1)S(1)} %get-tuple-element.50.bias_ref) | copy-start | bytes 491524
  72.2 0.8 copy-start.9
  73.1 38.4 %all-to-all-start = ((bf16[16,4,16,640]{3,2,1,0:T(8,128)(2,1)}), bf16[16,4,16,640]{3,2,1,0:T(8,128)(2,1)S(1)}, u32[]{:S(2)}, u32[]{:S(2)}) async-start(bf16[16,4,16,640]{3,2,1,0:T(8,128)(2,1)} %project.1), calls=%async_computation | async-start | bytes 2621440 | tf_op jit(solution)/shard_map/all_to_all | solution.py:413
  80.7 40.8 %collective-permute-start.19 = (bf16[2,128,1280]{2,1,0:T(8,128)(2,1)}, bf16[2,128,1280]{2,1,0:T(8,128)(2,1)S(1)}, u32[]{:S(2)}, u32[]{:S(2)}) collective-permute-start(bf16[2,128,1280]{2,1,0:T(8,128)(2,1)} %collective-permute-done.13.qg1_ref), channel_id=1, source_target_pairs={{2,0},{4,2},{6,4},{8,6},{10,8},{12,10},{14,12},{16,14},{18,16},{20... | collective-permute-start | bytes 1966088 | tf_op jit(solution)/shard_map/ppermute | solution.py:23
  116.5 5.0 %collective-permute-start.20 = (f32[2,16,128]{2,1,0:T(8,128)S(1)}, f32[2,16,128]{2,1,0:T(8,128)S(1)}, u32[]{:S(2)}, u32[]{:S(2)}) collective-permute-start(f32[2,16,128]{2,1,0:T(8,128)S(1)} %get-tuple-element.54.st0_ref), channel_id=1, source_target_pairs={{2,0},{4,2},{6,4},{8,6},{10,8},{12,10},{14,12},{16,14},{18,16},{20... | collective-permute-start | bytes 49160 | tf_op jit(solution)/shard_map/ppermute | solution.py:23
  119.4 5.6 %collective-permute-start.21 = (f32[2,16,128]{2,1,0:T(8,128)S(1)}, f32[2,16,128]{2,1,0:T(8,128)S(1)}, u32[]{:S(2)}, u32[]{:S(2)}) collective-permute-start(f32[2,16,128]{2,1,0:T(8,128)S(1)} %get-tuple-element.54.st0_ref), channel_id=1, source_target_pairs={{4,0},{6,2},{8,4},{10,6},{12,8},{14,10},{16,12},{18,14},{20,16},{2... | collective-permute-start | bytes 49160 | tf_op jit(solution)/shard_map/ppermute | solution.py:23

commit v15 on v14

--- a/solution.py
+++ b/solution.py
@@ -210,7 +210,7 @@
         a_ref[y ^ (i // n_z), source ^ (source >> 1)] = ref[...]
     for (m, first), piece in zip(layout, pieces):
         for k in range(piece.shape[0]):
-            w_ref[z ^ (first + k), p ^ m] = piece[k]
+            w_ref[z ^ (n_z - 1 - first - k), p ^ m] = piece[k]
     half = n_z // 2
     proj = sum(
         jnp.dot(
@@ -342,7 +342,7 @@
     if n_p == 4 and capacity % ROW_TILE == 0 and w_rows % ROW_TILE == 0:
         blocks = [column_block(w_kv, z ^ mask) for mask in range(n_z)]
         own = jnp.stack(
-            [blocks[0]] + [swapped(blocks[mask], "z", mask) for mask in range(1, n_z)], 0
+            [swapped(blocks[mask], "z", mask) for mask in range(n_z - 1, 0, -1)] + [blocks[0]], 0
         )
         other0 = swapped(cache, "head", 1)
         own, other0, cache = lax.optimization_barrier((own, other0, cache))

time: 129 us -> 127 us (0.984)
    ppermute x3, starting transfers between devices: 12.4 us -> 2.51 us  [ring_step(): lax.ppermute(value, 'z', [(b, a) for a, b in pairs] if back else pairs)]
    ppermute x6, starting transfers between devices: 15 us -> 20.4 us  [shifted(): return lax.ppermute(value, SEQ, pairs)]
    ppermute x13, starting transfers between devices: 10.7 us -> 14.3 us  [swapped(): lax.ppermute(value, axis, [(i, i ^ mask) for i in range(lax.axis_size(axi...]
    dynamic_slice x1 -> x0, local copies, waits for them, and re-layouts: 1.42 us -> none  [column_block(): return lax.dynamic_slice(w_kv, start, (1, w_rows, half))[0]]
    squeeze x0 -> x1, local copies, waits for them, and re-layouts: none -> 1.42 us  [column_block(): return lax.dynamic_slice(w_kv, start, (1, w_rows, half))[0]]
  transfers between devices with their start and end apart: 23 -> 23, of which waited for: 12 -> 13; matrix products, arithmetic and copies ran while one was open for 0% -> 0% of each run, Pallas kernels for 8% -> 8%
where the time goes in v15:
time: 127 us; the launch traced here: 126 us
  waiting for transfers between devices  64.7 us (51%)
  starting transfers between devices  44.6 us (35%)
  Pallas kernels  13.4 us (11%)
  local copies, waits for them, and re-layouts  2.37 us (2%)
    all_to_all x1, waiting for transfers between devices, body(): memory = lax.all_to_all(slots, SEQ, split_axis=0, concat_axis=0, tiled=True)  27.7 us
    ppermute x13, waiting for transfers between devices, swapped(): lax.ppermute(value, axis, [(i, i ^ mask) for i in range(lax.axis_size(axi...  22.2 us
    ppermute x6, starting transfers between devices, shifted(): return lax.ppermute(value, SEQ, pairs)  20.4 us
    ppermute x13, starting transfers between devices, swapped(): lax.ppermute(value, axis, [(i, i ^ mask) for i in range(lax.axis_size(axi...  14.3 us
    ppermute x3, waiting for transfers between devices, ring_step(): lax.ppermute(value, 'z', [(b, a) for a, b in pairs] if back else pairs)  11.2 us
    all_to_all x1, starting transfers between devices, body(): memory = lax.all_to_all(slots, SEQ, split_axis=0, concat_axis=0, tiled=True)  7.31 us
    pallas_call x1, Pallas kernels, attend(): pl.pallas_call(attend_kernel, grid=(steps,), in_specs=[whole, whole, whol...  5.03 us
    pallas_call x1, Pallas kernels, project(): pl.pallas_call(functools.partial(project_kernel, layout), in_specs=[whole...  4.6 us
  transfers between devices with their start and end apart: 23, of which 13 were waited for; matrix products, arithmetic and copies ran while one was open for 0% of the time, Pallas kernels for 8%

profile of v15, /device:TPU:16, one launch (start us, length us, event | category | flops | bytes accessed | tf_op | source)
XLA Modules:
  0.0 126.1 jit_solution(3469469541142850860)
XLA Ops:
  0.6 0.0 copy-start.4
  0.7 0.0 copy-start
  0.7 0.0 copy-start.1
  0.7 0.0 copy-start.2
  0.7 1.4 %dynamic-slice_bitcast_fusion.2 = (bf16[160,640]{1,0:T(8,128)(2,1)S(1)}, bf16[160,640]{1,0:T(8,128)(2,1)S(1)}, bf16[1,160,640]{2,1,0:T(8,128)(2,1)S(1)}, bf16[160,640]{1,0:T(8,128)(2,1)S(1)}) fusion(bf16[2,160,1280]{2,1,0:T(8,128)(2,1)} %param.13, s32[]{:T(128)S(6)} %select_n.24, s32[]{:T(128)S(6)} %select_n.25, s32[]{:T(128)S(6)} %select_n.26, ...), kind=kLoop, calls=%fused_computation.5 | loop fusion | bytes 1638432 | tf_op jit(solution)/shard_map/squeeze | solution.py:328
  2.1 1.6 %collective-permute-start.2 = (bf16[160,640]{1,0:T(8,128)(2,1)S(1)}, bf16[160,640]{1,0:T(8,128)(2,1)S(1)}, u32[]{:S(2)}, u32[]{:S(2)}) collective-permute-start(bf16[160,640]{1,0:T(8,128)(2,1)S(1)} %get-tuple-element.65), channel_id=1, source_target_pairs={{0,8},{8,0},{16,24},{24,16},{1,9},{9,1},{17,25},{25,17},{2,10},{10... | collective-permute-start | bytes 614408 | tf_op jit(solution)/shard_map/ppermute | solution.py:27
  3.8 0.3 collective-permute-start.1
  4.1 1.6 %collective-permute-start = (bf16[160,640]{1,0:T(8,128)(2,1)S(1)}, bf16[160,640]{1,0:T(8,128)(2,1)S(1)}, u32[]{:S(2)}, u32[]{:S(2)}) collective-permute-start(bf16[160,640]{1,0:T(8,128)(2,1)S(1)} %get-tuple-element.62), channel_id=1, source_target_pairs={{0,24},{8,16},{16,8},{24,0},{1,25},{9,17},{17,9},{25,1},{2,26},{10... | collective-permute-start | bytes 614408 | tf_op jit(solution)/shard_map/ppermute | solution.py:27
  5.7 1.5 %collective-permute-start.3 = (bf16[128,1280]{1,0:T(8,128)(2,1)S(1)}, bf16[128,1280]{1,0:T(8,128)(2,1)S(1)}, u32[]{:S(2)}, u32[]{:S(2)}) collective-permute-start(bf16[128,1280]{1,0:T(8,128)(2,1)S(1)} %copy-done.4), channel_id=1, source_target_pairs={{0,1},{1,0},{2,3},{3,2},{4,5},{5,4},{6,7},{7,6},{8,9},{9,8},{10,11... | collective-permute-start | bytes 983048 | tf_op jit(solution)/shard_map/ppermute | solution.py:27
  7.2 4.0 %collective-permute-done.2 = bf16[160,640]{1,0:T(8,128)(2,1)S(1)} collective-permute-done((bf16[160,640]{1,0:T(8,128)(2,1)S(1)}, bf16[160,640]{1,0:T(8,128)(2,1)S(1)}, u32[]{:S(2)}, u32[]{:S(2)}) %collective-permute-start.2) | collective-permute-done | bytes 204832 | tf_op jit(solution)/shard_map/ppermute | solution.py:27
  11.2 7.2 %collective-permute-done.1 = bf16[160,640]{1,0:T(8,128)(2,1)S(1)} collective-permute-done((bf16[160,640]{1,0:T(8,128)(2,1)S(1)}, bf16[160,640]{1,0:T(8,128)(2,1)S(1)}, u32[]{:S(2)}, u32[]{:S(2)}) %collective-permute-start.1) | collective-permute-done | bytes 204832 | tf_op jit(solution)/shard_map/ppermute | solution.py:27
  18.4 5.0 %collective-permute-done = bf16[160,640]{1,0:T(8,128)(2,1)S(1)} collective-permute-done((bf16[160,640]{1,0:T(8,128)(2,1)S(1)}, bf16[160,640]{1,0:T(8,128)(2,1)S(1)}, u32[]{:S(2)}, u32[]{:S(2)}) %collective-permute-start) | collective-permute-done | bytes 204832 | tf_op jit(solution)/shard_map/ppermute | solution.py:27
  23.4 0.1 pad_maximum_fusion.refs_8_
  23.5 0.0 collective-permute-done.3.refs_4_
  23.5 0.1 collective-permute-start.4
  23.6 0.1 collective-permute-start.7
  23.7 2.0 %collective-permute-start.6 = (bf16[128,1280]{1,0:T(8,128)(2,1)S(1)}, bf16[128,1280]{1,0:T(8,128)(2,1)S(1)}, u32[]{:S(2)}, u32[]{:S(2)}) collective-permute-start(bf16[128,1280]{1,0:T(8,128)(2,1)S(1)} %copy-done.4), channel_id=1, source_target_pairs={{8,0},{24,8},{16,24},{0,16},{9,1},{25,9},{17,25},{1,17},{10,2},{26... | collective-permute-start | bytes 983048 | tf_op jit(solution)/shard_map/ppermute | solution.py:333
  25.7 1.5 %collective-permute-start.11 = (bf16[4,160,640]{2,1,0:T(8,128)(2,1)S(1)}, bf16[4,160,640]{2,1,0:T(8,128)(2,1)S(1)}, u32[]{:S(2)}, u32[]{:S(2)}) collective-permute-start(bf16[4,160,640]{2,1,0:T(8,128)(2,1)S(1)} %pad_maximum_fusion.refs_8_), channel_id=1, source_target_pairs={{0,4},{2,6},{4,0},{6,2},{1,5},{3,7},{5,1},{7,3},{8,12},{10,14},{12... | collective-permute-start | bytes 2457608 | tf_op jit(solution)/shard_map/ppermute | solution.py:27
  27.2 0.0 copy-done.2
  27.2 0.1 pad_maximum_fusion.1
  27.3 0.0 copy-start.6
  27.3 0.0 copy-start.7
  27.4 6.8 %collective-permute-done.7.refs_1_ = bf16[128,1280]{1,0:T(8,128)(2,1)S(1)} collective-permute-done((bf16[128,1280]{1,0:T(8,128)(2,1)S(1)}, bf16[128,1280]{1,0:T(8,128)(2,1)S(1)}, u32[]{:S(2)}, u32[]{:S(2)}) %collective-permute-start.7) | collective-permute-done | bytes 327712 | tf_op jit(solution)/shard_map/ppermute | solution.py:333
  34.2 1.5 %collective-permute-start.8 = (bf16[128,1280]{1,0:T(8,128)(2,1)S(1)}, bf16[128,1280]{1,0:T(8,128)(2,1)S(1)}, u32[]{:S(2)}, u32[]{:S(2)}) collective-permute-start(bf16[128,1280]{1,0:T(8,128)(2,1)S(1)} %collective-permute-done.7.refs_1_), channel_id=1, source_target_pairs={{0,1},{1,0},{2,3},{3,2},{4,5},{5,4},{6,7},{7,6},{8,9},{9,8},{10,11... | collective-permute-start | bytes 983048 | tf_op jit(solution)/shard_map/ppermute | solution.py:27
  35.7 0.0 collective-permute-done.4.refs_9_
  35.7 1.9 %collective-permute-start.5 = (bf16[2,128,1280]{2,1,0:T(8,128)(2,1)S(1)}, bf16[2,128,1280]{2,1,0:T(8,128)(2,1)S(1)}, u32[]{:S(2)}, u32[]{:S(2)}) collective-permute-start(bf16[2,128,1280]{2,1,0:T(8,128)(2,1)S(1)} %get-tuple-element.32), channel_id=1, source_target_pairs={{0,2},{2,4},{4,6},{6,8},{8,10},{10,12},{12,14},{14,16},{16,18},{18... | collective-permute-start | bytes 1966088 | tf_op jit(solution)/shard_map/ppermute | solution.py:23
  37.6 0.4 collective-permute-start.10
  38.1 2.6 %collective-permute-done.6.refs_3_ = bf16[128,1280]{1,0:T(8,128)(2,1)S(1)} collective-permute-done((bf16[128,1280]{1,0:T(8,128)(2,1)S(1)}, bf16[128,1280]{1,0:T(8,128)(2,1)S(1)}, u32[]{:S(2)}, u32[]{:S(2)}) %collective-permute-start.6) | collective-permute-done | bytes 327712 | tf_op jit(solution)/shard_map/ppermute | solution.py:333
  40.7 3.6 %collective-permute-start.13 = (bf16[2,128,1280]{2,1,0:T(8,128)(2,1)S(1)}, bf16[2,128,1280]{2,1,0:T(8,128)(2,1)}, u32[]{:S(2)}, u32[]{:S(2)}) collective-permute-start(bf16[2,128,1280]{2,1,0:T(8,128)(2,1)S(1)} %get-tuple-element.40), channel_id=1, source_target_pairs={{2,0},{4,2},{6,4},{8,6},{10,8},{12,10},{14,12},{16,14},{18,16},{20... | collective-permute-start | bytes 1966088 | tf_op jit(solution)/shard_map/ppermute | solution.py:23
  44.3 0.0 collective-permute-done.8.refs_5_
  44.3 1.6 %collective-permute-start.9 = (bf16[128,1280]{1,0:T(8,128)(2,1)S(1)}, bf16[128,1280]{1,0:T(8,128)(2,1)S(1)}, u32[]{:S(2)}, u32[]{:S(2)}) collective-permute-start(bf16[128,1280]{1,0:T(8,128)(2,1)S(1)} %collective-permute-done.6.refs_3_), channel_id=1, source_target_pairs={{0,1},{1,0},{2,3},{3,2},{4,5},{5,4},{6,7},{7,6},{8,9},{9,8},{10,11... | collective-permute-start | bytes 983048 | tf_op jit(solution)/shard_map/ppermute | solution.py:27
  45.9 1.8 %collective-permute-done.10.refs_2_ = bf16[128,1280]{1,0:T(8,128)(2,1)S(1)} collective-permute-done((bf16[128,1280]{1,0:T(8,128)(2,1)S(1)}, bf16[128,1280]{1,0:T(8,128)(2,1)S(1)}, u32[]{:S(2)}, u32[]{:S(2)}) %collective-permute-start.10) | collective-permute-done | bytes 327712 | tf_op jit(solution)/shard_map/ppermute | solution.py:333
  47.7 1.5 %collective-permute-start.12 = (bf16[128,1280]{1,0:T(8,128)(2,1)S(1)}, bf16[128,1280]{1,0:T(8,128)(2,1)S(1)}, u32[]{:S(2)}, u32[]{:S(2)}) collective-permute-start(bf16[128,1280]{1,0:T(8,128)(2,1)S(1)} %collective-permute-done.10.refs_2_), channel_id=1, source_target_pairs={{0,1},{1,0},{2,3},{3,2},{4,5},{5,4},{6,7},{7,6},{8,9},{9,8},{10,11... | collective-permute-start | bytes 983048 | tf_op jit(solution)/shard_map/ppermute | solution.py:27
  49.2 4.8 %collective-permute-done.9.refs_7_ = bf16[128,1280]{1,0:T(8,128)(2,1)S(1)} collective-permute-done((bf16[128,1280]{1,0:T(8,128)(2,1)S(1)}, bf16[128,1280]{1,0:T(8,128)(2,1)S(1)}, u32[]{:S(2)}, u32[]{:S(2)}) %collective-permute-start.9) | collective-permute-done | bytes 327712 | tf_op jit(solution)/shard_map/ppermute | solution.py:27
  54.0 0.0 collective-permute-done.5.kv1_ref
  54.0 6.8 %collective-permute-start.18 = (bf16[2,128,1280]{2,1,0:T(8,128)(2,1)S(1)}, bf16[2,128,1280]{2,1,0:T(8,128)(2,1)S(1)}, u32[]{:S(2)}, u32[]{:S(2)}) collective-permute-start(bf16[2,128,1280]{2,1,0:T(8,128)(2,1)S(1)} %collective-permute-done.5.kv1_ref), channel_id=1, source_target_pairs={{0,2},{2,4},{4,6},{6,8},{8,10},{10,12},{12,14},{14,16},{16,18},{18... | collective-permute-start | bytes 1966088 | tf_op jit(solution)/shard_map/ppermute | solution.py:23
  60.8 0.0 collective-permute-done.11.refs_10_
  60.8 0.1 fusion
  60.9 0.0 collective-permute-done.12.refs_6_
  60.9 0.0 collective-permute-done.13.qg1_ref
  60.9 2.5 %collective-permute-start.14 = (bf16[1,160,640]{2,1,0:T(8,128)(2,1)S(1)}, bf16[1,160,640]{2,1,0:T(8,128)(2,1)S(1)}, u32[]{:S(2)}, u32[]{:S(2)}) collective-permute-start(bf16[1,160,640]{2,1,0:T(8,128)(2,1)S(1)} %get-tuple-element.44), channel_id=1, source_target_pairs={{0,2},{2,0},{4,6},{6,4},{1,3},{3,1},{5,7},{7,5},{8,10},{10,8},{12,... | collective-permute-start | bytes 614408 | tf_op jit(solution)/shard_map/ppermute | solution.py:27
  63.5 0.1 collective-permute-start.15
  63.5 0.4 collective-permute-start.16
  64.0 0.1 collective-permute-start.17
  64.1 0.2 prepare.1
  64.3 0.2 collective-permute-done.14.refs_11_
  64.6 0.4 collective-permute-done.15.refs_12_
  64.9 0.3 collective-permute-done.16.refs_13_
  65.2 0.3 collective-permute-done.17.refs_14_
  65.5 4.6 %project.1 = bf16[16,4,16,640]{3,2,1,0:T(8,128)(2,1)} custom-call(s32[4,1,128]{2,1,0:T(1,128)S(1)} %get-tuple-element.36.place_ref, bf16[128,1280]{1,0:T(8,128)(2,1)S(1)} %copy-done.4, bf16[128,1280]{1,0:T(8,128)(2,1)S(1)} %collective-permute-done.7.refs_1_, bf16[128,1280]{1,0:T(8,128)(2,1)S(1)} %collective-permute-done.10.refs_2_, ...), custom_call_target="tpu_custom_call" | custom-call | flops 1677721600 | bytes 1048576 | tf_op jit(solution)/shard_map/project/pallas_call | solution.py:241
  70.1 0.0 copy-done.5
  70.1 0.0 collective-permute-done.18.kv2_ref
  70.1 0.0 copy-start.9
  70.1 0.8 copy-done.9
  71.0 7.3 %all-to-all-start = ((bf16[16,4,16,640]{3,2,1,0:T(8,128)(2,1)}), bf16[16,4,16,640]{3,2,1,0:T(8,128)(2,1)S(1)}, u32[]{:S(2)}, u32[]{:S(2)}) async-start(bf16[16,4,16,640]{3,2,1,0:T(8,128)(2,1)} %project.1), calls=%async_computation | async-start | bytes 2621440 | tf_op jit(solution)/shard_map/all_to_all | solution.py:413
  78.3 3.1 %collective-permute-start.19 = (bf16[2,128,1280]{2,1,0:T(8,128)(2,1)}, bf16[2,128,1280]{2,1,0:T(8,128)(2,1)S(1)}, u32[]{:S(2)}, u32[]{:S(2)}) collective-permute-start(bf16[2,128,1280]{2,1,0:T(8,128)(2,1)} %collective-permute-done.13.qg1_ref), channel_id=1, source_target_pairs={{2,0},{4,2},{6,4},{8,6},{10,8},{12,10},{14,12},{16,14},{18,16},{20... | collective-permute-start | bytes 1966088 | tf_op jit(solution)/shard_map/ppermute | solution.py:23
  81.4 27.7 %all-to-all-done = bf16[16,4,16,640]{3,2,1,0:T(8,128)(2,1)S(1)} async-done(((bf16[16,4,16,640]{3,2,1,0:T(8,128)(2,1)}), bf16[16,4,16,640]{3,2,1,0:T(8,128)(2,1)S(1)}, u32[]{:S(2)}, u32[]{:S(2)}) %all-to-all-start) | async-done | bytes 1310752 | tf_op jit(solution)/shard_map/all_to_all | solution.py:413
  109.1 5.0 %attend.1 = (bf16[128,1280]{1,0:T(8,128)(2,1)}, bf16[128,1280]{1,0:T(8,128)(2,1)}, f32[2,16,128]{2,1,0:T(8,128)S(1)}) custom-call(bf16[128,1280]{1,0:T(8,128)(2,1)S(1)} %copy-done, bf16[128,1280]{1,0:T(8,128)(2,1)S(1)} %copy-done.1, bf16[128,1280]{1,0:T(8,128)(2,1)S(1)} %copy-done.2, bf16[128,1280]{1,0:T(8,128)(2,1)S(1)} %copy-done.3, ...), custom_call_target="tpu_custom_call" | custom-call | flops 838860800 | bytes 6291456 | tf_op jit(solution)/shard_map/attend/pallas_call | solution.py:106
  114.1 2.9 %collective-permute-start.20 = (f32[2,16,128]{2,1,0:T(8,128)S(1)}, f32[2,16,128]{2,1,0:T(8,128)S(1)}, u32[]{:S(2)}, u32[]{:S(2)}) collective-permute-start(f32[2,16,128]{2,1,0:T(8,128)S(1)} %get-tuple-element.54.st0_ref), channel_id=1, source_target_pairs={{2,0},{4,2},{6,4},{8,6},{10,8},{12,10},{14,12},{16,14},{18,16},{20... | collective-permute-start | bytes 49160 | tf_op jit(solution)/shard_map/ppermute | solution.py:23
  117.0 2.1 %collective-permute-start.21 = (f32[2,16,128]{2,1,0:T(8,128)S(1)}, f32[2,16,128]{2,1,0:T(8,128)S(1)}, u32[]{:S(2)}, u32[]{:S(2)}) collective-permute-start(f32[2,16,128]{2,1,0:T(8,128)S(1)} %get-tuple-element.54.st0_ref), channel_id=1, source_target_pairs={{4,0},{6,2},{8,4},{10,6},{12,8},{14,10},{16,12},{18,14},{20,16},{2... | collective-permute-start | bytes 49160 | tf_op jit(solution)/shard_map/ppermute | solution.py:23
  119.1 0.0 collective-permute-done.19.qg2_ref
  119.1 0.0 collective-permute-done.20.st1_ref
  119.1 3.5 %collective-permute-done.21.st2_ref = f32[2,16,128]{2,1,0:T(8,128)S(1)} collective-permute-done((f32[2,16,128]{2,1,0:T(8,128)S(1)}, f32[2,16,128]{2,1,0:T(8,128)S(1)}, u32[]{:S(2)}, u32[]{:S(2)}) %collective-permute-start.21) | collective-permute-done | bytes 16416 | tf_op jit(solution)/shard_map/ppermute | solution.py:23
  122.6 3.5 %key_grads.1 = (bf16[128,1280]{1,0:T(8,128)(2,1)}, bf16[128,1280]{1,0:T(8,128)(2,1)}) custom-call(bf16[128,1280]{1,0:T(8,128)(2,1)S(1)} %copy-done.2, bf16[128,1280]{1,0:T(8,128)(2,1)S(1)} %copy-done.3, bf16[128,1280]{1,0:T(8,128)(2,1)S(1)} %copy-done, bf16[128,1280]{1,0:T(8,128)(2,1)S(1)} %copy-done.1, ...), custom_call_target="tpu_custom_call" | custom-call | flops 503316480 | bytes 4194304 | tf_op jit(solution)/shard_map/key_grads/pallas_call | solution.py:175
  (10 shorter events, 0.0 us)
Async XLA Ops:
  0.6 5.1 %copy-start.4 = (bf16[128,1280]{1,0:T(8,128)(2,1)S(1)}, bf16[128,1280]{1,0:T(8,128)(2,1)}, u32[]{:S(2)}) copy-start(bf16[128,1280]{1,0:T(8,128)(2,1)} %refs_0_) | copy-start | bytes 983044
  0.7 26.5 %copy-start = (bf16[128,1280]{1,0:T(8,128)(2,1)S(1)}, bf16[128,1280]{1,0:T(8,128)(2,1)}, u32[]{:S(2)}) copy-start(bf16[128,1280]{1,0:T(8,128)(2,1)} %q_ref.3) | copy-start | bytes 983044
  0.7 26.5 %copy-start.1 = (bf16[128,1280]{1,0:T(8,128)(2,1)S(1)}, bf16[128,1280]{1,0:T(8,128)(2,1)}, u32[]{:S(2)}) copy-start(bf16[128,1280]{1,0:T(8,128)(2,1)} %g_ref.3) | copy-start | bytes 983044
  0.7 26.5 %copy-start.2 = (bf16[128,1280]{1,0:T(8,128)(2,1)S(1)}, bf16[128,1280]{1,0:T(8,128)(2,1)}, u32[]{:S(2)}) copy-start(bf16[128,1280]{1,0:T(8,128)(2,1)} %k_ref.3) | copy-start | bytes 983044
  0.7 26.5 %copy-start.3 = (bf16[128,1280]{1,0:T(8,128)(2,1)S(1)}, bf16[128,1280]{1,0:T(8,128)(2,1)}, u32[]{:S(2)}) copy-start(bf16[128,1280]{1,0:T(8,128)(2,1)} %v_ref.3) | copy-start | bytes 983044
  2.1 9.0 %collective-permute-start.2 = (bf16[160,640]{1,0:T(8,128)(2,1)S(1)}, bf16[160,640]{1,0:T(8,128)(2,1)S(1)}, u32[]{:S(2)}, u32[]{:S(2)}) collective-permute-start(bf16[160,640]{1,0:T(8,128)(2,1)S(1)} %get-tuple-element.65), channel_id=1, source_target_pairs={{0,8},{8,0},{16,24},{24,16},{1,9},{9,1},{17,25},{25,17},{2,10},{10... | collective-permute-start | bytes 614408 | tf_op jit(solution)/shard_map/ppermute | solution.py:27
  3.8 14.6 %collective-permute-start.1 = (bf16[160,640]{1,0:T(8,128)(2,1)S(1)}, bf16[160,640]{1,0:T(8,128)(2,1)S(1)}, u32[]{:S(2)}, u32[]{:S(2)}) collective-permute-start(bf16[160,640]{1,0:T(8,128)(2,1)S(1)} %get-tuple-element.63), channel_id=1, source_target_pairs={{0,16},{8,24},{16,0},{24,8},{1,17},{9,25},{17,1},{25,9},{2,18},{10... | collective-permute-start | bytes 614408 | tf_op jit(solution)/shard_map/ppermute | solution.py:27
  4.1 19.3 %collective-permute-start = (bf16[160,640]{1,0:T(8,128)(2,1)S(1)}, bf16[160,640]{1,0:T(8,128)(2,1)S(1)}, u32[]{:S(2)}, u32[]{:S(2)}) collective-permute-start(bf16[160,640]{1,0:T(8,128)(2,1)S(1)} %get-tuple-element.62), channel_id=1, source_target_pairs={{0,24},{8,16},{16,8},{24,0},{1,25},{9,17},{17,9},{25,1},{2,26},{10... | collective-permute-start | bytes 614408 | tf_op jit(solution)/shard_map/ppermute | solution.py:27
  5.7 17.8 %collective-permute-start.3 = (bf16[128,1280]{1,0:T(8,128)(2,1)S(1)}, bf16[128,1280]{1,0:T(8,128)(2,1)S(1)}, u32[]{:S(2)}, u32[]{:S(2)}) collective-permute-start(bf16[128,1280]{1,0:T(8,128)(2,1)S(1)} %copy-done.4), channel_id=1, source_target_pairs={{0,1},{1,0},{2,3},{3,2},{4,5},{5,4},{6,7},{7,6},{8,9},{9,8},{10,11... | collective-permute-start | bytes 983048 | tf_op jit(solution)/shard_map/ppermute | solution.py:27
  23.5 12.2 %collective-permute-start.4 = (bf16[4,160,640]{2,1,0:T(8,128)(2,1)S(1)}, bf16[4,160,640]{2,1,0:T(8,128)(2,1)S(1)}, u32[]{:S(2)}, u32[]{:S(2)}) collective-permute-start(bf16[4,160,640]{2,1,0:T(8,128)(2,1)S(1)} %pad_maximum_fusion.refs_8_), channel_id=1, source_target_pairs={{0,2},{2,0},{4,6},{6,4},{1,3},{3,1},{5,7},{7,5},{8,10},{10,8},{12,... | collective-permute-start | bytes 2457608 | tf_op jit(solution)/shard_map/ppermute | solution.py:27
  23.6 10.6 %collective-permute-start.7 = (bf16[128,1280]{1,0:T(8,128)(2,1)S(1)}, bf16[128,1280]{1,0:T(8,128)(2,1)S(1)}, u32[]{:S(2)}, u32[]{:S(2)}) collective-permute-start(bf16[128,1280]{1,0:T(8,128)(2,1)S(1)} %copy-done.4), channel_id=1, source_target_pairs={{0,8},{8,24},{24,16},{16,0},{1,9},{9,25},{25,17},{17,1},{2,10},{10... | collective-permute-start | bytes 983048 | tf_op jit(solution)/shard_map/ppermute | solution.py:333
  23.7 17.0 %collective-permute-start.6 = (bf16[128,1280]{1,0:T(8,128)(2,1)S(1)}, bf16[128,1280]{1,0:T(8,128)(2,1)S(1)}, u32[]{:S(2)}, u32[]{:S(2)}) collective-permute-start(bf16[128,1280]{1,0:T(8,128)(2,1)S(1)} %copy-done.4), channel_id=1, source_target_pairs={{8,0},{24,8},{16,24},{0,16},{9,1},{25,9},{17,25},{1,17},{10,2},{26... | collective-permute-start | bytes 983048 | tf_op jit(solution)/shard_map/ppermute | solution.py:333
  25.7 35.1 %collective-permute-start.11 = (bf16[4,160,640]{2,1,0:T(8,128)(2,1)S(1)}, bf16[4,160,640]{2,1,0:T(8,128)(2,1)S(1)}, u32[]{:S(2)}, u32[]{:S(2)}) collective-permute-start(bf16[4,160,640]{2,1,0:T(8,128)(2,1)S(1)} %pad_maximum_fusion.refs_8_), channel_id=1, source_target_pairs={{0,4},{2,6},{4,0},{6,2},{1,5},{3,7},{5,1},{7,3},{8,12},{10,14},{12... | collective-permute-start | bytes 2457608 | tf_op jit(solution)/shard_map/ppermute | solution.py:27
  27.3 36.7 %copy-start.6 = (s32[2048]{0:T(1024)S(1)}, s32[2048]{0:T(1024)}, u32[]{:S(2)}) copy-start(s32[2048]{0:T(1024)} %param.15) | copy-start | bytes 24580
  27.3 36.7 %copy-start.7 = (s32[2048]{0:T(1024)S(1)}, s32[2048]{0:T(1024)}, u32[]{:S(2)}) copy-start(s32[2048]{0:T(1024)} %param.14) | copy-start | bytes 24580
  34.2 10.1 %collective-permute-start.8 = (bf16[128,1280]{1,0:T(8,128)(2,1)S(1)}, bf16[128,1280]{1,0:T(8,128)(2,1)S(1)}, u32[]{:S(2)}, u32[]{:S(2)}) collective-permute-start(bf16[128,1280]{1,0:T(8,128)(2,1)S(1)} %collective-permute-done.7.refs_1_), channel_id=1, source_target_pairs={{0,1},{1,0},{2,3},{3,2},{4,5},{5,4},{6,7},{7,6},{8,9},{9,8},{10,11... | collective-permute-start | bytes 983048 | tf_op jit(solution)/shard_map/ppermute | solution.py:27
  35.7 18.3 %collective-permute-start.5 = (bf16[2,128,1280]{2,1,0:T(8,128)(2,1)S(1)}, bf16[2,128,1280]{2,1,0:T(8,128)(2,1)S(1)}, u32[]{:S(2)}, u32[]{:S(2)}) collective-permute-start(bf16[2,128,1280]{2,1,0:T(8,128)(2,1)S(1)} %get-tuple-element.32), channel_id=1, source_target_pairs={{0,2},{2,4},{4,6},{6,8},{8,10},{10,12},{12,14},{14,16},{16,18},{18... | collective-permute-start | bytes 1966088 | tf_op jit(solution)/shard_map/ppermute | solution.py:23
  37.6 10.1 %collective-permute-start.10 = (bf16[128,1280]{1,0:T(8,128)(2,1)S(1)}, bf16[128,1280]{1,0:T(8,128)(2,1)S(1)}, u32[]{:S(2)}, u32[]{:S(2)}) collective-permute-start(bf16[128,1280]{1,0:T(8,128)(2,1)S(1)} %collective-permute-done.7.refs_1_), channel_id=1, source_target_pairs={{0,8},{8,24},{24,16},{16,0},{1,9},{9,25},{25,17},{17,1},{2,10},{10... | collective-permute-start | bytes 983048 | tf_op jit(solution)/shard_map/ppermute | solution.py:333
  40.7 20.3 %collective-permute-start.13 = (bf16[2,128,1280]{2,1,0:T(8,128)(2,1)S(1)}, bf16[2,128,1280]{2,1,0:T(8,128)(2,1)}, u32[]{:S(2)}, u32[]{:S(2)}) collective-permute-start(bf16[2,128,1280]{2,1,0:T(8,128)(2,1)S(1)} %get-tuple-element.40), channel_id=1, source_target_pairs={{2,0},{4,2},{6,4},{8,6},{10,8},{12,10},{14,12},{16,14},{18,16},{20... | collective-permute-start | bytes 1966088 | tf_op jit(solution)/shard_map/ppermute | solution.py:23
  44.3 9.7 %collective-permute-start.9 = (bf16[128,1280]{1,0:T(8,128)(2,1)S(1)}, bf16[128,1280]{1,0:T(8,128)(2,1)S(1)}, u32[]{:S(2)}, u32[]{:S(2)}) collective-permute-start(bf16[128,1280]{1,0:T(8,128)(2,1)S(1)} %collective-permute-done.6.refs_3_), channel_id=1, source_target_pairs={{0,1},{1,0},{2,3},{3,2},{4,5},{5,4},{6,7},{7,6},{8,9},{9,8},{10,11... | collective-permute-start | bytes 983048 | tf_op jit(solution)/shard_map/ppermute | solution.py:27
  47.7 13.2 %collective-permute-start.12 = (bf16[128,1280]{1,0:T(8,128)(2,1)S(1)}, bf16[128,1280]{1,0:T(8,128)(2,1)S(1)}, u32[]{:S(2)}, u32[]{:S(2)}) collective-permute-start(bf16[128,1280]{1,0:T(8,128)(2,1)S(1)} %collective-permute-done.10.refs_2_), channel_id=1, source_target_pairs={{0,1},{1,0},{2,3},{3,2},{4,5},{5,4},{6,7},{7,6},{8,9},{9,8},{10,11... | collective-permute-start | bytes 983048 | tf_op jit(solution)/shard_map/ppermute | solution.py:27
  54.0 16.1 %copy-start.8 = (bf16[2,128,1280]{2,1,0:T(8,128)(2,1)}, bf16[2,128,1280]{2,1,0:T(8,128)(2,1)S(1)}, u32[]{:S(2)}) copy-start(bf16[2,128,1280]{2,1,0:T(8,128)(2,1)S(1)} %collective-permute-done.5.kv1_ref) | copy-start | bytes 1966084
  54.0 16.1 %collective-permute-start.18 = (bf16[2,128,1280]{2,1,0:T(8,128)(2,1)S(1)}, bf16[2,128,1280]{2,1,0:T(8,128)(2,1)S(1)}, u32[]{:S(2)}, u32[]{:S(2)}) collective-permute-start(bf16[2,128,1280]{2,1,0:T(8,128)(2,1)S(1)} %collective-permute-done.5.kv1_ref), channel_id=1, source_target_pairs={{0,2},{2,4},{4,6},{6,8},{8,10},{10,12},{12,14},{14,16},{16,18},{18... | collective-permute-start | bytes 1966088 | tf_op jit(solution)/shard_map/ppermute | solution.py:23
  60.9 3.6 %collective-permute-start.14 = (bf16[1,160,640]{2,1,0:T(8,128)(2,1)S(1)}, bf16[1,160,640]{2,1,0:T(8,128)(2,1)S(1)}, u32[]{:S(2)}, u32[]{:S(2)}) collective-permute-start(bf16[1,160,640]{2,1,0:T(8,128)(2,1)S(1)} %get-tuple-element.44), channel_id=1, source_target_pairs={{0,2},{2,0},{4,6},{6,4},{1,3},{3,1},{5,7},{7,5},{8,10},{10,8},{12,... | collective-permute-start | bytes 614408 | tf_op jit(solution)/shard_map/ppermute | solution.py:27
  63.5 1.5 %collective-permute-start.15 = (bf16[1,160,640]{2,1,0:T(8,128)(2,1)S(1)}, bf16[1,160,640]{2,1,0:T(8,128)(2,1)S(1)}, u32[]{:S(2)}, u32[]{:S(2)}) collective-permute-start(bf16[1,160,640]{2,1,0:T(8,128)(2,1)S(1)} %get-tuple-element.45), channel_id=1, source_target_pairs={{0,2},{2,0},{4,6},{6,4},{1,3},{3,1},{5,7},{7,5},{8,10},{10,8},{12,... | collective-permute-start | bytes 614408 | tf_op jit(solution)/shard_map/ppermute | solution.py:27
  63.5 1.7 %collective-permute-start.16 = (bf16[1,160,640]{2,1,0:T(8,128)(2,1)S(1)}, bf16[1,160,640]{2,1,0:T(8,128)(2,1)S(1)}, u32[]{:S(2)}, u32[]{:S(2)}) collective-permute-start(bf16[1,160,640]{2,1,0:T(8,128)(2,1)S(1)} %get-tuple-element.46), channel_id=1, source_target_pairs={{0,2},{2,0},{4,6},{6,4},{1,3},{3,1},{5,7},{7,5},{8,10},{10,8},{12,... | collective-permute-start | bytes 614408 | tf_op jit(solution)/shard_map/ppermute | solution.py:27
  64.0 1.5 %collective-permute-start.17 = (bf16[1,160,640]{2,1,0:T(8,128)(2,1)S(1)}, bf16[1,160,640]{2,1,0:T(8,128)(2,1)S(1)}, u32[]{:S(2)}, u32[]{:S(2)}) collective-permute-start(bf16[1,160,640]{2,1,0:T(8,128)(2,1)S(1)} %get-tuple-element.47), channel_id=1, source_target_pairs={{0,2},{2,0},{4,6},{6,4},{1,3},{3,1},{5,7},{7,5},{8,10},{10,8},{12,... | collective-permute-start | bytes 614408 | tf_op jit(solution)/shard_map/ppermute | solution.py:27
  64.3 5.8 %copy-start.5 = (bf16[128,640]{1,0:T(8,128)(2,1)}, bf16[128,640]{1,0:T(8,128)(2,1)S(1)}, u32[]{:S(2)}) copy-start(bf16[128,640]{1,0:T(8,128)(2,1)S(1)} %get-tuple-element.50.bias_ref) | copy-start | bytes 491524
  70.1 0.8 copy-start.9
  71.0 38.1 %all-to-all-start = ((bf16[16,4,16,640]{3,2,1,0:T(8,128)(2,1)}), bf16[16,4,16,640]{3,2,1,0:T(8,128)(2,1)S(1)}, u32[]{:S(2)}, u32[]{:S(2)}) async-start(bf16[16,4,16,640]{3,2,1,0:T(8,128)(2,1)} %project.1), calls=%async_computation | async-start | bytes 2621440 | tf_op jit(solution)/shard_map/all_to_all | solution.py:413
  78.3 40.8 %collective-permute-start.19 = (bf16[2,128,1280]{2,1,0:T(8,128)(2,1)}, bf16[2,128,1280]{2,1,0:T(8,128)(2,1)S(1)}, u32[]{:S(2)}, u32[]{:S(2)}) collective-permute-start(bf16[2,128,1280]{2,1,0:T(8,128)(2,1)} %collective-permute-done.13.qg1_ref), channel_id=1, source_target_pairs={{2,0},{4,2},{6,4},{8,6},{10,8},{12,10},{14,12},{16,14},{18,16},{20... | collective-permute-start | bytes 1966088 | tf_op jit(solution)/shard_map/ppermute | solution.py:23
  114.1 5.0 %collective-permute-start.20 = (f32[2,16,128]{2,1,0:T(8,128)S(1)}, f32[2,16,128]{2,1,0:T(8,128)S(1)}, u32[]{:S(2)}, u32[]{:S(2)}) collective-permute-start(f32[2,16,128]{2,1,0:T(8,128)S(1)} %get-tuple-element.54.st0_ref), channel_id=1, source_target_pairs={{2,0},{4,2},{6,4},{8,6},{10,8},{12,10},{14,12},{16,14},{18,16},{20... | collective-permute-start | bytes 49160 | tf_op jit(solution)/shard_map/ppermute | solution.py:23
  117.0 5.6 %collective-permute-start.21 = (f32[2,16,128]{2,1,0:T(8,128)S(1)}, f32[2,16,128]{2,1,0:T(8,128)S(1)}, u32[]{:S(2)}, u32[]{:S(2)}) collective-permute-start(f32[2,16,128]{2,1,0:T(8,128)S(1)} %get-tuple-element.54.st0_ref), channel_id=1, source_target_pairs={{4,0},{6,2},{8,4},{10,6},{12,8},{14,10},{16,12},{18,14},{20,16},{2... | collective-permute-start | bytes 49160 | tf_op jit(solution)/shard_map/ppermute | solution.py:23

commit v16 on v13

--- a/solution.py
+++ b/solution.py
@@ -205,18 +205,15 @@
     place_in_ring = z ^ (z >> 1)
     for i, ref in enumerate(rows):
         source = (place_in_ring - i % n_z + n_z) & (n_z - 1)
-        a_ref[y ^ (i // n_z), source ^ (source >> 1)] = ref[...]
+        columns = pl.ds(pl.multiple_of((y ^ (i // n_z)) * depth, HD), depth)
+        a_ref[source ^ (source >> 1), :, columns] = ref[...]
     for m in range(n_p):
         for k in range(n_z):
             w_ref[z ^ k, p ^ m] = pieces[m][k]
-    half = n_z // 2
-    proj = sum(
-        jnp.dot(
-            a_ref[i].reshape(n_z * cache_rows, depth),
-            w_ref[i * half : (i + 1) * half].reshape(depth, block),
-            preferred_element_type=jnp.float32,
-        )
-        for i in range(2)
+    proj = jnp.dot(
+        a_ref[...].reshape(n_z * cache_rows, 2 * depth),
+        w_ref[...].reshape(2 * depth, block),
+        preferred_element_type=jnp.float32,
     ).astype(jnp.bfloat16)
     slot_ids = lax.broadcasted_iota(jnp.int32, (devices * capacity, cache_rows), 0)
     for z in range(n_z):
@@ -242,7 +239,7 @@
         out_shape=pltpu.VMEM((devices, n_z, capacity, block), jnp.bfloat16),
         scratch_shapes=[
             pltpu.VMEM((n_z, n_p, w_rows, block), jnp.bfloat16),
-            pltpu.VMEM((2, n_z, cache_rows, depth), jnp.bfloat16),
+            pltpu.VMEM((n_z, cache_rows, 2 * depth), jnp.bfloat16),
         ],
         compiler_params=pltpu.CompilerParams(vmem_limit_bytes=VMEM),
         cost_estimate=pl.CostEstimate(

time: 126 us -> 126 us (level)
  no operation moved by 1% of the time
where the time goes in v16:
time: 126 us; the launch traced here: 125 us
  waiting for transfers between devices  75.3 us (60%)
  starting transfers between devices  34.2 us (27%)
  Pallas kernels  13.4 us (11%)
  local copies, waits for them, and re-layouts  1.46 us (1%)
    all_to_all x1, waiting for transfers between devices, body(): memory = lax.all_to_all(slots, SEQ, split_axis=0, concat_axis=0, tiled=True)  27.7 us
    ppermute x10, waiting for transfers between devices, swapped(): lax.ppermute(value, axis, [(i, i ^ mask) for i in range(lax.axis_size(axi...  27.1 us
    ppermute x6, starting transfers between devices, shifted(): return lax.ppermute(value, SEQ, pairs)  15.6 us
    ppermute x3, waiting for transfers between devices, ring_step(): lax.ppermute(value, 'z', [(b, a) for a, b in pairs] if back else pairs)  11.4 us
    ppermute x10, starting transfers between devices, swapped(): lax.ppermute(value, axis, [(i, i ^ mask) for i in range(lax.axis_size(axi...  11.3 us
    ppermute x6, waiting for transfers between devices, shifted(): return lax.ppermute(value, SEQ, pairs)  9.14 us
    pallas_call x1, Pallas kernels, attend(): pl.pallas_call(attend_kernel, grid=(steps,), in_specs=[whole, whole, whol...  5.02 us
    pallas_call x1, Pallas kernels, project(): pl.pallas_call(project_kernel, in_specs=[whole] * (1 + len(rows) + n_p),...  4.61 us
  transfers between devices with their start and end apart: 20, of which 11 were waited for; matrix products, arithmetic and copies ran while one was open for 0% of the time, Pallas kernels for 8%

profile of v16, /device:TPU:16, one launch (start us, length us, event | category | flops | bytes accessed | tf_op | source)
XLA Modules:
  0.0 125.5 jit_solution(15878614194337187273)
XLA Ops:
  0.6 0.0 copy-start.4
  0.7 0.0 copy-start
  0.7 0.0 copy-start.1
  0.7 0.0 copy-start.2
  0.7 0.0 copy-start.3
  0.7 1.4 %constant_dynamic-slice_fusion = (bf16[1,160,640]{2,1,0:T(8,128)(2,1)S(1)}, bf16[160,640]{1,0:T(8,128)(2,1)S(1)}, bf16[160,640]{1,0:T(8,128)(2,1)S(1)}, bf16[160,640]{1,0:T(8,128)(2,1)S(1)}) fusion(bf16[2,160,1280]{2,1,0:T(8,128)(2,1)} %param.13, s32[]{:T(128)S(6)} %select_n.24, s32[]{:T(128)S(6)} %select_n.25, s32[]{:T(128)S(6)} %select_n.26, ...), kind=kLoop, calls=%fused_computation.6 | loop fusion | bytes 1638432 | tf_op jit(solution)/shard_map/dynamic_slice | solution.py:322
  2.1 1.6 %collective-permute-start = (bf16[160,640]{1,0:T(8,128)(2,1)S(1)}, bf16[160,640]{1,0:T(8,128)(2,1)S(1)}, u32[]{:S(2)}, u32[]{:S(2)}) collective-permute-start(bf16[160,640]{1,0:T(8,128)(2,1)S(1)} %get-tuple-element.51), channel_id=1, source_target_pairs={{0,8},{8,0},{16,24},{24,16},{1,9},{9,1},{17,25},{25,17},{2,10},{10... | collective-permute-start | bytes 614408 | tf_op jit(solution)/shard_map/ppermute | solution.py:25
  3.8 0.3 collective-permute-start.1
  4.1 1.6 %collective-permute-start.2 = (bf16[160,640]{1,0:T(8,128)(2,1)S(1)}, bf16[160,640]{1,0:T(8,128)(2,1)S(1)}, u32[]{:S(2)}, u32[]{:S(2)}) collective-permute-start(bf16[160,640]{1,0:T(8,128)(2,1)S(1)} %get-tuple-element.52), channel_id=1, source_target_pairs={{0,24},{8,16},{16,8},{24,0},{1,25},{9,17},{17,9},{25,1},{2,26},{10... | collective-permute-start | bytes 614408 | tf_op jit(solution)/shard_map/ppermute | solution.py:25
  5.7 0.0 copy-done.4
  5.7 1.5 %collective-permute-start.3 = (bf16[128,1280]{1,0:T(8,128)(2,1)S(1)}, bf16[128,1280]{1,0:T(8,128)(2,1)S(1)}, u32[]{:S(2)}, u32[]{:S(2)}) collective-permute-start(bf16[128,1280]{1,0:T(8,128)(2,1)S(1)} %copy-done.4), channel_id=1, source_target_pairs={{0,1},{1,0},{2,3},{3,2},{4,5},{5,4},{6,7},{7,6},{8,9},{9,8},{10,11... | collective-permute-start | bytes 983048 | tf_op jit(solution)/shard_map/ppermute | solution.py:25
  7.2 4.0 %collective-permute-done = bf16[160,640]{1,0:T(8,128)(2,1)S(1)} collective-permute-done((bf16[160,640]{1,0:T(8,128)(2,1)S(1)}, bf16[160,640]{1,0:T(8,128)(2,1)S(1)}, u32[]{:S(2)}, u32[]{:S(2)}) %collective-permute-start) | collective-permute-done | bytes 204832 | tf_op jit(solution)/shard_map/ppermute | solution.py:25
  11.2 7.2 %collective-permute-done.1 = bf16[160,640]{1,0:T(8,128)(2,1)S(1)} collective-permute-done((bf16[160,640]{1,0:T(8,128)(2,1)S(1)}, bf16[160,640]{1,0:T(8,128)(2,1)S(1)}, u32[]{:S(2)}, u32[]{:S(2)}) %collective-permute-start.1) | collective-permute-done | bytes 204832 | tf_op jit(solution)/shard_map/ppermute | solution.py:25
  18.4 5.0 %collective-permute-done.2 = bf16[160,640]{1,0:T(8,128)(2,1)S(1)} collective-permute-done((bf16[160,640]{1,0:T(8,128)(2,1)S(1)}, bf16[160,640]{1,0:T(8,128)(2,1)S(1)}, u32[]{:S(2)}, u32[]{:S(2)}) %collective-permute-start.2) | collective-permute-done | bytes 204832 | tf_op jit(solution)/shard_map/ppermute | solution.py:25
  23.4 0.1 pad_maximum_fusion.refs_8_
  23.5 0.0 collective-permute-done.3.refs_4_
  23.5 0.1 collective-permute-start.11
  23.6 0.1 collective-permute-start.5
  23.7 2.0 %collective-permute-start.8 = (bf16[128,1280]{1,0:T(8,128)(2,1)S(1)}, bf16[128,1280]{1,0:T(8,128)(2,1)S(1)}, u32[]{:S(2)}, u32[]{:S(2)}) collective-permute-start(bf16[128,1280]{1,0:T(8,128)(2,1)S(1)} %copy-done.4), channel_id=1, source_target_pairs={{8,0},{24,8},{16,24},{0,16},{9,1},{25,9},{17,25},{1,17},{10,2},{26... | collective-permute-start | bytes 983048 | tf_op jit(solution)/shard_map/ppermute | solution.py:327
  25.7 1.5 %collective-permute-start.4 = (bf16[4,160,640]{2,1,0:T(8,128)(2,1)S(1)}, bf16[4,160,640]{2,1,0:T(8,128)(2,1)S(1)}, u32[]{:S(2)}, u32[]{:S(2)}) collective-permute-start(bf16[4,160,640]{2,1,0:T(8,128)(2,1)S(1)} %pad_maximum_fusion.refs_8_), channel_id=1, source_target_pairs={{0,4},{2,6},{4,0},{6,2},{1,5},{3,7},{5,1},{7,3},{8,12},{10,14},{12... | collective-permute-start | bytes 2457608 | tf_op jit(solution)/shard_map/ppermute | solution.py:25
  27.2 0.0 copy-done
  27.2 0.0 copy-done.1
  27.2 0.0 copy-done.2
  27.2 0.0 copy-done.3
  27.2 0.0 copy-start.6
  27.2 0.0 copy-start.7
  27.2 0.1 pad_maximum_fusion.1
  27.4 6.8 %collective-permute-done.5.refs_1_ = bf16[128,1280]{1,0:T(8,128)(2,1)S(1)} collective-permute-done((bf16[128,1280]{1,0:T(8,128)(2,1)S(1)}, bf16[128,1280]{1,0:T(8,128)(2,1)S(1)}, u32[]{:S(2)}, u32[]{:S(2)}) %collective-permute-start.5) | collective-permute-done | bytes 327712 | tf_op jit(solution)/shard_map/ppermute | solution.py:327
  34.2 1.5 %collective-permute-start.9 = (bf16[128,1280]{1,0:T(8,128)(2,1)S(1)}, bf16[128,1280]{1,0:T(8,128)(2,1)S(1)}, u32[]{:S(2)}, u32[]{:S(2)}) collective-permute-start(bf16[128,1280]{1,0:T(8,128)(2,1)S(1)} %collective-permute-done.5.refs_1_), channel_id=1, source_target_pairs={{0,1},{1,0},{2,3},{3,2},{4,5},{5,4},{6,7},{7,6},{8,9},{9,8},{10,11... | collective-permute-start | bytes 983048 | tf_op jit(solution)/shard_map/ppermute | solution.py:25
  35.7 0.8 collective-permute-start.6
  36.5 0.0 collective-permute-done.11.refs_9_
  36.5 1.9 %collective-permute-start.12 = (bf16[2,128,1280]{2,1,0:T(8,128)(2,1)S(1)}, bf16[2,128,1280]{2,1,0:T(8,128)(2,1)S(1)}, u32[]{:S(2)}, u32[]{:S(2)}) collective-permute-start(bf16[2,128,1280]{2,1,0:T(8,128)(2,1)S(1)} %get-tuple-element.30), channel_id=1, source_target_pairs={{0,2},{2,4},{4,6},{6,8},{8,10},{10,12},{12,14},{14,16},{16,18},{18... | collective-permute-start | bytes 1966088 | tf_op jit(solution)/shard_map/ppermute | solution.py:21
  38.5 2.7 %collective-permute-done.8.refs_3_ = bf16[128,1280]{1,0:T(8,128)(2,1)S(1)} collective-permute-done((bf16[128,1280]{1,0:T(8,128)(2,1)S(1)}, bf16[128,1280]{1,0:T(8,128)(2,1)S(1)}, u32[]{:S(2)}, u32[]{:S(2)}) %collective-permute-start.8) | collective-permute-done | bytes 327712 | tf_op jit(solution)/shard_map/ppermute | solution.py:327
  41.1 3.2 %collective-permute-start.13 = (bf16[2,128,1280]{2,1,0:T(8,128)(2,1)S(1)}, bf16[2,128,1280]{2,1,0:T(8,128)(2,1)}, u32[]{:S(2)}, u32[]{:S(2)}) collective-permute-start(bf16[2,128,1280]{2,1,0:T(8,128)(2,1)S(1)} %get-tuple-element.31), channel_id=1, source_target_pairs={{2,0},{4,2},{6,4},{8,6},{10,8},{12,10},{14,12},{16,14},{18,16},{20... | collective-permute-start | bytes 1966088 | tf_op jit(solution)/shard_map/ppermute | solution.py:21
  44.4 0.0 collective-permute-done.9.refs_5_
  44.4 1.6 %collective-permute-start.10 = (bf16[128,1280]{1,0:T(8,128)(2,1)S(1)}, bf16[128,1280]{1,0:T(8,128)(2,1)S(1)}, u32[]{:S(2)}, u32[]{:S(2)}) collective-permute-start(bf16[128,1280]{1,0:T(8,128)(2,1)S(1)} %collective-permute-done.8.refs_3_), channel_id=1, source_target_pairs={{0,1},{1,0},{2,3},{3,2},{4,5},{5,4},{6,7},{7,6},{8,9},{9,8},{10,11... | collective-permute-start | bytes 983048 | tf_op jit(solution)/shard_map/ppermute | solution.py:25
  46.0 1.9 %collective-permute-done.6.refs_2_ = bf16[128,1280]{1,0:T(8,128)(2,1)S(1)} collective-permute-done((bf16[128,1280]{1,0:T(8,128)(2,1)S(1)}, bf16[128,1280]{1,0:T(8,128)(2,1)S(1)}, u32[]{:S(2)}, u32[]{:S(2)}) %collective-permute-start.6) | collective-permute-done | bytes 327712 | tf_op jit(solution)/shard_map/ppermute | solution.py:327
  47.8 1.5 %collective-permute-start.7 = (bf16[128,1280]{1,0:T(8,128)(2,1)S(1)}, bf16[128,1280]{1,0:T(8,128)(2,1)S(1)}, u32[]{:S(2)}, u32[]{:S(2)}) collective-permute-start(bf16[128,1280]{1,0:T(8,128)(2,1)S(1)} %collective-permute-done.6.refs_2_), channel_id=1, source_target_pairs={{0,1},{1,0},{2,3},{3,2},{4,5},{5,4},{6,7},{7,6},{8,9},{9,8},{10,11... | collective-permute-start | bytes 983048 | tf_op jit(solution)/shard_map/ppermute | solution.py:25
  49.3 0.0 collective-permute-done.4.refs_10_
  49.3 5.7 %collective-permute-done.10.refs_7_ = bf16[128,1280]{1,0:T(8,128)(2,1)S(1)} collective-permute-done((bf16[128,1280]{1,0:T(8,128)(2,1)S(1)}, bf16[128,1280]{1,0:T(8,128)(2,1)S(1)}, u32[]{:S(2)}, u32[]{:S(2)}) %collective-permute-start.10) | collective-permute-done | bytes 327712 | tf_op jit(solution)/shard_map/ppermute | solution.py:25
  55.1 5.2 %collective-permute-done.7.refs_6_ = bf16[128,1280]{1,0:T(8,128)(2,1)S(1)} collective-permute-done((bf16[128,1280]{1,0:T(8,128)(2,1)S(1)}, bf16[128,1280]{1,0:T(8,128)(2,1)S(1)}, u32[]{:S(2)}, u32[]{:S(2)}) %collective-permute-start.7) | collective-permute-done | bytes 327712 | tf_op jit(solution)/shard_map/ppermute | solution.py:25
  60.3 0.0 collective-permute-done.12.kv1_ref
  60.3 0.0 copy-start.8
  60.3 0.0 collective-permute-done.13.qg1_ref
  60.3 0.1 collective-permute-start.14
  60.4 2.4 %collective-permute-start.15 = (bf16[2,128,1280]{2,1,0:T(8,128)(2,1)S(1)}, bf16[2,128,1280]{2,1,0:T(8,128)(2,1)}, u32[]{:S(2)}, u32[]{:S(2)}) collective-permute-start(bf16[2,128,1280]{2,1,0:T(8,128)(2,1)S(1)} %collective-permute-done.12.kv1_ref), channel_id=1, source_target_pairs={{0,2},{2,4},{4,6},{6,8},{8,10},{10,12},{12,14},{14,16},{16,18},{18... | collective-permute-start | bytes 1966088 | tf_op jit(solution)/shard_map/ppermute | solution.py:21
  62.8 0.0 copy-done.6
  62.8 0.0 copy-done.7
  62.8 0.3 prepare.1
  63.0 0.0 collective-permute-done.14.refs_11_
  63.0 4.6 %project.1 = bf16[16,4,16,640]{3,2,1,0:T(8,128)(2,1)} custom-call(s32[4,1,128]{2,1,0:T(1,128)S(1)} %get-tuple-element.33.place_ref, bf16[128,1280]{1,0:T(8,128)(2,1)S(1)} %copy-done.4, bf16[128,1280]{1,0:T(8,128)(2,1)S(1)} %collective-permute-done.5.refs_1_, bf16[128,1280]{1,0:T(8,128)(2,1)S(1)} %collective-permute-done.6.refs_2_, ...), custom_call_target="tpu_custom_call" | custom-call | flops 1677721600 | bytes 8388608 | tf_op jit(solution)/shard_map/project/pallas_call | solution.py:235
  67.7 0.0 copy-done.8
  67.7 0.0 copy-done.5
  67.7 5.6 %collective-permute-done.15.kv2_ref = bf16[2,128,1280]{2,1,0:T(8,128)(2,1)} collective-permute-done((bf16[2,128,1280]{2,1,0:T(8,128)(2,1)S(1)}, bf16[2,128,1280]{2,1,0:T(8,128)(2,1)}, u32[]{:S(2)}, u32[]{:S(2)}) %collective-permute-start.15) | collective-permute-done | bytes 655392 | tf_op jit(solution)/shard_map/ppermute | solution.py:21
  73.3 4.4 %all-to-all-start = ((bf16[16,4,16,640]{3,2,1,0:T(8,128)(2,1)}), bf16[16,4,16,640]{3,2,1,0:T(8,128)(2,1)S(1)}, u32[]{:S(2)}, u32[]{:S(2)}) async-start(bf16[16,4,16,640]{3,2,1,0:T(8,128)(2,1)} %project.1), calls=%async_computation | async-start | bytes 2621440 | tf_op jit(solution)/shard_map/all_to_all | solution.py:404
  77.6 3.1 %collective-permute-start.16 = (bf16[2,128,1280]{2,1,0:T(8,128)(2,1)}, bf16[2,128,1280]{2,1,0:T(8,128)(2,1)S(1)}, u32[]{:S(2)}, u32[]{:S(2)}) collective-permute-start(bf16[2,128,1280]{2,1,0:T(8,128)(2,1)} %collective-permute-done.13.qg1_ref), channel_id=1, source_target_pairs={{2,0},{4,2},{6,4},{8,6},{10,8},{12,10},{14,12},{16,14},{18,16},{20... | collective-permute-start | bytes 1966088 | tf_op jit(solution)/shard_map/ppermute | solution.py:21
  80.7 27.7 %all-to-all-done = bf16[16,4,16,640]{3,2,1,0:T(8,128)(2,1)S(1)} async-done(((bf16[16,4,16,640]{3,2,1,0:T(8,128)(2,1)}), bf16[16,4,16,640]{3,2,1,0:T(8,128)(2,1)S(1)}, u32[]{:S(2)}, u32[]{:S(2)}) %all-to-all-start) | async-done | bytes 1310752 | tf_op jit(solution)/shard_map/all_to_all | solution.py:404
  108.4 5.0 %attend.1 = (bf16[128,1280]{1,0:T(8,128)(2,1)}, bf16[128,1280]{1,0:T(8,128)(2,1)}, f32[2,16,128]{2,1,0:T(8,128)S(1)}) custom-call(bf16[128,1280]{1,0:T(8,128)(2,1)S(1)} %copy-done, bf16[128,1280]{1,0:T(8,128)(2,1)S(1)} %copy-done.1, bf16[128,1280]{1,0:T(8,128)(2,1)S(1)} %copy-done.2, bf16[128,1280]{1,0:T(8,128)(2,1)S(1)} %copy-done.3, ...), custom_call_target="tpu_custom_call" | custom-call | flops 838860800 | bytes 6291456 | tf_op jit(solution)/shard_map/attend/pallas_call | solution.py:104
  113.4 2.9 %collective-permute-start.17 = (f32[2,16,128]{2,1,0:T(8,128)S(1)}, f32[2,16,128]{2,1,0:T(8,128)S(1)}, u32[]{:S(2)}, u32[]{:S(2)}) collective-permute-start(f32[2,16,128]{2,1,0:T(8,128)S(1)} %get-tuple-element.46.st0_ref), channel_id=1, source_target_pairs={{2,0},{4,2},{6,4},{8,6},{10,8},{12,10},{14,12},{16,14},{18,16},{20... | collective-permute-start | bytes 49160 | tf_op jit(solution)/shard_map/ppermute | solution.py:21
  116.3 2.1 %collective-permute-start.18 = (f32[2,16,128]{2,1,0:T(8,128)S(1)}, f32[2,16,128]{2,1,0:T(8,128)S(1)}, u32[]{:S(2)}, u32[]{:S(2)}) collective-permute-start(f32[2,16,128]{2,1,0:T(8,128)S(1)} %get-tuple-element.46.st0_ref), channel_id=1, source_target_pairs={{4,0},{6,2},{8,4},{10,6},{12,8},{14,10},{16,12},{18,14},{20,16},{2... | collective-permute-start | bytes 49160 | tf_op jit(solution)/shard_map/ppermute | solution.py:21
  118.4 0.0 collective-permute-done.16.qg2_ref
  118.4 0.0 collective-permute-done.17.st1_ref
  118.5 3.5 %collective-permute-done.18.st2_ref = f32[2,16,128]{2,1,0:T(8,128)S(1)} collective-permute-done((f32[2,16,128]{2,1,0:T(8,128)S(1)}, f32[2,16,128]{2,1,0:T(8,128)S(1)}, u32[]{:S(2)}, u32[]{:S(2)}) %collective-permute-start.18) | collective-permute-done | bytes 16416 | tf_op jit(solution)/shard_map/ppermute | solution.py:21
  122.0 3.5 %key_grads.1 = (bf16[128,1280]{1,0:T(8,128)(2,1)}, bf16[128,1280]{1,0:T(8,128)(2,1)}) custom-call(bf16[128,1280]{1,0:T(8,128)(2,1)S(1)} %copy-done.2, bf16[128,1280]{1,0:T(8,128)(2,1)S(1)} %copy-done.3, bf16[128,1280]{1,0:T(8,128)(2,1)S(1)} %copy-done, bf16[128,1280]{1,0:T(8,128)(2,1)S(1)} %copy-done.1, ...), custom_call_target="tpu_custom_call" | custom-call | flops 503316480 | bytes 4194304 | tf_op jit(solution)/shard_map/key_grads/pallas_call | solution.py:173
  (1 shorter events, 0.0 us)
Async XLA Ops:
  0.6 5.1 %copy-start.4 = (bf16[128,1280]{1,0:T(8,128)(2,1)S(1)}, bf16[128,1280]{1,0:T(8,128)(2,1)}, u32[]{:S(2)}) copy-start(bf16[128,1280]{1,0:T(8,128)(2,1)} %refs_0_) | copy-start | bytes 983044
  0.7 26.5 %copy-start = (bf16[128,1280]{1,0:T(8,128)(2,1)S(1)}, bf16[128,1280]{1,0:T(8,128)(2,1)}, u32[]{:S(2)}) copy-start(bf16[128,1280]{1,0:T(8,128)(2,1)} %q_ref.3) | copy-start | bytes 983044
  0.7 26.5 %copy-start.1 = (bf16[128,1280]{1,0:T(8,128)(2,1)S(1)}, bf16[128,1280]{1,0:T(8,128)(2,1)}, u32[]{:S(2)}) copy-start(bf16[128,1280]{1,0:T(8,128)(2,1)} %g_ref.3) | copy-start | bytes 983044
  0.7 26.5 %copy-start.2 = (bf16[128,1280]{1,0:T(8,128)(2,1)S(1)}, bf16[128,1280]{1,0:T(8,128)(2,1)}, u32[]{:S(2)}) copy-start(bf16[128,1280]{1,0:T(8,128)(2,1)} %k_ref.3) | copy-start | bytes 983044
  0.7 26.5 %copy-start.3 = (bf16[128,1280]{1,0:T(8,128)(2,1)S(1)}, bf16[128,1280]{1,0:T(8,128)(2,1)}, u32[]{:S(2)}) copy-start(bf16[128,1280]{1,0:T(8,128)(2,1)} %v_ref.3) | copy-start | bytes 983044
  2.1 9.0 %collective-permute-start = (bf16[160,640]{1,0:T(8,128)(2,1)S(1)}, bf16[160,640]{1,0:T(8,128)(2,1)S(1)}, u32[]{:S(2)}, u32[]{:S(2)}) collective-permute-start(bf16[160,640]{1,0:T(8,128)(2,1)S(1)} %get-tuple-element.51), channel_id=1, source_target_pairs={{0,8},{8,0},{16,24},{24,16},{1,9},{9,1},{17,25},{25,17},{2,10},{10... | collective-permute-start | bytes 614408 | tf_op jit(solution)/shard_map/ppermute | solution.py:25
  3.8 14.6 %collective-permute-start.1 = (bf16[160,640]{1,0:T(8,128)(2,1)S(1)}, bf16[160,640]{1,0:T(8,128)(2,1)S(1)}, u32[]{:S(2)}, u32[]{:S(2)}) collective-permute-start(bf16[160,640]{1,0:T(8,128)(2,1)S(1)} %get-tuple-element.53), channel_id=1, source_target_pairs={{0,16},{8,24},{16,0},{24,8},{1,17},{9,25},{17,1},{25,9},{2,18},{10... | collective-permute-start | bytes 614408 | tf_op jit(solution)/shard_map/ppermute | solution.py:25
  4.1 19.3 %collective-permute-start.2 = (bf16[160,640]{1,0:T(8,128)(2,1)S(1)}, bf16[160,640]{1,0:T(8,128)(2,1)S(1)}, u32[]{:S(2)}, u32[]{:S(2)}) collective-permute-start(bf16[160,640]{1,0:T(8,128)(2,1)S(1)} %get-tuple-element.52), channel_id=1, source_target_pairs={{0,24},{8,16},{16,8},{24,0},{1,25},{9,17},{17,9},{25,1},{2,26},{10... | collective-permute-start | bytes 614408 | tf_op jit(solution)/shard_map/ppermute | solution.py:25
  5.7 17.8 %collective-permute-start.3 = (bf16[128,1280]{1,0:T(8,128)(2,1)S(1)}, bf16[128,1280]{1,0:T(8,128)(2,1)S(1)}, u32[]{:S(2)}, u32[]{:S(2)}) collective-permute-start(bf16[128,1280]{1,0:T(8,128)(2,1)S(1)} %copy-done.4), channel_id=1, source_target_pairs={{0,1},{1,0},{2,3},{3,2},{4,5},{5,4},{6,7},{7,6},{8,9},{9,8},{10,11... | collective-permute-start | bytes 983048 | tf_op jit(solution)/shard_map/ppermute | solution.py:25
  23.5 13.0 %collective-permute-start.11 = (bf16[4,160,640]{2,1,0:T(8,128)(2,1)S(1)}, bf16[4,160,640]{2,1,0:T(8,128)(2,1)S(1)}, u32[]{:S(2)}, u32[]{:S(2)}) collective-permute-start(bf16[4,160,640]{2,1,0:T(8,128)(2,1)S(1)} %pad_maximum_fusion.refs_8_), channel_id=1, source_target_pairs={{0,2},{2,0},{4,6},{6,4},{1,3},{3,1},{5,7},{7,5},{8,10},{10,8},{12,... | collective-permute-start | bytes 2457608 | tf_op jit(solution)/shard_map/ppermute | solution.py:25
  23.6 10.6 %collective-permute-start.5 = (bf16[128,1280]{1,0:T(8,128)(2,1)S(1)}, bf16[128,1280]{1,0:T(8,128)(2,1)S(1)}, u32[]{:S(2)}, u32[]{:S(2)}) collective-permute-start(bf16[128,1280]{1,0:T(8,128)(2,1)S(1)} %copy-done.4), channel_id=1, source_target_pairs={{0,8},{8,24},{24,16},{16,0},{1,9},{9,25},{25,17},{17,1},{2,10},{10... | collective-permute-start | bytes 983048 | tf_op jit(solution)/shard_map/ppermute | solution.py:327
  23.7 17.5 %collective-permute-start.8 = (bf16[128,1280]{1,0:T(8,128)(2,1)S(1)}, bf16[128,1280]{1,0:T(8,128)(2,1)S(1)}, u32[]{:S(2)}, u32[]{:S(2)}) collective-permute-start(bf16[128,1280]{1,0:T(8,128)(2,1)S(1)} %copy-done.4), channel_id=1, source_target_pairs={{8,0},{24,8},{16,24},{0,16},{9,1},{25,9},{17,25},{1,17},{10,2},{26... | collective-permute-start | bytes 983048 | tf_op jit(solution)/shard_map/ppermute | solution.py:327
  25.7 23.6 %collective-permute-start.4 = (bf16[4,160,640]{2,1,0:T(8,128)(2,1)S(1)}, bf16[4,160,640]{2,1,0:T(8,128)(2,1)S(1)}, u32[]{:S(2)}, u32[]{:S(2)}) collective-permute-start(bf16[4,160,640]{2,1,0:T(8,128)(2,1)S(1)} %pad_maximum_fusion.refs_8_), channel_id=1, source_target_pairs={{0,4},{2,6},{4,0},{6,2},{1,5},{3,7},{5,1},{7,3},{8,12},{10,14},{12... | collective-permute-start | bytes 2457608 | tf_op jit(solution)/shard_map/ppermute | solution.py:25
  27.2 35.6 %copy-start.6 = (s32[2048]{0:T(1024)S(1)}, s32[2048]{0:T(1024)}, u32[]{:S(2)}) copy-start(s32[2048]{0:T(1024)} %param.15) | copy-start | bytes 24580
  27.2 35.6 %copy-start.7 = (s32[2048]{0:T(1024)S(1)}, s32[2048]{0:T(1024)}, u32[]{:S(2)}) copy-start(s32[2048]{0:T(1024)} %param.14) | copy-start | bytes 24580
  34.2 10.2 %collective-permute-start.9 = (bf16[128,1280]{1,0:T(8,128)(2,1)S(1)}, bf16[128,1280]{1,0:T(8,128)(2,1)S(1)}, u32[]{:S(2)}, u32[]{:S(2)}) collective-permute-start(bf16[128,1280]{1,0:T(8,128)(2,1)S(1)} %collective-permute-done.5.refs_1_), channel_id=1, source_target_pairs={{0,1},{1,0},{2,3},{3,2},{4,5},{5,4},{6,7},{7,6},{8,9},{9,8},{10,11... | collective-permute-start | bytes 983048 | tf_op jit(solution)/shard_map/ppermute | solution.py:25
  35.7 12.1 %collective-permute-start.6 = (bf16[128,1280]{1,0:T(8,128)(2,1)S(1)}, bf16[128,1280]{1,0:T(8,128)(2,1)S(1)}, u32[]{:S(2)}, u32[]{:S(2)}) collective-permute-start(bf16[128,1280]{1,0:T(8,128)(2,1)S(1)} %collective-permute-done.5.refs_1_), channel_id=1, source_target_pairs={{0,8},{8,24},{24,16},{16,0},{1,9},{9,25},{25,17},{17,1},{2,10},{10... | collective-permute-start | bytes 983048 | tf_op jit(solution)/shard_map/ppermute | solution.py:327
  36.5 23.7 %collective-permute-start.12 = (bf16[2,128,1280]{2,1,0:T(8,128)(2,1)S(1)}, bf16[2,128,1280]{2,1,0:T(8,128)(2,1)S(1)}, u32[]{:S(2)}, u32[]{:S(2)}) collective-permute-start(bf16[2,128,1280]{2,1,0:T(8,128)(2,1)S(1)} %get-tuple-element.30), channel_id=1, source_target_pairs={{0,2},{2,4},{4,6},{6,8},{8,10},{10,12},{12,14},{14,16},{16,18},{18... | collective-permute-start | bytes 1966088 | tf_op jit(solution)/shard_map/ppermute | solution.py:21
  41.1 19.1 %collective-permute-start.13 = (bf16[2,128,1280]{2,1,0:T(8,128)(2,1)S(1)}, bf16[2,128,1280]{2,1,0:T(8,128)(2,1)}, u32[]{:S(2)}, u32[]{:S(2)}) collective-permute-start(bf16[2,128,1280]{2,1,0:T(8,128)(2,1)S(1)} %get-tuple-element.31), channel_id=1, source_target_pairs={{2,0},{4,2},{6,4},{8,6},{10,8},{12,10},{14,12},{16,14},{18,16},{20... | collective-permute-start | bytes 1966088 | tf_op jit(solution)/shard_map/ppermute | solution.py:21
  44.4 10.7 %collective-permute-start.10 = (bf16[128,1280]{1,0:T(8,128)(2,1)S(1)}, bf16[128,1280]{1,0:T(8,128)(2,1)S(1)}, u32[]{:S(2)}, u32[]{:S(2)}) collective-permute-start(bf16[128,1280]{1,0:T(8,128)(2,1)S(1)} %collective-permute-done.8.refs_3_), channel_id=1, source_target_pairs={{0,1},{1,0},{2,3},{3,2},{4,5},{5,4},{6,7},{7,6},{8,9},{9,8},{10,11... | collective-permute-start | bytes 983048 | tf_op jit(solution)/shard_map/ppermute | solution.py:25
  47.8 12.4 %collective-permute-start.7 = (bf16[128,1280]{1,0:T(8,128)(2,1)S(1)}, bf16[128,1280]{1,0:T(8,128)(2,1)S(1)}, u32[]{:S(2)}, u32[]{:S(2)}) collective-permute-start(bf16[128,1280]{1,0:T(8,128)(2,1)S(1)} %collective-permute-done.6.refs_2_), channel_id=1, source_target_pairs={{0,1},{1,0},{2,3},{3,2},{4,5},{5,4},{6,7},{7,6},{8,9},{9,8},{10,11... | collective-permute-start | bytes 983048 | tf_op jit(solution)/shard_map/ppermute | solution.py:25
  60.3 7.4 %copy-start.8 = (bf16[2,128,1280]{2,1,0:T(8,128)(2,1)}, bf16[2,128,1280]{2,1,0:T(8,128)(2,1)S(1)}, u32[]{:S(2)}) copy-start(bf16[2,128,1280]{2,1,0:T(8,128)(2,1)S(1)} %collective-permute-done.12.kv1_ref) | copy-start | bytes 1966084
  60.3 2.8 %collective-permute-start.14 = (bf16[4,160,640]{2,1,0:T(8,128)(2,1)S(1)}, bf16[4,160,640]{2,1,0:T(8,128)(2,1)S(1)}, u32[]{:S(2)}, u32[]{:S(2)}) collective-permute-start(bf16[4,160,640]{2,1,0:T(8,128)(2,1)S(1)} %collective-permute-done.4.refs_10_), channel_id=1, source_target_pairs={{0,2},{2,0},{4,6},{6,4},{1,3},{3,1},{5,7},{7,5},{8,10},{10,8},{12,... | collective-permute-start | bytes 2457608 | tf_op jit(solution)/shard_map/ppermute | solution.py:25
  60.4 12.9 %collective-permute-start.15 = (bf16[2,128,1280]{2,1,0:T(8,128)(2,1)S(1)}, bf16[2,128,1280]{2,1,0:T(8,128)(2,1)}, u32[]{:S(2)}, u32[]{:S(2)}) collective-permute-start(bf16[2,128,1280]{2,1,0:T(8,128)(2,1)S(1)} %collective-permute-done.12.kv1_ref), channel_id=1, source_target_pairs={{0,2},{2,4},{4,6},{6,8},{8,10},{10,12},{12,14},{14,16},{16,18},{18... | collective-permute-start | bytes 1966088 | tf_op jit(solution)/shard_map/ppermute | solution.py:21
  63.0 4.6 %copy-start.5 = (bf16[128,640]{1,0:T(8,128)(2,1)}, bf16[128,640]{1,0:T(8,128)(2,1)S(1)}, u32[]{:S(2)}) copy-start(bf16[128,640]{1,0:T(8,128)(2,1)S(1)} %get-tuple-element.42.bias_ref) | copy-start | bytes 491524
  73.3 35.1 %all-to-all-start = ((bf16[16,4,16,640]{3,2,1,0:T(8,128)(2,1)}), bf16[16,4,16,640]{3,2,1,0:T(8,128)(2,1)S(1)}, u32[]{:S(2)}, u32[]{:S(2)}) async-start(bf16[16,4,16,640]{3,2,1,0:T(8,128)(2,1)} %project.1), calls=%async_computation | async-start | bytes 2621440 | tf_op jit(solution)/shard_map/all_to_all | solution.py:404
  77.6 40.8 %collective-permute-start.16 = (bf16[2,128,1280]{2,1,0:T(8,128)(2,1)}, bf16[2,128,1280]{2,1,0:T(8,128)(2,1)S(1)}, u32[]{:S(2)}, u32[]{:S(2)}) collective-permute-start(bf16[2,128,1280]{2,1,0:T(8,128)(2,1)} %collective-permute-done.13.qg1_ref), channel_id=1, source_target_pairs={{2,0},{4,2},{6,4},{8,6},{10,8},{12,10},{14,12},{16,14},{18,16},{20... | collective-permute-start | bytes 1966088 | tf_op jit(solution)/shard_map/ppermute | solution.py:21
  113.4 5.0 %collective-permute-start.17 = (f32[2,16,128]{2,1,0:T(8,128)S(1)}, f32[2,16,128]{2,1,0:T(8,128)S(1)}, u32[]{:S(2)}, u32[]{:S(2)}) collective-permute-start(f32[2,16,128]{2,1,0:T(8,128)S(1)} %get-tuple-element.46.st0_ref), channel_id=1, source_target_pairs={{2,0},{4,2},{6,4},{8,6},{10,8},{12,10},{14,12},{16,14},{18,16},{20... | collective-permute-start | bytes 49160 | tf_op jit(solution)/shard_map/ppermute | solution.py:21
  116.3 5.6 %collective-permute-start.18 = (f32[2,16,128]{2,1,0:T(8,128)S(1)}, f32[2,16,128]{2,1,0:T(8,128)S(1)}, u32[]{:S(2)}, u32[]{:S(2)}) collective-permute-start(f32[2,16,128]{2,1,0:T(8,128)S(1)} %get-tuple-element.46.st0_ref), channel_id=1, source_target_pairs={{4,0},{6,2},{8,4},{10,6},{12,8},{14,10},{16,12},{18,14},{20,16},{2... | collective-permute-start | bytes 49160 | tf_op jit(solution)/shard_map/ppermute | solution.py:21

commit v17 on v13

--- a/solution.py
+++ b/solution.py
@@ -353,14 +353,12 @@
         other3 = swapped(row3, "head", 1)
         row2 = lax.optimization_barrier(row2)
         other2 = swapped(row2, "head", 1)
-        across, other2, other3, near, back1 = lax.optimization_barrier(
-            (across, other2, other3, near, back1)
-        )
+        across, other2, other3, near = lax.optimization_barrier((across, other2, other3, near))
         pieces = [own, beside, across, swapped(across, "p", 1)]
         far = shifted(near, 1)
         rows = [cache, row1, row2, row3, other0, other1, other2, other3]
         slots = project(place, rows, pieces, devices, capacity)
-        slots, far = lax.optimization_barrier((slots, far))
+        slots, far, back1 = lax.optimization_barrier((slots, far, back1))
         return slots, near, far, back1
     near, back1 = shifted(stream, 1), shifted(back, -1)
     far = shifted(near, 1)

time: 126 us -> 137 us (1.087)
  starting transfers between devices: 34.2 us -> 46.6 us
  waiting for transfers between devices: 75.3 us -> 73.6 us
    ppermute x10, waiting for transfers between devices: 27.1 us -> 19.7 us  [swapped(): lax.ppermute(value, axis, [(i, i ^ mask) for i in range(lax.axis_size(axi...]
    all_to_all x1, starting transfers between devices: 4.35 us -> 9.38 us  [body(): memory = lax.all_to_all(slots, SEQ, split_axis=0, concat_axis=0, tiled=True)]
    ppermute x3, waiting for transfers between devices: 11.4 us -> 16.3 us  [ring_step(): lax.ppermute(value, 'z', [(b, a) for a, b in pairs] if back else pairs)]
    ppermute x6, starting transfers between devices: 15.6 us -> 19.4 us  [shifted(): return lax.ppermute(value, SEQ, pairs)]
    ppermute x3, starting transfers between devices: 2.91 us -> 6.15 us  [ring_step(): lax.ppermute(value, 'z', [(b, a) for a, b in pairs] if back else pairs)]
  transfers between devices with their start and end apart: 20 -> 20, of which waited for: 11 -> 12; matrix products, arithmetic and copies ran while one was open for 0% -> 0% of each run, Pallas kernels for 8% -> 7%
where the time goes in v17:
time: 137 us
  waiting for transfers between devices  73.6 us (54%)
  starting transfers between devices  46.6 us (34%)
  Pallas kernels  13.4 us (10%)
  local copies, waits for them, and re-layouts  2.32 us (2%)
    all_to_all x1, waiting for transfers between devices, body(): memory = lax.all_to_all(slots, SEQ, split_axis=0, concat_axis=0, tiled=True)  27.7 us
    ppermute x10, waiting for transfers between devices, swapped(): lax.ppermute(value, axis, [(i, i ^ mask) for i in range(lax.axis_size(axi...  19.7 us
    ppermute x6, starting transfers between devices, shifted(): return lax.ppermute(value, SEQ, pairs)  19.4 us
    ppermute x3, waiting for transfers between devices, ring_step(): lax.ppermute(value, 'z', [(b, a) for a, b in pairs] if back else pairs)  16.3 us
    ppermute x10, starting transfers between devices, swapped(): lax.ppermute(value, axis, [(i, i ^ mask) for i in range(lax.axis_size(axi...  11.6 us
    ppermute x6, waiting for transfers between devices, shifted(): return lax.ppermute(value, SEQ, pairs)  9.97 us
    all_to_all x1, starting transfers between devices, body(): memory = lax.all_to_all(slots, SEQ, split_axis=0, concat_axis=0, tiled=True)  9.38 us
    ppermute x3, starting transfers between devices, ring_step(): lax.ppermute(value, 'z', [(b, a) for a, b in pairs] if back else pairs)  6.15 us
  transfers between devices with their start and end apart: 20, of which 12 were waited for; matrix products, arithmetic and copies ran while one was open for 0% of the time, Pallas kernels for 7%

profile of v17, /device:TPU:16, one launch (start us, length us, event | category | flops | bytes accessed | tf_op | source)
XLA Modules:
  0.0 137.0 jit_solution(4607626101620251576)
XLA Ops:
  0.6 0.0 copy-start.4
  0.7 0.0 copy-start
  0.7 0.0 copy-start.1
  0.7 0.0 copy-start.2
  0.7 0.0 copy-start.3
  0.7 1.4 %constant_dynamic-slice_fusion = (bf16[1,160,640]{2,1,0:T(8,128)(2,1)S(1)}, bf16[160,640]{1,0:T(8,128)(2,1)S(1)}, bf16[160,640]{1,0:T(8,128)(2,1)S(1)}, bf16[160,640]{1,0:T(8,128)(2,1)S(1)}) fusion(bf16[2,160,1280]{2,1,0:T(8,128)(2,1)} %param.13, s32[]{:T(128)S(6)} %select_n.24, s32[]{:T(128)S(6)} %select_n.25, s32[]{:T(128)S(6)} %select_n.26, ...), kind=kLoop, calls=%fused_computation.6 | loop fusion | bytes 1638432 | tf_op jit(solution)/shard_map/dynamic_slice | solution.py:325
  2.1 0.5 collective-permute-start.2
  2.6 3.5 %collective-permute-start.1 = (bf16[160,640]{1,0:T(8,128)(2,1)S(1)}, bf16[160,640]{1,0:T(8,128)(2,1)S(1)}, u32[]{:S(2)}, u32[]{:S(2)}) collective-permute-start(bf16[160,640]{1,0:T(8,128)(2,1)S(1)} %get-tuple-element.53), channel_id=1, source_target_pairs={{0,16},{8,24},{16,0},{24,8},{1,17},{9,25},{17,1},{25,9},{2,18},{10... | collective-permute-start | bytes 614408 | tf_op jit(solution)/shard_map/ppermute | solution.py:25
  6.1 0.0 collective-permute-start
  6.1 0.0 copy-done.4
  6.1 1.5 %collective-permute-start.3 = (bf16[128,1280]{1,0:T(8,128)(2,1)S(1)}, bf16[128,1280]{1,0:T(8,128)(2,1)S(1)}, u32[]{:S(2)}, u32[]{:S(2)}) collective-permute-start(bf16[128,1280]{1,0:T(8,128)(2,1)S(1)} %copy-done.4), channel_id=1, source_target_pairs={{0,1},{1,0},{2,3},{3,2},{4,5},{5,4},{6,7},{7,6},{8,9},{9,8},{10,11... | collective-permute-start | bytes 983048 | tf_op jit(solution)/shard_map/ppermute | solution.py:25
  7.7 11.3 %collective-permute-done.2 = bf16[160,640]{1,0:T(8,128)(2,1)S(1)} collective-permute-done((bf16[160,640]{1,0:T(8,128)(2,1)S(1)}, bf16[160,640]{1,0:T(8,128)(2,1)S(1)}, u32[]{:S(2)}, u32[]{:S(2)}) %collective-permute-start.2) | collective-permute-done | bytes 204832 | tf_op jit(solution)/shard_map/ppermute | solution.py:25
  18.9 1.2 collective-permute-done.1
  20.1 0.0 collective-permute-done
  20.2 0.1 pad_maximum_fusion.refs_8_
  20.3 0.0 collective-permute-done.3.refs_4_
  20.3 0.1 collective-permute-start.11
  20.4 3.4 %collective-permute-start.5 = (bf16[128,1280]{1,0:T(8,128)(2,1)S(1)}, bf16[128,1280]{1,0:T(8,128)(2,1)S(1)}, u32[]{:S(2)}, u32[]{:S(2)}) collective-permute-start(bf16[128,1280]{1,0:T(8,128)(2,1)S(1)} %copy-done.4), channel_id=1, source_target_pairs={{0,8},{8,24},{24,16},{16,0},{1,9},{9,25},{25,17},{17,1},{2,10},{10... | collective-permute-start | bytes 983048 | tf_op jit(solution)/shard_map/ppermute | solution.py:330
  23.8 1.5 %collective-permute-start.4 = (bf16[4,160,640]{2,1,0:T(8,128)(2,1)S(1)}, bf16[4,160,640]{2,1,0:T(8,128)(2,1)S(1)}, u32[]{:S(2)}, u32[]{:S(2)}) collective-permute-start(bf16[4,160,640]{2,1,0:T(8,128)(2,1)S(1)} %pad_maximum_fusion.refs_8_), channel_id=1, source_target_pairs={{0,4},{2,6},{4,0},{6,2},{1,5},{3,7},{5,1},{7,3},{8,12},{10,14},{12... | collective-permute-start | bytes 2457608 | tf_op jit(solution)/shard_map/ppermute | solution.py:25
  25.3 6.9 %collective-permute-done.5.refs_1_ = bf16[128,1280]{1,0:T(8,128)(2,1)S(1)} collective-permute-done((bf16[128,1280]{1,0:T(8,128)(2,1)S(1)}, bf16[128,1280]{1,0:T(8,128)(2,1)S(1)}, u32[]{:S(2)}, u32[]{:S(2)}) %collective-permute-start.5) | collective-permute-done | bytes 327712 | tf_op jit(solution)/shard_map/ppermute | solution.py:330
  32.2 2.5 %collective-permute-start.6 = (bf16[128,1280]{1,0:T(8,128)(2,1)S(1)}, bf16[128,1280]{1,0:T(8,128)(2,1)S(1)}, u32[]{:S(2)}, u32[]{:S(2)}) collective-permute-start(bf16[128,1280]{1,0:T(8,128)(2,1)S(1)} %collective-permute-done.5.refs_1_), channel_id=1, source_target_pairs={{0,8},{8,24},{24,16},{16,0},{1,9},{9,25},{25,17},{17,1},{2,10},{10... | collective-permute-start | bytes 983048 | tf_op jit(solution)/shard_map/ppermute | solution.py:330
  34.8 0.0 copy-done
  34.8 0.0 copy-done.1
  34.8 0.0 copy-done.2
  34.8 0.0 copy-done.3
  34.8 0.0 copy-start.6
  34.8 0.0 copy-start.7
  34.8 0.1 pad_maximum_fusion.1
  34.9 0.2 collective-permute-start.8
  35.1 1.5 %collective-permute-start.9 = (bf16[128,1280]{1,0:T(8,128)(2,1)S(1)}, bf16[128,1280]{1,0:T(8,128)(2,1)S(1)}, u32[]{:S(2)}, u32[]{:S(2)}) collective-permute-start(bf16[128,1280]{1,0:T(8,128)(2,1)S(1)} %collective-permute-done.5.refs_1_), channel_id=1, source_target_pairs={{0,1},{1,0},{2,3},{3,2},{4,5},{5,4},{6,7},{7,6},{8,9},{9,8},{10,11... | collective-permute-start | bytes 983048 | tf_op jit(solution)/shard_map/ppermute | solution.py:25
  36.6 0.0 collective-permute-done.11.refs_9_
  36.6 1.9 %collective-permute-start.12 = (bf16[2,128,1280]{2,1,0:T(8,128)(2,1)S(1)}, bf16[2,128,1280]{2,1,0:T(8,128)(2,1)S(1)}, u32[]{:S(2)}, u32[]{:S(2)}) collective-permute-start(bf16[2,128,1280]{2,1,0:T(8,128)(2,1)S(1)} %get-tuple-element.30), channel_id=1, source_target_pairs={{0,2},{2,4},{4,6},{6,8},{8,10},{10,12},{12,14},{14,16},{16,18},{18... | collective-permute-start | bytes 1966088 | tf_op jit(solution)/shard_map/ppermute | solution.py:21
  38.5 4.9 %collective-permute-done.6.refs_2_ = bf16[128,1280]{1,0:T(8,128)(2,1)S(1)} collective-permute-done((bf16[128,1280]{1,0:T(8,128)(2,1)S(1)}, bf16[128,1280]{1,0:T(8,128)(2,1)S(1)}, u32[]{:S(2)}, u32[]{:S(2)}) %collective-permute-start.6) | collective-permute-done | bytes 327712 | tf_op jit(solution)/shard_map/ppermute | solution.py:330
  43.4 1.5 %collective-permute-start.7 = (bf16[128,1280]{1,0:T(8,128)(2,1)S(1)}, bf16[128,1280]{1,0:T(8,128)(2,1)S(1)}, u32[]{:S(2)}, u32[]{:S(2)}) collective-permute-start(bf16[128,1280]{1,0:T(8,128)(2,1)S(1)} %collective-permute-done.6.refs_2_), channel_id=1, source_target_pairs={{0,1},{1,0},{2,3},{3,2},{4,5},{5,4},{6,7},{7,6},{8,9},{9,8},{10,11... | collective-permute-start | bytes 983048 | tf_op jit(solution)/shard_map/ppermute | solution.py:25
  45.0 4.5 %collective-permute-done.8.refs_3_ = bf16[128,1280]{1,0:T(8,128)(2,1)S(1)} collective-permute-done((bf16[128,1280]{1,0:T(8,128)(2,1)S(1)}, bf16[128,1280]{1,0:T(8,128)(2,1)S(1)}, u32[]{:S(2)}, u32[]{:S(2)}) %collective-permute-start.8) | collective-permute-done | bytes 327712 | tf_op jit(solution)/shard_map/ppermute | solution.py:330
  49.4 0.0 collective-permute-done.9.refs_5_
  49.4 1.5 %collective-permute-start.10 = (bf16[128,1280]{1,0:T(8,128)(2,1)S(1)}, bf16[128,1280]{1,0:T(8,128)(2,1)S(1)}, u32[]{:S(2)}, u32[]{:S(2)}) collective-permute-start(bf16[128,1280]{1,0:T(8,128)(2,1)S(1)} %collective-permute-done.8.refs_3_), channel_id=1, source_target_pairs={{0,1},{1,0},{2,3},{3,2},{4,5},{5,4},{6,7},{7,6},{8,9},{9,8},{10,11... | collective-permute-start | bytes 983048 | tf_op jit(solution)/shard_map/ppermute | solution.py:25
  50.9 0.0 collective-permute-done.4.refs_10_
  50.9 0.2 collective-permute-done.7.refs_6_
  51.1 7.0 %collective-permute-done.10.refs_7_ = bf16[128,1280]{1,0:T(8,128)(2,1)S(1)} collective-permute-done((bf16[128,1280]{1,0:T(8,128)(2,1)S(1)}, bf16[128,1280]{1,0:T(8,128)(2,1)S(1)}, u32[]{:S(2)}, u32[]{:S(2)}) %collective-permute-start.10) | collective-permute-done | bytes 327712 | tf_op jit(solution)/shard_map/ppermute | solution.py:25
  58.1 0.5 collective-permute-done.12.kv1_ref
  58.6 0.0 collective-permute-start.13
  58.6 7.5 %collective-permute-start.15 = (bf16[2,128,1280]{2,1,0:T(8,128)(2,1)S(1)}, bf16[2,128,1280]{2,1,0:T(8,128)(2,1)}, u32[]{:S(2)}, u32[]{:S(2)}) collective-permute-start(bf16[2,128,1280]{2,1,0:T(8,128)(2,1)S(1)} %get-tuple-element.39), channel_id=1, source_target_pairs={{2,0},{4,2},{6,4},{8,6},{10,8},{12,10},{14,12},{16,14},{18,16},{20... | collective-permute-start | bytes 1966088 | tf_op jit(solution)/shard_map/ppermute | solution.py:21
  66.1 1.9 %collective-permute-start.14 = (bf16[2,128,1280]{2,1,0:T(8,128)(2,1)S(1)}, bf16[2,128,1280]{2,1,0:T(8,128)(2,1)S(1)}, u32[]{:S(2)}, u32[]{:S(2)}) collective-permute-start(bf16[2,128,1280]{2,1,0:T(8,128)(2,1)S(1)} %collective-permute-done.12.kv1_ref), channel_id=1, source_target_pairs={{0,2},{2,4},{4,6},{6,8},{8,10},{10,12},{12,14},{14,16},{16,18},{18... | collective-permute-start | bytes 1966088 | tf_op jit(solution)/shard_map/ppermute | solution.py:21
  68.0 0.0 copy-done.6
  68.0 0.0 copy-done.7
  68.1 0.3 prepare.1
  68.3 0.0 collective-permute-done.13.refs_11_
  68.3 4.6 %project.1 = bf16[16,4,16,640]{3,2,1,0:T(8,128)(2,1)} custom-call(s32[4,1,128]{2,1,0:T(1,128)S(1)} %get-tuple-element.32.place_ref, bf16[128,1280]{1,0:T(8,128)(2,1)S(1)} %copy-done.4, bf16[128,1280]{1,0:T(8,128)(2,1)S(1)} %collective-permute-done.5.refs_1_, bf16[128,1280]{1,0:T(8,128)(2,1)S(1)} %collective-permute-done.6.refs_2_, ...), custom_call_target="tpu_custom_call" | custom-call | flops 1677721600 | bytes 8388608 | tf_op jit(solution)/shard_map/project/pallas_call | solution.py:238
  72.9 0.0 copy-done.8
  72.9 0.0 copy-done.5
  72.9 1.3 collective-permute-done.15.qg1_ref
  74.2 4.7 %collective-permute-done.14.kv2_ref = bf16[2,128,1280]{2,1,0:T(8,128)(2,1)S(1)} collective-permute-done((bf16[2,128,1280]{2,1,0:T(8,128)(2,1)S(1)}, bf16[2,128,1280]{2,1,0:T(8,128)(2,1)S(1)}, u32[]{:S(2)}, u32[]{:S(2)}) %collective-permute-start.14) | collective-permute-done | bytes 655392 | tf_op jit(solution)/shard_map/ppermute | solution.py:21
  78.9 0.9 copy-done.9
  79.8 9.4 %all-to-all-start = ((bf16[16,4,16,640]{3,2,1,0:T(8,128)(2,1)}), bf16[16,4,16,640]{3,2,1,0:T(8,128)(2,1)S(1)}, u32[]{:S(2)}, u32[]{:S(2)}) async-start(bf16[16,4,16,640]{3,2,1,0:T(8,128)(2,1)} %project.1), calls=%async_computation | async-start | bytes 2621440 | tf_op jit(solution)/shard_map/all_to_all | solution.py:405
  89.1 3.1 %collective-permute-start.16 = (bf16[2,128,1280]{2,1,0:T(8,128)(2,1)}, bf16[2,128,1280]{2,1,0:T(8,128)(2,1)S(1)}, u32[]{:S(2)}, u32[]{:S(2)}) collective-permute-start(bf16[2,128,1280]{2,1,0:T(8,128)(2,1)} %collective-permute-done.15.qg1_ref), channel_id=1, source_target_pairs={{2,0},{4,2},{6,4},{8,6},{10,8},{12,10},{14,12},{16,14},{18,16},{20... | collective-permute-start | bytes 1966088 | tf_op jit(solution)/shard_map/ppermute | solution.py:21
  92.3 27.7 %all-to-all-done = bf16[16,4,16,640]{3,2,1,0:T(8,128)(2,1)S(1)} async-done(((bf16[16,4,16,640]{3,2,1,0:T(8,128)(2,1)}), bf16[16,4,16,640]{3,2,1,0:T(8,128)(2,1)S(1)}, u32[]{:S(2)}, u32[]{:S(2)}) %all-to-all-start) | async-done | bytes 1310752 | tf_op jit(solution)/shard_map/all_to_all | solution.py:405
  119.9 5.0 %attend.1 = (bf16[128,1280]{1,0:T(8,128)(2,1)}, bf16[128,1280]{1,0:T(8,128)(2,1)}, f32[2,16,128]{2,1,0:T(8,128)S(1)}) custom-call(bf16[128,1280]{1,0:T(8,128)(2,1)S(1)} %copy-done, bf16[128,1280]{1,0:T(8,128)(2,1)S(1)} %copy-done.1, bf16[128,1280]{1,0:T(8,128)(2,1)S(1)} %copy-done.2, bf16[128,1280]{1,0:T(8,128)(2,1)S(1)} %copy-done.3, ...), custom_call_target="tpu_custom_call" | custom-call | flops 838860800 | bytes 6291456 | tf_op jit(solution)/shard_map/attend/pallas_call | solution.py:104
  125.0 2.9 %collective-permute-start.17 = (f32[2,16,128]{2,1,0:T(8,128)S(1)}, f32[2,16,128]{2,1,0:T(8,128)S(1)}, u32[]{:S(2)}, u32[]{:S(2)}) collective-permute-start(f32[2,16,128]{2,1,0:T(8,128)S(1)} %get-tuple-element.46.st0_ref), channel_id=1, source_target_pairs={{2,0},{4,2},{6,4},{8,6},{10,8},{12,10},{14,12},{16,14},{18,16},{20... | collective-permute-start | bytes 49160 | tf_op jit(solution)/shard_map/ppermute | solution.py:21
  127.9 2.1 %collective-permute-start.18 = (f32[2,16,128]{2,1,0:T(8,128)S(1)}, f32[2,16,128]{2,1,0:T(8,128)S(1)}, u32[]{:S(2)}, u32[]{:S(2)}) collective-permute-start(f32[2,16,128]{2,1,0:T(8,128)S(1)} %get-tuple-element.46.st0_ref), channel_id=1, source_target_pairs={{4,0},{6,2},{8,4},{10,6},{12,8},{14,10},{16,12},{18,14},{20,16},{2... | collective-permute-start | bytes 49160 | tf_op jit(solution)/shard_map/ppermute | solution.py:21
  130.0 0.0 collective-permute-done.16.qg2_ref
  130.0 0.0 collective-permute-done.17.st1_ref
  130.0 3.5 %collective-permute-done.18.st2_ref = f32[2,16,128]{2,1,0:T(8,128)S(1)} collective-permute-done((f32[2,16,128]{2,1,0:T(8,128)S(1)}, f32[2,16,128]{2,1,0:T(8,128)S(1)}, u32[]{:S(2)}, u32[]{:S(2)}) %collective-permute-start.18) | collective-permute-done | bytes 16416 | tf_op jit(solution)/shard_map/ppermute | solution.py:21
  133.5 3.5 %key_grads.1 = (bf16[128,1280]{1,0:T(8,128)(2,1)}, bf16[128,1280]{1,0:T(8,128)(2,1)}) custom-call(bf16[128,1280]{1,0:T(8,128)(2,1)S(1)} %copy-done.2, bf16[128,1280]{1,0:T(8,128)(2,1)S(1)} %copy-done.3, bf16[128,1280]{1,0:T(8,128)(2,1)S(1)} %copy-done, bf16[128,1280]{1,0:T(8,128)(2,1)S(1)} %copy-done.1, ...), custom_call_target="tpu_custom_call" | custom-call | flops 503316480 | bytes 4194304 | tf_op jit(solution)/shard_map/key_grads/pallas_call | solution.py:173
  (3 shorter events, 0.0 us)
Async XLA Ops:
  0.6 5.5 %copy-start.4 = (bf16[128,1280]{1,0:T(8,128)(2,1)S(1)}, bf16[128,1280]{1,0:T(8,128)(2,1)}, u32[]{:S(2)}) copy-start(bf16[128,1280]{1,0:T(8,128)(2,1)} %refs_0_) | copy-start | bytes 983044
  0.7 34.1 %copy-start = (bf16[128,1280]{1,0:T(8,128)(2,1)S(1)}, bf16[128,1280]{1,0:T(8,128)(2,1)}, u32[]{:S(2)}) copy-start(bf16[128,1280]{1,0:T(8,128)(2,1)} %q_ref.3) | copy-start | bytes 983044
  0.7 34.1 %copy-start.1 = (bf16[128,1280]{1,0:T(8,128)(2,1)S(1)}, bf16[128,1280]{1,0:T(8,128)(2,1)}, u32[]{:S(2)}) copy-start(bf16[128,1280]{1,0:T(8,128)(2,1)} %g_ref.3) | copy-start | bytes 983044
  0.7 34.1 %copy-start.2 = (bf16[128,1280]{1,0:T(8,128)(2,1)S(1)}, bf16[128,1280]{1,0:T(8,128)(2,1)}, u32[]{:S(2)}) copy-start(bf16[128,1280]{1,0:T(8,128)(2,1)} %k_ref.3) | copy-start | bytes 983044
  0.7 34.1 %copy-start.3 = (bf16[128,1280]{1,0:T(8,128)(2,1)S(1)}, bf16[128,1280]{1,0:T(8,128)(2,1)}, u32[]{:S(2)}) copy-start(bf16[128,1280]{1,0:T(8,128)(2,1)} %v_ref.3) | copy-start | bytes 983044
  2.1 16.8 %collective-permute-start.2 = (bf16[160,640]{1,0:T(8,128)(2,1)S(1)}, bf16[160,640]{1,0:T(8,128)(2,1)S(1)}, u32[]{:S(2)}, u32[]{:S(2)}) collective-permute-start(bf16[160,640]{1,0:T(8,128)(2,1)S(1)} %get-tuple-element.52), channel_id=1, source_target_pairs={{0,24},{8,16},{16,8},{24,0},{1,25},{9,17},{17,9},{25,1},{2,26},{10... | collective-permute-start | bytes 614408 | tf_op jit(solution)/shard_map/ppermute | solution.py:25
  2.6 17.5 %collective-permute-start.1 = (bf16[160,640]{1,0:T(8,128)(2,1)S(1)}, bf16[160,640]{1,0:T(8,128)(2,1)S(1)}, u32[]{:S(2)}, u32[]{:S(2)}) collective-permute-start(bf16[160,640]{1,0:T(8,128)(2,1)S(1)} %get-tuple-element.53), channel_id=1, source_target_pairs={{0,16},{8,24},{16,0},{24,8},{1,17},{9,25},{17,1},{25,9},{2,18},{10... | collective-permute-start | bytes 614408 | tf_op jit(solution)/shard_map/ppermute | solution.py:25
  6.1 14.0 %collective-permute-start = (bf16[160,640]{1,0:T(8,128)(2,1)S(1)}, bf16[160,640]{1,0:T(8,128)(2,1)S(1)}, u32[]{:S(2)}, u32[]{:S(2)}) collective-permute-start(bf16[160,640]{1,0:T(8,128)(2,1)S(1)} %get-tuple-element.51), channel_id=1, source_target_pairs={{0,8},{8,0},{16,24},{24,16},{1,9},{9,1},{17,25},{25,17},{2,10},{10... | collective-permute-start | bytes 614408 | tf_op jit(solution)/shard_map/ppermute | solution.py:25
  6.1 14.1 %collective-permute-start.3 = (bf16[128,1280]{1,0:T(8,128)(2,1)S(1)}, bf16[128,1280]{1,0:T(8,128)(2,1)S(1)}, u32[]{:S(2)}, u32[]{:S(2)}) collective-permute-start(bf16[128,1280]{1,0:T(8,128)(2,1)S(1)} %copy-done.4), channel_id=1, source_target_pairs={{0,1},{1,0},{2,3},{3,2},{4,5},{5,4},{6,7},{7,6},{8,9},{9,8},{10,11... | collective-permute-start | bytes 983048 | tf_op jit(solution)/shard_map/ppermute | solution.py:25
  20.3 16.3 %collective-permute-start.11 = (bf16[4,160,640]{2,1,0:T(8,128)(2,1)S(1)}, bf16[4,160,640]{2,1,0:T(8,128)(2,1)S(1)}, u32[]{:S(2)}, u32[]{:S(2)}) collective-permute-start(bf16[4,160,640]{2,1,0:T(8,128)(2,1)S(1)} %pad_maximum_fusion.refs_8_), channel_id=1, source_target_pairs={{0,2},{2,0},{4,6},{6,4},{1,3},{3,1},{5,7},{7,5},{8,10},{10,8},{12,... | collective-permute-start | bytes 2457608 | tf_op jit(solution)/shard_map/ppermute | solution.py:25
  20.4 11.9 %collective-permute-start.5 = (bf16[128,1280]{1,0:T(8,128)(2,1)S(1)}, bf16[128,1280]{1,0:T(8,128)(2,1)S(1)}, u32[]{:S(2)}, u32[]{:S(2)}) collective-permute-start(bf16[128,1280]{1,0:T(8,128)(2,1)S(1)} %copy-done.4), channel_id=1, source_target_pairs={{0,8},{8,24},{24,16},{16,0},{1,9},{9,25},{25,17},{17,1},{2,10},{10... | collective-permute-start | bytes 983048 | tf_op jit(solution)/shard_map/ppermute | solution.py:330
  23.8 27.1 %collective-permute-start.4 = (bf16[4,160,640]{2,1,0:T(8,128)(2,1)S(1)}, bf16[4,160,640]{2,1,0:T(8,128)(2,1)S(1)}, u32[]{:S(2)}, u32[]{:S(2)}) collective-permute-start(bf16[4,160,640]{2,1,0:T(8,128)(2,1)S(1)} %pad_maximum_fusion.refs_8_), channel_id=1, source_target_pairs={{0,4},{2,6},{4,0},{6,2},{1,5},{3,7},{5,1},{7,3},{8,12},{10,14},{12... | collective-permute-start | bytes 2457608 | tf_op jit(solution)/shard_map/ppermute | solution.py:25
  32.2 11.2 %collective-permute-start.6 = (bf16[128,1280]{1,0:T(8,128)(2,1)S(1)}, bf16[128,1280]{1,0:T(8,128)(2,1)S(1)}, u32[]{:S(2)}, u32[]{:S(2)}) collective-permute-start(bf16[128,1280]{1,0:T(8,128)(2,1)S(1)} %collective-permute-done.5.refs_1_), channel_id=1, source_target_pairs={{0,8},{8,24},{24,16},{16,0},{1,9},{9,25},{25,17},{17,1},{2,10},{10... | collective-permute-start | bytes 983048 | tf_op jit(solution)/shard_map/ppermute | solution.py:330
  34.8 33.3 %copy-start.6 = (s32[2048]{0:T(1024)S(1)}, s32[2048]{0:T(1024)}, u32[]{:S(2)}) copy-start(s32[2048]{0:T(1024)} %param.15) | copy-start | bytes 24580
  34.8 33.3 %copy-start.7 = (s32[2048]{0:T(1024)S(1)}, s32[2048]{0:T(1024)}, u32[]{:S(2)}) copy-start(s32[2048]{0:T(1024)} %param.14) | copy-start | bytes 24580
  34.9 14.5 %collective-permute-start.8 = (bf16[128,1280]{1,0:T(8,128)(2,1)S(1)}, bf16[128,1280]{1,0:T(8,128)(2,1)S(1)}, u32[]{:S(2)}, u32[]{:S(2)}) collective-permute-start(bf16[128,1280]{1,0:T(8,128)(2,1)S(1)} %copy-done.4), channel_id=1, source_target_pairs={{8,0},{24,8},{16,24},{0,16},{9,1},{25,9},{17,25},{1,17},{10,2},{26... | collective-permute-start | bytes 983048 | tf_op jit(solution)/shard_map/ppermute | solution.py:330
  35.1 14.3 %collective-permute-start.9 = (bf16[128,1280]{1,0:T(8,128)(2,1)S(1)}, bf16[128,1280]{1,0:T(8,128)(2,1)S(1)}, u32[]{:S(2)}, u32[]{:S(2)}) collective-permute-start(bf16[128,1280]{1,0:T(8,128)(2,1)S(1)} %collective-permute-done.5.refs_1_), channel_id=1, source_target_pairs={{0,1},{1,0},{2,3},{3,2},{4,5},{5,4},{6,7},{7,6},{8,9},{9,8},{10,11... | collective-permute-start | bytes 983048 | tf_op jit(solution)/shard_map/ppermute | solution.py:25
  36.6 22.0 %collective-permute-start.12 = (bf16[2,128,1280]{2,1,0:T(8,128)(2,1)S(1)}, bf16[2,128,1280]{2,1,0:T(8,128)(2,1)S(1)}, u32[]{:S(2)}, u32[]{:S(2)}) collective-permute-start(bf16[2,128,1280]{2,1,0:T(8,128)(2,1)S(1)} %get-tuple-element.30), channel_id=1, source_target_pairs={{0,2},{2,4},{4,6},{6,8},{8,10},{10,12},{12,14},{14,16},{16,18},{18... | collective-permute-start | bytes 1966088 | tf_op jit(solution)/shard_map/ppermute | solution.py:21
  43.4 7.7 %collective-permute-start.7 = (bf16[128,1280]{1,0:T(8,128)(2,1)S(1)}, bf16[128,1280]{1,0:T(8,128)(2,1)S(1)}, u32[]{:S(2)}, u32[]{:S(2)}) collective-permute-start(bf16[128,1280]{1,0:T(8,128)(2,1)S(1)} %collective-permute-done.6.refs_2_), channel_id=1, source_target_pairs={{0,1},{1,0},{2,3},{3,2},{4,5},{5,4},{6,7},{7,6},{8,9},{9,8},{10,11... | collective-permute-start | bytes 983048 | tf_op jit(solution)/shard_map/ppermute | solution.py:25
  49.4 8.7 %collective-permute-start.10 = (bf16[128,1280]{1,0:T(8,128)(2,1)S(1)}, bf16[128,1280]{1,0:T(8,128)(2,1)S(1)}, u32[]{:S(2)}, u32[]{:S(2)}) collective-permute-start(bf16[128,1280]{1,0:T(8,128)(2,1)S(1)} %collective-permute-done.8.refs_3_), channel_id=1, source_target_pairs={{0,1},{1,0},{2,3},{3,2},{4,5},{5,4},{6,7},{7,6},{8,9},{9,8},{10,11... | collective-permute-start | bytes 983048 | tf_op jit(solution)/shard_map/ppermute | solution.py:25
  58.6 14.3 %copy-start.8 = (bf16[2,128,1280]{2,1,0:T(8,128)(2,1)}, bf16[2,128,1280]{2,1,0:T(8,128)(2,1)S(1)}, u32[]{:S(2)}) copy-start(bf16[2,128,1280]{2,1,0:T(8,128)(2,1)S(1)} %collective-permute-done.12.kv1_ref) | copy-start | bytes 1966084
  58.6 9.7 %collective-permute-start.13 = (bf16[4,160,640]{2,1,0:T(8,128)(2,1)S(1)}, bf16[4,160,640]{2,1,0:T(8,128)(2,1)S(1)}, u32[]{:S(2)}, u32[]{:S(2)}) collective-permute-start(bf16[4,160,640]{2,1,0:T(8,128)(2,1)S(1)} %collective-permute-done.4.refs_10_), channel_id=1, source_target_pairs={{0,2},{2,0},{4,6},{6,4},{1,3},{3,1},{5,7},{7,5},{8,10},{10,8},{12,... | collective-permute-start | bytes 2457608 | tf_op jit(solution)/shard_map/ppermute | solution.py:25
  58.6 15.6 %collective-permute-start.15 = (bf16[2,128,1280]{2,1,0:T(8,128)(2,1)S(1)}, bf16[2,128,1280]{2,1,0:T(8,128)(2,1)}, u32[]{:S(2)}, u32[]{:S(2)}) collective-permute-start(bf16[2,128,1280]{2,1,0:T(8,128)(2,1)S(1)} %get-tuple-element.39), channel_id=1, source_target_pairs={{2,0},{4,2},{6,4},{8,6},{10,8},{12,10},{14,12},{16,14},{18,16},{20... | collective-permute-start | bytes 1966088 | tf_op jit(solution)/shard_map/ppermute | solution.py:21
  66.1 12.8 %collective-permute-start.14 = (bf16[2,128,1280]{2,1,0:T(8,128)(2,1)S(1)}, bf16[2,128,1280]{2,1,0:T(8,128)(2,1)S(1)}, u32[]{:S(2)}, u32[]{:S(2)}) collective-permute-start(bf16[2,128,1280]{2,1,0:T(8,128)(2,1)S(1)} %collective-permute-done.12.kv1_ref), channel_id=1, source_target_pairs={{0,2},{2,4},{4,6},{6,8},{8,10},{10,12},{12,14},{14,16},{16,18},{18... | collective-permute-start | bytes 1966088 | tf_op jit(solution)/shard_map/ppermute | solution.py:21
  68.3 4.6 %copy-start.5 = (bf16[128,640]{1,0:T(8,128)(2,1)}, bf16[128,640]{1,0:T(8,128)(2,1)S(1)}, u32[]{:S(2)}) copy-start(bf16[128,640]{1,0:T(8,128)(2,1)S(1)} %get-tuple-element.42.bias_ref) | copy-start | bytes 491524
  78.9 0.9 copy-start.9
  79.8 40.2 %all-to-all-start = ((bf16[16,4,16,640]{3,2,1,0:T(8,128)(2,1)}), bf16[16,4,16,640]{3,2,1,0:T(8,128)(2,1)S(1)}, u32[]{:S(2)}, u32[]{:S(2)}) async-start(bf16[16,4,16,640]{3,2,1,0:T(8,128)(2,1)} %project.1), calls=%async_computation | async-start | bytes 2621440 | tf_op jit(solution)/shard_map/all_to_all | solution.py:405
  89.1 40.8 %collective-permute-start.16 = (bf16[2,128,1280]{2,1,0:T(8,128)(2,1)}, bf16[2,128,1280]{2,1,0:T(8,128)(2,1)S(1)}, u32[]{:S(2)}, u32[]{:S(2)}) collective-permute-start(bf16[2,128,1280]{2,1,0:T(8,128)(2,1)} %collective-permute-done.15.qg1_ref), channel_id=1, source_target_pairs={{2,0},{4,2},{6,4},{8,6},{10,8},{12,10},{14,12},{16,14},{18,16},{20... | collective-permute-start | bytes 1966088 | tf_op jit(solution)/shard_map/ppermute | solution.py:21
  125.0 5.0 %collective-permute-start.17 = (f32[2,16,128]{2,1,0:T(8,128)S(1)}, f32[2,16,128]{2,1,0:T(8,128)S(1)}, u32[]{:S(2)}, u32[]{:S(2)}) collective-permute-start(f32[2,16,128]{2,1,0:T(8,128)S(1)} %get-tuple-element.46.st0_ref), channel_id=1, source_target_pairs={{2,0},{4,2},{6,4},{8,6},{10,8},{12,10},{14,12},{16,14},{18,16},{20... | collective-permute-start | bytes 49160 | tf_op jit(solution)/shard_map/ppermute | solution.py:21
  127.9 5.6 %collective-permute-start.18 = (f32[2,16,128]{2,1,0:T(8,128)S(1)}, f32[2,16,128]{2,1,0:T(8,128)S(1)}, u32[]{:S(2)}, u32[]{:S(2)}) collective-permute-start(f32[2,16,128]{2,1,0:T(8,128)S(1)} %get-tuple-element.46.st0_ref), channel_id=1, source_target_pairs={{4,0},{6,2},{8,4},{10,6},{12,8},{14,10},{16,12},{18,14},{20,16},{2... | collective-permute-start | bytes 49160 | tf_op jit(solution)/shard_map/ppermute | solution.py:21
